TPU v7x, 32 devices: a whole 2x2x4 slice. The times are simulated.
32 devices in a mesh: groups: 2 (over y), feat: 4 (over z), layer: 2 (over x), tok: 2 (over core).
Axes of the slice: x: 2, y: 2, z: 4, core: 2. Of those that a mesh axis runs over, the one named last changes fastest.
Arguments:
- residual_in: float32 [256, 2, 1792], P('groups', 'tok', 'feat'), parts along dimension 0, may hold values from -6 to 6
- attn_scale: float32 [2, 256], P('layer', 'groups'), parts along dimension 1, may hold values from 0.4 to 2.5
- mlp_scale: float32 [2, 256], P('layer', 'groups'), parts along dimension 1, may hold values from 0.4 to 2.5
- patterns: bfloat16 [2, 8, 4, 64, 64], P('layer', None, 'groups'), parts along dimension 2, may hold values from 0.0029907227 to 0.059814453
- lengths: int32 [4], P('groups'), parts along dimension 0, may hold values from 16 to 64
- value_proj: bfloat16 [2, 2, 1792, 1024], P('layer', 'tok', None, 'feat'), may hold values from -0.09375 to 0.09375
- out_proj: bfloat16 [2, 4, 256, 2, 2, 1792], P('layer', None, None, None, 'tok', 'feat'), may hold values from -0.125 to 0.125
- enc_weight: bfloat16 [2, 2, 1792, 512], P('layer', 'tok', None, 'feat'), may hold values from -0.09375 to 0.09375
- enc_bias: float32 [2, 512], P('layer', 'feat'), may hold values from -3 to 3
- dec_weight: bfloat16 [2, 2, 512, 2, 1792], P('layer', None, None, 'tok', 'feat'), may hold values from -0.25 to 0.25
- errors: float32 [2, 256, 2, 1792], P('layer', 'groups', 'tok', 'feat'), parts along dimension 1, may hold values from -4 to 4
- clamp_mode: int32 [2, 16384], P('layer', 'feat'), may hold values from 0 to 2
- clamp_index: int32 [2, 16384], P('layer', 'feat'), may hold values from 0 to 63
- clamp_values: float32 [64], replicated, may hold values from 0.25 to 3
- active_blocks: int32 [2, 4], P('layer', 'feat'), may hold values from 0 to 31
Outputs:
- residual_out: float32 [2, 256, 2, 1792], P('layer', 'groups', 'tok', 'feat'), parts along dimension 1
- features: bfloat16 [2, 256, 512], P('layer', 'groups', 'feat'), parts along dimension 1
There are 2 independent parts, one for each index of `groups`. A program takes and returns all parts, laid end to end along the dimension named above; an argument that names none is the same for every part. Nothing has to cross between parts.
Inputs may be any that keep to these rules, and one draw needn't show every extreme that they name: `clamp_mode`: 0 leaves a feature free, 1 sets it to its table value, 2 multiplies it by its table value. `lengths`: positions at or past a prompt's length are padding.
All inputs are finite; a program needn't handle non-finite values.
Results may differ from a plain program's by a relative error of at most 0.018.
Values may be sent and summed in bfloat16 or wider, within the bound.
No kernel may reach another device: no remote copies, remote signals or barrier semaphores. Data moves between devices by JAX's collectives and lax.ppermute only.
A program may use at most 64 MiB of HBM per device.

v0:
```python
import jax
import jax.numpy as jnp
from jax import lax
from jax.sharding import PartitionSpec as P


def passed_along(value, axis, steps):
    count = lax.axis_size(axis)
    initial, last = (max(0, -steps), min(count, count - steps))
    return lax.ppermute(value, axis, [(source, source + steps) for source in range(initial, last)])


def columns(normed_rows):
    return lax.all_gather(normed_rows, "feat", axis=1, tiled=True)


def halves(partial_sum):
    return lax.psum(partial_sum, "tok")


def pick_block(lookup_table, chosen, block_len):
    shaped = lookup_table.reshape(-1, block_len)
    return lax.dynamic_slice_in_dim(shaped, chosen, 1, 0)[0]


def local(
    residual_in,
    attn_scale,
    mlp_scale,
    patterns,
    lengths,
    value_proj,
    out_proj,
    enc_weight,
    enc_bias,
    dec_weight,
    errors,
    clamp_mode,
    clamp_index,
    clamp_values,
    active_blocks,
):
    layer_count = lax.axis_size("layer")
    my_layer = lax.axis_index("layer")
    my_range = lax.axis_index("feat")
    seq_len = patterns.shape[3]
    prompt_count = patterns.shape[2]
    head_dim = out_proj.shape[2]
    per_group = out_proj.shape[3]
    kv_cols = value_proj.shape[3]
    width_cols = residual_in.shape[2]
    block_len = enc_bias.shape[1]
    total_rows = residual_in.shape[0]
    split_count = 1
    block_rows = seq_len // split_count
    micro_count = prompt_count * split_count
    section_count = layer_count + micro_count - 1
    source_rows = residual_in[:, 0, :]
    error_rows = errors[0, :, 0, :]
    value_weight = value_proj[0, 0]
    out_weight = out_proj[0].reshape(-1, width_cols)
    enc_rows = enc_weight[0, 0]
    enc_shift = enc_bias[0]
    dec_rows = dec_weight[0, :, :, 0, :]
    chosen = active_blocks[0, 0]
    modes = pick_block(clamp_mode[0], chosen, block_len)
    table_pick = pick_block(clamp_index[0], chosen, block_len)
    table_ids = jnp.arange(clamp_values.shape[0], dtype=jnp.int32)
    levels = jnp.sum(
        jnp.where(table_pick[:, None] == table_ids[None, :], clamp_values[None, :], 0.0), axis=1
    )
    group_id = my_range * kv_cols // head_dim
    group_pat = lax.dynamic_slice_in_dim(patterns[0], group_id * per_group, per_group, 0)
    positions = jnp.arange(seq_len, dtype=jnp.int32)
    scale_attn = attn_scale[0]
    scale_mlp = mlp_scale[0]

    def add_heads(piece):
        return jnp.dot(piece, out_weight, preferred_element_type=jnp.float32)

    def add_writes(piece):
        return jnp.einsum("rf,tfc->trc", piece, dec_rows, preferred_element_type=jnp.float32)

    def section(step_num, carry):
        recv_rows, links, value_cache, kept_rows, kept_feats = carry
        micro_raw = step_num - my_layer
        is_live = (micro_raw >= 0) & (micro_raw < micro_count)
        micro_num = jnp.clip(micro_raw, 0, micro_count - 1)
        prompt_num = micro_num // split_count
        block_num = micro_num % split_count
        first_row = micro_num * block_rows
        first_pos = block_num * block_rows
        start_rows = lax.dynamic_slice_in_dim(source_rows, first_row, block_rows, 0)
        rows_in = jnp.where(my_layer == 0, start_rows, recv_rows)
        row_attn = lax.dynamic_slice_in_dim(scale_attn, first_row, block_rows, 0)
        normed = (rows_in * row_attn[:, None]).astype(jnp.bfloat16)
        values = halves(
            jnp.dot(columns(normed), value_weight, preferred_element_type=jnp.float32)
        ).astype(jnp.bfloat16)
        value_cache = values
        query_pos = first_pos + jnp.arange(block_rows, dtype=jnp.int32)
        prompt_len = lax.dynamic_index_in_dim(lengths, prompt_num, 0, keepdims=False)
        keep_keys = (positions[None, :] <= query_pos[:, None]) & (positions[None, :] < prompt_len)
        block_pat = lax.dynamic_slice(
            group_pat, (0, prompt_num, first_pos, 0), (per_group, 1, block_rows, seq_len)
        )[:, 0]
        block_pat = jnp.where(keep_keys[None], block_pat, jnp.zeros_like(block_pat))
        head_out = (
            jnp.einsum("uqk,kc->qcu", block_pat, value_cache, preferred_element_type=jnp.float32)
            .astype(jnp.bfloat16)
            .reshape(block_rows, -1)
        )
        attention = add_heads(lax.all_gather(head_out, "feat", axis=1, tiled=True))
        middle = rows_in + attention
        row_mlp = lax.dynamic_slice_in_dim(scale_mlp, first_row, block_rows, 0)
        normed_mlp = (middle * row_mlp[:, None]).astype(jnp.bfloat16)
        preact = (
            halves(jnp.dot(columns(normed_mlp), enc_rows, preferred_element_type=jnp.float32))
            + enc_shift
        )
        active = jnp.maximum(preact, 0.0)
        clamped = jnp.where(modes == 1, levels, jnp.where(modes == 2, active * levels, active))
        live_rows = query_pos < prompt_len
        block_feats = jnp.where(live_rows[:, None], clamped, 0.0).astype(jnp.bfloat16)
        writes = add_writes(lax.all_gather(block_feats, "feat", axis=1, tiled=True))
        error_block = lax.dynamic_slice_in_dim(error_rows, first_row, block_rows, 0)
        acc_in = jnp.where(my_layer == 0, jnp.zeros_like(links), links)
        running = acc_in + writes
        recon = lax.dynamic_index_in_dim(running, my_layer, 0, keepdims=False)
        rows_next = middle + recon + error_block
        recv_rows, links = passed_along((rows_next, running), "layer", 1)
        old_rows = lax.dynamic_slice_in_dim(kept_rows, first_row, block_rows, 0)
        kept_rows = lax.dynamic_update_slice_in_dim(
            kept_rows, jnp.where(is_live, rows_next, old_rows), first_row, 0
        )
        old_feats = lax.dynamic_slice_in_dim(kept_feats, first_row, block_rows, 0)
        kept_feats = lax.dynamic_update_slice_in_dim(
            kept_feats, jnp.where(is_live, block_feats, old_feats), first_row, 0
        )
        return (recv_rows, links, value_cache, kept_rows, kept_feats)

    link_start = jnp.zeros((layer_count, block_rows, width_cols), jnp.float32)
    initial = (
        jnp.zeros((block_rows, width_cols), jnp.float32),
        link_start,
        jnp.zeros((seq_len, kv_cols), jnp.bfloat16),
        jnp.zeros((total_rows, width_cols), jnp.float32),
        jnp.zeros((total_rows, block_len), jnp.bfloat16),
    )
    final = lax.fori_loop(0, section_count, section, initial)
    return (final[3][None, :, None, :], final[4][None])


def solution(mesh):
    return jax.shard_map(
        local,
        mesh=mesh,
        in_specs=(
            P("groups", "tok", "feat"),
            P("layer", "groups"),
            P("layer", "groups"),
            P("layer", None, "groups", None, None),
            P("groups"),
            P("layer", "tok", None, "feat"),
            P("layer", None, None, None, "tok", "feat"),
            P("layer", "tok", None, "feat"),
            P("layer", "feat"),
            P("layer", None, None, "tok", "feat"),
            P("layer", "groups", "tok", "feat"),
            P("layer", "feat"),
            P("layer", "feat"),
            P(),
            P("layer", "feat"),
        ),
        out_specs=(P("layer", "groups", "tok", "feat"), P("layer", "groups", "feat")),
        check_vma=False,
    )
```

profile of v0, /device:TPU:0, one launch (start us, length us, event | category | flops | bytes accessed | tf_op | source)
XLA Modules:
  0.0 265.2 jit_solution(8046609144955655287)
XLA Ops:
  3.7 6.1 %copy.43 = bf16[1,4,256,2,1,448]{5,3,2,1,4,0:T(2,128)(2,1)} copy(bf16[1,4,256,2,1,448]{2,5,4,3,1,0:T(8,128)(2,1)} %param.23) | data formatting | bytes 3670016 | tf_op args[6]
  9.9 3.5 %reshape_squeeze.9 = bf16[2048,448]{1,0:T(8,128)(2,1)S(1)} reshape(bf16[1,4,256,2,1,448]{5,3,2,1,4,0:T(2,128)(2,1)} %copy.43) | data formatting | bytes 3670016 | tf_op jit(solution)/shard_map/reshape;squeeze | solution.py:61
  15.9 247.6 %while.23 = (s32[]{:T(128)}, f32[64,448]{1,0:T(8,128)S(1)}, f32[2,64,448]{2,1,0:T(8,128)}, f32[128,448]{1,0:T(8,128)}, bf16[128,128]{1,0:T(8,128)(2,1)S(1)}, /*i...) while((s32[]{:T(128)}, f32[64,448]{1,0:T(8,128)S(1)}, ...), condition=%wide.region_4.5_spmd.clone.clone, body=%wide.region_1.4_spmd.clone.clone.sunk | while | flops 268976448 | bytes 11732813 | solution.py:150
  16.1 15.6 %all-gather.6 = bf16[4,448,64]{1,2,0:T(8,128)(2,1)S(1)} all-gather(bf16[1,448,64]{1,2,0:T(8,128)(2,1)S(1)} %fusion.57), channel_id=1, replica_groups=mesh['groups'=2,'feat'=4,'layer'=2,'tok'=2] {'feat'}, dimensions={0}, use_global_device_ids=true | all-gather | bytes 286720 | tf_op jit(solution)/shard_map/while/body/eval_jaxpr/all_gather | solution.py:14
  33.6 3.6 %psum.34 = bf16[64,256]{1,0:T(8,128)(2,1)S(1)} all-reduce(f32[64,256]{1,0:T(8,128)S(1)} %fusion.58), channel_id=1, replica_groups=mesh['groups'=2,'feat'=4,'layer'=2,'tok'=2] {'tok'}, use_global_device_ids=true, to_apply=%region_2.2 | all-reduce | flops 16384 | bytes 98304 | tf_op jit(solution)/shard_map/while/body/eval_jaxpr/psum | solution.py:18
  38.9 16.6 %all_gather.48 = bf16[64,2048]{0,1:T(8,128)(2,1)S(1)} all-gather(bf16[64,512]{0,1:T(8,128)(2,1)S(1)} %bitcast.101), channel_id=1, replica_groups=mesh['groups'=2,'feat'=4,'layer'=2,'tok'=2] {'feat'}, dimensions={1}, use_global_device_ids=true | all-gather | bytes 327680 | tf_op jit(solution)/shard_map/while/body/eval_jaxpr/all_gather | solution.py:113
  56.2 14.3 %all-gather.7 = bf16[4,448,64]{1,2,0:T(8,128)(2,1)S(1)} all-gather(bf16[1,448,64]{1,2,0:T(8,128)(2,1)S(1)} %fusion.61), channel_id=1, replica_groups=mesh['groups'=2,'feat'=4,'layer'=2,'tok'=2] {'feat'}, dimensions={0}, use_global_device_ids=true | all-gather | bytes 286720 | tf_op jit(solution)/shard_map/while/body/eval_jaxpr/all_gather | solution.py:14
  72.2 3.4 %psum.35 = f32[64,128]{1,0:T(8,128)S(1)} all-reduce(f32[64,128]{1,0:T(8,128)S(1)} %fusion.62), channel_id=1, replica_groups=mesh['groups'=2,'feat'=4,'layer'=2,'tok'=2] {'tok'}, use_global_device_ids=true, to_apply=%region_3.3 | all-reduce | flops 8192 | bytes 65536 | tf_op jit(solution)/shard_map/while/body/eval_jaxpr/psum | solution.py:18
  75.8 12.0 %all_gather.49 = bf16[64,512]{1,0:T(8,128)(2,1)S(1)} all-gather(bf16[64,128]{1,0:T(8,128)(2,1)S(1)} %get-tuple-element.762), channel_id=1, replica_groups=mesh['groups'=2,'feat'=4,'layer'=2,'tok'=2] {'feat'}, dimensions={1}, use_global_device_ids=true | all-gather | bytes 81920 | tf_op jit(solution)/shard_map/while/body/eval_jaxpr/all_gather | solution.py:125
  87.8 1.6 fusion.63
  89.3 4.2 %collective-permute-start.1 = (f32[2,64,448]{2,1,0:T(8,128)S(1)}, f32[2,64,448]{2,1,0:T(8,128)}, u32[]{:S(2)}, u32[]{:S(2)}) collective-permute-start(f32[2,64,448]{2,1,0:T(8,128)S(1)} %fusion.63), channel_id=1, source_target_pairs={{0,2},{1,3},{4,6},{5,7},{8,10},{9,11},{12,14},{13,15},{16,18},{17,... | collective-permute-start | bytes 688136 | tf_op jit(solution)/shard_map/while/body/eval_jaxpr/ppermute | solution.py:10
  93.5 1.6 select_dynamic-update-slice_fusion.5
  96.4 3.0 %collective-permute-done = f32[64,448]{1,0:T(8,128)S(1)} collective-permute-done((f32[64,448]{1,0:T(8,128)S(1)}, f32[64,448]{1,0:T(8,128)S(1)}, u32[]{:S(2)}, u32[]{:S(2)}) %collective-permute-start) | collective-permute-done | bytes 114720 | tf_op jit(solution)/shard_map/while/body/eval_jaxpr/ppermute | solution.py:10
  99.6 14.3 %all-gather.6 = bf16[4,448,64]{1,2,0:T(8,128)(2,1)S(1)} all-gather(bf16[1,448,64]{1,2,0:T(8,128)(2,1)S(1)} %fusion.57), channel_id=1, replica_groups=mesh['groups'=2,'feat'=4,'layer'=2,'tok'=2] {'feat'}, dimensions={0}, use_global_device_ids=true | all-gather | bytes 286720 | tf_op jit(solution)/shard_map/while/body/eval_jaxpr/all_gather | solution.py:14
  115.9 3.6 %psum.34 = bf16[64,256]{1,0:T(8,128)(2,1)S(1)} all-reduce(f32[64,256]{1,0:T(8,128)S(1)} %fusion.58), channel_id=1, replica_groups=mesh['groups'=2,'feat'=4,'layer'=2,'tok'=2] {'tok'}, use_global_device_ids=true, to_apply=%region_2.2 | all-reduce | flops 16384 | bytes 98304 | tf_op jit(solution)/shard_map/while/body/eval_jaxpr/psum | solution.py:18
  121.1 16.2 %all_gather.48 = bf16[64,2048]{0,1:T(8,128)(2,1)S(1)} all-gather(bf16[64,512]{0,1:T(8,128)(2,1)S(1)} %bitcast.101), channel_id=1, replica_groups=mesh['groups'=2,'feat'=4,'layer'=2,'tok'=2] {'feat'}, dimensions={1}, use_global_device_ids=true | all-gather | bytes 327680 | tf_op jit(solution)/shard_map/while/body/eval_jaxpr/all_gather | solution.py:113
  138.0 13.8 %all-gather.7 = bf16[4,448,64]{1,2,0:T(8,128)(2,1)S(1)} all-gather(bf16[1,448,64]{1,2,0:T(8,128)(2,1)S(1)} %fusion.61), channel_id=1, replica_groups=mesh['groups'=2,'feat'=4,'layer'=2,'tok'=2] {'feat'}, dimensions={0}, use_global_device_ids=true | all-gather | bytes 286720 | tf_op jit(solution)/shard_map/while/body/eval_jaxpr/all_gather | solution.py:14
  153.6 3.4 %psum.35 = f32[64,128]{1,0:T(8,128)S(1)} all-reduce(f32[64,128]{1,0:T(8,128)S(1)} %fusion.62), channel_id=1, replica_groups=mesh['groups'=2,'feat'=4,'layer'=2,'tok'=2] {'tok'}, use_global_device_ids=true, to_apply=%region_3.3 | all-reduce | flops 8192 | bytes 65536 | tf_op jit(solution)/shard_map/while/body/eval_jaxpr/psum | solution.py:18
  157.1 12.0 %all_gather.49 = bf16[64,512]{1,0:T(8,128)(2,1)S(1)} all-gather(bf16[64,128]{1,0:T(8,128)(2,1)S(1)} %get-tuple-element.762), channel_id=1, replica_groups=mesh['groups'=2,'feat'=4,'layer'=2,'tok'=2] {'feat'}, dimensions={1}, use_global_device_ids=true | all-gather | bytes 81920 | tf_op jit(solution)/shard_map/while/body/eval_jaxpr/all_gather | solution.py:125
  170.7 4.9 %collective-permute-start.1 = (f32[2,64,448]{2,1,0:T(8,128)S(1)}, f32[2,64,448]{2,1,0:T(8,128)}, u32[]{:S(2)}, u32[]{:S(2)}) collective-permute-start(f32[2,64,448]{2,1,0:T(8,128)S(1)} %fusion.63), channel_id=1, source_target_pairs={{0,2},{1,3},{4,6},{5,7},{8,10},{9,11},{12,14},{13,15},{16,18},{17,... | collective-permute-start | bytes 688136 | tf_op jit(solution)/shard_map/while/body/eval_jaxpr/ppermute | solution.py:10
  175.6 1.7 select_dynamic-update-slice_fusion.5
  178.6 3.0 %collective-permute-done = f32[64,448]{1,0:T(8,128)S(1)} collective-permute-done((f32[64,448]{1,0:T(8,128)S(1)}, f32[64,448]{1,0:T(8,128)S(1)}, u32[]{:S(2)}, u32[]{:S(2)}) %collective-permute-start) | collective-permute-done | bytes 114720 | tf_op jit(solution)/shard_map/while/body/eval_jaxpr/ppermute | solution.py:10
  181.8 13.8 %all-gather.6 = bf16[4,448,64]{1,2,0:T(8,128)(2,1)S(1)} all-gather(bf16[1,448,64]{1,2,0:T(8,128)(2,1)S(1)} %fusion.57), channel_id=1, replica_groups=mesh['groups'=2,'feat'=4,'layer'=2,'tok'=2] {'feat'}, dimensions={0}, use_global_device_ids=true | all-gather | bytes 286720 | tf_op jit(solution)/shard_map/while/body/eval_jaxpr/all_gather | solution.py:14
  197.5 3.6 %psum.34 = bf16[64,256]{1,0:T(8,128)(2,1)S(1)} all-reduce(f32[64,256]{1,0:T(8,128)S(1)} %fusion.58), channel_id=1, replica_groups=mesh['groups'=2,'feat'=4,'layer'=2,'tok'=2] {'tok'}, use_global_device_ids=true, to_apply=%region_2.2 | all-reduce | flops 16384 | bytes 98304 | tf_op jit(solution)/shard_map/while/body/eval_jaxpr/psum | solution.py:18
  202.8 16.1 %all_gather.48 = bf16[64,2048]{0,1:T(8,128)(2,1)S(1)} all-gather(bf16[64,512]{0,1:T(8,128)(2,1)S(1)} %bitcast.101), channel_id=1, replica_groups=mesh['groups'=2,'feat'=4,'layer'=2,'tok'=2] {'feat'}, dimensions={1}, use_global_device_ids=true | all-gather | bytes 327680 | tf_op jit(solution)/shard_map/while/body/eval_jaxpr/all_gather | solution.py:113
  219.6 13.9 %all-gather.7 = bf16[4,448,64]{1,2,0:T(8,128)(2,1)S(1)} all-gather(bf16[1,448,64]{1,2,0:T(8,128)(2,1)S(1)} %fusion.61), channel_id=1, replica_groups=mesh['groups'=2,'feat'=4,'layer'=2,'tok'=2] {'feat'}, dimensions={0}, use_global_device_ids=true | all-gather | bytes 286720 | tf_op jit(solution)/shard_map/while/body/eval_jaxpr/all_gather | solution.py:14
  235.1 3.4 %psum.35 = f32[64,128]{1,0:T(8,128)S(1)} all-reduce(f32[64,128]{1,0:T(8,128)S(1)} %fusion.62), channel_id=1, replica_groups=mesh['groups'=2,'feat'=4,'layer'=2,'tok'=2] {'tok'}, use_global_device_ids=true, to_apply=%region_3.3 | all-reduce | flops 8192 | bytes 65536 | tf_op jit(solution)/shard_map/while/body/eval_jaxpr/psum | solution.py:18
  238.7 12.1 %all_gather.49 = bf16[64,512]{1,0:T(8,128)(2,1)S(1)} all-gather(bf16[64,128]{1,0:T(8,128)(2,1)S(1)} %get-tuple-element.762), channel_id=1, replica_groups=mesh['groups'=2,'feat'=4,'layer'=2,'tok'=2] {'feat'}, dimensions={1}, use_global_device_ids=true | all-gather | bytes 81920 | tf_op jit(solution)/shard_map/while/body/eval_jaxpr/all_gather | solution.py:125
  252.3 5.1 %collective-permute-start.1 = (f32[2,64,448]{2,1,0:T(8,128)S(1)}, f32[2,64,448]{2,1,0:T(8,128)}, u32[]{:S(2)}, u32[]{:S(2)}) collective-permute-start(f32[2,64,448]{2,1,0:T(8,128)S(1)} %fusion.63), channel_id=1, source_target_pairs={{0,2},{1,3},{4,6},{5,7},{8,10},{9,11},{12,14},{13,15},{16,18},{17,... | collective-permute-start | bytes 688136 | tf_op jit(solution)/shard_map/while/body/eval_jaxpr/ppermute | solution.py:10
  257.4 1.7 select_dynamic-update-slice_fusion.5
  260.4 3.0 %collective-permute-done = f32[64,448]{1,0:T(8,128)S(1)} collective-permute-done((f32[64,448]{1,0:T(8,128)S(1)}, f32[64,448]{1,0:T(8,128)S(1)}, u32[]{:S(2)}, u32[]{:S(2)}) %collective-permute-start) | collective-permute-done | bytes 114720 | tf_op jit(solution)/shard_map/while/body/eval_jaxpr/ppermute | solution.py:10
  263.4 1.8 copy.45
  (87 shorter events, 30.2 us)
Async XLA Ops:
  0.6 1.0 copy-start
  9.8 3.5 %copy-start.2 = (f32[128,1,448]{0,2,1:T(8,128)S(1)}, f32[128,1,448]{0,2,1:T(8,128)}, u32[]{:S(2)}) copy-start(f32[128,1,448]{0,2,1:T(8,128)} %param.17) | copy-start | bytes 688132
  9.8 3.7 %copy-start.3 = (f32[1,128,1,448]{1,3,2,0:T(8,128)S(1)}, f32[1,128,1,448]{1,3,2,0:T(8,128)}, u32[]{:S(2)}) copy-start(f32[1,128,1,448]{1,3,2,0:T(8,128)} %param.27) | copy-start | bytes 688132
  9.8 6.0 %copy-start.4 = (f32[1,128]{1,0:T(1,128)S(1)}, f32[1,128]{1,0:T(1,128)}, u32[]{:S(2)}) copy-start(f32[1,128]{1,0:T(1,128)} %param.25) | copy-start | bytes 1540
  9.8 6.0 %copy-start.5 = (f32[1,128]{1,0:T(1,128)S(1)}, f32[1,128]{1,0:T(1,128)}, u32[]{:S(2)}) copy-start(f32[1,128]{1,0:T(1,128)} %param.18) | copy-start | bytes 1540
  9.9 6.0 %copy-start.6 = (s32[2]{0:T(128)S(1)}, s32[2]{0:T(128)}, u32[]{:S(2)}) copy-start(s32[2]{0:T(128)} %param.21) | copy-start | bytes 28
  9.9 6.0 %copy-start.7 = (f32[1,128]{1,0:T(1,128)S(1)}, f32[1,128]{1,0:T(1,128)}, u32[]{:S(2)}) copy-start(f32[1,128]{1,0:T(1,128)} %param.19) | copy-start | bytes 1540
  89.3 10.1 %collective-permute-start.1 = (f32[2,64,448]{2,1,0:T(8,128)S(1)}, f32[2,64,448]{2,1,0:T(8,128)}, u32[]{:S(2)}, u32[]{:S(2)}) collective-permute-start(f32[2,64,448]{2,1,0:T(8,128)S(1)} %fusion.63), channel_id=1, source_target_pairs={{0,2},{1,3},{4,6},{5,7},{8,10},{9,11},{12,14},{13,15},{16,18},{17,... | collective-permute-start | bytes 688136 | tf_op jit(solution)/shard_map/while/body/eval_jaxpr/ppermute | solution.py:10
  95.1 4.3 %collective-permute-start = (f32[64,448]{1,0:T(8,128)S(1)}, f32[64,448]{1,0:T(8,128)S(1)}, u32[]{:S(2)}, u32[]{:S(2)}) collective-permute-start(f32[64,448]{1,0:T(8,128)S(1)} %get-tuple-element.763), channel_id=1, source_target_pairs={{0,2},{1,3},{4,6},{5,7},{8,10},{9,11},{12,14},{13,15},{16,18},{17,... | collective-permute-start | bytes 344072 | tf_op jit(solution)/shard_map/while/body/eval_jaxpr/ppermute | solution.py:10
  170.7 10.9 %collective-permute-start.1 = (f32[2,64,448]{2,1,0:T(8,128)S(1)}, f32[2,64,448]{2,1,0:T(8,128)}, u32[]{:S(2)}, u32[]{:S(2)}) collective-permute-start(f32[2,64,448]{2,1,0:T(8,128)S(1)} %fusion.63), channel_id=1, source_target_pairs={{0,2},{1,3},{4,6},{5,7},{8,10},{9,11},{12,14},{13,15},{16,18},{17,... | collective-permute-start | bytes 688136 | tf_op jit(solution)/shard_map/while/body/eval_jaxpr/ppermute | solution.py:10
  177.3 4.3 %collective-permute-start = (f32[64,448]{1,0:T(8,128)S(1)}, f32[64,448]{1,0:T(8,128)S(1)}, u32[]{:S(2)}, u32[]{:S(2)}) collective-permute-start(f32[64,448]{1,0:T(8,128)S(1)} %get-tuple-element.763), channel_id=1, source_target_pairs={{0,2},{1,3},{4,6},{5,7},{8,10},{9,11},{12,14},{13,15},{16,18},{17,... | collective-permute-start | bytes 344072 | tf_op jit(solution)/shard_map/while/body/eval_jaxpr/ppermute | solution.py:10
  252.3 11.1 %collective-permute-start.1 = (f32[2,64,448]{2,1,0:T(8,128)S(1)}, f32[2,64,448]{2,1,0:T(8,128)}, u32[]{:S(2)}, u32[]{:S(2)}) collective-permute-start(f32[2,64,448]{2,1,0:T(8,128)S(1)} %fusion.63), channel_id=1, source_target_pairs={{0,2},{1,3},{4,6},{5,7},{8,10},{9,11},{12,14},{13,15},{16,18},{17,... | collective-permute-start | bytes 688136 | tf_op jit(solution)/shard_map/while/body/eval_jaxpr/ppermute | solution.py:10
  259.1 4.3 %collective-permute-start = (f32[64,448]{1,0:T(8,128)S(1)}, f32[64,448]{1,0:T(8,128)S(1)}, u32[]{:S(2)}, u32[]{:S(2)}) collective-permute-start(f32[64,448]{1,0:T(8,128)S(1)} %get-tuple-element.763), channel_id=1, source_target_pairs={{0,2},{1,3},{4,6},{5,7},{8,10},{9,11},{12,14},{13,15},{16,18},{17,... | collective-permute-start | bytes 344072 | tf_op jit(solution)/shard_map/while/body/eval_jaxpr/ppermute | solution.py:10
  263.4 1.8 copy-start.1
where the time goes:
time: 266 us; the launch traced here: 265 us
  blocking collectives  192 us (72%)
  local copies, waits for them, and re-layouts  21.1 us (8%)
  starting transfers between devices  18.1 us (7%)
  matrix products  14.7 us (6%)
  waiting for transfers between devices  9.11 us (3%)
  other arithmetic  8.55 us (3%)
    all_gather x6, blocking collectives, columns(): return lax.all_gather(normed_rows, 'feat', axis=1, tiled=True)  85.8 us
    all_gather x3, blocking collectives, section(): attention = add_heads(lax.all_gather(head_out, 'feat', axis=1, tiled=True))  49 us
    all_gather x3, blocking collectives, section(): writes = add_writes(lax.all_gather(block_feats, 'feat', axis=1, tiled=True))  36.1 us
    psum x6, blocking collectives, halves(): return lax.psum(partial_sum, 'tok')  21.1 us
    ppermute x6, starting transfers between devices, passed_along(): lax.ppermute(value, axis, [(source, source + steps) for source in range(i...  18.1 us
    ppermute x6, waiting for transfers between devices, passed_along(): lax.ppermute(value, axis, [(source, source + steps) for source in range(i...  9.11 us
    unnamed x19, local copies, waits for them, and re-layouts  8.06 us
  transfers between devices with their start and end apart: 6, of which 3 were waited for; matrix products, arithmetic and copies ran while one was open for 2% of the time, Pallas kernels for 0%

commit v1 on v0

v1 whole, which is shorter than its diff:
```python
import jax
import jax.numpy as jnp
from jax import lax
from jax.sharding import PartitionSpec as P

BF16 = jnp.bfloat16
F32 = jnp.float32


def peers(axis):
    count = lax.axis_size(axis)
    return range(1, count)


def partner(index, step, count):
    if count & (count - 1) == 0:
        return index ^ step
    return (step - index) % count


def swap(value, axis, step, first_layer=0):
    count = lax.axis_size(axis)
    if first_layer == 0:
        return lax.ppermute(value, axis, [(s, partner(s, step, count)) for s in range(count)])
    layers = lax.axis_size("layer")
    pairs = [
        (s * layers + n, partner(s, step, count) * layers + n)
        for s in range(count)
        for n in range(first_layer, layers)
    ]
    return lax.ppermute(value, (axis, "layer"), pairs)


def spread(value, axis="feat"):
    return [value] + [swap(value, axis, step) for step in peers(axis)]


def total(blocks):
    result = blocks[0].astype(F32)
    for block in blocks[1:]:
        result = result + block.astype(F32)
    return result


def dot_tn(left, right):
    return lax.dot_general(left, right, (((0,), (0,)), ((), ())), preferred_element_type=F32)


def dot_nt(left, right):
    return lax.dot_general(left, right, (((1,), (1,)), ((), ())), preferred_element_type=F32)


def pick(array, index):
    return lax.dynamic_index_in_dim(array, index, 0, keepdims=False)


def redistribute(weight, ranges, my_range, first_layer):
    blocks = weight.reshape(ranges, -1, weight.shape[1])
    got = [pick(blocks, my_range)]
    for step in peers("feat"):
        other = partner(my_range, step, ranges)
        got.append(swap(pick(blocks, other), "feat", step, first_layer))
    got = jnp.stack(got)
    return [pick(got, partner(my_range, n, ranges)) for n in range(ranges)]


def local(
    residual_in,
    attn_scale,
    mlp_scale,
    patterns,
    lengths,
    value_proj,
    out_proj,
    enc_weight,
    enc_bias,
    dec_weight,
    errors,
    clamp_mode,
    clamp_index,
    clamp_values,
    active_blocks,
):
    layers = lax.axis_size("layer")
    ranges = lax.axis_size("feat")
    my_layer = lax.axis_index("layer")
    my_range = lax.axis_index("feat")
    my_slab = lax.axis_index("tok")
    prompts, seq = patterns.shape[2:4]
    head_dim, per_group = out_proj.shape[2:4]
    kv_cols = value_proj.shape[3]
    half = kv_cols // 2
    width = residual_in.shape[2]
    block_len = enc_bias.shape[1]
    act = block_len * ranges
    rows = residual_in.shape[0]

    source = residual_in[:, 0, :].T
    error_cols = errors[0, :, 0, :].T
    scale_attn = attn_scale[0]
    scale_mlp = mlp_scale[0]

    chosen = active_blocks[0, 0]
    modes = pick(clamp_mode[0].reshape(-1, block_len), chosen)
    entries = pick(clamp_index[0].reshape(-1, block_len), chosen)
    table_ids = jnp.arange(clamp_values.shape[0], dtype=jnp.int32)
    levels = jnp.sum(jnp.where(entries[:, None] == table_ids[None, :], clamp_values[None, :], 0.0), axis=1)
    gain = jnp.where(modes == 1, 0.0, jnp.where(modes == 2, levels, 1.0))
    shift = jnp.where(modes == 1, levels, 0.0)
    mine = jnp.stack([enc_bias[0], gain, shift])
    got = jnp.stack(spread(mine))
    clamp_all = jnp.stack([pick(got, partner(my_range, n, ranges)) for n in range(ranges)], axis=1).reshape(3, act)
    clamp_half = lax.dynamic_slice_in_dim(clamp_all, my_slab * (act // 2), act // 2, 1)

    positions = jnp.arange(seq, dtype=jnp.int32)
    keep = (positions[None, None, :] <= positions[None, :, None]) & (positions[None, None, :] < lengths[:, None, None])
    masked = jnp.where(keep[None], patterns[0], jnp.zeros_like(patterns[0]))
    zero = jnp.zeros_like(masked[:, 0])
    mixing = jnp.concatenate(
        [
            jnp.concatenate([masked[:, p] if q == p else zero for q in range(prompts)], axis=2)
            for p in range(prompts)
        ],
        axis=1,
    ).reshape(-1, per_group * rows, rows)
    live = (positions[None, :] < lengths[:, None]).reshape(rows)

    value_rows = value_proj[0, 0]
    own_value, other_value = (
        lax.dynamic_slice_in_dim(value_rows, n * half, half, 1) for n in (my_slab, 1 - my_slab)
    )
    shares = kv_cols * ranges // head_dim
    out_cols = out_proj[0, :, :, :, 0, :].reshape(shares, head_dim // kv_cols if kv_cols < head_dim else 1, 2, half, per_group, width)
    out_cols = out_cols.reshape(ranges, 2, half, per_group, width).transpose(1, 0, 4, 3, 2).reshape(2, ranges, width, per_group * half)
    out_own, out_other = (pick(out_cols, n) for n in (my_slab, 1 - my_slab))
    group_of = [n * kv_cols // head_dim for n in range(ranges)]

    enc_blocks = jnp.concatenate(redistribute(enc_weight[0, 0], ranges, my_range, 0), axis=1)
    enc_own, enc_other = (
        lax.dynamic_slice_in_dim(enc_blocks, n * (act // 2), act // 2, 1) for n in (my_slab, 1 - my_slab)
    )
    value_blocks = redistribute(value_rows, ranges, my_range, 1)
    spread_own, spread_other = (
        jnp.concatenate([lax.dynamic_slice_in_dim(b, n * half, half, 1) for b in value_blocks], axis=1)
        for n in (my_slab, 1 - my_slab)
    )
    dec_cols = dec_weight[0, :, :, 0, :].transpose(0, 2, 1)

    def over_slabs(own, other):
        return own + swap(other, "tok", 1).astype(F32)

    def heads(values, group):
        mixed = jnp.dot(mixing[group] if isinstance(group, int) else pick(mixing, group), values, preferred_element_type=F32)
        return mixed.astype(BF16).reshape(per_group, rows, -1).transpose(1, 0, 2).reshape(rows, -1)

    def first_attention(state):
        normed = (state * scale_attn[None, :]).astype(BF16)
        blocks = spread(normed)
        own_rows, other_rows = (w.reshape(ranges, width, half) for w in (own_value, other_value))
        order = [partner(my_range, n, ranges) if n else my_range for n in range(ranges)]
        other = sum(dot_tn(b, pick(other_rows, n)) for b, n in zip(blocks, order))
        own = sum(dot_tn(b, pick(own_rows, n)) for b, n in zip(blocks, order))
        values = over_slabs(own, other).astype(BF16)
        mine = heads(values, my_range * kv_cols // head_dim)
        got = spread(mine)
        also = [swap(b, "tok", 1) for b in got]
        return sum(
            dot_nt(pick(out_own, n), b) + dot_nt(pick(out_other, n), c) for n, b, c in zip(order, got, also)
        )

    def later_attention(state_low):
        other = dot_tn(state_low, spread_other).astype(BF16)
        own = dot_tn(state_low, spread_own)
        part = over_slabs(own, other).astype(BF16)
        mine = (total(spread(part)) * scale_attn[:, None]).astype(BF16)
        also = swap(mine, "tok", 1)
        result = 0.0
        for n in range(ranges):
            cols = slice(n * half, (n + 1) * half)
            result = (
                result
                + dot_nt(out_own[n], heads(mine[:, cols], group_of[n]))
                + dot_nt(out_other[n], heads(also[:, cols], group_of[n]))
            )
        return result

    def code(middle):
        normed = (middle * scale_mlp[None, :]).astype(BF16)
        other = dot_tn(normed, enc_other).astype(BF16)
        own = dot_tn(normed, enc_own)
        part = over_slabs(own, other).astype(BF16)
        preact = total(spread(part)) + clamp_half[0][None, :]
        clamped = jnp.maximum(preact, 0.0) * clamp_half[1][None, :] + clamp_half[2][None, :]
        mine = jnp.where(live[:, None], clamped, 0.0).astype(BF16)
        also = swap(mine, "tok", 1)
        return jnp.concatenate(
            [jnp.where(my_slab == 0, mine, also), jnp.where(my_slab == 0, also, mine)], axis=1
        )

    def handed_on(value, layer):
        return lax.ppermute(value, "layer", [(layer, layer + 1)])

    states = jnp.zeros_like(source)
    feats = jnp.zeros((rows, block_len), BF16)
    state, links = source, None
    for layer in range(layers):
        if layer == 0:
            middle = state + first_attention(state)
        else:
            middle = low.astype(F32) + later_attention(low) + rest.astype(F32)
        kept = code(middle)
        recon = dot_nt(dec_cols[layer], kept)
        base = middle + error_cols
        if layer > 0:
            base = base + links[0]
        state = base + recon
        states = jnp.where(my_layer == layer, state, states)
        feats = jnp.where(
            my_layer == layer, lax.dynamic_slice_in_dim(kept, my_range * block_len, block_len, 1), feats
        )
        if layer + 1 < layers:
            low = state.astype(BF16)
            left = (state - low.astype(F32)).astype(BF16)
            low = handed_on(low, layer)
            writes = jnp.stack([dot_nt(dec_cols[n], kept) for n in range(layer + 1, layers)])
            if layer > 0:
                writes = writes + links[1:]
            rest = handed_on(left, layer)
            links = handed_on(writes, layer)
    return states.T[None, :, None, :], feats[None]


def solution(mesh):
    return jax.shard_map(
        local,
        mesh=mesh,
        in_specs=(
            P("groups", "tok", "feat"),
            P("layer", "groups"),
            P("layer", "groups"),
            P("layer", None, "groups", None, None),
            P("groups"),
            P("layer", "tok", None, "feat"),
            P("layer", None, None, None, "tok", "feat"),
            P("layer", "tok", None, "feat"),
            P("layer", "feat"),
            P("layer", None, None, "tok", "feat"),
            P("layer", "groups", "tok", "feat"),
            P("layer", "feat"),
            P("layer", "feat"),
            P(),
            P("layer", "feat"),
        ),
        out_specs=(P("layer", "groups", "tok", "feat"), P("layer", "groups", "feat")),
        check_vma=False,
    )
```

time: 266 us -> 171 us (0.64)
  blocking collectives: 192 us -> 0 us
  starting transfers between devices: 18.1 us -> 66 us
  waiting for transfers between devices: 9.11 us -> 33.2 us
  matrix products: 14.7 us -> 31.5 us
  local copies, waits for them, and re-layouts: 21.1 us -> 26.9 us
    all_gather x12 -> x0, blocking collectives: 171 us -> none  [the longest x6 85.8 us: columns(): return lax.all_gather(normed_rows, 'feat', axis=1, tiled=True)]
    ppermute x6 -> x38, starting transfers between devices: 18.1 us -> 66 us  [the longest x32 37.8 us: swap(): lax.ppermute(value, axis, [(s, partner(s, step, count)) for s in range(co...]
    ppermute x6 -> x38, waiting for transfers between devices: 9.11 us -> 33.2 us  [the longest x32 27.2 us: swap(): lax.ppermute(value, axis, [(s, partner(s, step, count)) for s in range(co...]
    psum x6 -> x0, blocking collectives: 21.1 us -> none  [halves(): return lax.psum(partial_sum, 'tok')]
    dot_general x15 -> x41, matrix products: 14.7 us -> 31.5 us  [the longest x19 12.5 us: dot_nt(): lax.dot_general(left, right, (((1,), (1,)), ((), ())), preferred_element_...]
    reshape x0 -> x10, local copies, waits for them, and re-layouts: none -> 13.1 us  [the longest x9 8.72 us: heads(): mixed.astype(BF16).reshape(per_group, rows, -1).transpose(1, 0, 2)]
    unnamed x19 -> x72, local copies, waits for them, and re-layouts: 8.06 us -> 0.81 us
    dynamic_update_slice x6 -> x0, other arithmetic: 5.24 us -> none  [the longest x3 4.95 us: section(): lax.dynamic_update_slice_in_dim(kept_rows, jnp.where(is_live, rows_next,...]
  transfers between devices with their start and end apart: 6 -> 38, of which waited for: 3 -> 15; matrix products, arithmetic and copies ran while one was open for 2% -> 34% of each run, Pallas kernels for 0% -> 0%
where the time goes in v1:
time: 171 us; the launch traced here: 169 us
  starting transfers between devices  66 us (39%)
  waiting for transfers between devices  33.2 us (19%)
  matrix products  31.5 us (18%)
  local copies, waits for them, and re-layouts  26.9 us (16%)
  other arithmetic  9.23 us (5%)
  between operations  2.21 us (1%)
    ppermute x32, starting transfers between devices, swap(): lax.ppermute(value, axis, [(s, partner(s, step, count)) for s in range(co...  37.8 us
    ppermute x32, waiting for transfers between devices, swap(): lax.ppermute(value, axis, [(s, partner(s, step, count)) for s in range(co...  27.2 us
    ppermute x3, starting transfers between devices, handed_on(): return lax.ppermute(value, 'layer', [(layer, layer + 1)])  24.8 us
    dot_general x19, matrix products, dot_nt(): lax.dot_general(left, right, (((1,), (1,)), ((), ())), preferred_element_...  12.5 us
    dot_general x9, matrix products, heads(): jnp.dot(mixing[group] if isinstance(group, int) else pick(mixing, group),...  10.6 us
    reshape x9, local copies, waits for them, and re-layouts, heads(): mixed.astype(BF16).reshape(per_group, rows, -1).transpose(1, 0, 2)  8.72 us
    dot_general x13, matrix products, dot_tn(): lax.dot_general(left, right, (((0,), (0,)), ((), ())), preferred_element_...  8.4 us
    another operation x2, local copies, waits for them, and re-layouts, local(): out_cols.reshape(ranges, 2, half, per_group, width).transpose(1, 0, 4, 3, 2)  6.81 us
  transfers between devices with their start and end apart: 38, of which 15 were waited for; matrix products, arithmetic and copies ran while one was open for 34% of the time, Pallas kernels for 0%

profile of v1, /device:TPU:0, one launch (start us, length us, event | category | flops | bytes accessed | tf_op | source)
XLA Modules:
  0.0 169.1 jit_solution(17534677540725368994)
XLA Ops:
  1.7 3.1 %collective-permute-start = (bf16[448,128]{1,0:T(8,128)(2,1)S(1)}, bf16[448,128]{1,0:T(8,128)(2,1)}, u32[]{:S(2)}, u32[]{:S(2)}) collective-permute-start(bf16[448,128]{1,0:T(8,128)(2,1)S(1)} %fusion.43), channel_id=1, source_target_pairs={{0,4},{4,0},{8,12},{12,8},{1,5},{5,1},{9,13},{13,9},{2,6},{6,2},{1... | collective-permute-start | bytes 344072 | tf_op jit(solution)/shard_map/ppermute | solution.py:24
  4.8 2.5 %collective-permute-start.2 = (bf16[448,128]{1,0:T(8,128)(2,1)S(1)}, bf16[448,128]{1,0:T(8,128)(2,1)}, u32[]{:S(2)}, u32[]{:S(2)}) collective-permute-start(bf16[448,128]{1,0:T(8,128)(2,1)S(1)} %fusion.43), channel_id=1, source_target_pairs={{0,12},{4,8},{8,4},{12,0},{1,13},{5,9},{9,5},{13,1},{2,14},{6,10},... | collective-permute-start | bytes 344072 | tf_op jit(solution)/shard_map/ppermute | solution.py:24
  12.6 2.5 %collective-permute-start.20 = (f32[3,128]{1,0:T(4,128)}, f32[3,128]{1,0:T(4,128)}, u32[]{:S(2)}, u32[]{:S(2)}) collective-permute-start(f32[3,128]{1,0:T(4,128)} %get-tuple-element.46), channel_id=1, source_target_pairs={{0,12},{4,8},{8,4},{12,0},{1,13},{5,9},{9,5},{13,1},{2,14},{6,10},... | collective-permute-start | bytes 4616 | tf_op jit(solution)/shard_map/ppermute | solution.py:24
  19.5 3.7 %reshape_reshape_squeeze.3 = bf16[4,2,128,2,448]{2,1,4,3,0:T(2,128)(2,1)S(1)} reshape(bf16[1,4,256,2,1,448]{2,5,4,3,1,0:T(8,128)(2,1)} %param.21) | data formatting | bytes 3670016 | tf_op jit(solution)/shard_map/reshape;reshape;squeeze | solution.py:134
  23.2 3.1 %copy.42 = bf16[4,2,128,2,448]{2,3,4,0,1:T(2,128)(2,1)} copy(bf16[4,2,128,2,448]{2,1,4,3,0:T(2,128)(2,1)S(1)} %reshape_reshape_squeeze.3) | data formatting | bytes 3670016 | tf_op jit(solution)/shard_map/reshape;reshape;squeeze | solution.py:134
  26.3 4.4 %reshape.187 = bf16[2,4,448,256]{3,2,1,0:T(8,128)(2,1)S(1)} reshape(bf16[2,4,448,2,128]{4,3,2,1,0:T(2,128)(2,1)} %bitcast.306) | data formatting | bytes 3670016 | tf_op jit(solution)/shard_map/reshape | solution.py:134
  30.8 1.9 %collective-permute-start.11 = (bf16[448,128]{1,0:T(8,128)(2,1)}, bf16[448,128]{1,0:T(8,128)(2,1)S(1)}, u32[]{:S(2)}, u32[]{:S(2)}) collective-permute-start(bf16[448,128]{1,0:T(8,128)(2,1)} %get-tuple-element.25), channel_id=1, source_target_pairs={{0,4},{4,0},{8,12},{12,8},{1,5},{5,1},{9,13},{13,9},{2,6},{6,2},{1... | collective-permute-start | bytes 344072 | tf_op jit(solution)/shard_map/ppermute | solution.py:24
  40.2 3.3 %collective-permute-done.1 = bf16[448,128]{1,0:T(8,128)(2,1)S(1)} collective-permute-done((bf16[448,128]{1,0:T(8,128)(2,1)S(1)}, bf16[448,128]{1,0:T(8,128)(2,1)S(1)}, u32[]{:S(2)}, u32[]{:S(2)}) %collective-permute-start.1) | collective-permute-done | bytes 114720 | tf_op jit(solution)/shard_map/ppermute | solution.py:24
  49.6 1.7 %collective-permute-start.5 = (bf16[128,256]{0,1:T(8,128)(2,1)S(1)}, bf16[128,256]{0,1:T(8,128)(2,1)S(1)}, u32[]{:S(2)}, u32[]{:S(2)}) collective-permute-start(bf16[128,256]{0,1:T(8,128)(2,1)S(1)} %bitcast.347), channel_id=1, source_target_pairs={{0,4},{4,0},{8,12},{12,8},{1,5},{5,1},{9,13},{13,9},{2,6},{6,2},{1... | collective-permute-start | bytes 196616 | tf_op jit(solution)/shard_map/ppermute | solution.py:24
  52.2 1.9 %collective-permute-done.5 = bf16[128,256]{0,1:T(8,128)(2,1)S(1)} collective-permute-done((bf16[128,256]{0,1:T(8,128)(2,1)S(1)}, bf16[128,256]{0,1:T(8,128)(2,1)S(1)}, u32[]{:S(2)}, u32[]{:S(2)}) %collective-permute-start.5) | collective-permute-done | bytes 65568 | tf_op jit(solution)/shard_map/ppermute | solution.py:24
  54.0 1.9 %collective-permute-start.9 = (bf16[128,256]{0,1:T(8,128)(2,1)S(1)}, bf16[128,256]{0,1:T(8,128)(2,1)S(1)}, u32[]{:S(2)}, u32[]{:S(2)}) collective-permute-start(bf16[128,256]{0,1:T(8,128)(2,1)S(1)} %bitcast.350), channel_id=1, source_target_pairs={{0,12},{4,8},{8,4},{12,0},{1,13},{5,9},{9,5},{13,1},{2,14},{6,10},... | collective-permute-start | bytes 196616 | tf_op jit(solution)/shard_map/ppermute | solution.py:24
  56.2 1.9 %collective-permute-done.7 = bf16[128,256]{0,1:T(8,128)(2,1)S(1)} collective-permute-done((bf16[128,256]{0,1:T(8,128)(2,1)S(1)}, bf16[128,256]{0,1:T(8,128)(2,1)S(1)}, u32[]{:S(2)}, u32[]{:S(2)}) %collective-permute-start.7) | collective-permute-done | bytes 65568 | tf_op jit(solution)/shard_map/ppermute | solution.py:24
  66.0 1.9 %collective-permute-start.17 = (bf16[128,256]{1,0:T(8,128)(2,1)S(1)}, bf16[128,256]{1,0:T(8,128)(2,1)S(1)}, u32[]{:S(2)}, u32[]{:S(2)}) collective-permute-start(bf16[128,256]{1,0:T(8,128)(2,1)S(1)} %add_convert_fusion), channel_id=1, source_target_pairs={{0,12},{4,8},{8,4},{12,0},{1,13},{5,9},{9,5},{13,1},{2,14},{6,10},... | collective-permute-start | bytes 196616 | tf_op jit(solution)/shard_map/ppermute | solution.py:24
  68.7 4.2 %collective-permute-done.16 = bf16[128,256]{1,0:T(8,128)(2,1)S(1)} collective-permute-done((bf16[128,256]{1,0:T(8,128)(2,1)S(1)}, bf16[128,256]{1,0:T(8,128)(2,1)S(1)}, u32[]{:S(2)}, u32[]{:S(2)}) %collective-permute-start.16) | collective-permute-done | bytes 65568 | tf_op jit(solution)/shard_map/ppermute | solution.py:24
  75.5 15.5 %collective-permute-start.22 = (bf16[448,128]{1,0:T(8,128)(2,1)S(1)}, bf16[448,128]{1,0:T(8,128)(2,1)S(1)}, u32[]{:S(2)}, u32[]{:S(2)}) collective-permute-start(bf16[448,128]{1,0:T(8,128)(2,1)S(1)} %get-tuple-element.3), channel_id=1, source_target_pairs={{0,2},{1,3},{4,6},{5,7},{8,10},{9,11},{12,14},{13,15},{16,18},{17,... | collective-permute-start | bytes 344072 | tf_op jit(solution)/shard_map/ppermute | solution.py:201
  94.9 1.7 collective-permute-done.26
  98.0 5.4 %collective-permute-start.27 = (bf16[128,512]{1,0:T(8,128)(2,1)S(1)}, bf16[128,512]{1,0:T(8,128)(2,1)S(1)}, u32[]{:S(2)}, u32[]{:S(2)}) collective-permute-start(bf16[128,512]{1,0:T(8,128)(2,1)S(1)} %fusion.4), channel_id=1, source_target_pairs={{0,4},{4,0},{8,12},{12,8},{1,5},{5,1},{9,13},{13,9},{2,6},{6,2},{1... | collective-permute-start | bytes 393224 | tf_op jit(solution)/shard_map/ppermute | solution.py:24
  103.5 2.3 %collective-permute-start.29 = (bf16[128,512]{1,0:T(8,128)(2,1)S(1)}, bf16[128,512]{1,0:T(8,128)(2,1)S(1)}, u32[]{:S(2)}, u32[]{:S(2)}) collective-permute-start(bf16[128,512]{1,0:T(8,128)(2,1)S(1)} %fusion.4), channel_id=1, source_target_pairs={{0,12},{4,8},{8,4},{12,0},{1,13},{5,9},{9,5},{13,1},{2,14},{6,10},... | collective-permute-start | bytes 393224 | tf_op jit(solution)/shard_map/ppermute | solution.py:24
  106.6 5.0 %collective-permute-start.31 = (bf16[448,128]{1,0:T(8,128)(2,1)}, bf16[448,128]{1,0:T(8,128)(2,1)}, u32[]{:S(2)}, u32[]{:S(2)}) collective-permute-start(bf16[448,128]{1,0:T(8,128)(2,1)} %get-tuple-element.2), channel_id=1, source_target_pairs={{0,2},{1,3},{4,6},{5,7},{8,10},{9,11},{12,14},{13,15},{16,18},{17,... | collective-permute-start | bytes 344072 | tf_op jit(solution)/shard_map/ppermute | solution.py:201
  111.5 4.7 %collective-permute-done.28 = bf16[128,512]{1,0:T(8,128)(2,1)S(1)} collective-permute-done((bf16[128,512]{1,0:T(8,128)(2,1)S(1)}, bf16[128,512]{1,0:T(8,128)(2,1)S(1)}, u32[]{:S(2)}, u32[]{:S(2)}) %collective-permute-start.28) | collective-permute-done | bytes 131104 | tf_op jit(solution)/shard_map/ppermute | solution.py:24
  124.8 1.6 convolution_convert_fusion.5
  126.5 1.6 copy.35
  128.0 1.6 convolution_convert_fusion.7
  129.7 1.6 copy.33
  131.2 1.6 convolution_convert_fusion.3
  141.6 2.0 %multiply_convert_fusion.1 = (bf16[448,128]{1,0:T(8,128)(2,1)S(1)}, f32[448,128]{1,0:T(8,128)}) fusion(f32[128]{0:T(128)S(1)} %bitcast.363, bf16[448,128]{1,0:T(8,128)(2,1)} %collective-permute-done.31, bf16[448,128]{1,0:T(8,128)(2,1)} %copy-done.13, f32[448,128]{1,0:T(8,128)} %convolution_add_fusion.2, bf16[128,256]{0,1:T(8,128)(2,1)S(1)} %bitcast.334, ...), kind=kOutput, calls=%fused_computation.99 | convolution fusion | flops 29761536 | bytes 1098248 | tf_op jit(solution)/shard_map/dot_general | solution.py:50
  145.6 2.5 %collective-permute-start.34 = (bf16[128,256]{1,0:T(8,128)(2,1)S(1)}, bf16[128,256]{1,0:T(8,128)(2,1)S(1)}, u32[]{:S(2)}, u32[]{:S(2)}) collective-permute-start(bf16[128,256]{1,0:T(8,128)(2,1)S(1)} %fusion.5), channel_id=1, source_target_pairs={{0,4},{4,0},{8,12},{12,8},{1,5},{5,1},{9,13},{13,9},{2,6},{6,2},{1... | collective-permute-start | bytes 196616 | tf_op jit(solution)/shard_map/ppermute | solution.py:24
  148.2 2.3 %collective-permute-start.36 = (bf16[128,256]{1,0:T(8,128)(2,1)S(1)}, bf16[128,256]{1,0:T(8,128)(2,1)S(1)}, u32[]{:S(2)}, u32[]{:S(2)}) collective-permute-start(bf16[128,256]{1,0:T(8,128)(2,1)S(1)} %fusion.5), channel_id=1, source_target_pairs={{0,12},{4,8},{8,4},{12,0},{1,13},{5,9},{9,5},{13,1},{2,14},{6,10},... | collective-permute-start | bytes 196616 | tf_op jit(solution)/shard_map/ppermute | solution.py:24
  150.6 5.5 %collective-permute-done.35 = bf16[128,256]{1,0:T(8,128)(2,1)S(1)} collective-permute-done((bf16[128,256]{1,0:T(8,128)(2,1)S(1)}, bf16[128,256]{1,0:T(8,128)(2,1)S(1)}, u32[]{:S(2)}, u32[]{:S(2)}) %collective-permute-start.35) | collective-permute-done | bytes 65568 | tf_op jit(solution)/shard_map/ppermute | solution.py:24
  157.4 4.3 %collective-permute-start.32 = (f32[1,448,128]{2,1,0:T(8,128)S(1)}, f32[1,448,128]{2,1,0:T(8,128)S(1)}, u32[]{:S(2)}, u32[]{:S(2)}) collective-permute-start(f32[1,448,128]{2,1,0:T(8,128)S(1)} %convolution_bitcast_fusion.1), channel_id=1, source_target_pairs={{0,2},{1,3},{4,6},{5,7},{8,10},{9,11},{12,14},{13,15},{16,18},{17,... | collective-permute-start | bytes 688136 | tf_op jit(solution)/shard_map/ppermute | solution.py:201
  162.4 4.8 %collective-permute-done.32 = f32[1,448,128]{2,1,0:T(8,128)S(1)} collective-permute-done((f32[1,448,128]{2,1,0:T(8,128)S(1)}, f32[1,448,128]{2,1,0:T(8,128)S(1)}, u32[]{:S(2)}, u32[]{:S(2)}) %collective-permute-start.32) | collective-permute-done | bytes 229408 | tf_op jit(solution)/shard_map/ppermute | solution.py:201
  167.2 1.9 %fusion.32 = f32[1,128,1,448]{1,3,2,0:T(8,128)} fusion(f32[1,128,1,448]{1,3,2,0:T(8,128)S(1)} %copy-done.7, f32[1,448,128]{2,1,0:T(8,128)S(1)} %collective-permute-done.32, f32[448,128]{1,0:T(8,128)S(1)} %copy-done.8, bf16[2,448,512]{2,1,0:T(8,128)(2,1)S(1)} %bitcast.310, bf16[128,256]{1,0:T(8,128)(2,1)S(1)} %get-tuple-element.33, ...), kind=kOutput, calls=%fused_computation.84 | convolution fusion | flops 59498496 | bytes 1966082 | tf_op jit(solution)/shard_map/dot_general | solution.py:50
  (200 shorter events, 63.0 us)
Async XLA Ops:
  1.7 33.4 %collective-permute-start = (bf16[448,128]{1,0:T(8,128)(2,1)S(1)}, bf16[448,128]{1,0:T(8,128)(2,1)}, u32[]{:S(2)}, u32[]{:S(2)}) collective-permute-start(bf16[448,128]{1,0:T(8,128)(2,1)S(1)} %fusion.43), channel_id=1, source_target_pairs={{0,4},{4,0},{8,12},{12,8},{1,5},{5,1},{9,13},{13,9},{2,6},{6,2},{1... | collective-permute-start | bytes 344072 | tf_op jit(solution)/shard_map/ppermute | solution.py:24
  4.8 32.9 %collective-permute-start.2 = (bf16[448,128]{1,0:T(8,128)(2,1)S(1)}, bf16[448,128]{1,0:T(8,128)(2,1)}, u32[]{:S(2)}, u32[]{:S(2)}) collective-permute-start(bf16[448,128]{1,0:T(8,128)(2,1)S(1)} %fusion.43), channel_id=1, source_target_pairs={{0,12},{4,8},{8,4},{12,0},{1,13},{5,9},{9,5},{13,1},{2,14},{6,10},... | collective-permute-start | bytes 344072 | tf_op jit(solution)/shard_map/ppermute | solution.py:24
  10.7 20.0 %collective-permute-start.18 = (f32[3,128]{1,0:T(4,128)}, f32[3,128]{1,0:T(4,128)}, u32[]{:S(2)}, u32[]{:S(2)}) collective-permute-start(f32[3,128]{1,0:T(4,128)} %get-tuple-element.46), channel_id=1, source_target_pairs={{0,4},{4,0},{8,12},{12,8},{1,5},{5,1},{9,13},{13,9},{2,6},{6,2},{1... | collective-permute-start | bytes 4616 | tf_op jit(solution)/shard_map/ppermute | solution.py:24
  11.3 19.5 %collective-permute-start.19 = (f32[3,128]{1,0:T(4,128)}, f32[3,128]{1,0:T(4,128)}, u32[]{:S(2)}, u32[]{:S(2)}) collective-permute-start(f32[3,128]{1,0:T(4,128)} %get-tuple-element.46), channel_id=1, source_target_pairs={{0,8},{4,12},{8,0},{12,4},{1,9},{5,13},{9,1},{13,5},{2,10},{6,14},... | collective-permute-start | bytes 4616 | tf_op jit(solution)/shard_map/ppermute | solution.py:24
  12.6 20.1 %collective-permute-start.20 = (f32[3,128]{1,0:T(4,128)}, f32[3,128]{1,0:T(4,128)}, u32[]{:S(2)}, u32[]{:S(2)}) collective-permute-start(f32[3,128]{1,0:T(4,128)} %get-tuple-element.46), channel_id=1, source_target_pairs={{0,12},{4,8},{8,4},{12,0},{1,13},{5,9},{9,5},{13,1},{2,14},{6,10},... | collective-permute-start | bytes 4616 | tf_op jit(solution)/shard_map/ppermute | solution.py:24
  30.7 12.8 %collective-permute-start.1 = (bf16[448,128]{1,0:T(8,128)(2,1)S(1)}, bf16[448,128]{1,0:T(8,128)(2,1)S(1)}, u32[]{:S(2)}, u32[]{:S(2)}) collective-permute-start(bf16[448,128]{1,0:T(8,128)(2,1)S(1)} %fusion.43), channel_id=1, source_target_pairs={{0,8},{4,12},{8,0},{12,4},{1,9},{5,13},{9,1},{13,5},{2,10},{6,14},... | collective-permute-start | bytes 344072 | tf_op jit(solution)/shard_map/ppermute | solution.py:24
  30.8 14.2 %collective-permute-start.11 = (bf16[448,128]{1,0:T(8,128)(2,1)}, bf16[448,128]{1,0:T(8,128)(2,1)S(1)}, u32[]{:S(2)}, u32[]{:S(2)}) collective-permute-start(bf16[448,128]{1,0:T(8,128)(2,1)} %get-tuple-element.25), channel_id=1, source_target_pairs={{0,4},{4,0},{8,12},{12,8},{1,5},{5,1},{9,13},{13,9},{2,6},{6,2},{1... | collective-permute-start | bytes 344072 | tf_op jit(solution)/shard_map/ppermute | solution.py:24
  32.7 12.8 %collective-permute-start.12 = (bf16[448,128]{1,0:T(8,128)(2,1)}, bf16[448,128]{1,0:T(8,128)(2,1)S(1)}, u32[]{:S(2)}, u32[]{:S(2)}) collective-permute-start(bf16[448,128]{1,0:T(8,128)(2,1)} %get-tuple-element.24), channel_id=1, source_target_pairs={{0,8},{4,12},{8,0},{12,4},{1,9},{5,13},{9,1},{13,5},{2,10},{6,14},... | collective-permute-start | bytes 344072 | tf_op jit(solution)/shard_map/ppermute | solution.py:24
  35.1 10.4 %collective-permute-start.13 = (bf16[448,128]{1,0:T(8,128)(2,1)}, bf16[448,128]{1,0:T(8,128)(2,1)S(1)}, u32[]{:S(2)}, u32[]{:S(2)}) collective-permute-start(bf16[448,128]{1,0:T(8,128)(2,1)} %get-tuple-element.23), channel_id=1, source_target_pairs={{0,12},{4,8},{8,4},{12,0},{1,13},{5,9},{9,5},{13,1},{2,14},{6,10},... | collective-permute-start | bytes 344072 | tf_op jit(solution)/shard_map/ppermute | solution.py:24
  37.7 35.4 %collective-permute-start.23 = (bf16[448,256]{1,0:T(8,128)(2,1)}, bf16[448,256]{1,0:T(8,128)(2,1)}, u32[]{:S(2)}, u32[]{:S(2)}) collective-permute-start(bf16[448,256]{1,0:T(8,128)(2,1)} %get-tuple-element.15), channel_id=1, source_target_pairs={{2,6},{6,2},{10,14},{14,10},{3,7},{7,3},{11,15},{15,11},{18,22},{2... | collective-permute-start | bytes 688136 | tf_op jit(solution)/shard_map/ppermute | solution.py:31
  43.5 29.7 %collective-permute-start.24 = (bf16[448,256]{1,0:T(8,128)(2,1)}, bf16[448,256]{1,0:T(8,128)(2,1)}, u32[]{:S(2)}, u32[]{:S(2)}) collective-permute-start(bf16[448,256]{1,0:T(8,128)(2,1)} %get-tuple-element.14), channel_id=1, source_target_pairs={{2,10},{6,14},{10,2},{14,6},{3,11},{7,15},{11,3},{15,7},{18,26},{2... | collective-permute-start | bytes 688136 | tf_op jit(solution)/shard_map/ppermute | solution.py:31
  45.1 3.8 %collective-permute-start.3 = (f32[128,128]{1,0:T(8,128)S(1)}, f32[128,128]{1,0:T(8,128)S(1)}, u32[]{:S(2)}, u32[]{:S(2)}) collective-permute-start(f32[128,128]{1,0:T(8,128)S(1)} %fusion.8), channel_id=1, source_target_pairs={{0,1},{1,0},{2,3},{3,2},{4,5},{5,4},{6,7},{7,6},{8,9},{9,8},{10,11... | collective-permute-start | bytes 196616 | tf_op jit(solution)/shard_map/ppermute | solution.py:24
  49.4 8.9 %collective-permute-start.4 = (bf16[128,256]{0,1:T(8,128)(2,1)S(1)}, bf16[128,256]{0,1:T(8,128)(2,1)S(1)}, u32[]{:S(2)}, u32[]{:S(2)}) collective-permute-start(bf16[128,256]{0,1:T(8,128)(2,1)S(1)} %bitcast.346), channel_id=1, source_target_pairs={{0,1},{1,0},{2,3},{3,2},{4,5},{5,4},{6,7},{7,6},{8,9},{9,8},{10,11... | collective-permute-start | bytes 196616 | tf_op jit(solution)/shard_map/ppermute | solution.py:24
  49.6 4.4 %collective-permute-start.5 = (bf16[128,256]{0,1:T(8,128)(2,1)S(1)}, bf16[128,256]{0,1:T(8,128)(2,1)S(1)}, u32[]{:S(2)}, u32[]{:S(2)}) collective-permute-start(bf16[128,256]{0,1:T(8,128)(2,1)S(1)} %bitcast.347), channel_id=1, source_target_pairs={{0,4},{4,0},{8,12},{12,8},{1,5},{5,1},{9,13},{13,9},{2,6},{6,2},{1... | collective-permute-start | bytes 196616 | tf_op jit(solution)/shard_map/ppermute | solution.py:24
  51.3 6.7 %collective-permute-start.7 = (bf16[128,256]{0,1:T(8,128)(2,1)S(1)}, bf16[128,256]{0,1:T(8,128)(2,1)S(1)}, u32[]{:S(2)}, u32[]{:S(2)}) collective-permute-start(bf16[128,256]{0,1:T(8,128)(2,1)S(1)} %bitcast.348), channel_id=1, source_target_pairs={{0,8},{4,12},{8,0},{12,4},{1,9},{5,13},{9,1},{13,5},{2,10},{6,14},... | collective-permute-start | bytes 196616 | tf_op jit(solution)/shard_map/ppermute | solution.py:24
  54.0 6.2 %collective-permute-start.9 = (bf16[128,256]{0,1:T(8,128)(2,1)S(1)}, bf16[128,256]{0,1:T(8,128)(2,1)S(1)}, u32[]{:S(2)}, u32[]{:S(2)}) collective-permute-start(bf16[128,256]{0,1:T(8,128)(2,1)S(1)} %bitcast.350), channel_id=1, source_target_pairs={{0,12},{4,8},{8,4},{12,0},{1,13},{5,9},{9,5},{13,1},{2,14},{6,10},... | collective-permute-start | bytes 196616 | tf_op jit(solution)/shard_map/ppermute | solution.py:24
  58.3 2.6 %collective-permute-start.8 = (bf16[128,256]{0,1:T(8,128)(2,1)S(1)}, bf16[128,256]{0,1:T(8,128)(2,1)S(1)}, u32[]{:S(2)}, u32[]{:S(2)}) collective-permute-start(bf16[128,256]{0,1:T(8,128)(2,1)S(1)} %collective-permute-done.7), channel_id=1, source_target_pairs={{0,1},{1,0},{2,3},{3,2},{4,5},{5,4},{6,7},{7,6},{8,9},{9,8},{10,11... | collective-permute-start | bytes 196616 | tf_op jit(solution)/shard_map/ppermute | solution.py:24
  63.5 4.5 %collective-permute-start.15 = (bf16[128,256]{1,0:T(8,128)(2,1)S(1)}, bf16[128,256]{1,0:T(8,128)(2,1)S(1)}, u32[]{:S(2)}, u32[]{:S(2)}) collective-permute-start(bf16[128,256]{1,0:T(8,128)(2,1)S(1)} %add_convert_fusion), channel_id=1, source_target_pairs={{0,4},{4,0},{8,12},{12,8},{1,5},{5,1},{9,13},{13,9},{2,6},{6,2},{1... | collective-permute-start | bytes 196616 | tf_op jit(solution)/shard_map/ppermute | solution.py:24
  64.6 8.4 %collective-permute-start.16 = (bf16[128,256]{1,0:T(8,128)(2,1)S(1)}, bf16[128,256]{1,0:T(8,128)(2,1)S(1)}, u32[]{:S(2)}, u32[]{:S(2)}) collective-permute-start(bf16[128,256]{1,0:T(8,128)(2,1)S(1)} %add_convert_fusion), channel_id=1, source_target_pairs={{0,8},{4,12},{8,0},{12,4},{1,9},{5,13},{9,1},{13,5},{2,10},{6,14},... | collective-permute-start | bytes 196616 | tf_op jit(solution)/shard_map/ppermute | solution.py:24
  66.0 6.9 %collective-permute-start.17 = (bf16[128,256]{1,0:T(8,128)(2,1)S(1)}, bf16[128,256]{1,0:T(8,128)(2,1)S(1)}, u32[]{:S(2)}, u32[]{:S(2)}) collective-permute-start(bf16[128,256]{1,0:T(8,128)(2,1)S(1)} %add_convert_fusion), channel_id=1, source_target_pairs={{0,12},{4,8},{8,4},{12,0},{1,13},{5,9},{9,5},{13,1},{2,14},{6,10},... | collective-permute-start | bytes 196616 | tf_op jit(solution)/shard_map/ppermute | solution.py:24
  68.1 5.1 %collective-permute-start.25 = (bf16[448,256]{1,0:T(8,128)(2,1)S(1)}, bf16[448,256]{1,0:T(8,128)(2,1)S(1)}, u32[]{:S(2)}, u32[]{:S(2)}) collective-permute-start(bf16[448,256]{1,0:T(8,128)(2,1)S(1)} %copy-done.22), channel_id=1, source_target_pairs={{2,14},{6,10},{10,6},{14,2},{3,15},{7,11},{11,7},{15,3},{18,30},{2... | collective-permute-start | bytes 688136 | tf_op jit(solution)/shard_map/ppermute | solution.py:31
  75.5 17.9 %collective-permute-start.22 = (bf16[448,128]{1,0:T(8,128)(2,1)S(1)}, bf16[448,128]{1,0:T(8,128)(2,1)S(1)}, u32[]{:S(2)}, u32[]{:S(2)}) collective-permute-start(bf16[448,128]{1,0:T(8,128)(2,1)S(1)} %get-tuple-element.3), channel_id=1, source_target_pairs={{0,2},{1,3},{4,6},{5,7},{8,10},{9,11},{12,14},{13,15},{16,18},{17,... | collective-permute-start | bytes 344072 | tf_op jit(solution)/shard_map/ppermute | solution.py:201
  98.0 13.5 %collective-permute-start.27 = (bf16[128,512]{1,0:T(8,128)(2,1)S(1)}, bf16[128,512]{1,0:T(8,128)(2,1)S(1)}, u32[]{:S(2)}, u32[]{:S(2)}) collective-permute-start(bf16[128,512]{1,0:T(8,128)(2,1)S(1)} %fusion.4), channel_id=1, source_target_pairs={{0,4},{4,0},{8,12},{12,8},{1,5},{5,1},{9,13},{13,9},{2,6},{6,2},{1... | collective-permute-start | bytes 393224 | tf_op jit(solution)/shard_map/ppermute | solution.py:24
  103.4 12.8 %collective-permute-start.28 = (bf16[128,512]{1,0:T(8,128)(2,1)S(1)}, bf16[128,512]{1,0:T(8,128)(2,1)S(1)}, u32[]{:S(2)}, u32[]{:S(2)}) collective-permute-start(bf16[128,512]{1,0:T(8,128)(2,1)S(1)} %fusion.4), channel_id=1, source_target_pairs={{0,8},{4,12},{8,0},{12,4},{1,9},{5,13},{9,1},{13,5},{2,10},{6,14},... | collective-permute-start | bytes 393224 | tf_op jit(solution)/shard_map/ppermute | solution.py:24
  103.5 12.7 %collective-permute-start.29 = (bf16[128,512]{1,0:T(8,128)(2,1)S(1)}, bf16[128,512]{1,0:T(8,128)(2,1)S(1)}, u32[]{:S(2)}, u32[]{:S(2)}) collective-permute-start(bf16[128,512]{1,0:T(8,128)(2,1)S(1)} %fusion.4), channel_id=1, source_target_pairs={{0,12},{4,8},{8,4},{12,0},{1,13},{5,9},{9,5},{13,1},{2,14},{6,10},... | collective-permute-start | bytes 393224 | tf_op jit(solution)/shard_map/ppermute | solution.py:24
  106.6 35.1 %collective-permute-start.31 = (bf16[448,128]{1,0:T(8,128)(2,1)}, bf16[448,128]{1,0:T(8,128)(2,1)}, u32[]{:S(2)}, u32[]{:S(2)}) collective-permute-start(bf16[448,128]{1,0:T(8,128)(2,1)} %get-tuple-element.2), channel_id=1, source_target_pairs={{0,2},{1,3},{4,6},{5,7},{8,10},{9,11},{12,14},{13,15},{16,18},{17,... | collective-permute-start | bytes 344072 | tf_op jit(solution)/shard_map/ppermute | solution.py:201
  117.0 7.9 %collective-permute-start.30 = (bf16[128,512]{1,0:T(8,128)(2,1)}, bf16[128,512]{1,0:T(8,128)(2,1)}, u32[]{:S(2)}, u32[]{:S(2)}) collective-permute-start(bf16[128,512]{1,0:T(8,128)(2,1)} %multiply_convert_fusion), channel_id=1, source_target_pairs={{0,1},{1,0},{2,3},{3,2},{4,5},{5,4},{6,7},{7,6},{8,9},{9,8},{10,11... | collective-permute-start | bytes 393224 | tf_op jit(solution)/shard_map/ppermute | solution.py:24
  145.6 5.1 %collective-permute-start.34 = (bf16[128,256]{1,0:T(8,128)(2,1)S(1)}, bf16[128,256]{1,0:T(8,128)(2,1)S(1)}, u32[]{:S(2)}, u32[]{:S(2)}) collective-permute-start(bf16[128,256]{1,0:T(8,128)(2,1)S(1)} %fusion.5), channel_id=1, source_target_pairs={{0,4},{4,0},{8,12},{12,8},{1,5},{5,1},{9,13},{13,9},{2,6},{6,2},{1... | collective-permute-start | bytes 196616 | tf_op jit(solution)/shard_map/ppermute | solution.py:24
  148.0 8.1 %collective-permute-start.35 = (bf16[128,256]{1,0:T(8,128)(2,1)S(1)}, bf16[128,256]{1,0:T(8,128)(2,1)S(1)}, u32[]{:S(2)}, u32[]{:S(2)}) collective-permute-start(bf16[128,256]{1,0:T(8,128)(2,1)S(1)} %fusion.5), channel_id=1, source_target_pairs={{0,8},{4,12},{8,0},{12,4},{1,9},{5,13},{9,1},{13,5},{2,10},{6,14},... | collective-permute-start | bytes 196616 | tf_op jit(solution)/shard_map/ppermute | solution.py:24
  148.2 8.0 %collective-permute-start.36 = (bf16[128,256]{1,0:T(8,128)(2,1)S(1)}, bf16[128,256]{1,0:T(8,128)(2,1)S(1)}, u32[]{:S(2)}, u32[]{:S(2)}) collective-permute-start(bf16[128,256]{1,0:T(8,128)(2,1)S(1)} %fusion.5), channel_id=1, source_target_pairs={{0,12},{4,8},{8,4},{12,0},{1,13},{5,9},{9,5},{13,1},{2,14},{6,10},... | collective-permute-start | bytes 196616 | tf_op jit(solution)/shard_map/ppermute | solution.py:24
  157.0 4.7 %collective-permute-start.37 = (bf16[128,256]{1,0:T(8,128)(2,1)S(1)}, bf16[128,256]{1,0:T(8,128)(2,1)S(1)}, u32[]{:S(2)}, u32[]{:S(2)}) collective-permute-start(bf16[128,256]{1,0:T(8,128)(2,1)S(1)} %select_convert_fusion), channel_id=1, source_target_pairs={{0,1},{1,0},{2,3},{3,2},{4,5},{5,4},{6,7},{7,6},{8,9},{9,8},{10,11... | collective-permute-start | bytes 196616 | tf_op jit(solution)/shard_map/ppermute | solution.py:24
  157.4 9.8 %collective-permute-start.32 = (f32[1,448,128]{2,1,0:T(8,128)S(1)}, f32[1,448,128]{2,1,0:T(8,128)S(1)}, u32[]{:S(2)}, u32[]{:S(2)}) collective-permute-start(f32[1,448,128]{2,1,0:T(8,128)S(1)} %convolution_bitcast_fusion.1), channel_id=1, source_target_pairs={{0,2},{1,3},{4,6},{5,7},{8,10},{9,11},{12,14},{13,15},{16,18},{17,... | collective-permute-start | bytes 688136 | tf_op jit(solution)/shard_map/ppermute | solution.py:201
  (42 other events, 325.5 us)

commit v2 on v1

--- a/solution.py
+++ b/solution.py
@@ -1,6 +1,10 @@
+import functools
+
 import jax
 import jax.numpy as jnp
 from jax import lax
+from jax.experimental import pallas as pl
+from jax.experimental.pallas import tpu as pltpu
 from jax.sharding import PartitionSpec as P
 
 BF16 = jnp.bfloat16
@@ -64,7 +68,7 @@
     return [pick(got, partner(my_range, n, ranges)) for n in range(ranges)]
 
 
-def local(
+def plain(
     residual_in,
     attn_scale,
     mlp_scale,
@@ -129,9 +133,7 @@
     own_value, other_value = (
         lax.dynamic_slice_in_dim(value_rows, n * half, half, 1) for n in (my_slab, 1 - my_slab)
     )
-    shares = kv_cols * ranges // head_dim
-    out_cols = out_proj[0, :, :, :, 0, :].reshape(shares, head_dim // kv_cols if kv_cols < head_dim else 1, 2, half, per_group, width)
-    out_cols = out_cols.reshape(ranges, 2, half, per_group, width).transpose(1, 0, 4, 3, 2).reshape(2, ranges, width, per_group * half)
+    out_cols = out_proj[0, :, :, :, 0, :].reshape(ranges, 2, half, per_group, width).transpose(1, 0, 4, 3, 2).reshape(2, ranges, width, per_group * half)
     out_own, out_other = (pick(out_cols, n) for n in (my_slab, 1 - my_slab))
     group_of = [n * kv_cols // head_dim for n in range(ranges)]
 
@@ -228,6 +230,316 @@
             rest = handed_on(left, layer)
             links = handed_on(writes, layer)
     return states.T[None, :, None, :], feats[None]
+
+
+LANES = 128
+INFO = 16
+
+
+def shape(*sizes, dtype=F32):
+    return jax.ShapeDtypeStruct(sizes, dtype)
+
+
+def kernel_call(body, outs, scalars, arrays, scratch=(), flops=0):
+    many = isinstance(outs, (list, tuple))
+    kept = list(outs) if many else [outs]
+    size = sum(a.size * a.dtype.itemsize for a in arrays) + sum(a.size * a.dtype.itemsize for a in kept)
+    return pl.pallas_call(
+        body,
+        out_shape=tuple(kept) if many else outs,
+        in_specs=[pl.BlockSpec(memory_space=pltpu.SMEM)] * len(scalars) + [pl.BlockSpec(memory_space=pltpu.VMEM)] * len(arrays),
+        out_specs=tuple(pl.BlockSpec(memory_space=pltpu.VMEM) for _ in kept) if many else pl.BlockSpec(memory_space=pltpu.VMEM),
+        scratch_shapes=list(scratch),
+        compiler_params=pltpu.CompilerParams(vmem_limit_bytes=16 * 1024 * 1024),
+        cost_estimate=pl.CostEstimate(flops=int(flops), bytes_accessed=int(size), transcendentals=0),
+    )(*scalars, *arrays)
+
+
+def split_terms(value):
+    high = value.astype(BF16)
+    left = value - high.astype(F32)
+    middle = left.astype(BF16)
+    low = (left - middle.astype(F32)).astype(BF16)
+    return [high, middle, low]
+
+
+def pack_body(ranges, place, chosen, table, mode, index, bias, enc, *sends):
+    width = enc.shape[0] // ranges
+    block = chosen[0, 0]
+    modes = mode[pl.ds(block, 1), :]
+    entries = index[pl.ds(block, 1), :]
+    levels = jnp.zeros(entries.shape, F32)
+    for n in range(table.shape[0]):
+        levels = jnp.where(entries == n, table[n], levels)
+    gain = jnp.where(modes == 1, 0.0, jnp.where(modes == 2, levels, 1.0))
+    shift = jnp.where(modes == 1, levels, 0.0)
+    terms = [t.astype(F32) for v in (bias[...], gain, shift) for t in split_terms(v)]
+    info = jnp.concatenate(terms + [jnp.zeros((INFO - len(terms), bias.shape[1]), F32)], axis=0).astype(BF16)
+    for step, send in enumerate(sends):
+        other = partner(place[0], step, ranges) if step else place[0]
+        send[0:width, :] = enc[pl.ds(pl.multiple_of(other * width, 16), width), :]
+        send[width:, :] = info
+
+
+def values_body(ranges, place, *refs):
+    blocks, (weight, own, other) = refs[:ranges], refs[ranges:]
+    width, half = blocks[0].shape[0], own.shape[1]
+    acc = None
+    for step, block in enumerate(blocks):
+        n = partner(place[0], step, ranges) if step else place[0]
+        part = dot_tn(block[...], weight[pl.ds(pl.multiple_of(n * width, 16), width), :])
+        acc = part if acc is None else acc + part
+    first = place[1] == 0
+    own[...] = jnp.where(first, acc[:, :half], acc[:, half:])
+    other[...] = jnp.where(first, acc[:, half:], acc[:, :half])
+
+
+def heads_body(kv_cols, head_dim, place, lengths, own, got, scale, patterns, out):
+    per_group, seq, prompts = out.shape[0], patterns.shape[2], patterns.shape[1]
+    values = ((own[...] + got[...]) * scale[...]).astype(BF16)
+    first = (place[0] * kv_cols // head_dim) * per_group
+    query = lax.broadcasted_iota(jnp.int32, (seq, seq), 0)
+    key = lax.broadcasted_iota(jnp.int32, (seq, seq), 1)
+    for p in range(prompts):
+        keep = (key <= query) & (key < lengths[p])
+        for u in range(per_group):
+            pattern = jnp.where(keep, patterns[first + u, p].astype(F32), 0.0).astype(BF16)
+            mixed = jnp.dot(pattern, values[p * seq : (p + 1) * seq, :], preferred_element_type=F32)
+            out[u, p * seq : (p + 1) * seq, :] = mixed.astype(BF16)
+
+
+def code_body(ranges, states, kv_cols, head_dim, place, *refs):
+    refs = list(refs)
+    got, also, state, packed = (
+        [refs.pop(0) for _ in range(count)] for count in (ranges, ranges, states, ranges)
+    )
+    weight, scale, middle, own, other, info, parts = refs
+    width = middle.shape[0]
+    per_group = got[0].shape[0]
+    first = place[1] == 0
+    acc = state[0][...].astype(F32)
+    for piece in state[1:]:
+        acc = acc + piece[...].astype(F32)
+    for step in range(ranges):
+        n = partner(place[0], step, ranges) if step else place[0]
+        group = n * kv_cols // head_dim
+        for u in range(per_group):
+            mine, theirs = got[step][u], also[step][u]
+            head = jnp.concatenate([jnp.where(first, mine, theirs), jnp.where(first, theirs, mine)], axis=1)
+            acc = acc + dot_nt(weight[group * per_group + u], head)
+    middle[...] = acc
+    normed = (acc * scale[...]).astype(BF16)
+    for step in range(ranges):
+        n = partner(place[0], step, ranges) if step else place[0]
+        parts[n] = dot_tn(normed, packed[step][0:width, :])
+        terms = packed[step][width:, :].astype(F32)
+        info[n] = jnp.concatenate(
+            [terms[3 * i : 3 * i + 1] + terms[3 * i + 1 : 3 * i + 2] + terms[3 * i + 2 : 3 * i + 3] for i in range(3)]
+            + [jnp.zeros((5, terms.shape[1]), F32)],
+            axis=0,
+        )
+    share = ranges // 2
+    own[...] = parts[pl.ds(place[1] * share, share)]
+    other[...] = parts[pl.ds((1 - place[1]) * share, share)].astype(BF16)
+
+
+def clamp_body(seq, place, lengths, *refs):
+    *blocks, info, out = refs
+    share, rows, _ = out.shape
+    row = lax.broadcasted_iota(jnp.int32, out.shape[1:], 0)
+    end = jnp.full(row.shape, lengths[0], jnp.int32)
+    for p in range(1, rows // seq):
+        end = jnp.where(row >= p * seq, p * seq + lengths[p], end)
+    live = row < end
+    for n in range(share):
+        facts = info[place[1] * share + n]
+        preact = total([b[n] for b in blocks]) + facts[0:1]
+        clamped = jnp.maximum(preact, 0.0) * facts[1:2] + facts[2:3]
+        out[n] = jnp.where(live, clamped, 0.0).astype(BF16)
+
+
+def ordered(place, mine, also):
+    first = place[1] == 0
+    share = mine.shape[0]
+    return [jnp.where(first, mine[n], also[n]) for n in range(share)] + [
+        jnp.where(first, also[n], mine[n]) for n in range(share)
+    ]
+
+
+def decode_body(layer, adds, sends, keeps, place, *refs):
+    refs = list(refs)
+    mine, also, dec = refs[:3]
+    added = refs[3 : 3 + adds]
+    refs = refs[3 + adds :]
+    before = refs[:2] if keeps else None
+    if keeps:
+        refs = refs[2:]
+    state_out, feats_out = refs[:2]
+    feats = ordered(place, mine, also)
+    acc = added[0][...]
+    for piece in added[1:]:
+        acc = acc + piece[...]
+    acc = acc + dot_nt(dec[layer], jnp.concatenate(feats, axis=1))
+    block = feats[0]
+    for n in range(1, len(feats)):
+        block = jnp.where(place[0] == n, feats[n], block)
+    if sends:
+        low = acc.astype(BF16)
+        refs[2][...] = low
+        refs[3][...] = (acc - low.astype(F32)).astype(BF16)
+    if keeps:
+        here = place[2] == layer
+        state_out[...] = jnp.where(here, acc, before[0][...])
+        feats_out[...] = jnp.where(here, block, before[1][...])
+    else:
+        state_out[...] = acc
+        feats_out[...] = block
+
+
+def writes_body(layer, has_links, place, mine, also, dec, *refs):
+    out = refs[-1]
+    feats = jnp.concatenate(ordered(place, mine, also), axis=1)
+    for n in range(out.shape[0]):
+        made = dot_nt(dec[layer + 1 + n], feats)
+        out[n] = made + refs[0][n + 1] if has_links else made
+
+
+def after(value, *others):
+    return lax.optimization_barrier((value, *others))[0]
+
+
+def tiled(
+    residual_in,
+    attn_scale,
+    mlp_scale,
+    patterns,
+    lengths,
+    value_proj,
+    out_proj,
+    enc_weight,
+    enc_bias,
+    dec_weight,
+    errors,
+    clamp_mode,
+    clamp_index,
+    clamp_values,
+    active_blocks,
+):
+    layers = lax.axis_size("layer")
+    ranges = lax.axis_size("feat")
+    seq = patterns.shape[3]
+    head_dim, per_group = out_proj.shape[2:4]
+    kv_cols = value_proj.shape[3]
+    half = kv_cols // 2
+    width = residual_in.shape[2]
+    block_len = enc_bias.shape[1]
+    rows = residual_in.shape[0]
+    share = ranges // 2
+    place = jnp.stack([lax.axis_index("feat"), lax.axis_index("tok"), lax.axis_index("layer")]).astype(jnp.int32)
+
+    source = residual_in[:, 0, :].T
+    error_cols = errors[0, :, 0, :].T
+    out_weight = out_proj[0, :, :, :, 0, :].transpose(0, 2, 3, 1).reshape(-1, width, head_dim)
+    dec_cols = dec_weight[0, :, :, 0, :].transpose(0, 2, 1)
+    value_rows = value_proj[0, 0]
+    scale_attn = attn_scale.reshape(rows, 1)
+
+    def handed_on(value, layer):
+        return lax.ppermute(value, "layer", [(layer, layer + 1)])
+
+    packed = None
+    low, links, kept = source.astype(BF16), None, None
+    state = [source]
+    for layer in range(layers):
+        blocks = spread(low)
+        if packed is None:
+            sends = kernel_call(
+                functools.partial(pack_body, ranges),
+                [shape(width + INFO, block_len, dtype=BF16)] * ranges,
+                [place, active_blocks, clamp_values],
+                [clamp_mode.reshape(-1, block_len), clamp_index.reshape(-1, block_len), enc_bias, enc_weight[0, 0]],
+            )
+            packed = [sends[0]] + [
+                swap(after(sends[step], *blocks), "feat", step) for step in peers("feat")
+            ]
+        own, other = kernel_call(
+            functools.partial(values_body, ranges),
+            [shape(rows, half)] * 2,
+            [place],
+            [*blocks, value_rows],
+            flops=4 * rows * value_rows.size,
+        )
+        mine = kernel_call(
+            functools.partial(heads_body, kv_cols, head_dim),
+            shape(per_group, rows, half, dtype=BF16),
+            [place, lengths],
+            [own, swap(other, "tok", 1), scale_attn, patterns[0]],
+        )
+        got = spread(mine)
+        also = [swap(b, "tok", 1) for b in got]
+        middle, own, other, info = kernel_call(
+            functools.partial(code_body, ranges, len(state), kv_cols, head_dim),
+            [
+                shape(width, rows),
+                shape(share, rows, block_len),
+                shape(share, rows, block_len, dtype=BF16),
+                shape(ranges, 8, block_len),
+            ],
+            [place],
+            [*got, *also, *state, *packed, out_weight, mlp_scale],
+            scratch=[pltpu.VMEM((ranges, rows, block_len), F32)],
+            flops=2 * rows * (out_weight.size + width * block_len * ranges),
+        )
+        part = (own + swap(other, "tok", 1).astype(F32)).astype(BF16)
+        mine = kernel_call(
+            functools.partial(clamp_body, seq),
+            shape(share, rows, block_len, dtype=BF16),
+            [place, lengths],
+            [*spread(part), info],
+        )
+        also = swap(mine, "tok", 1)
+        more = layer + 1 < layers
+        added = [middle, error_cols] + ([links[0]] if links is not None else [])
+        outs = [shape(width, rows), shape(rows, block_len, dtype=BF16)]
+        if more:
+            outs += [shape(width, rows, dtype=BF16)] * 2
+        made = kernel_call(
+            functools.partial(decode_body, layer, len(added), more, kept is not None),
+            outs,
+            [place],
+            [mine, also, dec_cols, *added, *(kept or ())],
+            flops=2 * rows * dec_cols.size // layers,
+        )
+        kept = made[:2]
+        if more:
+            low = handed_on(made[2], layer)
+            rest = handed_on(after(made[3], low), layer)
+            writes = kernel_call(
+                functools.partial(writes_body, layer, links is not None),
+                shape(layers - 1 - layer, width, rows),
+                [place],
+                [mine, also, dec_cols, *([links] if links is not None else [])],
+                flops=2 * rows * dec_cols.size,
+            )
+            links = handed_on(after(writes, rest), layer)
+            state = [low, rest]
+    return kept[0].T[None, :, None, :], kept[1][None]
+
+
+def local(residual_in, attn_scale, mlp_scale, patterns, lengths, value_proj, out_proj, enc_weight, enc_bias, *others):
+    whole = (
+        residual_in.shape[0] % LANES == 0
+        and residual_in.shape[2] % 16 == 0
+        and value_proj.shape[3] == out_proj.shape[2]
+        and value_proj.shape[3] % (2 * LANES) == 0
+        and enc_bias.shape[1] % LANES == 0
+        and lax.axis_size("feat") % 2 == 0
+        and lax.axis_size("tok") == 2
+    )
+    run = tiled if whole else plain
+    return run(
+        residual_in, attn_scale, mlp_scale, patterns, lengths, value_proj, out_proj, enc_weight, enc_bias, *others
+    )
 
 
 def solution(mesh):

time: 171 us -> 109 us (0.64)
  matrix products: 31.5 us -> 0 us
  local copies, waits for them, and re-layouts: 26.9 us -> 7.34 us
  starting transfers between devices: 66 us -> 48.7 us
  Pallas kernels: 0 us -> 11.7 us
  other arithmetic: 9.23 us -> 1.2 us
  waiting for transfers between devices: 33.2 us -> 38 us
    dot_general x41 -> x0, matrix products: 31.5 us -> none  [the longest x19 12.5 us: dot_nt(): lax.dot_general(left, right, (((1,), (1,)), ((), ())), preferred_element_...]
    ppermute x3, starting transfers between devices: 24.8 us -> 12.2 us  [handed_on(): return lax.ppermute(value, 'layer', [(layer, layer + 1)])]
    reshape x10 -> x1, local copies, waits for them, and re-layouts: 13.1 us -> 0.76 us  [tiled(): scale_attn = attn_scale.reshape(rows, 1)]
    pallas_call x0 -> x12, Pallas kernels: none -> 11.7 us  [kernel_call(): pl.pallas_call(body, out_shape=tuple(kept) if many else outs, in_specs=[p...]
    ppermute x32 -> x35, waiting for transfers between devices: 27.2 us -> 34.7 us  [swap(): lax.ppermute(value, axis, [(s, partner(s, step, count)) for s in range(co...]
    another operation x3 -> x0, local copies, waits for them, and re-layouts: 7.41 us -> none  [the longest x2 6.81 us: local(): out_cols.reshape(ranges, 2, half, per_group, width).transpose(1, 0, 4, 3, 2)]
    unnamed x72 -> x32, local copies, waits for them, and re-layouts: 0.81 us -> 6.58 us
    dynamic_slice x4 -> x0, local copies, waits for them, and re-layouts: 4.16 us -> none  [the longest x2 1.71 us: pick(): return lax.dynamic_index_in_dim(array, index, 0, keepdims=False)]
  transfers between devices with their start and end apart: 38 -> 38, of which waited for: 15 -> 18; matrix products, arithmetic and copies ran while one was open for 34% -> 1% of each run, Pallas kernels for 0% -> 3%
where the time goes in v2:
time: 109 us
  starting transfers between devices  48.7 us (45%)
  waiting for transfers between devices  38 us (35%)
  Pallas kernels  11.7 us (11%)
  local copies, waits for them, and re-layouts  7.34 us (7%)
  between operations  1.56 us (1%)
  other arithmetic  1.2 us (1%)
    ppermute x35, starting transfers between devices, swap(): lax.ppermute(value, axis, [(s, partner(s, step, count)) for s in range(co...  36.5 us
    ppermute x35, waiting for transfers between devices, swap(): lax.ppermute(value, axis, [(s, partner(s, step, count)) for s in range(co...  34.7 us
    ppermute x3, starting transfers between devices, handed_on(): return lax.ppermute(value, 'layer', [(layer, layer + 1)])  12.2 us
    pallas_call x12, Pallas kernels, kernel_call(): pl.pallas_call(body, out_shape=tuple(kept) if many else outs, in_specs=[p...  11.7 us
    unnamed x32, local copies, waits for them, and re-layouts  6.58 us
    ppermute x3, waiting for transfers between devices, handed_on(): return lax.ppermute(value, 'layer', [(layer, layer + 1)])  3.31 us
  transfers between devices with their start and end apart: 38, of which 18 were waited for; matrix products, arithmetic and copies ran while one was open for 1% of the time, Pallas kernels for 3%

profile of v2, /device:TPU:0, one launch (start us, length us, event | category | flops | bytes accessed | tf_op | source)
XLA Modules:
  0.0 108.5 jit_solution(7503043380169310020)
XLA Ops:
  1.7 3.1 %collective-permute-start = (bf16[448,128]{1,0:T(8,128)(2,1)S(1)}, bf16[448,128]{1,0:T(8,128)(2,1)S(1)}, u32[]{:S(2)}, u32[]{:S(2)}) collective-permute-start(bf16[448,128]{1,0:T(8,128)(2,1)S(1)} %bitcast_convert_fusion.refs_0_), channel_id=1, source_target_pairs={{0,4},{4,0},{8,12},{12,8},{1,5},{5,1},{9,13},{13,9},{2,6},{6,2},{1... | collective-permute-start | bytes 344072 | tf_op jit(solution)/shard_map/ppermute | solution.py:28
  4.8 2.6 %collective-permute-start.1 = (bf16[448,128]{1,0:T(8,128)(2,1)S(1)}, bf16[448,128]{1,0:T(8,128)(2,1)S(1)}, u32[]{:S(2)}, u32[]{:S(2)}) collective-permute-start(bf16[448,128]{1,0:T(8,128)(2,1)S(1)} %bitcast_convert_fusion.refs_0_), channel_id=1, source_target_pairs={{0,8},{4,12},{8,0},{12,4},{1,9},{5,13},{9,1},{13,5},{2,10},{6,14},... | collective-permute-start | bytes 344072 | tf_op jit(solution)/shard_map/ppermute | solution.py:28
  12.5 4.0 %collective-permute-done.1.refs_2_ = bf16[448,128]{1,0:T(8,128)(2,1)S(1)} collective-permute-done((bf16[448,128]{1,0:T(8,128)(2,1)S(1)}, bf16[448,128]{1,0:T(8,128)(2,1)S(1)}, u32[]{:S(2)}, u32[]{:S(2)}) %collective-permute-start.1) | collective-permute-done | bytes 114720 | tf_op jit(solution)/shard_map/ppermute | solution.py:28
  16.5 1.8 %collective-permute-start.11 = (bf16[464,128]{1,0:T(8,128)(2,1)S(1)}, bf16[464,128]{1,0:T(8,128)(2,1)S(1)}, u32[]{:S(2)}, u32[]{:S(2)}) collective-permute-start(bf16[464,128]{1,0:T(8,128)(2,1)S(1)} %get-tuple-element.33), channel_id=1, source_target_pairs={{0,4},{4,0},{8,12},{12,8},{1,5},{5,1},{9,13},{13,9},{2,6},{6,2},{1... | collective-permute-start | bytes 356360 | tf_op jit(solution)/shard_map/ppermute | solution.py:28
  18.3 1.2 %copy-done.2 = bf16[1,1,1792,256]{3,2,1,0:T(8,128)(2,1)S(1)} copy-done((bf16[1,1,1792,256]{3,2,1,0:T(8,128)(2,1)S(1)}, bf16[1,1,1792,256]{3,2,1,0:T(8,128)(2,1)}, u32[]{:S(2)}) %copy-start.2) | copy-done | bytes 917528
  20.4 1.3 %collective-permute-start.12 = (bf16[464,128]{1,0:T(8,128)(2,1)S(1)}, bf16[464,128]{1,0:T(8,128)(2,1)S(1)}, u32[]{:S(2)}, u32[]{:S(2)}) collective-permute-start(bf16[464,128]{1,0:T(8,128)(2,1)S(1)} %get-tuple-element.35), channel_id=1, source_target_pairs={{0,8},{4,12},{8,0},{12,4},{1,9},{5,13},{9,1},{13,5},{2,10},{6,14},... | collective-permute-start | bytes 356360 | tf_op jit(solution)/shard_map/ppermute | solution.py:28
  24.9 1.9 %collective-permute-start.4 = (bf16[2,128,128]{2,1,0:T(8,128)(2,1)S(1)}, bf16[2,128,128]{2,1,0:T(8,128)(2,1)S(1)}, u32[]{:S(2)}, u32[]{:S(2)}) collective-permute-start(bf16[2,128,128]{2,1,0:T(8,128)(2,1)S(1)} %shard_map.159.refs_0_), channel_id=1, source_target_pairs={{0,4},{4,0},{8,12},{12,8},{1,5},{5,1},{9,13},{13,9},{2,6},{6,2},{1... | collective-permute-start | bytes 196616 | tf_op jit(solution)/shard_map/ppermute | solution.py:28
  27.2 2.2 %collective-permute-start.6 = (bf16[2,128,128]{2,1,0:T(8,128)(2,1)S(1)}, bf16[2,128,128]{2,1,0:T(8,128)(2,1)S(1)}, u32[]{:S(2)}, u32[]{:S(2)}) collective-permute-start(bf16[2,128,128]{2,1,0:T(8,128)(2,1)S(1)} %shard_map.159.refs_0_), channel_id=1, source_target_pairs={{0,12},{4,8},{8,4},{12,0},{1,13},{5,9},{9,5},{13,1},{2,14},{6,10},... | collective-permute-start | bytes 196616 | tf_op jit(solution)/shard_map/ppermute | solution.py:28
  29.4 1.6 %collective-permute-start.13 = (bf16[464,128]{1,0:T(8,128)(2,1)S(1)}, bf16[464,128]{1,0:T(8,128)(2,1)S(1)}, u32[]{:S(2)}, u32[]{:S(2)}) collective-permute-start(bf16[464,128]{1,0:T(8,128)(2,1)S(1)} %get-tuple-element.37), channel_id=1, source_target_pairs={{0,12},{4,8},{8,4},{12,0},{1,13},{5,9},{9,5},{13,1},{2,14},{6,10},... | collective-permute-start | bytes 356360 | tf_op jit(solution)/shard_map/ppermute | solution.py:28
  31.5 5.7 %collective-permute-done.5.refs_2_ = bf16[2,128,128]{2,1,0:T(8,128)(2,1)S(1)} collective-permute-done((bf16[2,128,128]{2,1,0:T(8,128)(2,1)S(1)}, bf16[2,128,128]{2,1,0:T(8,128)(2,1)S(1)}, u32[]{:S(2)}, u32[]{:S(2)}) %collective-permute-start.5) | collective-permute-done | bytes 65568 | tf_op jit(solution)/shard_map/ppermute | solution.py:28
  38.7 1.8 %shard_map.161 = (f32[448,128]{1,0:T(8,128)S(1)}, f32[2,128,128]{2,1,0:T(8,128)S(1)}, bf16[2,128,128]{2,1,0:T(8,128)(2,1)S(1)}, f32[4,8,128]{2,1,0:T(8,128)S(1)}) custom-call(s32[3]{0:T(128)S(1)} %pad_add_fusion.place, bf16[2,128,128]{2,1,0:T(8,128)(2,1)S(1)} %shard_map.159.refs_0_, bf16[2,128,128]{2,1,0:T(8,128)(2,1)S(1)} %collective-permute-done.4.refs_1_, ...), custom_call_target="tpu_custom_call" | custom-call | flops 293601280 | bytes 3506688 | tf_op jit(solution)/shard_map/pallas_call | solution.py:247
  41.8 2.8 %collective-permute-start.15 = (bf16[2,128,128]{2,1,0:T(8,128)(2,1)S(1)}, bf16[2,128,128]{2,1,0:T(8,128)(2,1)S(1)}, u32[]{:S(2)}, u32[]{:S(2)}) collective-permute-start(bf16[2,128,128]{2,1,0:T(8,128)(2,1)S(1)} %add_convert_fusion.1.refs_0_), channel_id=1, source_target_pairs={{0,4},{4,0},{8,12},{12,8},{1,5},{5,1},{9,13},{13,9},{2,6},{6,2},{1... | collective-permute-start | bytes 196616 | tf_op jit(solution)/shard_map/ppermute | solution.py:28
  44.9 2.1 %collective-permute-start.17 = (bf16[2,128,128]{2,1,0:T(8,128)(2,1)S(1)}, bf16[2,128,128]{2,1,0:T(8,128)(2,1)S(1)}, u32[]{:S(2)}, u32[]{:S(2)}) collective-permute-start(bf16[2,128,128]{2,1,0:T(8,128)(2,1)S(1)} %add_convert_fusion.1.refs_0_), channel_id=1, source_target_pairs={{0,12},{4,8},{8,4},{12,0},{1,13},{5,9},{9,5},{13,1},{2,14},{6,10},... | collective-permute-start | bytes 196616 | tf_op jit(solution)/shard_map/ppermute | solution.py:28
  47.0 5.5 %collective-permute-done.16.refs_2_ = bf16[2,128,128]{2,1,0:T(8,128)(2,1)S(1)} collective-permute-done((bf16[2,128,128]{2,1,0:T(8,128)(2,1)S(1)}, bf16[2,128,128]{2,1,0:T(8,128)(2,1)S(1)}, u32[]{:S(2)}, u32[]{:S(2)}) %collective-permute-start.16) | collective-permute-done | bytes 65568 | tf_op jit(solution)/shard_map/ppermute | solution.py:28
  53.3 1.2 %collective-permute-done.18.refs_1_.also = bf16[2,128,128]{2,1,0:T(8,128)(2,1)S(1)} collective-permute-done((bf16[2,128,128]{2,1,0:T(8,128)(2,1)S(1)}, bf16[2,128,128]{2,1,0:T(8,128)(2,1)S(1)}, u32[]{:S(2)}, u32[]{:S(2)}) %collective-permute-start.18) | collective-permute-done | bytes 65568 | tf_op jit(solution)/shard_map/ppermute | solution.py:28
  55.4 3.4 %collective-permute-start.19 = (bf16[448,128]{1,0:T(8,128)(2,1)S(1)}, bf16[448,128]{1,0:T(8,128)(2,1)S(1)}, u32[]{:S(2)}, u32[]{:S(2)}) collective-permute-start(bf16[448,128]{1,0:T(8,128)(2,1)S(1)} %get-tuple-element.42), channel_id=1, source_target_pairs={{0,2},{1,3},{4,6},{5,7},{8,10},{9,11},{12,14},{13,15},{16,18},{17,... | collective-permute-start | bytes 344072 | tf_op jit(solution)/shard_map/ppermute | solution.py:448
  58.8 2.7 %collective-permute-done.19.refs_0_.refs_8_ = bf16[448,128]{1,0:T(8,128)(2,1)S(1)} collective-permute-done((bf16[448,128]{1,0:T(8,128)(2,1)S(1)}, bf16[448,128]{1,0:T(8,128)(2,1)S(1)}, u32[]{:S(2)}, u32[]{:S(2)}) %collective-permute-start.19) | collective-permute-done | bytes 114720 | tf_op jit(solution)/shard_map/ppermute | solution.py:448
  61.5 1.4 %collective-permute-start.20 = (bf16[448,128]{1,0:T(8,128)(2,1)S(1)}, bf16[448,128]{1,0:T(8,128)(2,1)S(1)}, u32[]{:S(2)}, u32[]{:S(2)}) collective-permute-start(bf16[448,128]{1,0:T(8,128)(2,1)S(1)} %collective-permute-done.19.refs_0_.refs_8_), channel_id=1, source_target_pairs={{0,4},{4,0},{8,12},{12,8},{1,5},{5,1},{9,13},{13,9},{2,6},{6,2},{1... | collective-permute-start | bytes 344072 | tf_op jit(solution)/shard_map/ppermute | solution.py:28
  63.9 1.9 %collective-permute-start.22 = (bf16[448,128]{1,0:T(8,128)(2,1)S(1)}, bf16[448,128]{1,0:T(8,128)(2,1)S(1)}, u32[]{:S(2)}, u32[]{:S(2)}) collective-permute-start(bf16[448,128]{1,0:T(8,128)(2,1)S(1)} %collective-permute-done.19.refs_0_.refs_8_), channel_id=1, source_target_pairs={{0,12},{4,8},{8,4},{12,0},{1,13},{5,9},{9,5},{13,1},{2,14},{6,10},... | collective-permute-start | bytes 344072 | tf_op jit(solution)/shard_map/ppermute | solution.py:28
  65.8 1.2 %collective-permute-done.20.refs_1_ = bf16[448,128]{1,0:T(8,128)(2,1)S(1)} collective-permute-done((bf16[448,128]{1,0:T(8,128)(2,1)S(1)}, bf16[448,128]{1,0:T(8,128)(2,1)S(1)}, u32[]{:S(2)}, u32[]{:S(2)}) %collective-permute-start.20) | collective-permute-done | bytes 114720 | tf_op jit(solution)/shard_map/ppermute | solution.py:28
  67.0 6.7 %collective-permute-done.21.refs_2_ = bf16[448,128]{1,0:T(8,128)(2,1)S(1)} collective-permute-done((bf16[448,128]{1,0:T(8,128)(2,1)S(1)}, bf16[448,128]{1,0:T(8,128)(2,1)S(1)}, u32[]{:S(2)}, u32[]{:S(2)}) %collective-permute-start.21) | collective-permute-done | bytes 114720 | tf_op jit(solution)/shard_map/ppermute | solution.py:28
  74.7 1.2 %collective-permute-done.23.got = f32[128,128]{1,0:T(8,128)S(1)} collective-permute-done((f32[128,128]{1,0:T(8,128)S(1)}, f32[128,128]{1,0:T(8,128)S(1)}, u32[]{:S(2)}, u32[]{:S(2)}) %collective-permute-start.23) | collective-permute-done | bytes 65568 | tf_op jit(solution)/shard_map/ppermute | solution.py:28
  76.8 2.1 %collective-permute-start.24 = (bf16[2,128,128]{2,1,0:T(8,128)(2,1)S(1)}, bf16[2,128,128]{2,1,0:T(8,128)(2,1)S(1)}, u32[]{:S(2)}, u32[]{:S(2)}) collective-permute-start(bf16[2,128,128]{2,1,0:T(8,128)(2,1)S(1)} %shard_map.165.refs_0_), channel_id=1, source_target_pairs={{0,4},{4,0},{8,12},{12,8},{1,5},{5,1},{9,13},{13,9},{2,6},{6,2},{1... | collective-permute-start | bytes 196616 | tf_op jit(solution)/shard_map/ppermute | solution.py:28
  79.3 2.0 %collective-permute-start.26 = (bf16[2,128,128]{2,1,0:T(8,128)(2,1)S(1)}, bf16[2,128,128]{2,1,0:T(8,128)(2,1)S(1)}, u32[]{:S(2)}, u32[]{:S(2)}) collective-permute-start(bf16[2,128,128]{2,1,0:T(8,128)(2,1)S(1)} %shard_map.165.refs_0_), channel_id=1, source_target_pairs={{0,12},{4,8},{8,4},{12,0},{1,13},{5,9},{9,5},{13,1},{2,14},{6,10},... | collective-permute-start | bytes 196616 | tf_op jit(solution)/shard_map/ppermute | solution.py:28
  81.3 4.4 %collective-permute-start.31 = (bf16[448,128]{1,0:T(8,128)(2,1)S(1)}, bf16[448,128]{1,0:T(8,128)(2,1)S(1)}, u32[]{:S(2)}, u32[]{:S(2)}) collective-permute-start(bf16[448,128]{1,0:T(8,128)(2,1)S(1)} %get-tuple-element.46), channel_id=1, source_target_pairs={{0,2},{1,3},{4,6},{5,7},{8,10},{9,11},{12,14},{13,15},{16,18},{17,... | collective-permute-start | bytes 344072 | tf_op jit(solution)/shard_map/ppermute | solution.py:448
  88.3 1.8 %shard_map.166 = (f32[448,128]{1,0:T(8,128)S(1)}, f32[2,128,128]{2,1,0:T(8,128)S(1)}, bf16[2,128,128]{2,1,0:T(8,128)(2,1)S(1)}, f32[4,8,128]{2,1,0:T(8,128)S(1)}) custom-call(s32[3]{0:T(128)S(1)} %pad_add_fusion.place, bf16[2,128,128]{2,1,0:T(8,128)(2,1)S(1)} %shard_map.165.refs_0_, bf16[2,128,128]{2,1,0:T(8,128)(2,1)S(1)} %collective-permute-done.24.refs_1_, ...), custom_call_target="tpu_custom_call" | custom-call | flops 293601280 | bytes 3506688 | tf_op jit(solution)/shard_map/pallas_call | solution.py:247
  91.3 4.4 %collective-permute-start.37 = (f32[1,448,128]{2,1,0:T(8,128)S(1)}, f32[1,448,128]{2,1,0:T(8,128)S(1)}, u32[]{:S(2)}, u32[]{:S(2)}) collective-permute-start(f32[1,448,128]{2,1,0:T(8,128)S(1)} %shard_map.168), channel_id=1, source_target_pairs={{0,2},{1,3},{4,6},{5,7},{8,10},{9,11},{12,14},{13,15},{16,18},{17,... | collective-permute-start | bytes 688136 | tf_op jit(solution)/shard_map/ppermute | solution.py:448
  96.9 1.4 %collective-permute-start.34 = (bf16[2,128,128]{2,1,0:T(8,128)(2,1)S(1)}, bf16[2,128,128]{2,1,0:T(8,128)(2,1)S(1)}, u32[]{:S(2)}, u32[]{:S(2)}) collective-permute-start(bf16[2,128,128]{2,1,0:T(8,128)(2,1)S(1)} %add_convert_fusion.refs_0_), channel_id=1, source_target_pairs={{0,8},{4,12},{8,0},{12,4},{1,9},{5,13},{9,1},{13,5},{2,10},{6,14},... | collective-permute-start | bytes 196616 | tf_op jit(solution)/shard_map/ppermute | solution.py:28
  98.3 1.9 %collective-permute-start.35 = (bf16[2,128,128]{2,1,0:T(8,128)(2,1)S(1)}, bf16[2,128,128]{2,1,0:T(8,128)(2,1)S(1)}, u32[]{:S(2)}, u32[]{:S(2)}) collective-permute-start(bf16[2,128,128]{2,1,0:T(8,128)(2,1)S(1)} %add_convert_fusion.refs_0_), channel_id=1, source_target_pairs={{0,12},{4,8},{8,4},{12,0},{1,13},{5,9},{9,5},{13,1},{2,14},{6,10},... | collective-permute-start | bytes 196616 | tf_op jit(solution)/shard_map/ppermute | solution.py:28
  100.2 4.9 %collective-permute-done.34.refs_2_ = bf16[2,128,128]{2,1,0:T(8,128)(2,1)S(1)} collective-permute-done((bf16[2,128,128]{2,1,0:T(8,128)(2,1)S(1)}, bf16[2,128,128]{2,1,0:T(8,128)(2,1)S(1)}, u32[]{:S(2)}, u32[]{:S(2)}) %collective-permute-start.34) | collective-permute-done | bytes 65568 | tf_op jit(solution)/shard_map/ppermute | solution.py:28
  105.8 1.2 %collective-permute-done.36.refs_1_ = bf16[2,128,128]{2,1,0:T(8,128)(2,1)S(1)} collective-permute-done((bf16[2,128,128]{2,1,0:T(8,128)(2,1)S(1)}, bf16[2,128,128]{2,1,0:T(8,128)(2,1)S(1)}, u32[]{:S(2)}, u32[]{:S(2)}) %collective-permute-start.36) | collective-permute-done | bytes 65568 | tf_op jit(solution)/shard_map/ppermute | solution.py:28
  107.0 1.5 %shard_map.169 = (f32[448,128]{1,0:T(8,128)}, bf16[128,128]{1,0:T(8,128)(2,1)}) custom-call(s32[3]{0:T(128)S(1)} %pad_add_fusion.place, bf16[2,128,128]{2,1,0:T(8,128)(2,1)S(1)} %shard_map.167.refs_0_, bf16[2,128,128]{2,1,0:T(8,128)(2,1)S(1)} %collective-permute-done.36.refs_1_, bf16[2,448,512]{2,1,0:T(8,128)(2,1)S(1)} %bitcast.31, ...), custom_call_target="tpu_custom_call" | custom-call | flops 58720256 | bytes 2260992 | tf_op jit(solution)/shard_map/pallas_call | solution.py:247
  (93 shorter events, 24.0 us)
Async XLA Ops:
  1.7 10.8 %collective-permute-start = (bf16[448,128]{1,0:T(8,128)(2,1)S(1)}, bf16[448,128]{1,0:T(8,128)(2,1)S(1)}, u32[]{:S(2)}, u32[]{:S(2)}) collective-permute-start(bf16[448,128]{1,0:T(8,128)(2,1)S(1)} %bitcast_convert_fusion.refs_0_), channel_id=1, source_target_pairs={{0,4},{4,0},{8,12},{12,8},{1,5},{5,1},{9,13},{13,9},{2,6},{6,2},{1... | collective-permute-start | bytes 344072 | tf_op jit(solution)/shard_map/ppermute | solution.py:28
  4.8 11.7 %collective-permute-start.1 = (bf16[448,128]{1,0:T(8,128)(2,1)S(1)}, bf16[448,128]{1,0:T(8,128)(2,1)S(1)}, u32[]{:S(2)}, u32[]{:S(2)}) collective-permute-start(bf16[448,128]{1,0:T(8,128)(2,1)S(1)} %bitcast_convert_fusion.refs_0_), channel_id=1, source_target_pairs={{0,8},{4,12},{8,0},{12,4},{1,9},{5,13},{9,1},{13,5},{2,10},{6,14},... | collective-permute-start | bytes 344072 | tf_op jit(solution)/shard_map/ppermute | solution.py:28
  7.4 9.1 %collective-permute-start.2 = (bf16[448,128]{1,0:T(8,128)(2,1)S(1)}, bf16[448,128]{1,0:T(8,128)(2,1)S(1)}, u32[]{:S(2)}, u32[]{:S(2)}) collective-permute-start(bf16[448,128]{1,0:T(8,128)(2,1)S(1)} %bitcast_convert_fusion.refs_0_), channel_id=1, source_target_pairs={{0,12},{4,8},{8,4},{12,0},{1,13},{5,9},{9,5},{13,1},{2,14},{6,10},... | collective-permute-start | bytes 344072 | tf_op jit(solution)/shard_map/ppermute | solution.py:28
  16.5 12.8 %collective-permute-start.11 = (bf16[464,128]{1,0:T(8,128)(2,1)S(1)}, bf16[464,128]{1,0:T(8,128)(2,1)S(1)}, u32[]{:S(2)}, u32[]{:S(2)}) collective-permute-start(bf16[464,128]{1,0:T(8,128)(2,1)S(1)} %get-tuple-element.33), channel_id=1, source_target_pairs={{0,4},{4,0},{8,12},{12,8},{1,5},{5,1},{9,13},{13,9},{2,6},{6,2},{1... | collective-permute-start | bytes 356360 | tf_op jit(solution)/shard_map/ppermute | solution.py:28
  20.4 2.2 %collective-permute-start.3 = (f32[128,128]{1,0:T(8,128)S(1)}, f32[128,128]{1,0:T(8,128)S(1)}, u32[]{:S(2)}, u32[]{:S(2)}) collective-permute-start(f32[128,128]{1,0:T(8,128)S(1)} %get-tuple-element.30), channel_id=1, source_target_pairs={{0,1},{1,0},{2,3},{3,2},{4,5},{5,4},{6,7},{7,6},{8,9},{9,8},{10,11... | collective-permute-start | bytes 196616 | tf_op jit(solution)/shard_map/ppermute | solution.py:28
  20.4 10.5 %collective-permute-start.12 = (bf16[464,128]{1,0:T(8,128)(2,1)S(1)}, bf16[464,128]{1,0:T(8,128)(2,1)S(1)}, u32[]{:S(2)}, u32[]{:S(2)}) collective-permute-start(bf16[464,128]{1,0:T(8,128)(2,1)S(1)} %get-tuple-element.35), channel_id=1, source_target_pairs={{0,8},{4,12},{8,0},{12,4},{1,9},{5,13},{9,1},{13,5},{2,10},{6,14},... | collective-permute-start | bytes 356360 | tf_op jit(solution)/shard_map/ppermute | solution.py:28
  24.9 6.3 %collective-permute-start.4 = (bf16[2,128,128]{2,1,0:T(8,128)(2,1)S(1)}, bf16[2,128,128]{2,1,0:T(8,128)(2,1)S(1)}, u32[]{:S(2)}, u32[]{:S(2)}) collective-permute-start(bf16[2,128,128]{2,1,0:T(8,128)(2,1)S(1)} %shard_map.159.refs_0_), channel_id=1, source_target_pairs={{0,4},{4,0},{8,12},{12,8},{1,5},{5,1},{9,13},{13,9},{2,6},{6,2},{1... | collective-permute-start | bytes 196616 | tf_op jit(solution)/shard_map/ppermute | solution.py:28
  26.7 10.4 %collective-permute-start.5 = (bf16[2,128,128]{2,1,0:T(8,128)(2,1)S(1)}, bf16[2,128,128]{2,1,0:T(8,128)(2,1)S(1)}, u32[]{:S(2)}, u32[]{:S(2)}) collective-permute-start(bf16[2,128,128]{2,1,0:T(8,128)(2,1)S(1)} %shard_map.159.refs_0_), channel_id=1, source_target_pairs={{0,8},{4,12},{8,0},{12,4},{1,9},{5,13},{9,1},{13,5},{2,10},{6,14},... | collective-permute-start | bytes 196616 | tf_op jit(solution)/shard_map/ppermute | solution.py:28
  27.2 10.0 %collective-permute-start.6 = (bf16[2,128,128]{2,1,0:T(8,128)(2,1)S(1)}, bf16[2,128,128]{2,1,0:T(8,128)(2,1)S(1)}, u32[]{:S(2)}, u32[]{:S(2)}) collective-permute-start(bf16[2,128,128]{2,1,0:T(8,128)(2,1)S(1)} %shard_map.159.refs_0_), channel_id=1, source_target_pairs={{0,12},{4,8},{8,4},{12,0},{1,13},{5,9},{9,5},{13,1},{2,14},{6,10},... | collective-permute-start | bytes 196616 | tf_op jit(solution)/shard_map/ppermute | solution.py:28
  29.4 8.4 %collective-permute-start.13 = (bf16[464,128]{1,0:T(8,128)(2,1)S(1)}, bf16[464,128]{1,0:T(8,128)(2,1)S(1)}, u32[]{:S(2)}, u32[]{:S(2)}) collective-permute-start(bf16[464,128]{1,0:T(8,128)(2,1)S(1)} %get-tuple-element.37), channel_id=1, source_target_pairs={{0,12},{4,8},{8,4},{12,0},{1,13},{5,9},{9,5},{13,1},{2,14},{6,10},... | collective-permute-start | bytes 356360 | tf_op jit(solution)/shard_map/ppermute | solution.py:28
  31.0 6.7 %collective-permute-start.7 = (bf16[2,128,128]{2,1,0:T(8,128)(2,1)S(1)}, bf16[2,128,128]{2,1,0:T(8,128)(2,1)S(1)}, u32[]{:S(2)}, u32[]{:S(2)}) collective-permute-start(bf16[2,128,128]{2,1,0:T(8,128)(2,1)S(1)} %shard_map.159.refs_0_), channel_id=1, source_target_pairs={{0,1},{1,0},{2,3},{3,2},{4,5},{5,4},{6,7},{7,6},{8,9},{9,8},{10,11... | collective-permute-start | bytes 196616 | tf_op jit(solution)/shard_map/ppermute | solution.py:28
  31.2 6.5 %collective-permute-start.8 = (bf16[2,128,128]{2,1,0:T(8,128)(2,1)S(1)}, bf16[2,128,128]{2,1,0:T(8,128)(2,1)S(1)}, u32[]{:S(2)}, u32[]{:S(2)}) collective-permute-start(bf16[2,128,128]{2,1,0:T(8,128)(2,1)S(1)} %collective-permute-done.4.refs_1_), channel_id=1, source_target_pairs={{0,1},{1,0},{2,3},{3,2},{4,5},{5,4},{6,7},{7,6},{8,9},{9,8},{10,11... | collective-permute-start | bytes 196616 | tf_op jit(solution)/shard_map/ppermute | solution.py:28
  37.2 1.4 %collective-permute-start.10 = (bf16[2,128,128]{2,1,0:T(8,128)(2,1)S(1)}, bf16[2,128,128]{2,1,0:T(8,128)(2,1)S(1)}, u32[]{:S(2)}, u32[]{:S(2)}) collective-permute-start(bf16[2,128,128]{2,1,0:T(8,128)(2,1)S(1)} %collective-permute-done.6.refs_3_), channel_id=1, source_target_pairs={{0,1},{1,0},{2,3},{3,2},{4,5},{5,4},{6,7},{7,6},{8,9},{9,8},{10,11... | collective-permute-start | bytes 196616 | tf_op jit(solution)/shard_map/ppermute | solution.py:28
  41.8 5.2 %collective-permute-start.15 = (bf16[2,128,128]{2,1,0:T(8,128)(2,1)S(1)}, bf16[2,128,128]{2,1,0:T(8,128)(2,1)S(1)}, u32[]{:S(2)}, u32[]{:S(2)}) collective-permute-start(bf16[2,128,128]{2,1,0:T(8,128)(2,1)S(1)} %add_convert_fusion.1.refs_0_), channel_id=1, source_target_pairs={{0,4},{4,0},{8,12},{12,8},{1,5},{5,1},{9,13},{13,9},{2,6},{6,2},{1... | collective-permute-start | bytes 196616 | tf_op jit(solution)/shard_map/ppermute | solution.py:28
  44.6 8.0 %collective-permute-start.16 = (bf16[2,128,128]{2,1,0:T(8,128)(2,1)S(1)}, bf16[2,128,128]{2,1,0:T(8,128)(2,1)S(1)}, u32[]{:S(2)}, u32[]{:S(2)}) collective-permute-start(bf16[2,128,128]{2,1,0:T(8,128)(2,1)S(1)} %add_convert_fusion.1.refs_0_), channel_id=1, source_target_pairs={{0,8},{4,12},{8,0},{12,4},{1,9},{5,13},{9,1},{13,5},{2,10},{6,14},... | collective-permute-start | bytes 196616 | tf_op jit(solution)/shard_map/ppermute | solution.py:28
  44.9 7.7 %collective-permute-start.17 = (bf16[2,128,128]{2,1,0:T(8,128)(2,1)S(1)}, bf16[2,128,128]{2,1,0:T(8,128)(2,1)S(1)}, u32[]{:S(2)}, u32[]{:S(2)}) collective-permute-start(bf16[2,128,128]{2,1,0:T(8,128)(2,1)S(1)} %add_convert_fusion.1.refs_0_), channel_id=1, source_target_pairs={{0,12},{4,8},{8,4},{12,0},{1,13},{5,9},{9,5},{13,1},{2,14},{6,10},... | collective-permute-start | bytes 196616 | tf_op jit(solution)/shard_map/ppermute | solution.py:28
  55.4 6.1 %collective-permute-start.19 = (bf16[448,128]{1,0:T(8,128)(2,1)S(1)}, bf16[448,128]{1,0:T(8,128)(2,1)S(1)}, u32[]{:S(2)}, u32[]{:S(2)}) collective-permute-start(bf16[448,128]{1,0:T(8,128)(2,1)S(1)} %get-tuple-element.42), channel_id=1, source_target_pairs={{0,2},{1,3},{4,6},{5,7},{8,10},{9,11},{12,14},{13,15},{16,18},{17,... | collective-permute-start | bytes 344072 | tf_op jit(solution)/shard_map/ppermute | solution.py:448
  61.5 5.6 %collective-permute-start.20 = (bf16[448,128]{1,0:T(8,128)(2,1)S(1)}, bf16[448,128]{1,0:T(8,128)(2,1)S(1)}, u32[]{:S(2)}, u32[]{:S(2)}) collective-permute-start(bf16[448,128]{1,0:T(8,128)(2,1)S(1)} %collective-permute-done.19.refs_0_.refs_8_), channel_id=1, source_target_pairs={{0,4},{4,0},{8,12},{12,8},{1,5},{5,1},{9,13},{13,9},{2,6},{6,2},{1... | collective-permute-start | bytes 344072 | tf_op jit(solution)/shard_map/ppermute | solution.py:28
  62.9 10.9 %collective-permute-start.21 = (bf16[448,128]{1,0:T(8,128)(2,1)S(1)}, bf16[448,128]{1,0:T(8,128)(2,1)S(1)}, u32[]{:S(2)}, u32[]{:S(2)}) collective-permute-start(bf16[448,128]{1,0:T(8,128)(2,1)S(1)} %collective-permute-done.19.refs_0_.refs_8_), channel_id=1, source_target_pairs={{0,8},{4,12},{8,0},{12,4},{1,9},{5,13},{9,1},{13,5},{2,10},{6,14},... | collective-permute-start | bytes 344072 | tf_op jit(solution)/shard_map/ppermute | solution.py:28
  63.9 9.9 %collective-permute-start.22 = (bf16[448,128]{1,0:T(8,128)(2,1)S(1)}, bf16[448,128]{1,0:T(8,128)(2,1)S(1)}, u32[]{:S(2)}, u32[]{:S(2)}) collective-permute-start(bf16[448,128]{1,0:T(8,128)(2,1)S(1)} %collective-permute-done.19.refs_0_.refs_8_), channel_id=1, source_target_pairs={{0,12},{4,8},{8,4},{12,0},{1,13},{5,9},{9,5},{13,1},{2,14},{6,10},... | collective-permute-start | bytes 344072 | tf_op jit(solution)/shard_map/ppermute | solution.py:28
  76.8 9.0 %collective-permute-start.24 = (bf16[2,128,128]{2,1,0:T(8,128)(2,1)S(1)}, bf16[2,128,128]{2,1,0:T(8,128)(2,1)S(1)}, u32[]{:S(2)}, u32[]{:S(2)}) collective-permute-start(bf16[2,128,128]{2,1,0:T(8,128)(2,1)S(1)} %shard_map.165.refs_0_), channel_id=1, source_target_pairs={{0,4},{4,0},{8,12},{12,8},{1,5},{5,1},{9,13},{13,9},{2,6},{6,2},{1... | collective-permute-start | bytes 196616 | tf_op jit(solution)/shard_map/ppermute | solution.py:28
  78.8 8.0 %collective-permute-start.25 = (bf16[2,128,128]{2,1,0:T(8,128)(2,1)S(1)}, bf16[2,128,128]{2,1,0:T(8,128)(2,1)S(1)}, u32[]{:S(2)}, u32[]{:S(2)}) collective-permute-start(bf16[2,128,128]{2,1,0:T(8,128)(2,1)S(1)} %shard_map.165.refs_0_), channel_id=1, source_target_pairs={{0,8},{4,12},{8,0},{12,4},{1,9},{5,13},{9,1},{13,5},{2,10},{6,14},... | collective-permute-start | bytes 196616 | tf_op jit(solution)/shard_map/ppermute | solution.py:28
  79.3 7.6 %collective-permute-start.26 = (bf16[2,128,128]{2,1,0:T(8,128)(2,1)S(1)}, bf16[2,128,128]{2,1,0:T(8,128)(2,1)S(1)}, u32[]{:S(2)}, u32[]{:S(2)}) collective-permute-start(bf16[2,128,128]{2,1,0:T(8,128)(2,1)S(1)} %shard_map.165.refs_0_), channel_id=1, source_target_pairs={{0,12},{4,8},{8,4},{12,0},{1,13},{5,9},{9,5},{13,1},{2,14},{6,10},... | collective-permute-start | bytes 196616 | tf_op jit(solution)/shard_map/ppermute | solution.py:28
  81.3 6.7 %collective-permute-start.31 = (bf16[448,128]{1,0:T(8,128)(2,1)S(1)}, bf16[448,128]{1,0:T(8,128)(2,1)S(1)}, u32[]{:S(2)}, u32[]{:S(2)}) collective-permute-start(bf16[448,128]{1,0:T(8,128)(2,1)S(1)} %get-tuple-element.46), channel_id=1, source_target_pairs={{0,2},{1,3},{4,6},{5,7},{8,10},{9,11},{12,14},{13,15},{16,18},{17,... | collective-permute-start | bytes 344072 | tf_op jit(solution)/shard_map/ppermute | solution.py:448
  85.7 2.3 %collective-permute-start.27 = (bf16[2,128,128]{2,1,0:T(8,128)(2,1)S(1)}, bf16[2,128,128]{2,1,0:T(8,128)(2,1)S(1)}, u32[]{:S(2)}, u32[]{:S(2)}) collective-permute-start(bf16[2,128,128]{2,1,0:T(8,128)(2,1)S(1)} %shard_map.165.refs_0_), channel_id=1, source_target_pairs={{0,1},{1,0},{2,3},{3,2},{4,5},{5,4},{6,7},{7,6},{8,9},{9,8},{10,11... | collective-permute-start | bytes 196616 | tf_op jit(solution)/shard_map/ppermute | solution.py:28
  85.7 2.3 %collective-permute-start.28 = (bf16[2,128,128]{2,1,0:T(8,128)(2,1)S(1)}, bf16[2,128,128]{2,1,0:T(8,128)(2,1)S(1)}, u32[]{:S(2)}, u32[]{:S(2)}) collective-permute-start(bf16[2,128,128]{2,1,0:T(8,128)(2,1)S(1)} %collective-permute-done.24.refs_1_), channel_id=1, source_target_pairs={{0,1},{1,0},{2,3},{3,2},{4,5},{5,4},{6,7},{7,6},{8,9},{9,8},{10,11... | collective-permute-start | bytes 196616 | tf_op jit(solution)/shard_map/ppermute | solution.py:28
  86.9 1.4 %collective-permute-start.30 = (bf16[2,128,128]{2,1,0:T(8,128)(2,1)S(1)}, bf16[2,128,128]{2,1,0:T(8,128)(2,1)S(1)}, u32[]{:S(2)}, u32[]{:S(2)}) collective-permute-start(bf16[2,128,128]{2,1,0:T(8,128)(2,1)S(1)} %collective-permute-done.26.refs_3_), channel_id=1, source_target_pairs={{0,1},{1,0},{2,3},{3,2},{4,5},{5,4},{6,7},{7,6},{8,9},{9,8},{10,11... | collective-permute-start | bytes 196616 | tf_op jit(solution)/shard_map/ppermute | solution.py:28
  90.1 5.7 %collective-permute-start.32 = (bf16[2,128,128]{2,1,0:T(8,128)(2,1)S(1)}, bf16[2,128,128]{2,1,0:T(8,128)(2,1)S(1)}, u32[]{:S(2)}, u32[]{:S(2)}) collective-permute-start(bf16[2,128,128]{2,1,0:T(8,128)(2,1)S(1)} %get-tuple-element.48), channel_id=1, source_target_pairs={{0,1},{1,0},{2,3},{3,2},{4,5},{5,4},{6,7},{7,6},{8,9},{9,8},{10,11... | collective-permute-start | bytes 196616 | tf_op jit(solution)/shard_map/ppermute | solution.py:28
  91.3 14.5 %collective-permute-start.37 = (f32[1,448,128]{2,1,0:T(8,128)S(1)}, f32[1,448,128]{2,1,0:T(8,128)S(1)}, u32[]{:S(2)}, u32[]{:S(2)}) collective-permute-start(f32[1,448,128]{2,1,0:T(8,128)S(1)} %shard_map.168), channel_id=1, source_target_pairs={{0,2},{1,3},{4,6},{5,7},{8,10},{9,11},{12,14},{13,15},{16,18},{17,... | collective-permute-start | bytes 688136 | tf_op jit(solution)/shard_map/ppermute | solution.py:448
  95.8 4.5 %collective-permute-start.33 = (bf16[2,128,128]{2,1,0:T(8,128)(2,1)S(1)}, bf16[2,128,128]{2,1,0:T(8,128)(2,1)S(1)}, u32[]{:S(2)}, u32[]{:S(2)}) collective-permute-start(bf16[2,128,128]{2,1,0:T(8,128)(2,1)S(1)} %add_convert_fusion.refs_0_), channel_id=1, source_target_pairs={{0,4},{4,0},{8,12},{12,8},{1,5},{5,1},{9,13},{13,9},{2,6},{6,2},{1... | collective-permute-start | bytes 196616 | tf_op jit(solution)/shard_map/ppermute | solution.py:28
  96.9 8.2 %collective-permute-start.34 = (bf16[2,128,128]{2,1,0:T(8,128)(2,1)S(1)}, bf16[2,128,128]{2,1,0:T(8,128)(2,1)S(1)}, u32[]{:S(2)}, u32[]{:S(2)}) collective-permute-start(bf16[2,128,128]{2,1,0:T(8,128)(2,1)S(1)} %add_convert_fusion.refs_0_), channel_id=1, source_target_pairs={{0,8},{4,12},{8,0},{12,4},{1,9},{5,13},{9,1},{13,5},{2,10},{6,14},... | collective-permute-start | bytes 196616 | tf_op jit(solution)/shard_map/ppermute | solution.py:28
  98.3 6.8 %collective-permute-start.35 = (bf16[2,128,128]{2,1,0:T(8,128)(2,1)S(1)}, bf16[2,128,128]{2,1,0:T(8,128)(2,1)S(1)}, u32[]{:S(2)}, u32[]{:S(2)}) collective-permute-start(bf16[2,128,128]{2,1,0:T(8,128)(2,1)S(1)} %add_convert_fusion.refs_0_), channel_id=1, source_target_pairs={{0,12},{4,8},{8,4},{12,0},{1,13},{5,9},{9,5},{13,1},{2,14},{6,10},... | collective-permute-start | bytes 196616 | tf_op jit(solution)/shard_map/ppermute | solution.py:28
  (22 other events, 221.5 us)

commit v3 on v2

--- a/solution.py
+++ b/solution.py
@@ -37,6 +37,10 @@
 
 def spread(value, axis="feat"):
     return [value] + [swap(value, axis, step) for step in peers(axis)]
+
+
+def exchange(sends):
+    return [sends[0]] + [swap(sends[step], "feat", step) for step in peers("feat")]
 
 
 def total(blocks):
@@ -240,19 +244,19 @@
     return jax.ShapeDtypeStruct(sizes, dtype)
 
 
-def kernel_call(body, outs, scalars, arrays, scratch=(), flops=0):
+def kernel_call(body, outs, scalars, arrays, left=(), scratch=(), flops=0):
     many = isinstance(outs, (list, tuple))
     kept = list(outs) if many else [outs]
     size = sum(a.size * a.dtype.itemsize for a in arrays) + sum(a.size * a.dtype.itemsize for a in kept)
     return pl.pallas_call(
         body,
         out_shape=tuple(kept) if many else outs,
-        in_specs=[pl.BlockSpec(memory_space=pltpu.SMEM)] * len(scalars) + [pl.BlockSpec(memory_space=pltpu.VMEM)] * len(arrays),
+        in_specs=[pl.BlockSpec(memory_space=pltpu.SMEM)] * len(scalars) + [pl.BlockSpec(memory_space=pltpu.VMEM)] * len(arrays) + [pl.BlockSpec(memory_space=pltpu.HBM)] * len(left),
         out_specs=tuple(pl.BlockSpec(memory_space=pltpu.VMEM) for _ in kept) if many else pl.BlockSpec(memory_space=pltpu.VMEM),
         scratch_shapes=list(scratch),
         compiler_params=pltpu.CompilerParams(vmem_limit_bytes=16 * 1024 * 1024),
         cost_estimate=pl.CostEstimate(flops=int(flops), bytes_accessed=int(size), transcendentals=0),
-    )(*scalars, *arrays)
+    )(*scalars, *arrays, *left)
 
 
 def split_terms(value):
@@ -263,8 +267,7 @@
     return [high, middle, low]
 
 
-def pack_body(ranges, place, chosen, table, mode, index, bias, enc, *sends):
-    width = enc.shape[0] // ranges
+def facts_body(place, lengths, chosen, table, mode, index, bias, scale, patterns, info, mixing, scales):
     block = chosen[0, 0]
     modes = mode[pl.ds(block, 1), :]
     entries = index[pl.ds(block, 1), :]
@@ -274,87 +277,213 @@
     gain = jnp.where(modes == 1, 0.0, jnp.where(modes == 2, levels, 1.0))
     shift = jnp.where(modes == 1, levels, 0.0)
     terms = [t.astype(F32) for v in (bias[...], gain, shift) for t in split_terms(v)]
-    info = jnp.concatenate(terms + [jnp.zeros((INFO - len(terms), bias.shape[1]), F32)], axis=0).astype(BF16)
-    for step, send in enumerate(sends):
-        other = partner(place[0], step, ranges) if step else place[0]
-        send[0:width, :] = enc[pl.ds(pl.multiple_of(other * width, 16), width), :]
-        send[width:, :] = info
+    info[...] = jnp.concatenate(terms + [jnp.zeros((INFO - len(terms), bias.shape[1]), F32)], axis=0).astype(BF16)
+    heads, prompts, seq, _ = patterns.shape
+    query = lax.broadcasted_iota(jnp.int32, (seq, seq), 0)
+    key = lax.broadcasted_iota(jnp.int32, (seq, seq), 1)
+    for p in range(prompts):
+        keep = (key <= query) & (key < lengths[p])
+        for head in range(heads):
+            pattern = jnp.where(keep, patterns[head, p].astype(F32), 0.0)
+            zero = jnp.zeros_like(pattern)
+            row = jnp.concatenate([pattern if q == p else zero for q in range(prompts)], axis=1)
+            mixing[head, p * seq : (p + 1) * seq, :] = row.astype(BF16)
+    rows = scale.shape[1]
+    scales[...] = jnp.broadcast_to(scale[...], (rows, rows)).T
+
+
+def start_body(ranges, place, state, weight, enc, *refs):
+    sends, sems = refs[:-1], refs[-1]
+    width, rows = state.shape
+    part = width // 2
+    low = state[...].astype(BF16)
+    sends[0][...] = low
+
+    def copies(source, first, size, at, group):
+        made = []
+        for step in range(1, ranges):
+            start = pl.multiple_of(partner(place[0], step, ranges) * width + first, 16)
+            made.append(
+                pltpu.make_async_copy(
+                    source.at[pl.ds(start, size), pl.ds(0, rows)],
+                    sends[step].at[pl.ds(at, size)],
+                    sems.at[group, step - 1],
+                )
+            )
+        return made
+
+    rest = copies(enc, place[3] * part, part, width, 0)
+    for copy in rest:
+        copy.start()
+
+    @pl.when(place[2] == 0)
+    def _():
+        for send in sends[1:]:
+            send[0:width] = low
+
+    @pl.when(place[2] > 0)
+    def _():
+        carried = copies(weight, 0, width, 0, 1)
+        for copy in carried:
+            copy.start()
+        for copy in carried:
+            copy.wait()
+
+    for copy in rest:
+        copy.wait()
+
+
+def carry(place, ranges, weight, width, first, count, made, sends):
+    rows, half = made[0].shape
+    for n, block in enumerate(made):
+        sends[0][n * rows : (n + 1) * rows] = block
+    for step in range(1, ranges):
+        other = partner(place[0], step, ranges)
+        for n, block in enumerate(made):
+            at, size = n * rows, min(max(count - n * rows, 0), rows)
+            if size > 0:
+                start = pl.multiple_of(other * width + first + at, 16)
+                carried = weight[pl.ds(start, size), half:]
+                sends[step][at : at + size] = jnp.where(place[2] == 0, block[0:size], carried)
+            if size < rows:
+                sends[step][at + size : at + rows] = block[size:]
 
 
 def values_body(ranges, place, *refs):
-    blocks, (weight, own, other) = refs[:ranges], refs[ranges:]
+    blocks, (weight, own, other, passed) = refs[:ranges], refs[ranges:]
     width, half = blocks[0].shape[0], own.shape[1]
     acc = None
     for step, block in enumerate(blocks):
         n = partner(place[0], step, ranges) if step else place[0]
-        part = dot_tn(block[...], weight[pl.ds(pl.multiple_of(n * width, 16), width), :])
+        if step:
+            size = block.shape[0] - width
+            passed[(step - 1) * size : step * size] = block[width:]
+        part = dot_tn(block[0:width], weight[pl.ds(pl.multiple_of(n * width, 16), width), :])
         acc = part if acc is None else acc + part
     first = place[1] == 0
     own[...] = jnp.where(first, acc[:, :half], acc[:, half:])
     other[...] = jnp.where(first, acc[:, half:], acc[:, :half])
 
 
-def heads_body(kv_cols, head_dim, place, lengths, own, got, scale, patterns, out):
-    per_group, seq, prompts = out.shape[0], patterns.shape[2], patterns.shape[1]
-    values = ((own[...] + got[...]) * scale[...]).astype(BF16)
-    first = (place[0] * kv_cols // head_dim) * per_group
-    query = lax.broadcasted_iota(jnp.int32, (seq, seq), 0)
-    key = lax.broadcasted_iota(jnp.int32, (seq, seq), 1)
-    for p in range(prompts):
-        keep = (key <= query) & (key < lengths[p])
-        for u in range(per_group):
-            pattern = jnp.where(keep, patterns[first + u, p].astype(F32), 0.0).astype(BF16)
-            mixed = jnp.dot(pattern, values[p * seq : (p + 1) * seq, :], preferred_element_type=F32)
-            out[u, p * seq : (p + 1) * seq, :] = mixed.astype(BF16)
-
-
-def code_body(ranges, states, kv_cols, head_dim, place, *refs):
-    refs = list(refs)
-    got, also, state, packed = (
-        [refs.pop(0) for _ in range(count)] for count in (ranges, ranges, states, ranges)
-    )
-    weight, scale, middle, own, other, info, parts = refs
+def mix(mixing, head, values):
+    return jnp.dot(mixing[head], values, preferred_element_type=F32).astype(BF16)
+
+
+def heads_body(ranges, per_group, width, place, own, got, scales, mixing, weight, *sends):
+    values = ((own[...] + got[...]) * scales[...]).astype(BF16)
+    made = [mix(mixing, place[0] * per_group + u, values) for u in range(per_group)]
+    carry(place, ranges, weight, width, 0, sends[0].shape[0], made, sends)
+
+
+def sums_body(ranges, width, done, place, own, got, weight, info, *sends):
+    made = [(own[n] + got[n].astype(F32)).astype(BF16) for n in range(own.shape[0])]
+    carry(place, ranges, weight, width, done, width - done, made, sends)
+    for send in sends:
+        send[send.shape[0] - INFO :] = info[...]
+
+
+def halves_of(first, mine, theirs):
+    return jnp.concatenate([jnp.where(first, mine, theirs), jnp.where(first, theirs, mine)], axis=1)
+
+
+def spread_values_body(ranges, carried, place, low, weight, *refs):
+    others = ranges - 1
+    firsts, seconds, thirds = (refs[i * others : (i + 1) * others] for i in range(3))
+    own, other = refs[3 * others :]
+    width, rows = low.shape
+    first = place[1] == 0
+    state = low[...]
+    for step in range(ranges):
+        if step == 0:
+            n = place[0]
+            both = dot_tn(state, weight[pl.ds(pl.multiple_of(n * width, 16), width), :])
+            even, odd = both[:, : own.shape[2]], both[:, own.shape[2] :]
+        else:
+            n = partner(place[0], step, ranges)
+            even = dot_tn(state, firsts[step - 1][0:width])
+            odd, at = None, 0
+            for piece in (seconds[step - 1], thirds[step - 1]):
+                size = min(carried, width - at)
+                part = dot_tn(state[at : at + size], piece[0:size])
+                odd = part if odd is None else odd + part
+                at += size
+        own[n] = jnp.where(first, even, odd)
+        other[n] = jnp.where(first, odd, even).astype(BF16)
+
+
+def scaled_body(scales, *refs):
+    *blocks, out = refs
+    for n in range(out.shape[0]):
+        out[n] = (total([b[n] for b in blocks]) * scales[...]).astype(BF16)
+
+
+def finish(ranges, place, acc, blocks, passed, enc, weight_scale, middle, own, other, parts):
     width = middle.shape[0]
-    per_group = got[0].shape[0]
-    first = place[1] == 0
-    acc = state[0][...].astype(F32)
-    for piece in state[1:]:
-        acc = acc + piece[...].astype(F32)
-    for step in range(ranges):
-        n = partner(place[0], step, ranges) if step else place[0]
-        group = n * kv_cols // head_dim
-        for u in range(per_group):
-            mine, theirs = got[step][u], also[step][u]
-            head = jnp.concatenate([jnp.where(first, mine, theirs), jnp.where(first, theirs, mine)], axis=1)
-            acc = acc + dot_nt(weight[group * per_group + u], head)
+    size = width // 2
     middle[...] = acc
-    normed = (acc * scale[...]).astype(BF16)
-    for step in range(ranges):
-        n = partner(place[0], step, ranges) if step else place[0]
-        parts[n] = dot_tn(normed, packed[step][0:width, :])
-        terms = packed[step][width:, :].astype(F32)
-        info[n] = jnp.concatenate(
-            [terms[3 * i : 3 * i + 1] + terms[3 * i + 1 : 3 * i + 2] + terms[3 * i + 2 : 3 * i + 3] for i in range(3)]
-            + [jnp.zeros((5, terms.shape[1]), F32)],
-            axis=0,
+    normed = (acc * weight_scale[...]).astype(BF16)
+    here = place[3] == 0
+    mine = jnp.where(here, normed[:size], normed[size:])
+    theirs = jnp.where(here, normed[size:], normed[:size])
+    parts[place[0]] = dot_tn(normed, enc[pl.ds(pl.multiple_of(place[0] * width, 16), width), :])
+    for step in range(1, ranges):
+        parts[partner(place[0], step, ranges)] = dot_tn(mine, blocks[step - 1][width:]) + dot_tn(
+            theirs, passed[(step - 1) * size : step * size]
         )
     share = ranges // 2
     own[...] = parts[pl.ds(place[1] * share, share)]
     other[...] = parts[pl.ds((1 - place[1]) * share, share)].astype(BF16)
 
 
+def first_code_body(ranges, per_group, place, *refs):
+    got, also = (refs[i * ranges : (i + 1) * ranges] for i in range(2))
+    blocks = refs[2 * ranges : 3 * ranges - 1]
+    passed, state, weight, *ends = refs[3 * ranges - 1 :]
+    rows = state.shape[1]
+    first = place[1] == 0
+    acc = state[...]
+    for step in range(ranges):
+        n = partner(place[0], step, ranges) if step else place[0]
+        for u in range(per_group):
+            span = slice(u * rows, (u + 1) * rows)
+            acc = acc + dot_nt(weight[n * per_group + u], halves_of(first, got[step][span], also[step][span]))
+    finish(ranges, place, acc, blocks, passed, *ends)
+
+
+def later_code_body(ranges, per_group, place, mine, also, low, rest, mixing, *refs):
+    blocks = refs[: ranges - 1]
+    passed, weight, *ends = refs[ranges - 1 :]
+    first = place[1] == 0
+    acc = low[...].astype(F32) + rest[0].astype(F32)
+    for n in range(ranges):
+        values = halves_of(first, mine[n], also[n])
+        for u in range(per_group):
+            acc = acc + dot_nt(weight[n * per_group + u], mix(mixing, n * per_group + u, values))
+    finish(ranges, place, acc, blocks, passed, *ends)
+
+
 def clamp_body(seq, place, lengths, *refs):
-    *blocks, info, out = refs
-    share, rows, _ = out.shape
+    *refs, out = refs
+    blocks, facts = refs[: len(refs) // 2], refs[len(refs) // 2 :]
+    share, rows, cols = out.shape
+    ranges = len(blocks)
     row = lax.broadcasted_iota(jnp.int32, out.shape[1:], 0)
     end = jnp.full(row.shape, lengths[0], jnp.int32)
     for p in range(1, rows // seq):
         end = jnp.where(row >= p * seq, p * seq + lengths[p], end)
     live = row < end
+    terms = [f[f.shape[0] - INFO :].astype(F32) for f in facts]
+    terms = [
+        [t[3 * i : 3 * i + 1] + t[3 * i + 1 : 3 * i + 2] + t[3 * i + 2 : 3 * i + 3] for i in range(3)] for t in terms
+    ]
     for n in range(share):
-        facts = info[place[1] * share + n]
-        preact = total([b[n] for b in blocks]) + facts[0:1]
-        clamped = jnp.maximum(preact, 0.0) * facts[1:2] + facts[2:3]
+        number = place[1] * share + n
+        bias, gain, shift = terms[0]
+        for step in range(1, ranges):
+            here = partner(place[0], step, ranges) == number
+            bias, gain, shift = (jnp.where(here, b, a) for a, b in zip((bias, gain, shift), terms[step]))
+        preact = total([b[n * rows : (n + 1) * rows] for b in blocks]) + bias
+        clamped = jnp.maximum(preact, 0.0) * gain + shift
         out[n] = jnp.where(live, clamped, 0.0).astype(BF16)
 
 
@@ -366,27 +495,25 @@
     ]
 
 
-def decode_body(layer, adds, sends, keeps, place, *refs):
+def decode_body(layer, adds, linked, sends, keeps, place, *refs):
     refs = list(refs)
-    mine, also, dec = refs[:3]
-    added = refs[3 : 3 + adds]
-    refs = refs[3 + adds :]
-    before = refs[:2] if keeps else None
-    if keeps:
-        refs = refs[2:]
-    state_out, feats_out = refs[:2]
+    take = lambda count: [refs.pop(0) for _ in range(count)]
+    (mine, also, dec), added, links, before = take(3), take(adds), take(linked), take(2 if keeps else 0)
+    state_out, feats_out = take(2)
     feats = ordered(place, mine, also)
     acc = added[0][...]
     for piece in added[1:]:
         acc = acc + piece[...]
+    for piece in links:
+        acc = acc + piece[1].astype(F32)
     acc = acc + dot_nt(dec[layer], jnp.concatenate(feats, axis=1))
     block = feats[0]
     for n in range(1, len(feats)):
         block = jnp.where(place[0] == n, feats[n], block)
     if sends:
         low = acc.astype(BF16)
-        refs[2][...] = low
-        refs[3][...] = (acc - low.astype(F32)).astype(BF16)
+        refs[0][...] = low
+        refs[1][...] = (acc - low.astype(F32)).astype(BF16)
     if keeps:
         here = place[2] == layer
         state_out[...] = jnp.where(here, acc, before[0][...])
@@ -396,12 +523,13 @@
         feats_out[...] = block
 
 
-def writes_body(layer, has_links, place, mine, also, dec, *refs):
+def writes_body(layer, linked, place, mine, also, dec, left, *refs):
     out = refs[-1]
     feats = jnp.concatenate(ordered(place, mine, also), axis=1)
-    for n in range(out.shape[0]):
-        made = dot_nt(dec[layer + 1 + n], feats)
-        out[n] = made + refs[0][n + 1] if has_links else made
+    out[0] = left[...]
+    for n in range(1, out.shape[0]):
+        made = dot_nt(dec[layer + n], feats)
+        out[n] = (made + refs[0][n + 1].astype(F32) if linked else made).astype(BF16)
 
 
 def after(value, *others):
@@ -435,106 +563,148 @@
     block_len = enc_bias.shape[1]
     rows = residual_in.shape[0]
     share = ranges // 2
-    place = jnp.stack([lax.axis_index("feat"), lax.axis_index("tok"), lax.axis_index("layer")]).astype(jnp.int32)
+    place = jnp.stack([lax.axis_index("feat"), lax.axis_index("tok"), lax.axis_index("layer"), lax.axis_index("groups")]).astype(jnp.int32)
 
     source = residual_in[:, 0, :].T
     error_cols = errors[0, :, 0, :].T
     out_weight = out_proj[0, :, :, :, 0, :].transpose(0, 2, 3, 1).reshape(-1, width, head_dim)
     dec_cols = dec_weight[0, :, :, 0, :].transpose(0, 2, 1)
     value_rows = value_proj[0, 0]
-    scale_attn = attn_scale.reshape(rows, 1)
-
-    def handed_on(value, layer):
-        return lax.ppermute(value, "layer", [(layer, layer + 1)])
-
-    packed = None
-    low, links, kept = source.astype(BF16), None, None
-    state = [source]
+    enc_rows = enc_weight[0, 0]
+
+    def handed_on(value):
+        return lax.ppermute(value, "layer", [(n, (n + 1) % layers) for n in range(layers)])
+
+    packed = carried = rest = low = kept = None
     for layer in range(layers):
-        blocks = spread(low)
-        if packed is None:
+        if layer == 0:
             sends = kernel_call(
-                functools.partial(pack_body, ranges),
-                [shape(width + INFO, block_len, dtype=BF16)] * ranges,
-                [place, active_blocks, clamp_values],
-                [clamp_mode.reshape(-1, block_len), clamp_index.reshape(-1, block_len), enc_bias, enc_weight[0, 0]],
-            )
-            packed = [sends[0]] + [
-                swap(after(sends[step], *blocks), "feat", step) for step in peers("feat")
-            ]
-        own, other = kernel_call(
-            functools.partial(values_body, ranges),
-            [shape(rows, half)] * 2,
-            [place],
-            [*blocks, value_rows],
-            flops=4 * rows * value_rows.size,
-        )
-        mine = kernel_call(
-            functools.partial(heads_body, kv_cols, head_dim),
-            shape(per_group, rows, half, dtype=BF16),
-            [place, lengths],
-            [own, swap(other, "tok", 1), scale_attn, patterns[0]],
-        )
-        got = spread(mine)
-        also = [swap(b, "tok", 1) for b in got]
-        middle, own, other, info = kernel_call(
-            functools.partial(code_body, ranges, len(state), kv_cols, head_dim),
+                functools.partial(start_body, ranges),
+                [shape(width, rows, dtype=BF16)] + [shape(width + width // 2, rows, dtype=BF16)] * (ranges - 1),
+                [place],
+                [source],
+                left=[value_rows, enc_rows],
+                scratch=[pltpu.SemaphoreType.DMA((2, ranges - 1))],
+            )
+            blocks = exchange(sends)
+            info, mixing, scales = kernel_call(
+                facts_body,
+                [
+                    shape(INFO, block_len, dtype=BF16),
+                    shape(patterns.shape[1], rows, rows, dtype=BF16),
+                    shape(rows, half),
+                ],
+                [place, lengths, active_blocks, clamp_values],
+                [
+                    clamp_mode.reshape(-1, block_len),
+                    clamp_index.reshape(-1, block_len),
+                    enc_bias,
+                    attn_scale,
+                    patterns[0],
+                ],
+            )
+            blocks[0], info, mixing, scales = lax.optimization_barrier((blocks[0], info, mixing, scales))
+            own, other, passed = kernel_call(
+                functools.partial(values_body, ranges),
+                [shape(rows, half)] * 2 + [shape((ranges - 1) * (width // 2), rows, dtype=BF16)],
+                [place],
+                [*blocks, value_rows],
+                flops=4 * rows * value_rows.size,
+            )
+            got = swap(other, "tok", 1)
+            passed = swap(passed, "groups", 1)
+            packed = [*blocks[1:], passed]
+            sends = kernel_call(
+                functools.partial(heads_body, ranges, per_group, width),
+                [shape(per_group * rows, half, dtype=BF16)] * ranges,
+                [place],
+                [own, got, scales, mixing, value_rows],
+            )
+            got = exchange(sends)
+            also = [swap(b, "tok", 1) for b in got]
+            carried = [*blocks[1:], *got[1:]]
+            code = functools.partial(first_code_body, ranges, per_group)
+            scalars, given = [place], [*got, *also, *packed, source]
+        else:
+            own, other = kernel_call(
+                functools.partial(spread_values_body, ranges, per_group * rows),
+                [shape(ranges, rows, half), shape(ranges, rows, half, dtype=BF16)],
+                [place],
+                [low, value_rows, *carried],
+                flops=2 * rows * value_rows.size,
+            )
+            part = (own + swap(other, "tok", 1).astype(F32)).astype(BF16)
+            blocks = spread(part)
+            rest = handed_on(after(rest, low))
+            mine = kernel_call(scaled_body, shape(ranges, rows, half, dtype=BF16), [], [scales, *blocks])
+            code = functools.partial(later_code_body, ranges, per_group)
+            scalars, given = [place], [mine, swap(mine, "tok", 1), low, rest, mixing, *packed]
+        middle, own, other = kernel_call(
+            code,
             [
                 shape(width, rows),
                 shape(share, rows, block_len),
                 shape(share, rows, block_len, dtype=BF16),
-                shape(ranges, 8, block_len),
             ],
-            [place],
-            [*got, *also, *state, *packed, out_weight, mlp_scale],
+            scalars,
+            [*given, out_weight, enc_rows, mlp_scale],
             scratch=[pltpu.VMEM((ranges, rows, block_len), F32)],
             flops=2 * rows * (out_weight.size + width * block_len * ranges),
         )
-        part = (own + swap(other, "tok", 1).astype(F32)).astype(BF16)
+        got = swap(other, "tok", 1)
+        if layer == 0:
+            sends = kernel_call(
+                functools.partial(sums_body, ranges, width, per_group * rows),
+                [shape(share * rows + INFO, block_len, dtype=BF16)] * ranges,
+                [place],
+                [own, got, value_rows, info],
+            )
+            blocks = facts = exchange(sends)
+            carried += blocks[1:]
+        else:
+            blocks = spread((own + got.astype(F32)).astype(BF16).reshape(-1, block_len))
         mine = kernel_call(
             functools.partial(clamp_body, seq),
             shape(share, rows, block_len, dtype=BF16),
             [place, lengths],
-            [*spread(part), info],
+            [*blocks, *facts],
         )
         also = swap(mine, "tok", 1)
         more = layer + 1 < layers
-        added = [middle, error_cols] + ([links[0]] if links is not None else [])
+        added = [middle, error_cols]
+        links = [rest] if layer > 0 else []
         outs = [shape(width, rows), shape(rows, block_len, dtype=BF16)]
         if more:
             outs += [shape(width, rows, dtype=BF16)] * 2
         made = kernel_call(
-            functools.partial(decode_body, layer, len(added), more, kept is not None),
+            functools.partial(decode_body, layer, len(added), len(links), more, kept is not None),
             outs,
             [place],
-            [mine, also, dec_cols, *added, *(kept or ())],
+            [mine, also, dec_cols, *added, *links, *(kept or ())],
             flops=2 * rows * dec_cols.size // layers,
         )
         kept = made[:2]
         if more:
-            low = handed_on(made[2], layer)
-            rest = handed_on(after(made[3], low), layer)
-            writes = kernel_call(
-                functools.partial(writes_body, layer, links is not None),
-                shape(layers - 1 - layer, width, rows),
+            low = handed_on(made[2])
+            rest = kernel_call(
+                functools.partial(writes_body, layer, len(links)),
+                shape(layers - layer, width, rows, dtype=BF16),
                 [place],
-                [mine, also, dec_cols, *([links] if links is not None else [])],
+                [mine, also, dec_cols, made[3], *links],
                 flops=2 * rows * dec_cols.size,
             )
-            links = handed_on(after(writes, rest), layer)
-            state = [low, rest]
     return kept[0].T[None, :, None, :], kept[1][None]
 
 
 def local(residual_in, attn_scale, mlp_scale, patterns, lengths, value_proj, out_proj, enc_weight, enc_bias, *others):
     whole = (
         residual_in.shape[0] % LANES == 0
-        and residual_in.shape[2] % 16 == 0
+        and residual_in.shape[2] % 32 == 0
         and value_proj.shape[3] == out_proj.shape[2]
-        and value_proj.shape[3] % (2 * LANES) == 0
-        and enc_bias.shape[1] % LANES == 0
+        and value_proj.shape[3] == 2 * enc_bias.shape[1] == 2 * residual_in.shape[0]
+        and residual_in.shape[2] <= residual_in.shape[0] * (out_proj.shape[3] + lax.axis_size("feat") // 2)
         and lax.axis_size("feat") % 2 == 0
-        and lax.axis_size("tok") == 2
+        and lax.axis_size("tok") == lax.axis_size("groups") == 2
     )
     run = tiled if whole else plain
     return run(

time: 109 us -> 96 us (0.88)
  starting transfers between devices: 48.7 us -> 31.2 us
  waiting for transfers between devices: 38 us -> 41.3 us
  Pallas kernels: 11.7 us -> 13.3 us
    ppermute x3 -> x2, starting transfers between devices: 12.2 us -> 3.23 us  [handed_on(): lax.ppermute(value, 'layer', [(n, (n + 1) % layers) for n in range(layers)])]
    ppermute x35 -> x27, starting transfers between devices: 36.5 us -> 28 us  [swap(): lax.ppermute(value, axis, [(s, partner(s, step, count)) for s in range(co...]
    ppermute x35 -> x27, waiting for transfers between devices: 34.7 us -> 37.6 us  [swap(): lax.ppermute(value, axis, [(s, partner(s, step, count)) for s in range(co...]
    unnamed x32 -> x34, local copies, waits for them, and re-layouts: 6.58 us -> 8.17 us
    pallas_call x12 -> x14, Pallas kernels: 11.7 us -> 13.3 us  [kernel_call(): pl.pallas_call(body, out_shape=tuple(kept) if many else outs, in_specs=[p...]
    ppermute x3 -> x2, waiting for transfers between devices: 3.31 us -> 3.66 us  [handed_on(): lax.ppermute(value, 'layer', [(n, (n + 1) % layers) for n in range(layers)])]
  transfers between devices with their start and end apart: 38 -> 29, of which waited for: 18 -> 16; matrix products, arithmetic and copies ran while one was open for 1% -> 0% of each run, Pallas kernels for 3% -> 2%
where the time goes in v3:
time: 96 us; the launch traced here: 95.6 us
  waiting for transfers between devices  41.3 us (43%)
  starting transfers between devices  31.2 us (32%)
  Pallas kernels  13.3 us (14%)
  local copies, waits for them, and re-layouts  8.17 us (9%)
  between operations  1.51 us (2%)
    ppermute x27, waiting for transfers between devices, swap(): lax.ppermute(value, axis, [(s, partner(s, step, count)) for s in range(co...  37.6 us
    ppermute x27, starting transfers between devices, swap(): lax.ppermute(value, axis, [(s, partner(s, step, count)) for s in range(co...  28 us
    pallas_call x14, Pallas kernels, kernel_call(): pl.pallas_call(body, out_shape=tuple(kept) if many else outs, in_specs=[p...  13.3 us
    unnamed x34, local copies, waits for them, and re-layouts  8.17 us
    ppermute x2, waiting for transfers between devices, handed_on(): lax.ppermute(value, 'layer', [(n, (n + 1) % layers) for n in range(layers)])  3.66 us
    ppermute x2, starting transfers between devices, handed_on(): lax.ppermute(value, 'layer', [(n, (n + 1) % layers) for n in range(layers)])  3.23 us
  transfers between devices with their start and end apart: 29, of which 16 were waited for; matrix products, arithmetic and copies ran while one was open for 0% of the time, Pallas kernels for 2%

profile of v3, /device:TPU:0, one launch (start us, length us, event | category | flops | bytes accessed | tf_op | source)
XLA Modules:
  0.0 95.6 jit_solution(3415697254807239553)
XLA Ops:
  0.7 1.2 %copy-done = bf16[1,1,1792,256]{3,2,1,0:T(8,128)(2,1)S(1)} copy-done((bf16[1,1,1792,256]{3,2,1,0:T(8,128)(2,1)S(1)}, bf16[1,1,1792,256]{3,2,1,0:T(8,128)(2,1)}, u32[]{:S(2)}) %copy-start) | copy-done | bytes 917528
  4.8 3.1 %collective-permute-start = (bf16[672,128]{1,0:T(8,128)(2,1)S(1)}, bf16[672,128]{1,0:T(8,128)(2,1)S(1)}, u32[]{:S(2)}, u32[]{:S(2)}) collective-permute-start(bf16[672,128]{1,0:T(8,128)(2,1)S(1)} %get-tuple-element.45), channel_id=1, source_target_pairs={{0,4},{4,0},{8,12},{12,8},{1,5},{5,1},{9,13},{13,9},{2,6},{6,2},{1... | collective-permute-start | bytes 516104 | tf_op jit(solution)/shard_map/ppermute | solution.py:28
  7.9 2.6 %collective-permute-start.1 = (bf16[672,128]{1,0:T(8,128)(2,1)S(1)}, bf16[672,128]{1,0:T(8,128)(2,1)S(1)}, u32[]{:S(2)}, u32[]{:S(2)}) collective-permute-start(bf16[672,128]{1,0:T(8,128)(2,1)S(1)} %get-tuple-element.46), channel_id=1, source_target_pairs={{0,8},{4,12},{8,0},{12,4},{1,9},{5,13},{9,1},{13,5},{2,10},{6,14},... | collective-permute-start | bytes 516104 | tf_op jit(solution)/shard_map/ppermute | solution.py:28
  16.8 6.6 %collective-permute-done.1.refs_2_.refs_9_.refs_1_ = bf16[672,128]{1,0:T(8,128)(2,1)S(1)} collective-permute-done((bf16[672,128]{1,0:T(8,128)(2,1)S(1)}, bf16[672,128]{1,0:T(8,128)(2,1)S(1)}, u32[]{:S(2)}, u32[]{:S(2)}) %collective-permute-start.1) | collective-permute-done | bytes 172064 | tf_op jit(solution)/shard_map/ppermute | solution.py:28
  24.4 1.6 %collective-permute-start.11 = (bf16[672,128]{1,0:T(8,128)(2,1)S(1)}, bf16[672,128]{1,0:T(8,128)(2,1)S(1)}, u32[]{:S(2)}, u32[]{:S(2)}) collective-permute-start(bf16[672,128]{1,0:T(8,128)(2,1)S(1)} %get-tuple-element.55), channel_id=1, source_target_pairs={{0,16},{16,0},{1,17},{17,1},{2,18},{18,2},{3,19},{19,3},{4,20},{20... | collective-permute-start | bytes 516104 | tf_op jit(solution)/shard_map/ppermute | solution.py:28
  26.7 2.9 %collective-permute-start.4 = (bf16[256,128]{1,0:T(8,128)(2,1)S(1)}, bf16[256,128]{1,0:T(8,128)(2,1)S(1)}, u32[]{:S(2)}, u32[]{:S(2)}) collective-permute-start(bf16[256,128]{1,0:T(8,128)(2,1)S(1)} %get-tuple-element.52), channel_id=1, source_target_pairs={{0,4},{4,0},{8,12},{12,8},{1,5},{5,1},{9,13},{13,9},{2,6},{6,2},{1... | collective-permute-start | bytes 196616 | tf_op jit(solution)/shard_map/ppermute | solution.py:28
  29.6 1.1 %collective-permute-start.5 = (bf16[256,128]{1,0:T(8,128)(2,1)S(1)}, bf16[256,128]{1,0:T(8,128)(2,1)S(1)}, u32[]{:S(2)}, u32[]{:S(2)}) collective-permute-start(bf16[256,128]{1,0:T(8,128)(2,1)S(1)} %get-tuple-element.53), channel_id=1, source_target_pairs={{0,8},{4,12},{8,0},{12,4},{1,9},{5,13},{9,1},{13,5},{2,10},{6,14},... | collective-permute-start | bytes 196616 | tf_op jit(solution)/shard_map/ppermute | solution.py:28
  30.7 1.4 %collective-permute-start.6 = (bf16[256,128]{1,0:T(8,128)(2,1)S(1)}, bf16[256,128]{1,0:T(8,128)(2,1)S(1)}, u32[]{:S(2)}, u32[]{:S(2)}) collective-permute-start(bf16[256,128]{1,0:T(8,128)(2,1)S(1)} %get-tuple-element.54), channel_id=1, source_target_pairs={{0,12},{4,8},{8,4},{12,0},{1,13},{5,9},{9,5},{13,1},{2,14},{6,10},... | collective-permute-start | bytes 196616 | tf_op jit(solution)/shard_map/ppermute | solution.py:28
  32.6 5.3 %collective-permute-done.5.refs_2_.refs_4_ = bf16[256,128]{1,0:T(8,128)(2,1)S(1)} collective-permute-done((bf16[256,128]{1,0:T(8,128)(2,1)S(1)}, bf16[256,128]{1,0:T(8,128)(2,1)S(1)}, u32[]{:S(2)}, u32[]{:S(2)}) %collective-permute-start.5) | collective-permute-done | bytes 65568 | tf_op jit(solution)/shard_map/ppermute | solution.py:28
  39.3 1.8 %shard_map.162 = (f32[448,128]{1,0:T(8,128)S(1)}, f32[2,128,128]{2,1,0:T(8,128)S(1)}, bf16[2,128,128]{2,1,0:T(8,128)(2,1)S(1)}) custom-call(s32[4]{0:T(128)S(1)} %pad_add_fusion.place, bf16[256,128]{1,0:T(8,128)(2,1)S(1)} %get-tuple-element.51.refs_0_, bf16[256,128]{1,0:T(8,128)(2,1)S(1)} %collective-permute-done.4.refs_1_.refs_3_, ...), custom_call_target="tpu_custom_call" | custom-call | flops 293601280 | bytes 4162048 | tf_op jit(solution)/shard_map/pallas_call | solution.py:251
  43.0 1.3 %collective-permute-start.13 = (bf16[272,128]{1,0:T(8,128)(2,1)S(1)}, bf16[272,128]{1,0:T(8,128)(2,1)S(1)}, u32[]{:S(2)}, u32[]{:S(2)}) collective-permute-start(bf16[272,128]{1,0:T(8,128)(2,1)S(1)} %get-tuple-element.60), channel_id=1, source_target_pairs={{0,4},{4,0},{8,12},{12,8},{1,5},{5,1},{9,13},{13,9},{2,6},{6,2},{1... | collective-permute-start | bytes 208904 | tf_op jit(solution)/shard_map/ppermute | solution.py:28
  44.3 1.5 %collective-permute-start.14 = (bf16[272,128]{1,0:T(8,128)(2,1)S(1)}, bf16[272,128]{1,0:T(8,128)(2,1)S(1)}, u32[]{:S(2)}, u32[]{:S(2)}) collective-permute-start(bf16[272,128]{1,0:T(8,128)(2,1)S(1)} %get-tuple-element.61), channel_id=1, source_target_pairs={{0,8},{4,12},{8,0},{12,4},{1,9},{5,13},{9,1},{13,5},{2,10},{6,14},... | collective-permute-start | bytes 208904 | tf_op jit(solution)/shard_map/ppermute | solution.py:28
  45.8 1.7 %collective-permute-start.15 = (bf16[272,128]{1,0:T(8,128)(2,1)S(1)}, bf16[272,128]{1,0:T(8,128)(2,1)S(1)}, u32[]{:S(2)}, u32[]{:S(2)}) collective-permute-start(bf16[272,128]{1,0:T(8,128)(2,1)S(1)} %get-tuple-element.62), channel_id=1, source_target_pairs={{0,12},{4,8},{8,4},{12,0},{1,13},{5,9},{9,5},{13,1},{2,14},{6,10},... | collective-permute-start | bytes 208904 | tf_op jit(solution)/shard_map/ppermute | solution.py:28
  47.5 5.4 %collective-permute-done.14.refs_2_.refs_6_.refs_7_ = bf16[272,128]{1,0:T(8,128)(2,1)S(1)} collective-permute-done((bf16[272,128]{1,0:T(8,128)(2,1)S(1)}, bf16[272,128]{1,0:T(8,128)(2,1)S(1)}, u32[]{:S(2)}, u32[]{:S(2)}) %collective-permute-start.14) | collective-permute-done | bytes 69664 | tf_op jit(solution)/shard_map/ppermute | solution.py:28
  53.6 1.2 %collective-permute-done.16.refs_1_.also = bf16[2,128,128]{2,1,0:T(8,128)(2,1)S(1)} collective-permute-done((bf16[2,128,128]{2,1,0:T(8,128)(2,1)S(1)}, bf16[2,128,128]{2,1,0:T(8,128)(2,1)S(1)}, u32[]{:S(2)}, u32[]{:S(2)}) %collective-permute-start.16) | collective-permute-done | bytes 65568 | tf_op jit(solution)/shard_map/ppermute | solution.py:28
  55.6 1.6 %collective-permute-start.17 = (bf16[448,128]{1,0:T(8,128)(2,1)S(1)}, bf16[448,128]{1,0:T(8,128)(2,1)S(1)}, u32[]{:S(2)}, u32[]{:S(2)}) collective-permute-start(bf16[448,128]{1,0:T(8,128)(2,1)S(1)} %get-tuple-element.64), channel_id=1, source_target_pairs={{0,2},{2,0},{1,3},{3,1},{4,6},{6,4},{5,7},{7,5},{8,10},{10,8},{9,1... | collective-permute-start | bytes 344072 | tf_op jit(solution)/shard_map/ppermute | solution.py:576
  57.3 3.7 %collective-permute-done.17.low = bf16[448,128]{1,0:T(8,128)(2,1)S(1)} collective-permute-done((bf16[448,128]{1,0:T(8,128)(2,1)S(1)}, bf16[448,128]{1,0:T(8,128)(2,1)S(1)}, u32[]{:S(2)}, u32[]{:S(2)}) %collective-permute-start.17) | collective-permute-done | bytes 114720 | tf_op jit(solution)/shard_map/ppermute | solution.py:576
  62.0 1.3 %collective-permute-done.18 = bf16[4,128,128]{2,1,0:T(8,128)(2,1)S(1)} collective-permute-done((bf16[4,128,128]{2,1,0:T(8,128)(2,1)S(1)}, bf16[4,128,128]{2,1,0:T(8,128)(2,1)S(1)}, u32[]{:S(2)}, u32[]{:S(2)}) %collective-permute-start.18) | collective-permute-done | bytes 131104 | tf_op jit(solution)/shard_map/ppermute | solution.py:28
  63.4 2.1 %collective-permute-start.21 = (bf16[4,128,128]{2,1,0:T(8,128)(2,1)S(1)}, bf16[4,128,128]{2,1,0:T(8,128)(2,1)S(1)}, u32[]{:S(2)}, u32[]{:S(2)}) collective-permute-start(bf16[4,128,128]{2,1,0:T(8,128)(2,1)S(1)} %add_convert_fusion.refs_0_), channel_id=1, source_target_pairs={{0,12},{4,8},{8,4},{12,0},{1,13},{5,9},{9,5},{13,1},{2,14},{6,10},... | collective-permute-start | bytes 393224 | tf_op jit(solution)/shard_map/ppermute | solution.py:28
  66.2 1.6 %collective-permute-start.19 = (bf16[4,128,128]{2,1,0:T(8,128)(2,1)S(1)}, bf16[4,128,128]{2,1,0:T(8,128)(2,1)S(1)}, u32[]{:S(2)}, u32[]{:S(2)}) collective-permute-start(bf16[4,128,128]{2,1,0:T(8,128)(2,1)S(1)} %add_convert_fusion.refs_0_), channel_id=1, source_target_pairs={{0,4},{4,0},{8,12},{12,8},{1,5},{5,1},{9,13},{13,9},{2,6},{6,2},{1... | collective-permute-start | bytes 393224 | tf_op jit(solution)/shard_map/ppermute | solution.py:28
  68.6 1.6 %collective-permute-start.23 = (bf16[2,448,128]{2,1,0:T(8,128)(2,1)S(1)}, bf16[2,448,128]{2,1,0:T(8,128)(2,1)S(1)}, u32[]{:S(2)}, u32[]{:S(2)}) collective-permute-start(bf16[2,448,128]{2,1,0:T(8,128)(2,1)S(1)} %shard_map.168), channel_id=1, source_target_pairs={{0,2},{2,0},{1,3},{3,1},{4,6},{6,4},{5,7},{7,5},{8,10},{10,8},{9,1... | collective-permute-start | bytes 688136 | tf_op jit(solution)/shard_map/ppermute | solution.py:576
  70.3 1.4 %collective-permute-done.21.refs_3_ = bf16[4,128,128]{2,1,0:T(8,128)(2,1)S(1)} collective-permute-done((bf16[4,128,128]{2,1,0:T(8,128)(2,1)S(1)}, bf16[4,128,128]{2,1,0:T(8,128)(2,1)S(1)}, u32[]{:S(2)}, u32[]{:S(2)}) %collective-permute-start.21) | collective-permute-done | bytes 131104 | tf_op jit(solution)/shard_map/ppermute | solution.py:28
  71.7 6.5 %collective-permute-done.20.refs_2_ = bf16[4,128,128]{2,1,0:T(8,128)(2,1)S(1)} collective-permute-done((bf16[4,128,128]{2,1,0:T(8,128)(2,1)S(1)}, bf16[4,128,128]{2,1,0:T(8,128)(2,1)S(1)}, u32[]{:S(2)}, u32[]{:S(2)}) %collective-permute-start.20) | collective-permute-done | bytes 131104 | tf_op jit(solution)/shard_map/ppermute | solution.py:28
  78.3 1.3 %collective-permute-done.22.also = bf16[4,128,128]{2,1,0:T(8,128)(2,1)S(1)} collective-permute-done((bf16[4,128,128]{2,1,0:T(8,128)(2,1)S(1)}, bf16[4,128,128]{2,1,0:T(8,128)(2,1)S(1)}, u32[]{:S(2)}, u32[]{:S(2)}) %collective-permute-start.22) | collective-permute-done | bytes 131104 | tf_op jit(solution)/shard_map/ppermute | solution.py:28
  79.7 2.3 %shard_map.169 = (f32[448,128]{1,0:T(8,128)S(1)}, f32[2,128,128]{2,1,0:T(8,128)S(1)}, bf16[2,128,128]{2,1,0:T(8,128)(2,1)S(1)}) custom-call(s32[4]{0:T(128)S(1)} %pad_add_fusion.place, bf16[4,128,128]{2,1,0:T(8,128)(2,1)S(1)} %shard_map.167.mine, bf16[4,128,128]{2,1,0:T(8,128)(2,1)S(1)} %collective-permute-done.22.also, ...), custom_call_target="tpu_custom_call" | custom-call | flops 293601280 | bytes 4276736 | tf_op jit(solution)/shard_map/pallas_call | solution.py:251
  82.2 1.1 %collective-permute-done.24 = bf16[2,128,128]{2,1,0:T(8,128)(2,1)S(1)} collective-permute-done((bf16[2,128,128]{2,1,0:T(8,128)(2,1)S(1)}, bf16[2,128,128]{2,1,0:T(8,128)(2,1)S(1)}, u32[]{:S(2)}, u32[]{:S(2)}) %collective-permute-start.24) | collective-permute-done | bytes 65568 | tf_op jit(solution)/shard_map/ppermute | solution.py:28
  83.3 2.4 %collective-permute-start.27 = (bf16[256,128]{1,0:T(8,128)(2,1)S(1)}, bf16[256,128]{1,0:T(8,128)(2,1)S(1)}, u32[]{:S(2)}, u32[]{:S(2)}) collective-permute-start(bf16[256,128]{1,0:T(8,128)(2,1)S(1)} %bitcast.46), channel_id=1, source_target_pairs={{0,12},{4,8},{8,4},{12,0},{1,13},{5,9},{9,5},{13,1},{2,14},{6,10},... | collective-permute-start | bytes 196616 | tf_op jit(solution)/shard_map/ppermute | solution.py:28
  85.7 2.1 %collective-permute-start.25 = (bf16[256,128]{1,0:T(8,128)(2,1)S(1)}, bf16[256,128]{1,0:T(8,128)(2,1)S(1)}, u32[]{:S(2)}, u32[]{:S(2)}) collective-permute-start(bf16[256,128]{1,0:T(8,128)(2,1)S(1)} %bitcast.48), channel_id=1, source_target_pairs={{0,4},{4,0},{8,12},{12,8},{1,5},{5,1},{9,13},{13,9},{2,6},{6,2},{1... | collective-permute-start | bytes 196616 | tf_op jit(solution)/shard_map/ppermute | solution.py:28
  87.7 2.4 %collective-permute-done.27.refs_3_ = bf16[256,128]{1,0:T(8,128)(2,1)S(1)} collective-permute-done((bf16[256,128]{1,0:T(8,128)(2,1)S(1)}, bf16[256,128]{1,0:T(8,128)(2,1)S(1)}, u32[]{:S(2)}, u32[]{:S(2)}) %collective-permute-start.27) | collective-permute-done | bytes 65568 | tf_op jit(solution)/shard_map/ppermute | solution.py:28
  90.1 2.0 %collective-permute-done.26.refs_2_ = bf16[256,128]{1,0:T(8,128)(2,1)S(1)} collective-permute-done((bf16[256,128]{1,0:T(8,128)(2,1)S(1)}, bf16[256,128]{1,0:T(8,128)(2,1)S(1)}, u32[]{:S(2)}, u32[]{:S(2)}) %collective-permute-start.26) | collective-permute-done | bytes 65568 | tf_op jit(solution)/shard_map/ppermute | solution.py:28
  92.8 1.2 %collective-permute-done.28.refs_1_ = bf16[2,128,128]{2,1,0:T(8,128)(2,1)S(1)} collective-permute-done((bf16[2,128,128]{2,1,0:T(8,128)(2,1)S(1)}, bf16[2,128,128]{2,1,0:T(8,128)(2,1)S(1)}, u32[]{:S(2)}, u32[]{:S(2)}) %collective-permute-start.28) | collective-permute-done | bytes 65568 | tf_op jit(solution)/shard_map/ppermute | solution.py:28
  94.1 1.5 %shard_map.171 = (f32[448,128]{1,0:T(8,128)}, bf16[128,128]{1,0:T(8,128)(2,1)}) custom-call(s32[4]{0:T(128)S(1)} %pad_add_fusion.place, bf16[2,128,128]{2,1,0:T(8,128)(2,1)S(1)} %shard_map.170.refs_0_, bf16[2,128,128]{2,1,0:T(8,128)(2,1)S(1)} %collective-permute-done.28.refs_1_, bf16[2,448,512]{2,1,0:T(8,128)(2,1)S(1)} %bitcast.35, ...), custom_call_target="tpu_custom_call" | custom-call | flops 58720256 | bytes 2260992 | tf_op jit(solution)/shard_map/pallas_call | solution.py:251
  (77 shorter events, 19.5 us)
Async XLA Ops:
  3.9 35.4 %copy-start.13 = (f32[1,128]{1,0:T(1,128)S(1)}, f32[1,128]{1,0:T(1,128)}, u32[]{:S(2)}) copy-start(f32[1,128]{1,0:T(1,128)} %refs_6_.1) | copy-start | bytes 1540
  4.7 34.5 %copy-start.3 = (bf16[1,4,256,2,1,448]{2,5,4,3,1,0:T(8,128)(2,1)S(1)}, bf16[1,4,256,2,1,448]{2,5,4,3,1,0:T(8,128)(2,1)}, u32[]{:S(2)}) copy-start(bf16[1,4,256,2,1,448]{2,5,4,3,1,0:T(8,128)(2,1)} %param.21) | copy-start | bytes 5505028
  4.7 34.5 %copy-start.5 = (bf16[1,1,1792,128]{3,2,1,0:T(8,128)(2,1)S(1)}, bf16[1,1,1792,128]{3,2,1,0:T(8,128)(2,1)}, u32[]{:S(2)}) copy-start(bf16[1,1,1792,128]{3,2,1,0:T(8,128)(2,1)} %param.22) | copy-start | bytes 1376260
  4.8 12.1 %collective-permute-start = (bf16[672,128]{1,0:T(8,128)(2,1)S(1)}, bf16[672,128]{1,0:T(8,128)(2,1)S(1)}, u32[]{:S(2)}, u32[]{:S(2)}) collective-permute-start(bf16[672,128]{1,0:T(8,128)(2,1)S(1)} %get-tuple-element.45), channel_id=1, source_target_pairs={{0,4},{4,0},{8,12},{12,8},{1,5},{5,1},{9,13},{13,9},{2,6},{6,2},{1... | collective-permute-start | bytes 516104 | tf_op jit(solution)/shard_map/ppermute | solution.py:28
  7.9 15.6 %collective-permute-start.1 = (bf16[672,128]{1,0:T(8,128)(2,1)S(1)}, bf16[672,128]{1,0:T(8,128)(2,1)S(1)}, u32[]{:S(2)}, u32[]{:S(2)}) collective-permute-start(bf16[672,128]{1,0:T(8,128)(2,1)S(1)} %get-tuple-element.46), channel_id=1, source_target_pairs={{0,8},{4,12},{8,0},{12,4},{1,9},{5,13},{9,1},{13,5},{2,10},{6,14},... | collective-permute-start | bytes 516104 | tf_op jit(solution)/shard_map/ppermute | solution.py:28
  10.4 13.0 %collective-permute-start.2 = (bf16[672,128]{1,0:T(8,128)(2,1)S(1)}, bf16[672,128]{1,0:T(8,128)(2,1)S(1)}, u32[]{:S(2)}, u32[]{:S(2)}) collective-permute-start(bf16[672,128]{1,0:T(8,128)(2,1)S(1)} %get-tuple-element.47), channel_id=1, source_target_pairs={{0,12},{4,8},{8,4},{12,0},{1,13},{5,9},{9,5},{13,1},{2,14},{6,10},... | collective-permute-start | bytes 516104 | tf_op jit(solution)/shard_map/ppermute | solution.py:28
  24.3 1.7 %collective-permute-start.3 = (f32[128,128]{1,0:T(8,128)S(1)}, f32[128,128]{1,0:T(8,128)S(1)}, u32[]{:S(2)}, u32[]{:S(2)}) collective-permute-start(f32[128,128]{1,0:T(8,128)S(1)} %get-tuple-element.49), channel_id=1, source_target_pairs={{0,1},{1,0},{2,3},{3,2},{4,5},{5,4},{6,7},{7,6},{8,9},{9,8},{10,11... | collective-permute-start | bytes 196616 | tf_op jit(solution)/shard_map/ppermute | solution.py:28
  24.4 14.0 %collective-permute-start.11 = (bf16[672,128]{1,0:T(8,128)(2,1)S(1)}, bf16[672,128]{1,0:T(8,128)(2,1)S(1)}, u32[]{:S(2)}, u32[]{:S(2)}) collective-permute-start(bf16[672,128]{1,0:T(8,128)(2,1)S(1)} %get-tuple-element.55), channel_id=1, source_target_pairs={{0,16},{16,0},{1,17},{17,1},{2,18},{18,2},{3,19},{19,3},{4,20},{20... | collective-permute-start | bytes 516104 | tf_op jit(solution)/shard_map/ppermute | solution.py:28
  26.7 5.4 %collective-permute-start.4 = (bf16[256,128]{1,0:T(8,128)(2,1)S(1)}, bf16[256,128]{1,0:T(8,128)(2,1)S(1)}, u32[]{:S(2)}, u32[]{:S(2)}) collective-permute-start(bf16[256,128]{1,0:T(8,128)(2,1)S(1)} %get-tuple-element.52), channel_id=1, source_target_pairs={{0,4},{4,0},{8,12},{12,8},{1,5},{5,1},{9,13},{13,9},{2,6},{6,2},{1... | collective-permute-start | bytes 196616 | tf_op jit(solution)/shard_map/ppermute | solution.py:28
  29.6 8.3 %collective-permute-start.5 = (bf16[256,128]{1,0:T(8,128)(2,1)S(1)}, bf16[256,128]{1,0:T(8,128)(2,1)S(1)}, u32[]{:S(2)}, u32[]{:S(2)}) collective-permute-start(bf16[256,128]{1,0:T(8,128)(2,1)S(1)} %get-tuple-element.53), channel_id=1, source_target_pairs={{0,8},{4,12},{8,0},{12,4},{1,9},{5,13},{9,1},{13,5},{2,10},{6,14},... | collective-permute-start | bytes 196616 | tf_op jit(solution)/shard_map/ppermute | solution.py:28
  30.7 7.2 %collective-permute-start.6 = (bf16[256,128]{1,0:T(8,128)(2,1)S(1)}, bf16[256,128]{1,0:T(8,128)(2,1)S(1)}, u32[]{:S(2)}, u32[]{:S(2)}) collective-permute-start(bf16[256,128]{1,0:T(8,128)(2,1)S(1)} %get-tuple-element.54), channel_id=1, source_target_pairs={{0,12},{4,8},{8,4},{12,0},{1,13},{5,9},{9,5},{13,1},{2,14},{6,10},... | collective-permute-start | bytes 196616 | tf_op jit(solution)/shard_map/ppermute | solution.py:28
  32.1 6.3 %collective-permute-start.7 = (bf16[256,128]{1,0:T(8,128)(2,1)S(1)}, bf16[256,128]{1,0:T(8,128)(2,1)S(1)}, u32[]{:S(2)}, u32[]{:S(2)}) collective-permute-start(bf16[256,128]{1,0:T(8,128)(2,1)S(1)} %get-tuple-element.51.refs_0_), channel_id=1, source_target_pairs={{0,1},{1,0},{2,3},{3,2},{4,5},{5,4},{6,7},{7,6},{8,9},{9,8},{10,11... | collective-permute-start | bytes 196616 | tf_op jit(solution)/shard_map/ppermute | solution.py:28
  32.1 6.3 %collective-permute-start.8 = (bf16[256,128]{1,0:T(8,128)(2,1)S(1)}, bf16[256,128]{1,0:T(8,128)(2,1)S(1)}, u32[]{:S(2)}, u32[]{:S(2)}) collective-permute-start(bf16[256,128]{1,0:T(8,128)(2,1)S(1)} %collective-permute-done.4.refs_1_.refs_3_), channel_id=1, source_target_pairs={{0,1},{1,0},{2,3},{3,2},{4,5},{5,4},{6,7},{7,6},{8,9},{9,8},{10,11... | collective-permute-start | bytes 196616 | tf_op jit(solution)/shard_map/ppermute | solution.py:28
  37.8 1.3 %collective-permute-start.9 = (bf16[256,128]{1,0:T(8,128)(2,1)S(1)}, bf16[256,128]{1,0:T(8,128)(2,1)S(1)}, u32[]{:S(2)}, u32[]{:S(2)}) collective-permute-start(bf16[256,128]{1,0:T(8,128)(2,1)S(1)} %collective-permute-done.5.refs_2_.refs_4_), channel_id=1, source_target_pairs={{0,1},{1,0},{2,3},{3,2},{4,5},{5,4},{6,7},{7,6},{8,9},{9,8},{10,11... | collective-permute-start | bytes 196616 | tf_op jit(solution)/shard_map/ppermute | solution.py:28
  37.9 1.4 %collective-permute-start.10 = (bf16[256,128]{1,0:T(8,128)(2,1)S(1)}, bf16[256,128]{1,0:T(8,128)(2,1)S(1)}, u32[]{:S(2)}, u32[]{:S(2)}) collective-permute-start(bf16[256,128]{1,0:T(8,128)(2,1)S(1)} %collective-permute-done.6.refs_3_.refs_5_), channel_id=1, source_target_pairs={{0,1},{1,0},{2,3},{3,2},{4,5},{5,4},{6,7},{7,6},{8,9},{9,8},{10,11... | collective-permute-start | bytes 196616 | tf_op jit(solution)/shard_map/ppermute | solution.py:28
  41.1 1.3 %collective-permute-start.12 = (bf16[2,128,128]{2,1,0:T(8,128)(2,1)S(1)}, bf16[2,128,128]{2,1,0:T(8,128)(2,1)S(1)}, u32[]{:S(2)}, u32[]{:S(2)}) collective-permute-start(bf16[2,128,128]{2,1,0:T(8,128)(2,1)S(1)} %get-tuple-element.57), channel_id=1, source_target_pairs={{0,1},{1,0},{2,3},{3,2},{4,5},{5,4},{6,7},{7,6},{8,9},{9,8},{10,11... | collective-permute-start | bytes 196616 | tf_op jit(solution)/shard_map/ppermute | solution.py:28
  43.0 4.5 %collective-permute-start.13 = (bf16[272,128]{1,0:T(8,128)(2,1)S(1)}, bf16[272,128]{1,0:T(8,128)(2,1)S(1)}, u32[]{:S(2)}, u32[]{:S(2)}) collective-permute-start(bf16[272,128]{1,0:T(8,128)(2,1)S(1)} %get-tuple-element.60), channel_id=1, source_target_pairs={{0,4},{4,0},{8,12},{12,8},{1,5},{5,1},{9,13},{13,9},{2,6},{6,2},{1... | collective-permute-start | bytes 208904 | tf_op jit(solution)/shard_map/ppermute | solution.py:28
  44.3 8.6 %collective-permute-start.14 = (bf16[272,128]{1,0:T(8,128)(2,1)S(1)}, bf16[272,128]{1,0:T(8,128)(2,1)S(1)}, u32[]{:S(2)}, u32[]{:S(2)}) collective-permute-start(bf16[272,128]{1,0:T(8,128)(2,1)S(1)} %get-tuple-element.61), channel_id=1, source_target_pairs={{0,8},{4,12},{8,0},{12,4},{1,9},{5,13},{9,1},{13,5},{2,10},{6,14},... | collective-permute-start | bytes 208904 | tf_op jit(solution)/shard_map/ppermute | solution.py:28
  45.8 7.1 %collective-permute-start.15 = (bf16[272,128]{1,0:T(8,128)(2,1)S(1)}, bf16[272,128]{1,0:T(8,128)(2,1)S(1)}, u32[]{:S(2)}, u32[]{:S(2)}) collective-permute-start(bf16[272,128]{1,0:T(8,128)(2,1)S(1)} %get-tuple-element.62), channel_id=1, source_target_pairs={{0,12},{4,8},{8,4},{12,0},{1,13},{5,9},{9,5},{13,1},{2,14},{6,10},... | collective-permute-start | bytes 208904 | tf_op jit(solution)/shard_map/ppermute | solution.py:28
  53.5 1.3 %collective-permute-start.16 = (bf16[2,128,128]{2,1,0:T(8,128)(2,1)S(1)}, bf16[2,128,128]{2,1,0:T(8,128)(2,1)S(1)}, u32[]{:S(2)}, u32[]{:S(2)}) collective-permute-start(bf16[2,128,128]{2,1,0:T(8,128)(2,1)S(1)} %shard_map.164.refs_0_.mine), channel_id=1, source_target_pairs={{0,1},{1,0},{2,3},{3,2},{4,5},{5,4},{6,7},{7,6},{8,9},{9,8},{10,11... | collective-permute-start | bytes 196616 | tf_op jit(solution)/shard_map/ppermute | solution.py:28
  55.6 5.3 %collective-permute-start.17 = (bf16[448,128]{1,0:T(8,128)(2,1)S(1)}, bf16[448,128]{1,0:T(8,128)(2,1)S(1)}, u32[]{:S(2)}, u32[]{:S(2)}) collective-permute-start(bf16[448,128]{1,0:T(8,128)(2,1)S(1)} %get-tuple-element.64), channel_id=1, source_target_pairs={{0,2},{2,0},{1,3},{3,1},{4,6},{6,4},{5,7},{7,5},{8,10},{10,8},{9,1... | collective-permute-start | bytes 344072 | tf_op jit(solution)/shard_map/ppermute | solution.py:576
  61.9 1.4 %collective-permute-start.18 = (bf16[4,128,128]{2,1,0:T(8,128)(2,1)S(1)}, bf16[4,128,128]{2,1,0:T(8,128)(2,1)S(1)}, u32[]{:S(2)}, u32[]{:S(2)}) collective-permute-start(bf16[4,128,128]{2,1,0:T(8,128)(2,1)S(1)} %get-tuple-element.66), channel_id=1, source_target_pairs={{0,1},{1,0},{2,3},{3,2},{4,5},{5,4},{6,7},{7,6},{8,9},{9,8},{10,11... | collective-permute-start | bytes 393224 | tf_op jit(solution)/shard_map/ppermute | solution.py:28
  63.4 8.3 %collective-permute-start.21 = (bf16[4,128,128]{2,1,0:T(8,128)(2,1)S(1)}, bf16[4,128,128]{2,1,0:T(8,128)(2,1)S(1)}, u32[]{:S(2)}, u32[]{:S(2)}) collective-permute-start(bf16[4,128,128]{2,1,0:T(8,128)(2,1)S(1)} %add_convert_fusion.refs_0_), channel_id=1, source_target_pairs={{0,12},{4,8},{8,4},{12,0},{1,13},{5,9},{9,5},{13,1},{2,14},{6,10},... | collective-permute-start | bytes 393224 | tf_op jit(solution)/shard_map/ppermute | solution.py:28
  65.4 12.7 %collective-permute-start.20 = (bf16[4,128,128]{2,1,0:T(8,128)(2,1)S(1)}, bf16[4,128,128]{2,1,0:T(8,128)(2,1)S(1)}, u32[]{:S(2)}, u32[]{:S(2)}) collective-permute-start(bf16[4,128,128]{2,1,0:T(8,128)(2,1)S(1)} %add_convert_fusion.refs_0_), channel_id=1, source_target_pairs={{0,8},{4,12},{8,0},{12,4},{1,9},{5,13},{9,1},{13,5},{2,10},{6,14},... | collective-permute-start | bytes 393224 | tf_op jit(solution)/shard_map/ppermute | solution.py:28
  66.2 12.0 %collective-permute-start.19 = (bf16[4,128,128]{2,1,0:T(8,128)(2,1)S(1)}, bf16[4,128,128]{2,1,0:T(8,128)(2,1)S(1)}, u32[]{:S(2)}, u32[]{:S(2)}) collective-permute-start(bf16[4,128,128]{2,1,0:T(8,128)(2,1)S(1)} %add_convert_fusion.refs_0_), channel_id=1, source_target_pairs={{0,4},{4,0},{8,12},{12,8},{1,5},{5,1},{9,13},{13,9},{2,6},{6,2},{1... | collective-permute-start | bytes 393224 | tf_op jit(solution)/shard_map/ppermute | solution.py:28
  68.6 9.7 %collective-permute-start.23 = (bf16[2,448,128]{2,1,0:T(8,128)(2,1)S(1)}, bf16[2,448,128]{2,1,0:T(8,128)(2,1)S(1)}, u32[]{:S(2)}, u32[]{:S(2)}) collective-permute-start(bf16[2,448,128]{2,1,0:T(8,128)(2,1)S(1)} %shard_map.168), channel_id=1, source_target_pairs={{0,2},{2,0},{1,3},{3,1},{4,6},{6,4},{5,7},{7,5},{8,10},{10,8},{9,1... | collective-permute-start | bytes 688136 | tf_op jit(solution)/shard_map/ppermute | solution.py:576
  78.3 1.4 %collective-permute-start.22 = (bf16[4,128,128]{2,1,0:T(8,128)(2,1)S(1)}, bf16[4,128,128]{2,1,0:T(8,128)(2,1)S(1)}, u32[]{:S(2)}, u32[]{:S(2)}) collective-permute-start(bf16[4,128,128]{2,1,0:T(8,128)(2,1)S(1)} %shard_map.167.mine), channel_id=1, source_target_pairs={{0,1},{1,0},{2,3},{3,2},{4,5},{5,4},{6,7},{7,6},{8,9},{9,8},{10,11... | collective-permute-start | bytes 393224 | tf_op jit(solution)/shard_map/ppermute | solution.py:28
  81.9 1.3 %collective-permute-start.24 = (bf16[2,128,128]{2,1,0:T(8,128)(2,1)S(1)}, bf16[2,128,128]{2,1,0:T(8,128)(2,1)S(1)}, u32[]{:S(2)}, u32[]{:S(2)}) collective-permute-start(bf16[2,128,128]{2,1,0:T(8,128)(2,1)S(1)} %get-tuple-element.70), channel_id=1, source_target_pairs={{0,1},{1,0},{2,3},{3,2},{4,5},{5,4},{6,7},{7,6},{8,9},{9,8},{10,11... | collective-permute-start | bytes 196616 | tf_op jit(solution)/shard_map/ppermute | solution.py:28
  83.3 6.8 %collective-permute-start.27 = (bf16[256,128]{1,0:T(8,128)(2,1)S(1)}, bf16[256,128]{1,0:T(8,128)(2,1)S(1)}, u32[]{:S(2)}, u32[]{:S(2)}) collective-permute-start(bf16[256,128]{1,0:T(8,128)(2,1)S(1)} %bitcast.46), channel_id=1, source_target_pairs={{0,12},{4,8},{8,4},{12,0},{1,13},{5,9},{9,5},{13,1},{2,14},{6,10},... | collective-permute-start | bytes 196616 | tf_op jit(solution)/shard_map/ppermute | solution.py:28
  85.6 6.5 %collective-permute-start.26 = (bf16[256,128]{1,0:T(8,128)(2,1)S(1)}, bf16[256,128]{1,0:T(8,128)(2,1)S(1)}, u32[]{:S(2)}, u32[]{:S(2)}) collective-permute-start(bf16[256,128]{1,0:T(8,128)(2,1)S(1)} %bitcast.47), channel_id=1, source_target_pairs={{0,8},{4,12},{8,0},{12,4},{1,9},{5,13},{9,1},{13,5},{2,10},{6,14},... | collective-permute-start | bytes 196616 | tf_op jit(solution)/shard_map/ppermute | solution.py:28
  85.7 6.5 %collective-permute-start.25 = (bf16[256,128]{1,0:T(8,128)(2,1)S(1)}, bf16[256,128]{1,0:T(8,128)(2,1)S(1)}, u32[]{:S(2)}, u32[]{:S(2)}) collective-permute-start(bf16[256,128]{1,0:T(8,128)(2,1)S(1)} %bitcast.48), channel_id=1, source_target_pairs={{0,4},{4,0},{8,12},{12,8},{1,5},{5,1},{9,13},{13,9},{2,6},{6,2},{1... | collective-permute-start | bytes 196616 | tf_op jit(solution)/shard_map/ppermute | solution.py:28
  92.7 1.3 %collective-permute-start.28 = (bf16[2,128,128]{2,1,0:T(8,128)(2,1)S(1)}, bf16[2,128,128]{2,1,0:T(8,128)(2,1)S(1)}, u32[]{:S(2)}, u32[]{:S(2)}) collective-permute-start(bf16[2,128,128]{2,1,0:T(8,128)(2,1)S(1)} %shard_map.170.refs_0_), channel_id=1, source_target_pairs={{0,1},{1,0},{2,3},{3,2},{4,5},{5,4},{6,7},{7,6},{8,9},{9,8},{10,11... | collective-permute-start | bytes 196616 | tf_op jit(solution)/shard_map/ppermute | solution.py:28
  (14 other events, 93.3 us)

commit v4 on v3

--- a/solution.py
+++ b/solution.py
@@ -40,7 +40,8 @@
 
 
 def exchange(sends):
-    return [sends[0]] + [swap(sends[step], "feat", step) for step in peers("feat")]
+    got = {step: swap(sends[step], "feat", step) for step in reversed(peers("feat"))}
+    return [sends[0]] + [got[step] for step in peers("feat")]
 
 
 def total(blocks):
@@ -244,7 +245,7 @@
     return jax.ShapeDtypeStruct(sizes, dtype)
 
 
-def kernel_call(body, outs, scalars, arrays, left=(), scratch=(), flops=0):
+def kernel_call(body, outs, scalars, arrays, left=(), scratch=(), flops=0, room=16 * 1024 * 1024):
     many = isinstance(outs, (list, tuple))
     kept = list(outs) if many else [outs]
     size = sum(a.size * a.dtype.itemsize for a in arrays) + sum(a.size * a.dtype.itemsize for a in kept)
@@ -254,9 +255,13 @@
         in_specs=[pl.BlockSpec(memory_space=pltpu.SMEM)] * len(scalars) + [pl.BlockSpec(memory_space=pltpu.VMEM)] * len(arrays) + [pl.BlockSpec(memory_space=pltpu.HBM)] * len(left),
         out_specs=tuple(pl.BlockSpec(memory_space=pltpu.VMEM) for _ in kept) if many else pl.BlockSpec(memory_space=pltpu.VMEM),
         scratch_shapes=list(scratch),
-        compiler_params=pltpu.CompilerParams(vmem_limit_bytes=16 * 1024 * 1024),
+        compiler_params=pltpu.CompilerParams(vmem_limit_bytes=room),
         cost_estimate=pl.CostEstimate(flops=int(flops), bytes_accessed=int(size), transcendentals=0),
     )(*scalars, *arrays, *left)
+
+
+def place_of():
+    return [lax.axis_index(axis) for axis in ("feat", "tok", "layer", "groups")]
 
 
 def split_terms(value):
@@ -267,7 +272,7 @@
     return [high, middle, low]
 
 
-def facts_body(place, lengths, chosen, table, mode, index, bias, scale, patterns, info, mixing, scales):
+def facts_body(lengths, chosen, table, mode, index, bias, scale, patterns, info, mixing, scales, lives):
     block = chosen[0, 0]
     modes = mode[pl.ds(block, 1), :]
     entries = index[pl.ds(block, 1), :]
@@ -290,14 +295,19 @@
             mixing[head, p * seq : (p + 1) * seq, :] = row.astype(BF16)
     rows = scale.shape[1]
     scales[...] = jnp.broadcast_to(scale[...], (rows, rows)).T
-
-
-def start_body(ranges, place, state, weight, enc, *refs):
-    sends, sems = refs[:-1], refs[-1]
+    row = lax.broadcasted_iota(jnp.int32, lives.shape, 0)
+    end = jnp.full(row.shape, lengths[0], jnp.int32)
+    for p in range(1, prompts):
+        end = jnp.where(row >= p * seq, p * seq + lengths[p], end)
+    lives[...] = jnp.where(row < end, 1.0, 0.0)
+
+
+def start_body(ranges, state, weight, enc, *refs):
+    place = place_of()
+    sends, sems = (None, *refs[:-1]), refs[-1]
     width, rows = state.shape
     part = width // 2
     low = state[...].astype(BF16)
-    sends[0][...] = low
 
     def copies(source, first, size, at, group):
         made = []
@@ -349,33 +359,37 @@
                 sends[step][at + size : at + rows] = block[size:]
 
 
-def values_body(ranges, place, *refs):
-    blocks, (weight, own, other, passed) = refs[:ranges], refs[ranges:]
-    width, half = blocks[0].shape[0], own.shape[1]
+def values_body(ranges, *refs):
+    blocks, (weight, own, passed) = refs[:ranges], refs[ranges:]
+    width = passed.shape[0] // (ranges - 1) * 2
+    place = place_of()
     acc = None
     for step, block in enumerate(blocks):
         n = partner(place[0], step, ranges) if step else place[0]
         if step:
             size = block.shape[0] - width
             passed[(step - 1) * size : step * size] = block[width:]
-        part = dot_tn(block[0:width], weight[pl.ds(pl.multiple_of(n * width, 16), width), :])
+        part = dot_tn(block[0:width].astype(BF16), weight[pl.ds(pl.multiple_of(n * width, 16), width), :])
         acc = part if acc is None else acc + part
-    first = place[1] == 0
-    own[...] = jnp.where(first, acc[:, :half], acc[:, half:])
-    other[...] = jnp.where(first, acc[:, half:], acc[:, :half])
+    own[...] = acc
 
 
 def mix(mixing, head, values):
     return jnp.dot(mixing[head], values, preferred_element_type=F32).astype(BF16)
 
 
-def heads_body(ranges, per_group, width, place, own, got, scales, mixing, weight, *sends):
-    values = ((own[...] + got[...]) * scales[...]).astype(BF16)
-    made = [mix(mixing, place[0] * per_group + u, values) for u in range(per_group)]
-    carry(place, ranges, weight, width, 0, sends[0].shape[0], made, sends)
-
-
-def sums_body(ranges, width, done, place, own, got, weight, info, *sends):
+def whole_values_body(ranges, width, own, got, scales, weight, *sends):
+    place = place_of()
+    rows, half = scales.shape
+    made = [
+        ((own[:, n * half : (n + 1) * half] + got[:, n * half : (n + 1) * half]) * scales[...]).astype(BF16)
+        for n in range(2)
+    ]
+    carry(place, ranges, weight, width, 0, 2 * rows, made, sends)
+
+
+def sums_body(ranges, width, done, own, got, weight, info, *sends):
+    place = place_of()
     made = [(own[n] + got[n].astype(F32)).astype(BF16) for n in range(own.shape[0])]
     carry(place, ranges, weight, width, done, width - done, made, sends)
     for send in sends:
@@ -386,7 +400,8 @@
     return jnp.concatenate([jnp.where(first, mine, theirs), jnp.where(first, theirs, mine)], axis=1)
 
 
-def spread_values_body(ranges, carried, place, low, weight, *refs):
+def spread_values_body(ranges, carried, low, weight, *refs):
+    place = place_of()
     others = ranges - 1
     firsts, seconds, thirds = (refs[i * others : (i + 1) * others] for i in range(3))
     own, other = refs[3 * others :]
@@ -435,22 +450,22 @@
     other[...] = parts[pl.ds((1 - place[1]) * share, share)].astype(BF16)
 
 
-def first_code_body(ranges, per_group, place, *refs):
-    got, also = (refs[i * ranges : (i + 1) * ranges] for i in range(2))
-    blocks = refs[2 * ranges : 3 * ranges - 1]
-    passed, state, weight, *ends = refs[3 * ranges - 1 :]
+def first_code_body(ranges, per_group, *refs):
+    place = place_of()
+    got, blocks = refs[:ranges], refs[ranges : 2 * ranges - 1]
+    passed, state, mixing, weight, *ends = refs[2 * ranges - 1 :]
     rows = state.shape[1]
-    first = place[1] == 0
     acc = state[...]
     for step in range(ranges):
         n = partner(place[0], step, ranges) if step else place[0]
+        values = jnp.concatenate([got[step][0:rows], got[step][rows:]], axis=1)
         for u in range(per_group):
-            span = slice(u * rows, (u + 1) * rows)
-            acc = acc + dot_nt(weight[n * per_group + u], halves_of(first, got[step][span], also[step][span]))
+            acc = acc + dot_nt(weight[n * per_group + u], mix(mixing, n * per_group + u, values))
     finish(ranges, place, acc, blocks, passed, *ends)
 
 
-def later_code_body(ranges, per_group, place, mine, also, low, rest, mixing, *refs):
+def later_code_body(ranges, per_group, mine, also, low, rest, mixing, *refs):
+    place = place_of()
     blocks = refs[: ranges - 1]
     passed, weight, *ends = refs[ranges - 1 :]
     first = place[1] == 0
@@ -462,16 +477,13 @@
     finish(ranges, place, acc, blocks, passed, *ends)
 
 
-def clamp_body(seq, place, lengths, *refs):
-    *refs, out = refs
+def clamp_body(*refs):
+    place = place_of()
+    *refs, lives, out = refs
     blocks, facts = refs[: len(refs) // 2], refs[len(refs) // 2 :]
-    share, rows, cols = out.shape
+    share, rows, _ = out.shape
     ranges = len(blocks)
-    row = lax.broadcasted_iota(jnp.int32, out.shape[1:], 0)
-    end = jnp.full(row.shape, lengths[0], jnp.int32)
-    for p in range(1, rows // seq):
-        end = jnp.where(row >= p * seq, p * seq + lengths[p], end)
-    live = row < end
+    live = lives[...] > 0.5
     terms = [f[f.shape[0] - INFO :].astype(F32) for f in facts]
     terms = [
         [t[3 * i : 3 * i + 1] + t[3 * i + 1 : 3 * i + 2] + t[3 * i + 2 : 3 * i + 3] for i in range(3)] for t in terms
@@ -495,7 +507,8 @@
     ]
 
 
-def decode_body(layer, adds, linked, sends, keeps, place, *refs):
+def decode_body(layer, adds, linked, sends, keeps, *refs):
+    place = place_of()
     refs = list(refs)
     take = lambda count: [refs.pop(0) for _ in range(count)]
     (mine, also, dec), added, links, before = take(3), take(adds), take(linked), take(2 if keeps else 0)
@@ -523,7 +536,8 @@
         feats_out[...] = block
 
 
-def writes_body(layer, linked, place, mine, also, dec, left, *refs):
+def writes_body(layer, linked, mine, also, dec, left, *refs):
+    place = place_of()
     out = refs[-1]
     feats = jnp.concatenate(ordered(place, mine, also), axis=1)
     out[0] = left[...]
@@ -563,7 +577,6 @@
     block_len = enc_bias.shape[1]
     rows = residual_in.shape[0]
     share = ranges // 2
-    place = jnp.stack([lax.axis_index("feat"), lax.axis_index("tok"), lax.axis_index("layer"), lax.axis_index("groups")]).astype(jnp.int32)
 
     source = residual_in[:, 0, :].T
     error_cols = errors[0, :, 0, :].T
@@ -580,21 +593,23 @@
         if layer == 0:
             sends = kernel_call(
                 functools.partial(start_body, ranges),
-                [shape(width, rows, dtype=BF16)] + [shape(width + width // 2, rows, dtype=BF16)] * (ranges - 1),
-                [place],
+                [shape(width + width // 2, rows, dtype=BF16)] * (ranges - 1),
+                [],
                 [source],
                 left=[value_rows, enc_rows],
                 scratch=[pltpu.SemaphoreType.DMA((2, ranges - 1))],
-            )
-            blocks = exchange(sends)
-            info, mixing, scales = kernel_call(
+                room=60 * 1024 * 1024,
+            )
+            blocks = exchange([source, *sends])
+            info, mixing, scales, live = kernel_call(
                 facts_body,
                 [
                     shape(INFO, block_len, dtype=BF16),
                     shape(patterns.shape[1], rows, rows, dtype=BF16),
                     shape(rows, half),
+                    shape(rows, block_len),
                 ],
-                [place, lengths, active_blocks, clamp_values],
+                [lengths, active_blocks, clamp_values],
                 [
                     clamp_mode.reshape(-1, block_len),
                     clamp_index.reshape(-1, block_len),
@@ -603,33 +618,32 @@
                     patterns[0],
                 ],
             )
-            blocks[0], info, mixing, scales = lax.optimization_barrier((blocks[0], info, mixing, scales))
-            own, other, passed = kernel_call(
+            blocks[1], info, mixing, scales, live = lax.optimization_barrier((blocks[1], info, mixing, scales, live))
+            own, passed = kernel_call(
                 functools.partial(values_body, ranges),
-                [shape(rows, half)] * 2 + [shape((ranges - 1) * (width // 2), rows, dtype=BF16)],
-                [place],
+                [shape(rows, kv_cols), shape((ranges - 1) * (width // 2), rows, dtype=BF16)],
+                [],
                 [*blocks, value_rows],
                 flops=4 * rows * value_rows.size,
             )
-            got = swap(other, "tok", 1)
+            got = swap(own, "tok", 1)
             passed = swap(passed, "groups", 1)
             packed = [*blocks[1:], passed]
             sends = kernel_call(
-                functools.partial(heads_body, ranges, per_group, width),
-                [shape(per_group * rows, half, dtype=BF16)] * ranges,
-                [place],
-                [own, got, scales, mixing, value_rows],
+                functools.partial(whole_values_body, ranges, width),
+                [shape(2 * rows, half, dtype=BF16)] * ranges,
+                [],
+                [own, got, scales, value_rows],
             )
             got = exchange(sends)
-            also = [swap(b, "tok", 1) for b in got]
             carried = [*blocks[1:], *got[1:]]
             code = functools.partial(first_code_body, ranges, per_group)
-            scalars, given = [place], [*got, *also, *packed, source]
+            given = [*got, *packed, source, mixing]
         else:
             own, other = kernel_call(
-                functools.partial(spread_values_body, ranges, per_group * rows),
+                functools.partial(spread_values_body, ranges, 2 * rows),
                 [shape(ranges, rows, half), shape(ranges, rows, half, dtype=BF16)],
-                [place],
+                [],
                 [low, value_rows, *carried],
                 flops=2 * rows * value_rows.size,
             )
@@ -638,7 +652,7 @@
             rest = handed_on(after(rest, low))
             mine = kernel_call(scaled_body, shape(ranges, rows, half, dtype=BF16), [], [scales, *blocks])
             code = functools.partial(later_code_body, ranges, per_group)
-            scalars, given = [place], [mine, swap(mine, "tok", 1), low, rest, mixing, *packed]
+            scalars, given = [], [mine, swap(mine, "tok", 1), low, rest, mixing, *packed]
         middle, own, other = kernel_call(
             code,
             [
@@ -646,7 +660,7 @@
                 shape(share, rows, block_len),
                 shape(share, rows, block_len, dtype=BF16),
             ],
-            scalars,
+            [],
             [*given, out_weight, enc_rows, mlp_scale],
             scratch=[pltpu.VMEM((ranges, rows, block_len), F32)],
             flops=2 * rows * (out_weight.size + width * block_len * ranges),
@@ -654,9 +668,9 @@
         got = swap(other, "tok", 1)
         if layer == 0:
             sends = kernel_call(
-                functools.partial(sums_body, ranges, width, per_group * rows),
+                functools.partial(sums_body, ranges, width, 2 * rows),
                 [shape(share * rows + INFO, block_len, dtype=BF16)] * ranges,
-                [place],
+                [],
                 [own, got, value_rows, info],
             )
             blocks = facts = exchange(sends)
@@ -664,10 +678,10 @@
         else:
             blocks = spread((own + got.astype(F32)).astype(BF16).reshape(-1, block_len))
         mine = kernel_call(
-            functools.partial(clamp_body, seq),
+            clamp_body,
             shape(share, rows, block_len, dtype=BF16),
-            [place, lengths],
-            [*blocks, *facts],
+            [],
+            [*blocks, *facts, live],
         )
         also = swap(mine, "tok", 1)
         more = layer + 1 < layers
@@ -679,7 +693,7 @@
         made = kernel_call(
             functools.partial(decode_body, layer, len(added), len(links), more, kept is not None),
             outs,
-            [place],
+            [],
             [mine, also, dec_cols, *added, *links, *(kept or ())],
             flops=2 * rows * dec_cols.size // layers,
         )
@@ -689,7 +703,7 @@
             rest = kernel_call(
                 functools.partial(writes_body, layer, len(links)),
                 shape(layers - layer, width, rows, dtype=BF16),
-                [place],
+                [],
                 [mine, also, dec_cols, made[3], *links],
                 flops=2 * rows * dec_cols.size,
             )
@@ -702,7 +716,7 @@
         and residual_in.shape[2] % 32 == 0
         and value_proj.shape[3] == out_proj.shape[2]
         and value_proj.shape[3] == 2 * enc_bias.shape[1] == 2 * residual_in.shape[0]
-        and residual_in.shape[2] <= residual_in.shape[0] * (out_proj.shape[3] + lax.axis_size("feat") // 2)
+        and residual_in.shape[2] <= residual_in.shape[0] * (2 + lax.axis_size("feat") // 2)
         and lax.axis_size("feat") % 2 == 0
         and lax.axis_size("tok") == lax.axis_size("groups") == 2
     )

time: 96 us -> 88.5 us (0.922)
  Pallas kernels: 13.3 us -> 9.56 us
  local copies, waits for them, and re-layouts: 8.17 us -> 5.04 us
  starting transfers between devices: 31.2 us -> 30.2 us
    pallas_call x14, Pallas kernels: 13.3 us -> 9.56 us  [kernel_call(): pl.pallas_call(body, out_shape=tuple(kept) if many else outs, in_specs=[p...]
    unnamed x34 -> x28, local copies, waits for them, and re-layouts: 8.17 us -> 5.04 us
    ppermute x27 -> x23, starting transfers between devices: 28 us -> 26.6 us  [swap(): lax.ppermute(value, axis, [(s, partner(s, step, count)) for s in range(co...]
    ppermute x27 -> x23, waiting for transfers between devices: 37.6 us -> 38.3 us  [swap(): lax.ppermute(value, axis, [(s, partner(s, step, count)) for s in range(co...]
  transfers between devices with their start and end apart: 29 -> 25, of which waited for: 16 -> 14; matrix products, arithmetic and copies ran while one was open for 0% -> 0% of each run, Pallas kernels for 2% -> 1%
where the time goes in v4:
time: 88.5 us; the launch traced here: 88.1 us
  waiting for transfers between devices  41.7 us (47%)
  starting transfers between devices  30.2 us (34%)
  Pallas kernels  9.56 us (11%)
  local copies, waits for them, and re-layouts  5.04 us (6%)
  between operations  1.52 us (2%)
    ppermute x23, waiting for transfers between devices, swap(): lax.ppermute(value, axis, [(s, partner(s, step, count)) for s in range(co...  38.3 us
    ppermute x23, starting transfers between devices, swap(): lax.ppermute(value, axis, [(s, partner(s, step, count)) for s in range(co...  26.6 us
    pallas_call x14, Pallas kernels, kernel_call(): pl.pallas_call(body, out_shape=tuple(kept) if many else outs, in_specs=[p...  9.56 us
    unnamed x28, local copies, waits for them, and re-layouts  5.04 us
    ppermute x2, starting transfers between devices, handed_on(): lax.ppermute(value, 'layer', [(n, (n + 1) % layers) for n in range(layers)])  3.6 us
    ppermute x2, waiting for transfers between devices, handed_on(): lax.ppermute(value, 'layer', [(n, (n + 1) % layers) for n in range(layers)])  3.48 us
  transfers between devices with their start and end apart: 25, of which 14 were waited for; matrix products, arithmetic and copies ran while one was open for 0% of the time, Pallas kernels for 1%

profile of v4, /device:TPU:0, one launch (start us, length us, event | category | flops | bytes accessed | tf_op | source)
XLA Modules:
  0.0 88.1 jit_solution(6750236177660103455)
XLA Ops:
  0.7 2.8 %shard_map.158 = (bf16[672,128]{1,0:T(8,128)(2,1)}, bf16[672,128]{1,0:T(8,128)(2,1)}, bf16[672,128]{1,0:T(8,128)(2,1)}) custom-call(f32[448,128]{1,0:T(8,128)} %bitcast.37, bf16[1792,256]{1,0:T(8,128)(2,1)} %bitcast.24, bf16[1792,128]{1,0:T(8,128)(2,1)} %bitcast.34), custom_call_target="tpu_custom_call" | custom-call | bytes 745472 | tf_op jit(solution)/shard_map/pallas_call | solution.py:252
  3.4 3.1 %collective-permute-start = (bf16[672,128]{1,0:T(8,128)(2,1)}, bf16[672,128]{1,0:T(8,128)(2,1)S(1)}, u32[]{:S(2)}, u32[]{:S(2)}) collective-permute-start(bf16[672,128]{1,0:T(8,128)(2,1)} %get-tuple-element.39), channel_id=1, source_target_pairs={{0,4},{4,0},{8,12},{12,8},{1,5},{5,1},{9,13},{13,9},{2,6},{6,2},{1... | collective-permute-start | bytes 516104 | tf_op jit(solution)/shard_map/ppermute | solution.py:28
  6.5 2.6 %collective-permute-start.1 = (bf16[672,128]{1,0:T(8,128)(2,1)}, bf16[672,128]{1,0:T(8,128)(2,1)S(1)}, u32[]{:S(2)}, u32[]{:S(2)}) collective-permute-start(bf16[672,128]{1,0:T(8,128)(2,1)} %get-tuple-element.46), channel_id=1, source_target_pairs={{0,8},{4,12},{8,0},{12,4},{1,9},{5,13},{9,1},{13,5},{2,10},{6,14},... | collective-permute-start | bytes 516104 | tf_op jit(solution)/shard_map/ppermute | solution.py:28
  15.5 6.8 %collective-permute-done.1.refs_2_.refs_5_.refs_1_ = bf16[672,128]{1,0:T(8,128)(2,1)S(1)} collective-permute-done((bf16[672,128]{1,0:T(8,128)(2,1)}, bf16[672,128]{1,0:T(8,128)(2,1)S(1)}, u32[]{:S(2)}, u32[]{:S(2)}) %collective-permute-start.1) | collective-permute-done | bytes 172064 | tf_op jit(solution)/shard_map/ppermute | solution.py:28
  22.8 1.6 %collective-permute-start.7 = (bf16[672,128]{1,0:T(8,128)(2,1)S(1)}, bf16[672,128]{1,0:T(8,128)(2,1)S(1)}, u32[]{:S(2)}, u32[]{:S(2)}) collective-permute-start(bf16[672,128]{1,0:T(8,128)(2,1)S(1)} %get-tuple-element.53), channel_id=1, source_target_pairs={{0,16},{16,0},{1,17},{17,1},{2,18},{18,2},{3,19},{19,3},{4,20},{20... | collective-permute-start | bytes 516104 | tf_op jit(solution)/shard_map/ppermute | solution.py:28
  24.4 2.9 %collective-permute-start.4 = (bf16[256,128]{1,0:T(8,128)(2,1)S(1)}, bf16[256,128]{1,0:T(8,128)(2,1)S(1)}, u32[]{:S(2)}, u32[]{:S(2)}) collective-permute-start(bf16[256,128]{1,0:T(8,128)(2,1)S(1)} %get-tuple-element.50), channel_id=1, source_target_pairs={{0,4},{4,0},{8,12},{12,8},{1,5},{5,1},{9,13},{13,9},{2,6},{6,2},{1... | collective-permute-start | bytes 196616 | tf_op jit(solution)/shard_map/ppermute | solution.py:28
  27.3 1.1 %collective-permute-start.5 = (bf16[256,128]{1,0:T(8,128)(2,1)S(1)}, bf16[256,128]{1,0:T(8,128)(2,1)S(1)}, u32[]{:S(2)}, u32[]{:S(2)}) collective-permute-start(bf16[256,128]{1,0:T(8,128)(2,1)S(1)} %get-tuple-element.51), channel_id=1, source_target_pairs={{0,8},{4,12},{8,0},{12,4},{1,9},{5,13},{9,1},{13,5},{2,10},{6,14},... | collective-permute-start | bytes 196616 | tf_op jit(solution)/shard_map/ppermute | solution.py:28
  28.4 1.4 %collective-permute-start.6 = (bf16[256,128]{1,0:T(8,128)(2,1)S(1)}, bf16[256,128]{1,0:T(8,128)(2,1)S(1)}, u32[]{:S(2)}, u32[]{:S(2)}) collective-permute-start(bf16[256,128]{1,0:T(8,128)(2,1)S(1)} %get-tuple-element.52), channel_id=1, source_target_pairs={{0,12},{4,8},{8,4},{12,0},{1,13},{5,9},{9,5},{13,1},{2,14},{6,10},... | collective-permute-start | bytes 196616 | tf_op jit(solution)/shard_map/ppermute | solution.py:28
  29.8 5.8 %collective-permute-done.5.refs_2_.refs_4_ = bf16[256,128]{1,0:T(8,128)(2,1)S(1)} collective-permute-done((bf16[256,128]{1,0:T(8,128)(2,1)S(1)}, bf16[256,128]{1,0:T(8,128)(2,1)S(1)}, u32[]{:S(2)}, u32[]{:S(2)}) %collective-permute-start.5) | collective-permute-done | bytes 65568 | tf_op jit(solution)/shard_map/ppermute | solution.py:28
  35.6 1.7 %shard_map.162 = (f32[448,128]{1,0:T(8,128)S(1)}, f32[2,128,128]{2,1,0:T(8,128)S(1)}, bf16[2,128,128]{2,1,0:T(8,128)(2,1)S(1)}) custom-call(bf16[256,128]{1,0:T(8,128)(2,1)S(1)} %get-tuple-element.49.refs_0_, bf16[256,128]{1,0:T(8,128)(2,1)S(1)} %collective-permute-done.4.refs_1_.refs_3_, bf16[256,128]{1,0:T(8,128)(2,1)S(1)} %collective-permute-done.5.refs_2_.refs_4_, ...), custom_call_target="tpu_custom_call" | custom-call | flops 293601280 | bytes 4162048 | tf_op jit(solution)/shard_map/pallas_call | solution.py:252
  37.4 1.2 %collective-permute-done.8.got = bf16[2,128,128]{2,1,0:T(8,128)(2,1)S(1)} collective-permute-done((bf16[2,128,128]{2,1,0:T(8,128)(2,1)S(1)}, bf16[2,128,128]{2,1,0:T(8,128)(2,1)S(1)}, u32[]{:S(2)}, u32[]{:S(2)}) %collective-permute-start.8) | collective-permute-done | bytes 65568 | tf_op jit(solution)/shard_map/ppermute | solution.py:28
  38.7 1.4 %collective-permute-start.9 = (bf16[272,128]{1,0:T(8,128)(2,1)S(1)}, bf16[272,128]{1,0:T(8,128)(2,1)S(1)}, u32[]{:S(2)}, u32[]{:S(2)}) collective-permute-start(bf16[272,128]{1,0:T(8,128)(2,1)S(1)} %get-tuple-element.59), channel_id=1, source_target_pairs={{0,4},{4,0},{8,12},{12,8},{1,5},{5,1},{9,13},{13,9},{2,6},{6,2},{1... | collective-permute-start | bytes 208904 | tf_op jit(solution)/shard_map/ppermute | solution.py:28
  40.1 1.3 %collective-permute-start.10 = (bf16[272,128]{1,0:T(8,128)(2,1)S(1)}, bf16[272,128]{1,0:T(8,128)(2,1)S(1)}, u32[]{:S(2)}, u32[]{:S(2)}) collective-permute-start(bf16[272,128]{1,0:T(8,128)(2,1)S(1)} %get-tuple-element.60), channel_id=1, source_target_pairs={{0,8},{4,12},{8,0},{12,4},{1,9},{5,13},{9,1},{13,5},{2,10},{6,14},... | collective-permute-start | bytes 208904 | tf_op jit(solution)/shard_map/ppermute | solution.py:28
  41.4 1.7 %collective-permute-start.11 = (bf16[272,128]{1,0:T(8,128)(2,1)S(1)}, bf16[272,128]{1,0:T(8,128)(2,1)S(1)}, u32[]{:S(2)}, u32[]{:S(2)}) collective-permute-start(bf16[272,128]{1,0:T(8,128)(2,1)S(1)} %get-tuple-element.61), channel_id=1, source_target_pairs={{0,12},{4,8},{8,4},{12,0},{1,13},{5,9},{9,5},{13,1},{2,14},{6,10},... | collective-permute-start | bytes 208904 | tf_op jit(solution)/shard_map/ppermute | solution.py:28
  43.1 5.5 %collective-permute-done.10.refs_2_.refs_6_.refs_7_ = bf16[272,128]{1,0:T(8,128)(2,1)S(1)} collective-permute-done((bf16[272,128]{1,0:T(8,128)(2,1)S(1)}, bf16[272,128]{1,0:T(8,128)(2,1)S(1)}, u32[]{:S(2)}, u32[]{:S(2)}) %collective-permute-start.10) | collective-permute-done | bytes 69664 | tf_op jit(solution)/shard_map/ppermute | solution.py:28
  48.8 1.2 %collective-permute-done.12.refs_1_.also = bf16[2,128,128]{2,1,0:T(8,128)(2,1)S(1)} collective-permute-done((bf16[2,128,128]{2,1,0:T(8,128)(2,1)S(1)}, bf16[2,128,128]{2,1,0:T(8,128)(2,1)S(1)}, u32[]{:S(2)}, u32[]{:S(2)}) %collective-permute-start.12) | collective-permute-done | bytes 65568 | tf_op jit(solution)/shard_map/ppermute | solution.py:28
  50.4 1.8 %collective-permute-start.13 = (bf16[448,128]{1,0:T(8,128)(2,1)S(1)}, bf16[448,128]{1,0:T(8,128)(2,1)S(1)}, u32[]{:S(2)}, u32[]{:S(2)}) collective-permute-start(bf16[448,128]{1,0:T(8,128)(2,1)S(1)} %get-tuple-element.64), channel_id=1, source_target_pairs={{0,2},{2,0},{1,3},{3,1},{4,6},{6,4},{5,7},{7,5},{8,10},{10,8},{9,1... | collective-permute-start | bytes 344072 | tf_op jit(solution)/shard_map/ppermute | solution.py:589
  52.2 3.5 %collective-permute-done.13.low = bf16[448,128]{1,0:T(8,128)(2,1)S(1)} collective-permute-done((bf16[448,128]{1,0:T(8,128)(2,1)S(1)}, bf16[448,128]{1,0:T(8,128)(2,1)S(1)}, u32[]{:S(2)}, u32[]{:S(2)}) %collective-permute-start.13) | collective-permute-done | bytes 114720 | tf_op jit(solution)/shard_map/ppermute | solution.py:589
  56.2 1.3 %collective-permute-done.14 = bf16[4,128,128]{2,1,0:T(8,128)(2,1)S(1)} collective-permute-done((bf16[4,128,128]{2,1,0:T(8,128)(2,1)S(1)}, bf16[4,128,128]{2,1,0:T(8,128)(2,1)S(1)}, u32[]{:S(2)}, u32[]{:S(2)}) %collective-permute-start.14) | collective-permute-done | bytes 131104 | tf_op jit(solution)/shard_map/ppermute | solution.py:28
  57.5 2.2 %collective-permute-start.17 = (bf16[4,128,128]{2,1,0:T(8,128)(2,1)S(1)}, bf16[4,128,128]{2,1,0:T(8,128)(2,1)S(1)}, u32[]{:S(2)}, u32[]{:S(2)}) collective-permute-start(bf16[4,128,128]{2,1,0:T(8,128)(2,1)S(1)} %add_convert_fusion.refs_0_), channel_id=1, source_target_pairs={{0,12},{4,8},{8,4},{12,0},{1,13},{5,9},{9,5},{13,1},{2,14},{6,10},... | collective-permute-start | bytes 393224 | tf_op jit(solution)/shard_map/ppermute | solution.py:28
  60.4 1.6 %collective-permute-start.15 = (bf16[4,128,128]{2,1,0:T(8,128)(2,1)S(1)}, bf16[4,128,128]{2,1,0:T(8,128)(2,1)S(1)}, u32[]{:S(2)}, u32[]{:S(2)}) collective-permute-start(bf16[4,128,128]{2,1,0:T(8,128)(2,1)S(1)} %add_convert_fusion.refs_0_), channel_id=1, source_target_pairs={{0,4},{4,0},{8,12},{12,8},{1,5},{5,1},{9,13},{13,9},{2,6},{6,2},{1... | collective-permute-start | bytes 393224 | tf_op jit(solution)/shard_map/ppermute | solution.py:28
  62.3 1.8 %collective-permute-start.19 = (bf16[2,448,128]{2,1,0:T(8,128)(2,1)S(1)}, bf16[2,448,128]{2,1,0:T(8,128)(2,1)S(1)}, u32[]{:S(2)}, u32[]{:S(2)}) collective-permute-start(bf16[2,448,128]{2,1,0:T(8,128)(2,1)S(1)} %shard_map.168), channel_id=1, source_target_pairs={{0,2},{2,0},{1,3},{3,1},{4,6},{6,4},{5,7},{7,5},{8,10},{10,8},{9,1... | collective-permute-start | bytes 688136 | tf_op jit(solution)/shard_map/ppermute | solution.py:589
  64.1 1.8 %collective-permute-done.17.refs_3_ = bf16[4,128,128]{2,1,0:T(8,128)(2,1)S(1)} collective-permute-done((bf16[4,128,128]{2,1,0:T(8,128)(2,1)S(1)}, bf16[4,128,128]{2,1,0:T(8,128)(2,1)S(1)}, u32[]{:S(2)}, u32[]{:S(2)}) %collective-permute-start.17) | collective-permute-done | bytes 131104 | tf_op jit(solution)/shard_map/ppermute | solution.py:28
  65.9 6.5 %collective-permute-done.16.refs_2_ = bf16[4,128,128]{2,1,0:T(8,128)(2,1)S(1)} collective-permute-done((bf16[4,128,128]{2,1,0:T(8,128)(2,1)S(1)}, bf16[4,128,128]{2,1,0:T(8,128)(2,1)S(1)}, u32[]{:S(2)}, u32[]{:S(2)}) %collective-permute-start.16) | collective-permute-done | bytes 131104 | tf_op jit(solution)/shard_map/ppermute | solution.py:28
  72.5 1.3 %collective-permute-done.18.also = bf16[4,128,128]{2,1,0:T(8,128)(2,1)S(1)} collective-permute-done((bf16[4,128,128]{2,1,0:T(8,128)(2,1)S(1)}, bf16[4,128,128]{2,1,0:T(8,128)(2,1)S(1)}, u32[]{:S(2)}, u32[]{:S(2)}) %collective-permute-start.18) | collective-permute-done | bytes 131104 | tf_op jit(solution)/shard_map/ppermute | solution.py:28
  73.8 1.7 %shard_map.169 = (f32[448,128]{1,0:T(8,128)S(1)}, f32[2,128,128]{2,1,0:T(8,128)S(1)}, bf16[2,128,128]{2,1,0:T(8,128)(2,1)S(1)}) custom-call(bf16[4,128,128]{2,1,0:T(8,128)(2,1)S(1)} %shard_map.167.mine, bf16[4,128,128]{2,1,0:T(8,128)(2,1)S(1)} %collective-permute-done.18.also, bf16[448,128]{1,0:T(8,128)(2,1)S(1)} %collective-permute-done.13.low, ...), custom_call_target="tpu_custom_call" | custom-call | flops 293601280 | bytes 4276736 | tf_op jit(solution)/shard_map/pallas_call | solution.py:252
  75.8 1.1 %collective-permute-done.20 = bf16[2,128,128]{2,1,0:T(8,128)(2,1)S(1)} collective-permute-done((bf16[2,128,128]{2,1,0:T(8,128)(2,1)S(1)}, bf16[2,128,128]{2,1,0:T(8,128)(2,1)S(1)}, u32[]{:S(2)}, u32[]{:S(2)}) %collective-permute-start.20) | collective-permute-done | bytes 65568 | tf_op jit(solution)/shard_map/ppermute | solution.py:28
  76.9 2.3 %collective-permute-start.23 = (bf16[256,128]{1,0:T(8,128)(2,1)S(1)}, bf16[256,128]{1,0:T(8,128)(2,1)S(1)}, u32[]{:S(2)}, u32[]{:S(2)}) collective-permute-start(bf16[256,128]{1,0:T(8,128)(2,1)S(1)} %bitcast.43), channel_id=1, source_target_pairs={{0,12},{4,8},{8,4},{12,0},{1,13},{5,9},{9,5},{13,1},{2,14},{6,10},... | collective-permute-start | bytes 196616 | tf_op jit(solution)/shard_map/ppermute | solution.py:28
  79.3 2.1 %collective-permute-start.21 = (bf16[256,128]{1,0:T(8,128)(2,1)S(1)}, bf16[256,128]{1,0:T(8,128)(2,1)S(1)}, u32[]{:S(2)}, u32[]{:S(2)}) collective-permute-start(bf16[256,128]{1,0:T(8,128)(2,1)S(1)} %bitcast.45), channel_id=1, source_target_pairs={{0,4},{4,0},{8,12},{12,8},{1,5},{5,1},{9,13},{13,9},{2,6},{6,2},{1... | collective-permute-start | bytes 196616 | tf_op jit(solution)/shard_map/ppermute | solution.py:28
  81.4 2.4 %collective-permute-done.23.refs_3_ = bf16[256,128]{1,0:T(8,128)(2,1)S(1)} collective-permute-done((bf16[256,128]{1,0:T(8,128)(2,1)S(1)}, bf16[256,128]{1,0:T(8,128)(2,1)S(1)}, u32[]{:S(2)}, u32[]{:S(2)}) %collective-permute-start.23) | collective-permute-done | bytes 65568 | tf_op jit(solution)/shard_map/ppermute | solution.py:28
  83.7 2.0 %collective-permute-done.22.refs_2_ = bf16[256,128]{1,0:T(8,128)(2,1)S(1)} collective-permute-done((bf16[256,128]{1,0:T(8,128)(2,1)S(1)}, bf16[256,128]{1,0:T(8,128)(2,1)S(1)}, u32[]{:S(2)}, u32[]{:S(2)}) %collective-permute-start.22) | collective-permute-done | bytes 65568 | tf_op jit(solution)/shard_map/ppermute | solution.py:28
  85.9 1.2 %collective-permute-done.24.refs_1_ = bf16[2,128,128]{2,1,0:T(8,128)(2,1)S(1)} collective-permute-done((bf16[2,128,128]{2,1,0:T(8,128)(2,1)S(1)}, bf16[2,128,128]{2,1,0:T(8,128)(2,1)S(1)}, u32[]{:S(2)}, u32[]{:S(2)}) %collective-permute-start.24) | collective-permute-done | bytes 65568 | tf_op jit(solution)/shard_map/ppermute | solution.py:28
  (62 shorter events, 9.8 us)
Async XLA Ops:
  0.6 21.7 %copy-start = (bf16[1,1,1792,256]{3,2,1,0:T(8,128)(2,1)S(1)}, bf16[1,1,1792,256]{3,2,1,0:T(8,128)(2,1)}, u32[]{:S(2)}) copy-start(bf16[1,1,1792,256]{3,2,1,0:T(8,128)(2,1)} %param.20) | copy-start | bytes 2752516
  0.6 21.7 %copy-start.4 = (f32[128,1,448]{0,2,1:T(8,128)S(1)}, f32[128,1,448]{0,2,1:T(8,128)}, u32[]{:S(2)}) copy-start(f32[128,1,448]{0,2,1:T(8,128)} %param.15) | copy-start | bytes 688132
  0.6 34.9 %copy-start.9 = (f32[1,128]{1,0:T(1,128)S(1)}, f32[1,128]{1,0:T(1,128)}, u32[]{:S(2)}) copy-start(f32[1,128]{1,0:T(1,128)} %refs_6_.1) | copy-start | bytes 1540
  3.4 32.1 %copy-start.2 = (bf16[1,4,256,2,1,448]{2,5,4,3,1,0:T(8,128)(2,1)S(1)}, bf16[1,4,256,2,1,448]{2,5,4,3,1,0:T(8,128)(2,1)}, u32[]{:S(2)}) copy-start(bf16[1,4,256,2,1,448]{2,5,4,3,1,0:T(8,128)(2,1)} %param.21) | copy-start | bytes 5505028
  3.4 32.1 %copy-start.3 = (bf16[1,1,1792,128]{3,2,1,0:T(8,128)(2,1)S(1)}, bf16[1,1,1792,128]{3,2,1,0:T(8,128)(2,1)}, u32[]{:S(2)}) copy-start(bf16[1,1,1792,128]{3,2,1,0:T(8,128)(2,1)} %param.22) | copy-start | bytes 1376260
  3.4 12.1 %collective-permute-start = (bf16[672,128]{1,0:T(8,128)(2,1)}, bf16[672,128]{1,0:T(8,128)(2,1)S(1)}, u32[]{:S(2)}, u32[]{:S(2)}) collective-permute-start(bf16[672,128]{1,0:T(8,128)(2,1)} %get-tuple-element.39), channel_id=1, source_target_pairs={{0,4},{4,0},{8,12},{12,8},{1,5},{5,1},{9,13},{13,9},{2,6},{6,2},{1... | collective-permute-start | bytes 516104 | tf_op jit(solution)/shard_map/ppermute | solution.py:28
  6.5 15.8 %collective-permute-start.1 = (bf16[672,128]{1,0:T(8,128)(2,1)}, bf16[672,128]{1,0:T(8,128)(2,1)S(1)}, u32[]{:S(2)}, u32[]{:S(2)}) collective-permute-start(bf16[672,128]{1,0:T(8,128)(2,1)} %get-tuple-element.46), channel_id=1, source_target_pairs={{0,8},{4,12},{8,0},{12,4},{1,9},{5,13},{9,1},{13,5},{2,10},{6,14},... | collective-permute-start | bytes 516104 | tf_op jit(solution)/shard_map/ppermute | solution.py:28
  9.1 13.2 %collective-permute-start.2 = (bf16[672,128]{1,0:T(8,128)(2,1)}, bf16[672,128]{1,0:T(8,128)(2,1)S(1)}, u32[]{:S(2)}, u32[]{:S(2)}) collective-permute-start(bf16[672,128]{1,0:T(8,128)(2,1)} %get-tuple-element.47), channel_id=1, source_target_pairs={{0,12},{4,8},{8,4},{12,0},{1,13},{5,9},{9,5},{13,1},{2,14},{6,10},... | collective-permute-start | bytes 516104 | tf_op jit(solution)/shard_map/ppermute | solution.py:28
  22.7 1.7 %collective-permute-start.3 = (f32[128,256]{1,0:T(8,128)S(1)}, f32[128,256]{1,0:T(8,128)S(1)}, u32[]{:S(2)}, u32[]{:S(2)}) collective-permute-start(f32[128,256]{1,0:T(8,128)S(1)} %get-tuple-element.48.own), channel_id=1, source_target_pairs={{0,1},{1,0},{2,3},{3,2},{4,5},{5,4},{6,7},{7,6},{8,9},{9,8},{10,11... | collective-permute-start | bytes 393224 | tf_op jit(solution)/shard_map/ppermute | solution.py:28
  22.8 7.0 %collective-permute-start.7 = (bf16[672,128]{1,0:T(8,128)(2,1)S(1)}, bf16[672,128]{1,0:T(8,128)(2,1)S(1)}, u32[]{:S(2)}, u32[]{:S(2)}) collective-permute-start(bf16[672,128]{1,0:T(8,128)(2,1)S(1)} %get-tuple-element.53), channel_id=1, source_target_pairs={{0,16},{16,0},{1,17},{17,1},{2,18},{18,2},{3,19},{19,3},{4,20},{20... | collective-permute-start | bytes 516104 | tf_op jit(solution)/shard_map/ppermute | solution.py:28
  24.4 5.4 %collective-permute-start.4 = (bf16[256,128]{1,0:T(8,128)(2,1)S(1)}, bf16[256,128]{1,0:T(8,128)(2,1)S(1)}, u32[]{:S(2)}, u32[]{:S(2)}) collective-permute-start(bf16[256,128]{1,0:T(8,128)(2,1)S(1)} %get-tuple-element.50), channel_id=1, source_target_pairs={{0,4},{4,0},{8,12},{12,8},{1,5},{5,1},{9,13},{13,9},{2,6},{6,2},{1... | collective-permute-start | bytes 196616 | tf_op jit(solution)/shard_map/ppermute | solution.py:28
  27.3 8.3 %collective-permute-start.5 = (bf16[256,128]{1,0:T(8,128)(2,1)S(1)}, bf16[256,128]{1,0:T(8,128)(2,1)S(1)}, u32[]{:S(2)}, u32[]{:S(2)}) collective-permute-start(bf16[256,128]{1,0:T(8,128)(2,1)S(1)} %get-tuple-element.51), channel_id=1, source_target_pairs={{0,8},{4,12},{8,0},{12,4},{1,9},{5,13},{9,1},{13,5},{2,10},{6,14},... | collective-permute-start | bytes 196616 | tf_op jit(solution)/shard_map/ppermute | solution.py:28
  28.4 7.2 %collective-permute-start.6 = (bf16[256,128]{1,0:T(8,128)(2,1)S(1)}, bf16[256,128]{1,0:T(8,128)(2,1)S(1)}, u32[]{:S(2)}, u32[]{:S(2)}) collective-permute-start(bf16[256,128]{1,0:T(8,128)(2,1)S(1)} %get-tuple-element.52), channel_id=1, source_target_pairs={{0,12},{4,8},{8,4},{12,0},{1,13},{5,9},{9,5},{13,1},{2,14},{6,10},... | collective-permute-start | bytes 196616 | tf_op jit(solution)/shard_map/ppermute | solution.py:28
  37.3 12.8 %copy-start.1 = (bf16[1,2,512,1,448]{2,4,3,1,0:T(8,128)(2,1)S(1)}, bf16[1,2,512,1,448]{2,4,3,1,0:T(8,128)(2,1)}, u32[]{:S(2)}) copy-start(bf16[1,2,512,1,448]{2,4,3,1,0:T(8,128)(2,1)} %param.24) | copy-start | bytes 2752516
  37.3 12.8 %copy-start.5 = (f32[1,128,1,448]{1,3,2,0:T(8,128)S(1)}, f32[1,128,1,448]{1,3,2,0:T(8,128)}, u32[]{:S(2)}) copy-start(f32[1,128,1,448]{1,3,2,0:T(8,128)} %param.25) | copy-start | bytes 688132
  37.3 1.3 %collective-permute-start.8 = (bf16[2,128,128]{2,1,0:T(8,128)(2,1)S(1)}, bf16[2,128,128]{2,1,0:T(8,128)(2,1)S(1)}, u32[]{:S(2)}, u32[]{:S(2)}) collective-permute-start(bf16[2,128,128]{2,1,0:T(8,128)(2,1)S(1)} %get-tuple-element.56), channel_id=1, source_target_pairs={{0,1},{1,0},{2,3},{3,2},{4,5},{5,4},{6,7},{7,6},{8,9},{9,8},{10,11... | collective-permute-start | bytes 196616 | tf_op jit(solution)/shard_map/ppermute | solution.py:28
  38.7 4.5 %collective-permute-start.9 = (bf16[272,128]{1,0:T(8,128)(2,1)S(1)}, bf16[272,128]{1,0:T(8,128)(2,1)S(1)}, u32[]{:S(2)}, u32[]{:S(2)}) collective-permute-start(bf16[272,128]{1,0:T(8,128)(2,1)S(1)} %get-tuple-element.59), channel_id=1, source_target_pairs={{0,4},{4,0},{8,12},{12,8},{1,5},{5,1},{9,13},{13,9},{2,6},{6,2},{1... | collective-permute-start | bytes 208904 | tf_op jit(solution)/shard_map/ppermute | solution.py:28
  40.1 8.6 %collective-permute-start.10 = (bf16[272,128]{1,0:T(8,128)(2,1)S(1)}, bf16[272,128]{1,0:T(8,128)(2,1)S(1)}, u32[]{:S(2)}, u32[]{:S(2)}) collective-permute-start(bf16[272,128]{1,0:T(8,128)(2,1)S(1)} %get-tuple-element.60), channel_id=1, source_target_pairs={{0,8},{4,12},{8,0},{12,4},{1,9},{5,13},{9,1},{13,5},{2,10},{6,14},... | collective-permute-start | bytes 208904 | tf_op jit(solution)/shard_map/ppermute | solution.py:28
  41.4 7.3 %collective-permute-start.11 = (bf16[272,128]{1,0:T(8,128)(2,1)S(1)}, bf16[272,128]{1,0:T(8,128)(2,1)S(1)}, u32[]{:S(2)}, u32[]{:S(2)}) collective-permute-start(bf16[272,128]{1,0:T(8,128)(2,1)S(1)} %get-tuple-element.61), channel_id=1, source_target_pairs={{0,12},{4,8},{8,4},{12,0},{1,13},{5,9},{9,5},{13,1},{2,14},{6,10},... | collective-permute-start | bytes 208904 | tf_op jit(solution)/shard_map/ppermute | solution.py:28
  48.8 1.3 %collective-permute-start.12 = (bf16[2,128,128]{2,1,0:T(8,128)(2,1)S(1)}, bf16[2,128,128]{2,1,0:T(8,128)(2,1)S(1)}, u32[]{:S(2)}, u32[]{:S(2)}) collective-permute-start(bf16[2,128,128]{2,1,0:T(8,128)(2,1)S(1)} %shard_map.164.refs_0_.mine), channel_id=1, source_target_pairs={{0,1},{1,0},{2,3},{3,2},{4,5},{5,4},{6,7},{7,6},{8,9},{9,8},{10,11... | collective-permute-start | bytes 196616 | tf_op jit(solution)/shard_map/ppermute | solution.py:28
  50.4 5.3 %collective-permute-start.13 = (bf16[448,128]{1,0:T(8,128)(2,1)S(1)}, bf16[448,128]{1,0:T(8,128)(2,1)S(1)}, u32[]{:S(2)}, u32[]{:S(2)}) collective-permute-start(bf16[448,128]{1,0:T(8,128)(2,1)S(1)} %get-tuple-element.64), channel_id=1, source_target_pairs={{0,2},{2,0},{1,3},{3,1},{4,6},{6,4},{5,7},{7,5},{8,10},{10,8},{9,1... | collective-permute-start | bytes 344072 | tf_op jit(solution)/shard_map/ppermute | solution.py:589
  56.1 1.4 %collective-permute-start.14 = (bf16[4,128,128]{2,1,0:T(8,128)(2,1)S(1)}, bf16[4,128,128]{2,1,0:T(8,128)(2,1)S(1)}, u32[]{:S(2)}, u32[]{:S(2)}) collective-permute-start(bf16[4,128,128]{2,1,0:T(8,128)(2,1)S(1)} %get-tuple-element.66), channel_id=1, source_target_pairs={{0,1},{1,0},{2,3},{3,2},{4,5},{5,4},{6,7},{7,6},{8,9},{9,8},{10,11... | collective-permute-start | bytes 393224 | tf_op jit(solution)/shard_map/ppermute | solution.py:28
  57.5 8.3 %collective-permute-start.17 = (bf16[4,128,128]{2,1,0:T(8,128)(2,1)S(1)}, bf16[4,128,128]{2,1,0:T(8,128)(2,1)S(1)}, u32[]{:S(2)}, u32[]{:S(2)}) collective-permute-start(bf16[4,128,128]{2,1,0:T(8,128)(2,1)S(1)} %add_convert_fusion.refs_0_), channel_id=1, source_target_pairs={{0,12},{4,8},{8,4},{12,0},{1,13},{5,9},{9,5},{13,1},{2,14},{6,10},... | collective-permute-start | bytes 393224 | tf_op jit(solution)/shard_map/ppermute | solution.py:28
  59.7 12.6 %collective-permute-start.16 = (bf16[4,128,128]{2,1,0:T(8,128)(2,1)S(1)}, bf16[4,128,128]{2,1,0:T(8,128)(2,1)S(1)}, u32[]{:S(2)}, u32[]{:S(2)}) collective-permute-start(bf16[4,128,128]{2,1,0:T(8,128)(2,1)S(1)} %add_convert_fusion.refs_0_), channel_id=1, source_target_pairs={{0,8},{4,12},{8,0},{12,4},{1,9},{5,13},{9,1},{13,5},{2,10},{6,14},... | collective-permute-start | bytes 393224 | tf_op jit(solution)/shard_map/ppermute | solution.py:28
  60.4 12.0 %collective-permute-start.15 = (bf16[4,128,128]{2,1,0:T(8,128)(2,1)S(1)}, bf16[4,128,128]{2,1,0:T(8,128)(2,1)S(1)}, u32[]{:S(2)}, u32[]{:S(2)}) collective-permute-start(bf16[4,128,128]{2,1,0:T(8,128)(2,1)S(1)} %add_convert_fusion.refs_0_), channel_id=1, source_target_pairs={{0,4},{4,0},{8,12},{12,8},{1,5},{5,1},{9,13},{13,9},{2,6},{6,2},{1... | collective-permute-start | bytes 393224 | tf_op jit(solution)/shard_map/ppermute | solution.py:28
  62.3 10.2 %collective-permute-start.19 = (bf16[2,448,128]{2,1,0:T(8,128)(2,1)S(1)}, bf16[2,448,128]{2,1,0:T(8,128)(2,1)S(1)}, u32[]{:S(2)}, u32[]{:S(2)}) collective-permute-start(bf16[2,448,128]{2,1,0:T(8,128)(2,1)S(1)} %shard_map.168), channel_id=1, source_target_pairs={{0,2},{2,0},{1,3},{3,1},{4,6},{6,4},{5,7},{7,5},{8,10},{10,8},{9,1... | collective-permute-start | bytes 688136 | tf_op jit(solution)/shard_map/ppermute | solution.py:589
  72.4 1.4 %collective-permute-start.18 = (bf16[4,128,128]{2,1,0:T(8,128)(2,1)S(1)}, bf16[4,128,128]{2,1,0:T(8,128)(2,1)S(1)}, u32[]{:S(2)}, u32[]{:S(2)}) collective-permute-start(bf16[4,128,128]{2,1,0:T(8,128)(2,1)S(1)} %shard_map.167.mine), channel_id=1, source_target_pairs={{0,1},{1,0},{2,3},{3,2},{4,5},{5,4},{6,7},{7,6},{8,9},{9,8},{10,11... | collective-permute-start | bytes 393224 | tf_op jit(solution)/shard_map/ppermute | solution.py:28
  75.6 1.3 %collective-permute-start.20 = (bf16[2,128,128]{2,1,0:T(8,128)(2,1)S(1)}, bf16[2,128,128]{2,1,0:T(8,128)(2,1)S(1)}, u32[]{:S(2)}, u32[]{:S(2)}) collective-permute-start(bf16[2,128,128]{2,1,0:T(8,128)(2,1)S(1)} %get-tuple-element.70), channel_id=1, source_target_pairs={{0,1},{1,0},{2,3},{3,2},{4,5},{5,4},{6,7},{7,6},{8,9},{9,8},{10,11... | collective-permute-start | bytes 196616 | tf_op jit(solution)/shard_map/ppermute | solution.py:28
  76.9 6.8 %collective-permute-start.23 = (bf16[256,128]{1,0:T(8,128)(2,1)S(1)}, bf16[256,128]{1,0:T(8,128)(2,1)S(1)}, u32[]{:S(2)}, u32[]{:S(2)}) collective-permute-start(bf16[256,128]{1,0:T(8,128)(2,1)S(1)} %bitcast.43), channel_id=1, source_target_pairs={{0,12},{4,8},{8,4},{12,0},{1,13},{5,9},{9,5},{13,1},{2,14},{6,10},... | collective-permute-start | bytes 196616 | tf_op jit(solution)/shard_map/ppermute | solution.py:28
  79.3 6.5 %collective-permute-start.22 = (bf16[256,128]{1,0:T(8,128)(2,1)S(1)}, bf16[256,128]{1,0:T(8,128)(2,1)S(1)}, u32[]{:S(2)}, u32[]{:S(2)}) collective-permute-start(bf16[256,128]{1,0:T(8,128)(2,1)S(1)} %bitcast.44), channel_id=1, source_target_pairs={{0,8},{4,12},{8,0},{12,4},{1,9},{5,13},{9,1},{13,5},{2,10},{6,14},... | collective-permute-start | bytes 196616 | tf_op jit(solution)/shard_map/ppermute | solution.py:28
  79.3 6.5 %collective-permute-start.21 = (bf16[256,128]{1,0:T(8,128)(2,1)S(1)}, bf16[256,128]{1,0:T(8,128)(2,1)S(1)}, u32[]{:S(2)}, u32[]{:S(2)}) collective-permute-start(bf16[256,128]{1,0:T(8,128)(2,1)S(1)} %bitcast.45), channel_id=1, source_target_pairs={{0,4},{4,0},{8,12},{12,8},{1,5},{5,1},{9,13},{13,9},{2,6},{6,2},{1... | collective-permute-start | bytes 196616 | tf_op jit(solution)/shard_map/ppermute | solution.py:28
  85.8 1.3 %collective-permute-start.24 = (bf16[2,128,128]{2,1,0:T(8,128)(2,1)S(1)}, bf16[2,128,128]{2,1,0:T(8,128)(2,1)S(1)}, u32[]{:S(2)}, u32[]{:S(2)}) collective-permute-start(bf16[2,128,128]{2,1,0:T(8,128)(2,1)S(1)} %shard_map.170.refs_0_), channel_id=1, source_target_pairs={{0,1},{1,0},{2,3},{3,2},{4,5},{5,4},{6,7},{7,6},{8,9},{9,8},{10,11... | collective-permute-start | bytes 196616 | tf_op jit(solution)/shard_map/ppermute | solution.py:28
  (7 other events, 5.0 us)

commit v5 on v4

--- a/solution.py
+++ b/solution.py
@@ -18,7 +18,7 @@
 
 def partner(index, step, count):
     if count & (count - 1) == 0:
-        return index ^ step
+        return index ^ (count - step)
     return (step - index) % count
 
 
@@ -37,6 +37,10 @@
 
 def spread(value, axis="feat"):
     return [value] + [swap(value, axis, step) for step in peers(axis)]
+
+
+def spread_any(value):
+    return [value] + [swap(value, "feat", step) for step in reversed(peers("feat"))]
 
 
 def exchange(sends):
@@ -304,7 +308,7 @@
 
 def start_body(ranges, state, weight, enc, *refs):
     place = place_of()
-    sends, sems = (None, *refs[:-1]), refs[-1]
+    sends, sems = (None, *refs[-2::-1]), refs[-1]
     width, rows = state.shape
     part = width // 2
     low = state[...].astype(BF16)
@@ -385,12 +389,14 @@
         ((own[:, n * half : (n + 1) * half] + got[:, n * half : (n + 1) * half]) * scales[...]).astype(BF16)
         for n in range(2)
     ]
+    sends = (sends[0], *sends[:0:-1])
     carry(place, ranges, weight, width, 0, 2 * rows, made, sends)
 
 
 def sums_body(ranges, width, done, own, got, weight, info, *sends):
     place = place_of()
     made = [(own[n] + got[n].astype(F32)).astype(BF16) for n in range(own.shape[0])]
+    sends = (sends[0], *sends[:0:-1])
     carry(place, ranges, weight, width, done, width - done, made, sends)
     for send in sends:
         send[send.shape[0] - INFO :] = info[...]
@@ -600,7 +606,7 @@
                 scratch=[pltpu.SemaphoreType.DMA((2, ranges - 1))],
                 room=60 * 1024 * 1024,
             )
-            blocks = exchange([source, *sends])
+            blocks = exchange([source, *sends[::-1]])
             info, mixing, scales, live = kernel_call(
                 facts_body,
                 [
@@ -635,7 +641,7 @@
                 [],
                 [own, got, scales, value_rows],
             )
-            got = exchange(sends)
+            got = exchange([sends[0], *sends[:0:-1]])
             carried = [*blocks[1:], *got[1:]]
             code = functools.partial(first_code_body, ranges, per_group)
             given = [*got, *packed, source, mixing]
@@ -648,7 +654,7 @@
                 flops=2 * rows * value_rows.size,
             )
             part = (own + swap(other, "tok", 1).astype(F32)).astype(BF16)
-            blocks = spread(part)
+            blocks = spread_any(part)
             rest = handed_on(after(rest, low))
             mine = kernel_call(scaled_body, shape(ranges, rows, half, dtype=BF16), [], [scales, *blocks])
             code = functools.partial(later_code_body, ranges, per_group)
@@ -673,10 +679,10 @@
                 [],
                 [own, got, value_rows, info],
             )
-            blocks = facts = exchange(sends)
+            blocks = facts = exchange([sends[0], *sends[:0:-1]])
             carried += blocks[1:]
         else:
-            blocks = spread((own + got.astype(F32)).astype(BF16).reshape(-1, block_len))
+            blocks = spread_any((own + got.astype(F32)).astype(BF16).reshape(-1, block_len))
         mine = kernel_call(
             clamp_body,
             shape(share, rows, block_len, dtype=BF16),

time: 88.5 us -> 85.7 us (0.968)
  waiting for transfers between devices: 41.7 us -> 39.8 us
    ppermute x23, waiting for transfers between devices: 38.3 us -> 36.3 us  [swap(): lax.ppermute(value, axis, [(s, partner(s, step, count)) for s in range(co...]
  transfers between devices with their start and end apart: 25 -> 25, of which waited for: 14 -> 17; matrix products, arithmetic and copies ran while one was open for 0% -> 0% of each run, Pallas kernels for 1% -> 1%
where the time goes in v5:
time: 85.7 us; the launch traced here: 85.3 us
  waiting for transfers between devices  39.8 us (46%)
  starting transfers between devices  29.4 us (34%)
  Pallas kernels  9.55 us (11%)
  local copies, waits for them, and re-layouts  5.04 us (6%)
  between operations  1.5 us (2%)
    ppermute x23, waiting for transfers between devices, swap(): lax.ppermute(value, axis, [(s, partner(s, step, count)) for s in range(co...  36.3 us
    ppermute x23, starting transfers between devices, swap(): lax.ppermute(value, axis, [(s, partner(s, step, count)) for s in range(co...  25.8 us
    pallas_call x14, Pallas kernels, kernel_call(): pl.pallas_call(body, out_shape=tuple(kept) if many else outs, in_specs=[p...  9.55 us
    unnamed x28, local copies, waits for them, and re-layouts  5.04 us
    ppermute x2, starting transfers between devices, handed_on(): lax.ppermute(value, 'layer', [(n, (n + 1) % layers) for n in range(layers)])  3.61 us
    ppermute x2, waiting for transfers between devices, handed_on(): lax.ppermute(value, 'layer', [(n, (n + 1) % layers) for n in range(layers)])  3.48 us
  transfers between devices with their start and end apart: 25, of which 17 were waited for; matrix products, arithmetic and copies ran while one was open for 0% of the time, Pallas kernels for 1%

profile of v5, /device:TPU:0, one launch (start us, length us, event | category | flops | bytes accessed | tf_op | source)
XLA Modules:
  0.0 85.3 jit_solution(13966343182369274305)
XLA Ops:
  0.7 2.8 %shard_map.158 = (bf16[672,128]{1,0:T(8,128)(2,1)}, bf16[672,128]{1,0:T(8,128)(2,1)}, bf16[672,128]{1,0:T(8,128)(2,1)}) custom-call(f32[448,128]{1,0:T(8,128)} %bitcast.37, bf16[1792,256]{1,0:T(8,128)(2,1)} %bitcast.24, bf16[1792,128]{1,0:T(8,128)(2,1)} %bitcast.34), custom_call_target="tpu_custom_call" | custom-call | bytes 745472 | tf_op jit(solution)/shard_map/pallas_call | solution.py:256
  3.4 5.1 %collective-permute-start = (bf16[672,128]{1,0:T(8,128)(2,1)}, bf16[672,128]{1,0:T(8,128)(2,1)S(1)}, u32[]{:S(2)}, u32[]{:S(2)}) collective-permute-start(bf16[672,128]{1,0:T(8,128)(2,1)} %get-tuple-element.39), channel_id=1, source_target_pairs={{0,12},{4,8},{8,4},{12,0},{1,13},{5,9},{9,5},{13,1},{2,14},{6,10},... | collective-permute-start | bytes 516104 | tf_op jit(solution)/shard_map/ppermute | solution.py:28
  15.6 7.8 %collective-permute-done.1.refs_2_.refs_5_.refs_1_ = bf16[672,128]{1,0:T(8,128)(2,1)S(1)} collective-permute-done((bf16[672,128]{1,0:T(8,128)(2,1)}, bf16[672,128]{1,0:T(8,128)(2,1)S(1)}, u32[]{:S(2)}, u32[]{:S(2)}) %collective-permute-start.1) | collective-permute-done | bytes 172064 | tf_op jit(solution)/shard_map/ppermute | solution.py:28
  23.8 1.6 %collective-permute-start.7 = (bf16[672,128]{1,0:T(8,128)(2,1)S(1)}, bf16[672,128]{1,0:T(8,128)(2,1)S(1)}, u32[]{:S(2)}, u32[]{:S(2)}) collective-permute-start(bf16[672,128]{1,0:T(8,128)(2,1)S(1)} %get-tuple-element.53), channel_id=1, source_target_pairs={{0,16},{16,0},{1,17},{17,1},{2,18},{18,2},{3,19},{19,3},{4,20},{20... | collective-permute-start | bytes 516104 | tf_op jit(solution)/shard_map/ppermute | solution.py:28
  25.4 2.5 %collective-permute-start.4 = (bf16[256,128]{1,0:T(8,128)(2,1)S(1)}, bf16[256,128]{1,0:T(8,128)(2,1)S(1)}, u32[]{:S(2)}, u32[]{:S(2)}) collective-permute-start(bf16[256,128]{1,0:T(8,128)(2,1)S(1)} %get-tuple-element.50), channel_id=1, source_target_pairs={{0,12},{4,8},{8,4},{12,0},{1,13},{5,9},{9,5},{13,1},{2,14},{6,10},... | collective-permute-start | bytes 196616 | tf_op jit(solution)/shard_map/ppermute | solution.py:28
  28.0 1.9 %collective-permute-start.6 = (bf16[256,128]{1,0:T(8,128)(2,1)S(1)}, bf16[256,128]{1,0:T(8,128)(2,1)S(1)}, u32[]{:S(2)}, u32[]{:S(2)}) collective-permute-start(bf16[256,128]{1,0:T(8,128)(2,1)S(1)} %get-tuple-element.52), channel_id=1, source_target_pairs={{0,4},{4,0},{8,12},{12,8},{1,5},{5,1},{9,13},{13,9},{2,6},{6,2},{1... | collective-permute-start | bytes 196616 | tf_op jit(solution)/shard_map/ppermute | solution.py:28
  30.6 1.7 %collective-permute-done.4.refs_1_.refs_3_ = bf16[256,128]{1,0:T(8,128)(2,1)S(1)} collective-permute-done((bf16[256,128]{1,0:T(8,128)(2,1)S(1)}, bf16[256,128]{1,0:T(8,128)(2,1)S(1)}, u32[]{:S(2)}, u32[]{:S(2)}) %collective-permute-start.4) | collective-permute-done | bytes 65568 | tf_op jit(solution)/shard_map/ppermute | solution.py:28
  32.3 2.0 %collective-permute-done.5.refs_2_.refs_4_ = bf16[256,128]{1,0:T(8,128)(2,1)S(1)} collective-permute-done((bf16[256,128]{1,0:T(8,128)(2,1)S(1)}, bf16[256,128]{1,0:T(8,128)(2,1)S(1)}, u32[]{:S(2)}, u32[]{:S(2)}) %collective-permute-start.5) | collective-permute-done | bytes 65568 | tf_op jit(solution)/shard_map/ppermute | solution.py:28
  34.3 1.7 %shard_map.162 = (f32[448,128]{1,0:T(8,128)S(1)}, f32[2,128,128]{2,1,0:T(8,128)S(1)}, bf16[2,128,128]{2,1,0:T(8,128)(2,1)S(1)}) custom-call(bf16[256,128]{1,0:T(8,128)(2,1)S(1)} %get-tuple-element.49.refs_0_, bf16[256,128]{1,0:T(8,128)(2,1)S(1)} %collective-permute-done.4.refs_1_.refs_3_, bf16[256,128]{1,0:T(8,128)(2,1)S(1)} %collective-permute-done.5.refs_2_.refs_4_, ...), custom_call_target="tpu_custom_call" | custom-call | flops 293601280 | bytes 4162048 | tf_op jit(solution)/shard_map/pallas_call | solution.py:256
  36.1 1.2 %collective-permute-done.8.got = bf16[2,128,128]{2,1,0:T(8,128)(2,1)S(1)} collective-permute-done((bf16[2,128,128]{2,1,0:T(8,128)(2,1)S(1)}, bf16[2,128,128]{2,1,0:T(8,128)(2,1)S(1)}, u32[]{:S(2)}, u32[]{:S(2)}) %collective-permute-start.8) | collective-permute-done | bytes 65568 | tf_op jit(solution)/shard_map/ppermute | solution.py:28
  37.4 2.5 %collective-permute-start.9 = (bf16[272,128]{1,0:T(8,128)(2,1)S(1)}, bf16[272,128]{1,0:T(8,128)(2,1)S(1)}, u32[]{:S(2)}, u32[]{:S(2)}) collective-permute-start(bf16[272,128]{1,0:T(8,128)(2,1)S(1)} %get-tuple-element.59), channel_id=1, source_target_pairs={{0,12},{4,8},{8,4},{12,0},{1,13},{5,9},{9,5},{13,1},{2,14},{6,10},... | collective-permute-start | bytes 208904 | tf_op jit(solution)/shard_map/ppermute | solution.py:28
  39.9 1.9 %collective-permute-start.11 = (bf16[272,128]{1,0:T(8,128)(2,1)S(1)}, bf16[272,128]{1,0:T(8,128)(2,1)S(1)}, u32[]{:S(2)}, u32[]{:S(2)}) collective-permute-start(bf16[272,128]{1,0:T(8,128)(2,1)S(1)} %get-tuple-element.61), channel_id=1, source_target_pairs={{0,4},{4,0},{8,12},{12,8},{1,5},{5,1},{9,13},{13,9},{2,6},{6,2},{1... | collective-permute-start | bytes 208904 | tf_op jit(solution)/shard_map/ppermute | solution.py:28
  41.9 2.5 %collective-permute-done.9.refs_1_.refs_5_.refs_6_ = bf16[272,128]{1,0:T(8,128)(2,1)S(1)} collective-permute-done((bf16[272,128]{1,0:T(8,128)(2,1)S(1)}, bf16[272,128]{1,0:T(8,128)(2,1)S(1)}, u32[]{:S(2)}, u32[]{:S(2)}) %collective-permute-start.9) | collective-permute-done | bytes 69664 | tf_op jit(solution)/shard_map/ppermute | solution.py:28
  44.4 2.1 %collective-permute-done.10.refs_2_.refs_6_.refs_7_ = bf16[272,128]{1,0:T(8,128)(2,1)S(1)} collective-permute-done((bf16[272,128]{1,0:T(8,128)(2,1)S(1)}, bf16[272,128]{1,0:T(8,128)(2,1)S(1)}, u32[]{:S(2)}, u32[]{:S(2)}) %collective-permute-start.10) | collective-permute-done | bytes 69664 | tf_op jit(solution)/shard_map/ppermute | solution.py:28
  46.6 1.2 %collective-permute-done.12.refs_1_.also = bf16[2,128,128]{2,1,0:T(8,128)(2,1)S(1)} collective-permute-done((bf16[2,128,128]{2,1,0:T(8,128)(2,1)S(1)}, bf16[2,128,128]{2,1,0:T(8,128)(2,1)S(1)}, u32[]{:S(2)}, u32[]{:S(2)}) %collective-permute-start.12) | collective-permute-done | bytes 65568 | tf_op jit(solution)/shard_map/ppermute | solution.py:28
  48.2 1.8 %collective-permute-start.13 = (bf16[448,128]{1,0:T(8,128)(2,1)S(1)}, bf16[448,128]{1,0:T(8,128)(2,1)S(1)}, u32[]{:S(2)}, u32[]{:S(2)}) collective-permute-start(bf16[448,128]{1,0:T(8,128)(2,1)S(1)} %get-tuple-element.64), channel_id=1, source_target_pairs={{0,2},{2,0},{1,3},{3,1},{4,6},{6,4},{5,7},{7,5},{8,10},{10,8},{9,1... | collective-permute-start | bytes 344072 | tf_op jit(solution)/shard_map/ppermute | solution.py:595
  50.0 3.5 %collective-permute-done.13.low = bf16[448,128]{1,0:T(8,128)(2,1)S(1)} collective-permute-done((bf16[448,128]{1,0:T(8,128)(2,1)S(1)}, bf16[448,128]{1,0:T(8,128)(2,1)S(1)}, u32[]{:S(2)}, u32[]{:S(2)}) %collective-permute-start.13) | collective-permute-done | bytes 114720 | tf_op jit(solution)/shard_map/ppermute | solution.py:595
  54.0 1.3 %collective-permute-done.14 = bf16[4,128,128]{2,1,0:T(8,128)(2,1)S(1)} collective-permute-done((bf16[4,128,128]{2,1,0:T(8,128)(2,1)S(1)}, bf16[4,128,128]{2,1,0:T(8,128)(2,1)S(1)}, u32[]{:S(2)}, u32[]{:S(2)}) %collective-permute-start.14) | collective-permute-done | bytes 131104 | tf_op jit(solution)/shard_map/ppermute | solution.py:28
  55.3 2.6 %collective-permute-start.17 = (bf16[4,128,128]{2,1,0:T(8,128)(2,1)S(1)}, bf16[4,128,128]{2,1,0:T(8,128)(2,1)S(1)}, u32[]{:S(2)}, u32[]{:S(2)}) collective-permute-start(bf16[4,128,128]{2,1,0:T(8,128)(2,1)S(1)} %add_convert_fusion.refs_0_), channel_id=1, source_target_pairs={{0,12},{4,8},{8,4},{12,0},{1,13},{5,9},{9,5},{13,1},{2,14},{6,10},... | collective-permute-start | bytes 393224 | tf_op jit(solution)/shard_map/ppermute | solution.py:28
  57.9 1.9 %collective-permute-start.15 = (bf16[4,128,128]{2,1,0:T(8,128)(2,1)S(1)}, bf16[4,128,128]{2,1,0:T(8,128)(2,1)S(1)}, u32[]{:S(2)}, u32[]{:S(2)}) collective-permute-start(bf16[4,128,128]{2,1,0:T(8,128)(2,1)S(1)} %add_convert_fusion.refs_0_), channel_id=1, source_target_pairs={{0,4},{4,0},{8,12},{12,8},{1,5},{5,1},{9,13},{13,9},{2,6},{6,2},{1... | collective-permute-start | bytes 393224 | tf_op jit(solution)/shard_map/ppermute | solution.py:28
  60.1 1.8 %collective-permute-start.19 = (bf16[2,448,128]{2,1,0:T(8,128)(2,1)S(1)}, bf16[2,448,128]{2,1,0:T(8,128)(2,1)S(1)}, u32[]{:S(2)}, u32[]{:S(2)}) collective-permute-start(bf16[2,448,128]{2,1,0:T(8,128)(2,1)S(1)} %shard_map.168), channel_id=1, source_target_pairs={{0,2},{2,0},{1,3},{3,1},{4,6},{6,4},{5,7},{7,5},{8,10},{10,8},{9,1... | collective-permute-start | bytes 688136 | tf_op jit(solution)/shard_map/ppermute | solution.py:595
  61.9 1.8 %collective-permute-done.17.refs_3_ = bf16[4,128,128]{2,1,0:T(8,128)(2,1)S(1)} collective-permute-done((bf16[4,128,128]{2,1,0:T(8,128)(2,1)S(1)}, bf16[4,128,128]{2,1,0:T(8,128)(2,1)S(1)}, u32[]{:S(2)}, u32[]{:S(2)}) %collective-permute-start.17) | collective-permute-done | bytes 131104 | tf_op jit(solution)/shard_map/ppermute | solution.py:28
  63.7 5.9 %collective-permute-done.16.refs_2_ = bf16[4,128,128]{2,1,0:T(8,128)(2,1)S(1)} collective-permute-done((bf16[4,128,128]{2,1,0:T(8,128)(2,1)S(1)}, bf16[4,128,128]{2,1,0:T(8,128)(2,1)S(1)}, u32[]{:S(2)}, u32[]{:S(2)}) %collective-permute-start.16) | collective-permute-done | bytes 131104 | tf_op jit(solution)/shard_map/ppermute | solution.py:28
  69.7 1.3 %collective-permute-done.18.also = bf16[4,128,128]{2,1,0:T(8,128)(2,1)S(1)} collective-permute-done((bf16[4,128,128]{2,1,0:T(8,128)(2,1)S(1)}, bf16[4,128,128]{2,1,0:T(8,128)(2,1)S(1)}, u32[]{:S(2)}, u32[]{:S(2)}) %collective-permute-start.18) | collective-permute-done | bytes 131104 | tf_op jit(solution)/shard_map/ppermute | solution.py:28
  71.1 1.7 %shard_map.169 = (f32[448,128]{1,0:T(8,128)S(1)}, f32[2,128,128]{2,1,0:T(8,128)S(1)}, bf16[2,128,128]{2,1,0:T(8,128)(2,1)S(1)}) custom-call(bf16[4,128,128]{2,1,0:T(8,128)(2,1)S(1)} %shard_map.167.mine, bf16[4,128,128]{2,1,0:T(8,128)(2,1)S(1)} %collective-permute-done.18.also, bf16[448,128]{1,0:T(8,128)(2,1)S(1)} %collective-permute-done.13.low, ...), custom_call_target="tpu_custom_call" | custom-call | flops 293601280 | bytes 4276736 | tf_op jit(solution)/shard_map/pallas_call | solution.py:256
  73.0 1.1 %collective-permute-done.20 = bf16[2,128,128]{2,1,0:T(8,128)(2,1)S(1)} collective-permute-done((bf16[2,128,128]{2,1,0:T(8,128)(2,1)S(1)}, bf16[2,128,128]{2,1,0:T(8,128)(2,1)S(1)}, u32[]{:S(2)}, u32[]{:S(2)}) %collective-permute-start.20) | collective-permute-done | bytes 65568 | tf_op jit(solution)/shard_map/ppermute | solution.py:28
  74.1 1.7 %collective-permute-start.23 = (bf16[256,128]{1,0:T(8,128)(2,1)S(1)}, bf16[256,128]{1,0:T(8,128)(2,1)S(1)}, u32[]{:S(2)}, u32[]{:S(2)}) collective-permute-start(bf16[256,128]{1,0:T(8,128)(2,1)S(1)} %bitcast.43), channel_id=1, source_target_pairs={{0,12},{4,8},{8,4},{12,0},{1,13},{5,9},{9,5},{13,1},{2,14},{6,10},... | collective-permute-start | bytes 196616 | tf_op jit(solution)/shard_map/ppermute | solution.py:28
  75.8 2.8 %collective-permute-start.21 = (bf16[256,128]{1,0:T(8,128)(2,1)S(1)}, bf16[256,128]{1,0:T(8,128)(2,1)S(1)}, u32[]{:S(2)}, u32[]{:S(2)}) collective-permute-start(bf16[256,128]{1,0:T(8,128)(2,1)S(1)} %bitcast.45), channel_id=1, source_target_pairs={{0,4},{4,0},{8,12},{12,8},{1,5},{5,1},{9,13},{13,9},{2,6},{6,2},{1... | collective-permute-start | bytes 196616 | tf_op jit(solution)/shard_map/ppermute | solution.py:28
  78.6 2.4 %collective-permute-done.23.refs_3_ = bf16[256,128]{1,0:T(8,128)(2,1)S(1)} collective-permute-done((bf16[256,128]{1,0:T(8,128)(2,1)S(1)}, bf16[256,128]{1,0:T(8,128)(2,1)S(1)}, u32[]{:S(2)}, u32[]{:S(2)}) %collective-permute-start.23) | collective-permute-done | bytes 65568 | tf_op jit(solution)/shard_map/ppermute | solution.py:28
  81.0 2.0 %collective-permute-done.22.refs_2_ = bf16[256,128]{1,0:T(8,128)(2,1)S(1)} collective-permute-done((bf16[256,128]{1,0:T(8,128)(2,1)S(1)}, bf16[256,128]{1,0:T(8,128)(2,1)S(1)}, u32[]{:S(2)}, u32[]{:S(2)}) %collective-permute-start.22) | collective-permute-done | bytes 65568 | tf_op jit(solution)/shard_map/ppermute | solution.py:28
  83.1 1.2 %collective-permute-done.24.refs_1_ = bf16[2,128,128]{2,1,0:T(8,128)(2,1)S(1)} collective-permute-done((bf16[2,128,128]{2,1,0:T(8,128)(2,1)S(1)}, bf16[2,128,128]{2,1,0:T(8,128)(2,1)S(1)}, u32[]{:S(2)}, u32[]{:S(2)}) %collective-permute-start.24) | collective-permute-done | bytes 65568 | tf_op jit(solution)/shard_map/ppermute | solution.py:28
  84.4 1.0 %shard_map.171 = (f32[448,128]{1,0:T(8,128)}, bf16[128,128]{1,0:T(8,128)(2,1)}) custom-call(bf16[2,128,128]{2,1,0:T(8,128)(2,1)S(1)} %shard_map.170.refs_0_, bf16[2,128,128]{2,1,0:T(8,128)(2,1)S(1)} %collective-permute-done.24.refs_1_, bf16[2,448,512]{2,1,0:T(8,128)(2,1)S(1)} %bitcast.31, f32[448,128]{1,0:T(8,128)S(1)} %get-tuple-element.71.refs_3_, ...), custom_call_target="tpu_custom_call" | custom-call | flops 58720256 | bytes 2260992 | tf_op jit(solution)/shard_map/pallas_call | solution.py:256
  (62 shorter events, 9.5 us)
Async XLA Ops:
  0.6 22.7 %copy-start = (bf16[1,1,1792,256]{3,2,1,0:T(8,128)(2,1)S(1)}, bf16[1,1,1792,256]{3,2,1,0:T(8,128)(2,1)}, u32[]{:S(2)}) copy-start(bf16[1,1,1792,256]{3,2,1,0:T(8,128)(2,1)} %param.20) | copy-start | bytes 2752516
  0.6 22.7 %copy-start.4 = (f32[128,1,448]{0,2,1:T(8,128)S(1)}, f32[128,1,448]{0,2,1:T(8,128)}, u32[]{:S(2)}) copy-start(f32[128,1,448]{0,2,1:T(8,128)} %param.15) | copy-start | bytes 688132
  0.6 33.6 %copy-start.9 = (f32[1,128]{1,0:T(1,128)S(1)}, f32[1,128]{1,0:T(1,128)}, u32[]{:S(2)}) copy-start(f32[1,128]{1,0:T(1,128)} %refs_6_.1) | copy-start | bytes 1540
  3.4 30.9 %copy-start.2 = (bf16[1,4,256,2,1,448]{2,5,4,3,1,0:T(8,128)(2,1)S(1)}, bf16[1,4,256,2,1,448]{2,5,4,3,1,0:T(8,128)(2,1)}, u32[]{:S(2)}) copy-start(bf16[1,4,256,2,1,448]{2,5,4,3,1,0:T(8,128)(2,1)} %param.21) | copy-start | bytes 5505028
  3.4 30.8 %copy-start.3 = (bf16[1,1,1792,128]{3,2,1,0:T(8,128)(2,1)S(1)}, bf16[1,1,1792,128]{3,2,1,0:T(8,128)(2,1)}, u32[]{:S(2)}) copy-start(bf16[1,1,1792,128]{3,2,1,0:T(8,128)(2,1)} %param.22) | copy-start | bytes 1376260
  3.4 12.1 %collective-permute-start = (bf16[672,128]{1,0:T(8,128)(2,1)}, bf16[672,128]{1,0:T(8,128)(2,1)S(1)}, u32[]{:S(2)}, u32[]{:S(2)}) collective-permute-start(bf16[672,128]{1,0:T(8,128)(2,1)} %get-tuple-element.39), channel_id=1, source_target_pairs={{0,12},{4,8},{8,4},{12,0},{1,13},{5,9},{9,5},{13,1},{2,14},{6,10},... | collective-permute-start | bytes 516104 | tf_op jit(solution)/shard_map/ppermute | solution.py:28
  8.6 14.8 %collective-permute-start.1 = (bf16[672,128]{1,0:T(8,128)(2,1)}, bf16[672,128]{1,0:T(8,128)(2,1)S(1)}, u32[]{:S(2)}, u32[]{:S(2)}) collective-permute-start(bf16[672,128]{1,0:T(8,128)(2,1)} %get-tuple-element.46), channel_id=1, source_target_pairs={{0,8},{4,12},{8,0},{12,4},{1,9},{5,13},{9,1},{13,5},{2,10},{6,14},... | collective-permute-start | bytes 516104 | tf_op jit(solution)/shard_map/ppermute | solution.py:28
  8.6 14.8 %collective-permute-start.2 = (bf16[672,128]{1,0:T(8,128)(2,1)}, bf16[672,128]{1,0:T(8,128)(2,1)S(1)}, u32[]{:S(2)}, u32[]{:S(2)}) collective-permute-start(bf16[672,128]{1,0:T(8,128)(2,1)} %get-tuple-element.47), channel_id=1, source_target_pairs={{0,4},{4,0},{8,12},{12,8},{1,5},{5,1},{9,13},{13,9},{2,6},{6,2},{1... | collective-permute-start | bytes 516104 | tf_op jit(solution)/shard_map/ppermute | solution.py:28
  23.7 1.7 %collective-permute-start.3 = (f32[128,256]{1,0:T(8,128)S(1)}, f32[128,256]{1,0:T(8,128)S(1)}, u32[]{:S(2)}, u32[]{:S(2)}) collective-permute-start(f32[128,256]{1,0:T(8,128)S(1)} %get-tuple-element.48.own), channel_id=1, source_target_pairs={{0,1},{1,0},{2,3},{3,2},{4,5},{5,4},{6,7},{7,6},{8,9},{9,8},{10,11... | collective-permute-start | bytes 393224 | tf_op jit(solution)/shard_map/ppermute | solution.py:28
  23.8 6.8 %collective-permute-start.7 = (bf16[672,128]{1,0:T(8,128)(2,1)S(1)}, bf16[672,128]{1,0:T(8,128)(2,1)S(1)}, u32[]{:S(2)}, u32[]{:S(2)}) collective-permute-start(bf16[672,128]{1,0:T(8,128)(2,1)S(1)} %get-tuple-element.53), channel_id=1, source_target_pairs={{0,16},{16,0},{1,17},{17,1},{2,18},{18,2},{3,19},{19,3},{4,20},{20... | collective-permute-start | bytes 516104 | tf_op jit(solution)/shard_map/ppermute | solution.py:28
  25.4 6.8 %collective-permute-start.4 = (bf16[256,128]{1,0:T(8,128)(2,1)S(1)}, bf16[256,128]{1,0:T(8,128)(2,1)S(1)}, u32[]{:S(2)}, u32[]{:S(2)}) collective-permute-start(bf16[256,128]{1,0:T(8,128)(2,1)S(1)} %get-tuple-element.50), channel_id=1, source_target_pairs={{0,12},{4,8},{8,4},{12,0},{1,13},{5,9},{9,5},{13,1},{2,14},{6,10},... | collective-permute-start | bytes 196616 | tf_op jit(solution)/shard_map/ppermute | solution.py:28
  28.0 6.3 %collective-permute-start.5 = (bf16[256,128]{1,0:T(8,128)(2,1)S(1)}, bf16[256,128]{1,0:T(8,128)(2,1)S(1)}, u32[]{:S(2)}, u32[]{:S(2)}) collective-permute-start(bf16[256,128]{1,0:T(8,128)(2,1)S(1)} %get-tuple-element.51), channel_id=1, source_target_pairs={{0,8},{4,12},{8,0},{12,4},{1,9},{5,13},{9,1},{13,5},{2,10},{6,14},... | collective-permute-start | bytes 196616 | tf_op jit(solution)/shard_map/ppermute | solution.py:28
  28.0 6.3 %collective-permute-start.6 = (bf16[256,128]{1,0:T(8,128)(2,1)S(1)}, bf16[256,128]{1,0:T(8,128)(2,1)S(1)}, u32[]{:S(2)}, u32[]{:S(2)}) collective-permute-start(bf16[256,128]{1,0:T(8,128)(2,1)S(1)} %get-tuple-element.52), channel_id=1, source_target_pairs={{0,4},{4,0},{8,12},{12,8},{1,5},{5,1},{9,13},{13,9},{2,6},{6,2},{1... | collective-permute-start | bytes 196616 | tf_op jit(solution)/shard_map/ppermute | solution.py:28
  36.0 11.9 %copy-start.1 = (bf16[1,2,512,1,448]{2,4,3,1,0:T(8,128)(2,1)S(1)}, bf16[1,2,512,1,448]{2,4,3,1,0:T(8,128)(2,1)}, u32[]{:S(2)}) copy-start(bf16[1,2,512,1,448]{2,4,3,1,0:T(8,128)(2,1)} %param.24) | copy-start | bytes 2752516
  36.0 11.9 %copy-start.5 = (f32[1,128,1,448]{1,3,2,0:T(8,128)S(1)}, f32[1,128,1,448]{1,3,2,0:T(8,128)}, u32[]{:S(2)}) copy-start(f32[1,128,1,448]{1,3,2,0:T(8,128)} %param.25) | copy-start | bytes 688132
  36.0 1.3 %collective-permute-start.8 = (bf16[2,128,128]{2,1,0:T(8,128)(2,1)S(1)}, bf16[2,128,128]{2,1,0:T(8,128)(2,1)S(1)}, u32[]{:S(2)}, u32[]{:S(2)}) collective-permute-start(bf16[2,128,128]{2,1,0:T(8,128)(2,1)S(1)} %get-tuple-element.56), channel_id=1, source_target_pairs={{0,1},{1,0},{2,3},{3,2},{4,5},{5,4},{6,7},{7,6},{8,9},{9,8},{10,11... | collective-permute-start | bytes 196616 | tf_op jit(solution)/shard_map/ppermute | solution.py:28
  37.4 7.0 %collective-permute-start.9 = (bf16[272,128]{1,0:T(8,128)(2,1)S(1)}, bf16[272,128]{1,0:T(8,128)(2,1)S(1)}, u32[]{:S(2)}, u32[]{:S(2)}) collective-permute-start(bf16[272,128]{1,0:T(8,128)(2,1)S(1)} %get-tuple-element.59), channel_id=1, source_target_pairs={{0,12},{4,8},{8,4},{12,0},{1,13},{5,9},{9,5},{13,1},{2,14},{6,10},... | collective-permute-start | bytes 208904 | tf_op jit(solution)/shard_map/ppermute | solution.py:28
  39.9 6.5 %collective-permute-start.10 = (bf16[272,128]{1,0:T(8,128)(2,1)S(1)}, bf16[272,128]{1,0:T(8,128)(2,1)S(1)}, u32[]{:S(2)}, u32[]{:S(2)}) collective-permute-start(bf16[272,128]{1,0:T(8,128)(2,1)S(1)} %get-tuple-element.60), channel_id=1, source_target_pairs={{0,8},{4,12},{8,0},{12,4},{1,9},{5,13},{9,1},{13,5},{2,10},{6,14},... | collective-permute-start | bytes 208904 | tf_op jit(solution)/shard_map/ppermute | solution.py:28
  39.9 6.5 %collective-permute-start.11 = (bf16[272,128]{1,0:T(8,128)(2,1)S(1)}, bf16[272,128]{1,0:T(8,128)(2,1)S(1)}, u32[]{:S(2)}, u32[]{:S(2)}) collective-permute-start(bf16[272,128]{1,0:T(8,128)(2,1)S(1)} %get-tuple-element.61), channel_id=1, source_target_pairs={{0,4},{4,0},{8,12},{12,8},{1,5},{5,1},{9,13},{13,9},{2,6},{6,2},{1... | collective-permute-start | bytes 208904 | tf_op jit(solution)/shard_map/ppermute | solution.py:28
  46.6 1.3 %collective-permute-start.12 = (bf16[2,128,128]{2,1,0:T(8,128)(2,1)S(1)}, bf16[2,128,128]{2,1,0:T(8,128)(2,1)S(1)}, u32[]{:S(2)}, u32[]{:S(2)}) collective-permute-start(bf16[2,128,128]{2,1,0:T(8,128)(2,1)S(1)} %shard_map.164.refs_0_.mine), channel_id=1, source_target_pairs={{0,1},{1,0},{2,3},{3,2},{4,5},{5,4},{6,7},{7,6},{8,9},{9,8},{10,11... | collective-permute-start | bytes 196616 | tf_op jit(solution)/shard_map/ppermute | solution.py:28
  48.2 5.3 %collective-permute-start.13 = (bf16[448,128]{1,0:T(8,128)(2,1)S(1)}, bf16[448,128]{1,0:T(8,128)(2,1)S(1)}, u32[]{:S(2)}, u32[]{:S(2)}) collective-permute-start(bf16[448,128]{1,0:T(8,128)(2,1)S(1)} %get-tuple-element.64), channel_id=1, source_target_pairs={{0,2},{2,0},{1,3},{3,1},{4,6},{6,4},{5,7},{7,5},{8,10},{10,8},{9,1... | collective-permute-start | bytes 344072 | tf_op jit(solution)/shard_map/ppermute | solution.py:595
  53.9 1.4 %collective-permute-start.14 = (bf16[4,128,128]{2,1,0:T(8,128)(2,1)S(1)}, bf16[4,128,128]{2,1,0:T(8,128)(2,1)S(1)}, u32[]{:S(2)}, u32[]{:S(2)}) collective-permute-start(bf16[4,128,128]{2,1,0:T(8,128)(2,1)S(1)} %get-tuple-element.66), channel_id=1, source_target_pairs={{0,1},{1,0},{2,3},{3,2},{4,5},{5,4},{6,7},{7,6},{8,9},{9,8},{10,11... | collective-permute-start | bytes 393224 | tf_op jit(solution)/shard_map/ppermute | solution.py:28
  55.3 8.3 %collective-permute-start.17 = (bf16[4,128,128]{2,1,0:T(8,128)(2,1)S(1)}, bf16[4,128,128]{2,1,0:T(8,128)(2,1)S(1)}, u32[]{:S(2)}, u32[]{:S(2)}) collective-permute-start(bf16[4,128,128]{2,1,0:T(8,128)(2,1)S(1)} %add_convert_fusion.refs_0_), channel_id=1, source_target_pairs={{0,12},{4,8},{8,4},{12,0},{1,13},{5,9},{9,5},{13,1},{2,14},{6,10},... | collective-permute-start | bytes 393224 | tf_op jit(solution)/shard_map/ppermute | solution.py:28
  57.9 11.6 %collective-permute-start.16 = (bf16[4,128,128]{2,1,0:T(8,128)(2,1)S(1)}, bf16[4,128,128]{2,1,0:T(8,128)(2,1)S(1)}, u32[]{:S(2)}, u32[]{:S(2)}) collective-permute-start(bf16[4,128,128]{2,1,0:T(8,128)(2,1)S(1)} %add_convert_fusion.refs_0_), channel_id=1, source_target_pairs={{0,8},{4,12},{8,0},{12,4},{1,9},{5,13},{9,1},{13,5},{2,10},{6,14},... | collective-permute-start | bytes 393224 | tf_op jit(solution)/shard_map/ppermute | solution.py:28
  57.9 11.6 %collective-permute-start.15 = (bf16[4,128,128]{2,1,0:T(8,128)(2,1)S(1)}, bf16[4,128,128]{2,1,0:T(8,128)(2,1)S(1)}, u32[]{:S(2)}, u32[]{:S(2)}) collective-permute-start(bf16[4,128,128]{2,1,0:T(8,128)(2,1)S(1)} %add_convert_fusion.refs_0_), channel_id=1, source_target_pairs={{0,4},{4,0},{8,12},{12,8},{1,5},{5,1},{9,13},{13,9},{2,6},{6,2},{1... | collective-permute-start | bytes 393224 | tf_op jit(solution)/shard_map/ppermute | solution.py:28
  60.1 9.6 %collective-permute-start.19 = (bf16[2,448,128]{2,1,0:T(8,128)(2,1)S(1)}, bf16[2,448,128]{2,1,0:T(8,128)(2,1)S(1)}, u32[]{:S(2)}, u32[]{:S(2)}) collective-permute-start(bf16[2,448,128]{2,1,0:T(8,128)(2,1)S(1)} %shard_map.168), channel_id=1, source_target_pairs={{0,2},{2,0},{1,3},{3,1},{4,6},{6,4},{5,7},{7,5},{8,10},{10,8},{9,1... | collective-permute-start | bytes 688136 | tf_op jit(solution)/shard_map/ppermute | solution.py:595
  69.6 1.4 %collective-permute-start.18 = (bf16[4,128,128]{2,1,0:T(8,128)(2,1)S(1)}, bf16[4,128,128]{2,1,0:T(8,128)(2,1)S(1)}, u32[]{:S(2)}, u32[]{:S(2)}) collective-permute-start(bf16[4,128,128]{2,1,0:T(8,128)(2,1)S(1)} %shard_map.167.mine), channel_id=1, source_target_pairs={{0,1},{1,0},{2,3},{3,2},{4,5},{5,4},{6,7},{7,6},{8,9},{9,8},{10,11... | collective-permute-start | bytes 393224 | tf_op jit(solution)/shard_map/ppermute | solution.py:28
  72.8 1.3 %collective-permute-start.20 = (bf16[2,128,128]{2,1,0:T(8,128)(2,1)S(1)}, bf16[2,128,128]{2,1,0:T(8,128)(2,1)S(1)}, u32[]{:S(2)}, u32[]{:S(2)}) collective-permute-start(bf16[2,128,128]{2,1,0:T(8,128)(2,1)S(1)} %get-tuple-element.70), channel_id=1, source_target_pairs={{0,1},{1,0},{2,3},{3,2},{4,5},{5,4},{6,7},{7,6},{8,9},{9,8},{10,11... | collective-permute-start | bytes 196616 | tf_op jit(solution)/shard_map/ppermute | solution.py:28
  74.1 6.8 %collective-permute-start.23 = (bf16[256,128]{1,0:T(8,128)(2,1)S(1)}, bf16[256,128]{1,0:T(8,128)(2,1)S(1)}, u32[]{:S(2)}, u32[]{:S(2)}) collective-permute-start(bf16[256,128]{1,0:T(8,128)(2,1)S(1)} %bitcast.43), channel_id=1, source_target_pairs={{0,12},{4,8},{8,4},{12,0},{1,13},{5,9},{9,5},{13,1},{2,14},{6,10},... | collective-permute-start | bytes 196616 | tf_op jit(solution)/shard_map/ppermute | solution.py:28
  75.8 7.1 %collective-permute-start.22 = (bf16[256,128]{1,0:T(8,128)(2,1)S(1)}, bf16[256,128]{1,0:T(8,128)(2,1)S(1)}, u32[]{:S(2)}, u32[]{:S(2)}) collective-permute-start(bf16[256,128]{1,0:T(8,128)(2,1)S(1)} %bitcast.44), channel_id=1, source_target_pairs={{0,8},{4,12},{8,0},{12,4},{1,9},{5,13},{9,1},{13,5},{2,10},{6,14},... | collective-permute-start | bytes 196616 | tf_op jit(solution)/shard_map/ppermute | solution.py:28
  75.8 7.1 %collective-permute-start.21 = (bf16[256,128]{1,0:T(8,128)(2,1)S(1)}, bf16[256,128]{1,0:T(8,128)(2,1)S(1)}, u32[]{:S(2)}, u32[]{:S(2)}) collective-permute-start(bf16[256,128]{1,0:T(8,128)(2,1)S(1)} %bitcast.45), channel_id=1, source_target_pairs={{0,4},{4,0},{8,12},{12,8},{1,5},{5,1},{9,13},{13,9},{2,6},{6,2},{1... | collective-permute-start | bytes 196616 | tf_op jit(solution)/shard_map/ppermute | solution.py:28
  83.0 1.3 %collective-permute-start.24 = (bf16[2,128,128]{2,1,0:T(8,128)(2,1)S(1)}, bf16[2,128,128]{2,1,0:T(8,128)(2,1)S(1)}, u32[]{:S(2)}, u32[]{:S(2)}) collective-permute-start(bf16[2,128,128]{2,1,0:T(8,128)(2,1)S(1)} %shard_map.170.refs_0_), channel_id=1, source_target_pairs={{0,1},{1,0},{2,3},{3,2},{4,5},{5,4},{6,7},{7,6},{8,9},{9,8},{10,11... | collective-permute-start | bytes 196616 | tf_op jit(solution)/shard_map/ppermute | solution.py:28
  (7 other events, 5.0 us)

commit v6 on v5

--- a/solution.py
+++ b/solution.py
@@ -249,19 +249,19 @@
     return jax.ShapeDtypeStruct(sizes, dtype)
 
 
-def kernel_call(body, outs, scalars, arrays, left=(), scratch=(), flops=0, room=16 * 1024 * 1024):
+def kernel_call(body, outs, scalars, arrays, scratch=(), flops=0):
     many = isinstance(outs, (list, tuple))
     kept = list(outs) if many else [outs]
     size = sum(a.size * a.dtype.itemsize for a in arrays) + sum(a.size * a.dtype.itemsize for a in kept)
     return pl.pallas_call(
         body,
         out_shape=tuple(kept) if many else outs,
-        in_specs=[pl.BlockSpec(memory_space=pltpu.SMEM)] * len(scalars) + [pl.BlockSpec(memory_space=pltpu.VMEM)] * len(arrays) + [pl.BlockSpec(memory_space=pltpu.HBM)] * len(left),
+        in_specs=[pl.BlockSpec(memory_space=pltpu.SMEM)] * len(scalars) + [pl.BlockSpec(memory_space=pltpu.VMEM)] * len(arrays),
         out_specs=tuple(pl.BlockSpec(memory_space=pltpu.VMEM) for _ in kept) if many else pl.BlockSpec(memory_space=pltpu.VMEM),
         scratch_shapes=list(scratch),
-        compiler_params=pltpu.CompilerParams(vmem_limit_bytes=room),
+        compiler_params=pltpu.CompilerParams(vmem_limit_bytes=16 * 1024 * 1024),
         cost_estimate=pl.CostEstimate(flops=int(flops), bytes_accessed=int(size), transcendentals=0),
-    )(*scalars, *arrays, *left)
+    )(*scalars, *arrays)
 
 
 def place_of():
@@ -308,43 +308,45 @@
 
 def start_body(ranges, state, weight, enc, *refs):
     place = place_of()
-    sends, sems = (None, *refs[-2::-1]), refs[-1]
+    sends, (wide, load_sem, sems) = refs[: ranges - 1], refs[ranges - 1 :]
     width, rows = state.shape
     part = width // 2
-    low = state[...].astype(BF16)
-
-    def copies(source, first, size, at, group):
+
+    def copies(source, first, count, at, group):
         made = []
         for step in range(1, ranges):
             start = pl.multiple_of(partner(place[0], step, ranges) * width + first, 16)
             made.append(
                 pltpu.make_async_copy(
-                    source.at[pl.ds(start, size), pl.ds(0, rows)],
-                    sends[step].at[pl.ds(at, size)],
+                    source.at[pl.ds(start, count), pl.ds(0, rows)],
+                    sends[step - 1].at[pl.ds(at, count)],
                     sems.at[group, step - 1],
                 )
             )
         return made
 
+    load = pltpu.make_async_copy(state, wide, load_sem)
     rest = copies(enc, place[3] * part, part, width, 0)
-    for copy in rest:
-        copy.start()
+    carried = copies(weight, 0, width, 0, 1)
 
     @pl.when(place[2] == 0)
     def _():
-        for send in sends[1:]:
+        load.start()
+        for copy in rest:
+            copy.start()
+        load.wait()
+        low = wide[...].astype(BF16)
+        for send in sends:
             send[0:width] = low
+        for copy in rest:
+            copy.wait()
 
     @pl.when(place[2] > 0)
     def _():
-        carried = copies(weight, 0, width, 0, 1)
-        for copy in carried:
+        for copy in carried + rest:
             copy.start()
-        for copy in carried:
+        for copy in carried + rest:
             copy.wait()
-
-    for copy in rest:
-        copy.wait()
 
 
 def carry(place, ranges, weight, width, first, count, made, sends):
@@ -597,16 +599,19 @@
     packed = carried = rest = low = kept = None
     for layer in range(layers):
         if layer == 0:
-            sends = kernel_call(
+            sends = pl.pallas_call(
                 functools.partial(start_body, ranges),
-                [shape(width + width // 2, rows, dtype=BF16)] * (ranges - 1),
-                [],
-                [source],
-                left=[value_rows, enc_rows],
-                scratch=[pltpu.SemaphoreType.DMA((2, ranges - 1))],
-                room=60 * 1024 * 1024,
-            )
-            blocks = exchange([source, *sends[::-1]])
+                out_shape=(shape(width + width // 2, rows, dtype=BF16),) * (ranges - 1),
+                in_specs=[pl.BlockSpec(memory_space=pltpu.HBM)] * 3,
+                out_specs=(pl.BlockSpec(memory_space=pltpu.VMEM),) * (ranges - 1),
+                scratch_shapes=[
+                    pltpu.VMEM((width, rows), F32),
+                    pltpu.SemaphoreType.DMA,
+                    pltpu.SemaphoreType.DMA((2, ranges - 1)),
+                ],
+                compiler_params=pltpu.CompilerParams(vmem_limit_bytes=60 * 1024 * 1024),
+            )(source, value_rows, enc_rows)
+            blocks = exchange([source, *sends])
             info, mixing, scales, live = kernel_call(
                 facts_body,
                 [

time: 85.7 us -> 84.9 us (level)
    pallas_call x14 -> x13, Pallas kernels: 9.55 us -> 6.83 us  [kernel_call(): pl.pallas_call(body, out_shape=tuple(kept) if many else outs, in_specs=[p...]
    pallas_call x0 -> x1, Pallas kernels: none -> 1.98 us  [tiled(): pl.pallas_call(functools.partial(start_body, ranges), out_shape=(shape(wi...]
where the time goes in v6:
time: 84.9 us; the launch traced here: 84.6 us
  waiting for transfers between devices  40.3 us (47%)
  starting transfers between devices  28.9 us (34%)
  Pallas kernels  8.81 us (10%)
  local copies, waits for them, and re-layouts  5.04 us (6%)
  between operations  1.5 us (2%)
    ppermute x23, waiting for transfers between devices, swap(): lax.ppermute(value, axis, [(s, partner(s, step, count)) for s in range(co...  36.5 us
    ppermute x23, starting transfers between devices, swap(): lax.ppermute(value, axis, [(s, partner(s, step, count)) for s in range(co...  25.8 us
    pallas_call x13, Pallas kernels, kernel_call(): pl.pallas_call(body, out_shape=tuple(kept) if many else outs, in_specs=[p...  6.83 us
    unnamed x28, local copies, waits for them, and re-layouts  5.04 us
    ppermute x2, waiting for transfers between devices, handed_on(): lax.ppermute(value, 'layer', [(n, (n + 1) % layers) for n in range(layers)])  3.71 us
    ppermute x2, starting transfers between devices, handed_on(): lax.ppermute(value, 'layer', [(n, (n + 1) % layers) for n in range(layers)])  3.13 us
    pallas_call x1, Pallas kernels, tiled(): pl.pallas_call(functools.partial(start_body, ranges), out_shape=(shape(wi...  1.98 us
  transfers between devices with their start and end apart: 25, of which 17 were waited for; matrix products, arithmetic and copies ran while one was open for 0% of the time, Pallas kernels for 1%

profile of v6, /device:TPU:0, one launch (start us, length us, event | category | flops | bytes accessed | tf_op | source)
XLA Modules:
  0.0 84.6 jit_solution(16351975855920428600)
XLA Ops:
  0.7 2.0 %shard_map.158 = (bf16[672,128]{1,0:T(8,128)(2,1)}, bf16[672,128]{1,0:T(8,128)(2,1)}, bf16[672,128]{1,0:T(8,128)(2,1)}) custom-call(f32[448,128]{1,0:T(8,128)} %bitcast.37, bf16[1792,256]{1,0:T(8,128)(2,1)} %bitcast.24, bf16[1792,128]{1,0:T(8,128)(2,1)} %bitcast.34), custom_call_target="tpu_custom_call" | custom-call | tf_op jit(solution)/shard_map/pallas_call | solution.py:602
  2.7 5.1 %collective-permute-start = (bf16[672,128]{1,0:T(8,128)(2,1)}, bf16[672,128]{1,0:T(8,128)(2,1)S(1)}, u32[]{:S(2)}, u32[]{:S(2)}) collective-permute-start(bf16[672,128]{1,0:T(8,128)(2,1)} %get-tuple-element.39), channel_id=1, source_target_pairs={{0,12},{4,8},{8,4},{12,0},{1,13},{5,9},{9,5},{13,1},{2,14},{6,10},... | collective-permute-start | bytes 516104 | tf_op jit(solution)/shard_map/ppermute | solution.py:28
  14.8 7.8 %collective-permute-done.1.refs_2_.refs_5_.refs_1_ = bf16[672,128]{1,0:T(8,128)(2,1)S(1)} collective-permute-done((bf16[672,128]{1,0:T(8,128)(2,1)}, bf16[672,128]{1,0:T(8,128)(2,1)S(1)}, u32[]{:S(2)}, u32[]{:S(2)}) %collective-permute-start.1) | collective-permute-done | bytes 172064 | tf_op jit(solution)/shard_map/ppermute | solution.py:28
  23.0 1.6 %collective-permute-start.7 = (bf16[672,128]{1,0:T(8,128)(2,1)S(1)}, bf16[672,128]{1,0:T(8,128)(2,1)S(1)}, u32[]{:S(2)}, u32[]{:S(2)}) collective-permute-start(bf16[672,128]{1,0:T(8,128)(2,1)S(1)} %get-tuple-element.53), channel_id=1, source_target_pairs={{0,16},{16,0},{1,17},{17,1},{2,18},{18,2},{3,19},{19,3},{4,20},{20... | collective-permute-start | bytes 516104 | tf_op jit(solution)/shard_map/ppermute | solution.py:28
  24.7 2.5 %collective-permute-start.4 = (bf16[256,128]{1,0:T(8,128)(2,1)S(1)}, bf16[256,128]{1,0:T(8,128)(2,1)S(1)}, u32[]{:S(2)}, u32[]{:S(2)}) collective-permute-start(bf16[256,128]{1,0:T(8,128)(2,1)S(1)} %get-tuple-element.50), channel_id=1, source_target_pairs={{0,12},{4,8},{8,4},{12,0},{1,13},{5,9},{9,5},{13,1},{2,14},{6,10},... | collective-permute-start | bytes 196616 | tf_op jit(solution)/shard_map/ppermute | solution.py:28
  27.2 1.9 %collective-permute-start.6 = (bf16[256,128]{1,0:T(8,128)(2,1)S(1)}, bf16[256,128]{1,0:T(8,128)(2,1)S(1)}, u32[]{:S(2)}, u32[]{:S(2)}) collective-permute-start(bf16[256,128]{1,0:T(8,128)(2,1)S(1)} %get-tuple-element.52), channel_id=1, source_target_pairs={{0,4},{4,0},{8,12},{12,8},{1,5},{5,1},{9,13},{13,9},{2,6},{6,2},{1... | collective-permute-start | bytes 196616 | tf_op jit(solution)/shard_map/ppermute | solution.py:28
  29.8 1.7 %collective-permute-done.4.refs_1_.refs_3_ = bf16[256,128]{1,0:T(8,128)(2,1)S(1)} collective-permute-done((bf16[256,128]{1,0:T(8,128)(2,1)S(1)}, bf16[256,128]{1,0:T(8,128)(2,1)S(1)}, u32[]{:S(2)}, u32[]{:S(2)}) %collective-permute-start.4) | collective-permute-done | bytes 65568 | tf_op jit(solution)/shard_map/ppermute | solution.py:28
  31.5 2.0 %collective-permute-done.5.refs_2_.refs_4_ = bf16[256,128]{1,0:T(8,128)(2,1)S(1)} collective-permute-done((bf16[256,128]{1,0:T(8,128)(2,1)S(1)}, bf16[256,128]{1,0:T(8,128)(2,1)S(1)}, u32[]{:S(2)}, u32[]{:S(2)}) %collective-permute-start.5) | collective-permute-done | bytes 65568 | tf_op jit(solution)/shard_map/ppermute | solution.py:28
  33.5 1.7 %shard_map.162 = (f32[448,128]{1,0:T(8,128)S(1)}, f32[2,128,128]{2,1,0:T(8,128)S(1)}, bf16[2,128,128]{2,1,0:T(8,128)(2,1)S(1)}) custom-call(bf16[256,128]{1,0:T(8,128)(2,1)S(1)} %get-tuple-element.49.refs_0_, bf16[256,128]{1,0:T(8,128)(2,1)S(1)} %collective-permute-done.4.refs_1_.refs_3_, bf16[256,128]{1,0:T(8,128)(2,1)S(1)} %collective-permute-done.5.refs_2_.refs_4_, ...), custom_call_target="tpu_custom_call" | custom-call | flops 293601280 | bytes 4162048 | tf_op jit(solution)/shard_map/pallas_call | solution.py:256
  35.4 1.2 %collective-permute-done.8.got = bf16[2,128,128]{2,1,0:T(8,128)(2,1)S(1)} collective-permute-done((bf16[2,128,128]{2,1,0:T(8,128)(2,1)S(1)}, bf16[2,128,128]{2,1,0:T(8,128)(2,1)S(1)}, u32[]{:S(2)}, u32[]{:S(2)}) %collective-permute-start.8) | collective-permute-done | bytes 65568 | tf_op jit(solution)/shard_map/ppermute | solution.py:28
  36.6 2.5 %collective-permute-start.9 = (bf16[272,128]{1,0:T(8,128)(2,1)S(1)}, bf16[272,128]{1,0:T(8,128)(2,1)S(1)}, u32[]{:S(2)}, u32[]{:S(2)}) collective-permute-start(bf16[272,128]{1,0:T(8,128)(2,1)S(1)} %get-tuple-element.59), channel_id=1, source_target_pairs={{0,12},{4,8},{8,4},{12,0},{1,13},{5,9},{9,5},{13,1},{2,14},{6,10},... | collective-permute-start | bytes 208904 | tf_op jit(solution)/shard_map/ppermute | solution.py:28
  39.2 1.9 %collective-permute-start.11 = (bf16[272,128]{1,0:T(8,128)(2,1)S(1)}, bf16[272,128]{1,0:T(8,128)(2,1)S(1)}, u32[]{:S(2)}, u32[]{:S(2)}) collective-permute-start(bf16[272,128]{1,0:T(8,128)(2,1)S(1)} %get-tuple-element.61), channel_id=1, source_target_pairs={{0,4},{4,0},{8,12},{12,8},{1,5},{5,1},{9,13},{13,9},{2,6},{6,2},{1... | collective-permute-start | bytes 208904 | tf_op jit(solution)/shard_map/ppermute | solution.py:28
  41.1 2.5 %collective-permute-done.9.refs_1_.refs_5_.refs_6_ = bf16[272,128]{1,0:T(8,128)(2,1)S(1)} collective-permute-done((bf16[272,128]{1,0:T(8,128)(2,1)S(1)}, bf16[272,128]{1,0:T(8,128)(2,1)S(1)}, u32[]{:S(2)}, u32[]{:S(2)}) %collective-permute-start.9) | collective-permute-done | bytes 69664 | tf_op jit(solution)/shard_map/ppermute | solution.py:28
  43.6 2.1 %collective-permute-done.10.refs_2_.refs_6_.refs_7_ = bf16[272,128]{1,0:T(8,128)(2,1)S(1)} collective-permute-done((bf16[272,128]{1,0:T(8,128)(2,1)S(1)}, bf16[272,128]{1,0:T(8,128)(2,1)S(1)}, u32[]{:S(2)}, u32[]{:S(2)}) %collective-permute-start.10) | collective-permute-done | bytes 69664 | tf_op jit(solution)/shard_map/ppermute | solution.py:28
  45.9 1.2 %collective-permute-done.12.refs_1_.also = bf16[2,128,128]{2,1,0:T(8,128)(2,1)S(1)} collective-permute-done((bf16[2,128,128]{2,1,0:T(8,128)(2,1)S(1)}, bf16[2,128,128]{2,1,0:T(8,128)(2,1)S(1)}, u32[]{:S(2)}, u32[]{:S(2)}) %collective-permute-start.12) | collective-permute-done | bytes 65568 | tf_op jit(solution)/shard_map/ppermute | solution.py:28
  47.4 1.6 %collective-permute-start.13 = (bf16[448,128]{1,0:T(8,128)(2,1)S(1)}, bf16[448,128]{1,0:T(8,128)(2,1)S(1)}, u32[]{:S(2)}, u32[]{:S(2)}) collective-permute-start(bf16[448,128]{1,0:T(8,128)(2,1)S(1)} %get-tuple-element.64), channel_id=1, source_target_pairs={{0,2},{2,0},{1,3},{3,1},{4,6},{6,4},{5,7},{7,5},{8,10},{10,8},{9,1... | collective-permute-start | bytes 344072 | tf_op jit(solution)/shard_map/ppermute | solution.py:597
  49.0 3.7 %collective-permute-done.13.low = bf16[448,128]{1,0:T(8,128)(2,1)S(1)} collective-permute-done((bf16[448,128]{1,0:T(8,128)(2,1)S(1)}, bf16[448,128]{1,0:T(8,128)(2,1)S(1)}, u32[]{:S(2)}, u32[]{:S(2)}) %collective-permute-start.13) | collective-permute-done | bytes 114720 | tf_op jit(solution)/shard_map/ppermute | solution.py:597
  53.2 1.3 %collective-permute-done.14 = bf16[4,128,128]{2,1,0:T(8,128)(2,1)S(1)} collective-permute-done((bf16[4,128,128]{2,1,0:T(8,128)(2,1)S(1)}, bf16[4,128,128]{2,1,0:T(8,128)(2,1)S(1)}, u32[]{:S(2)}, u32[]{:S(2)}) %collective-permute-start.14) | collective-permute-done | bytes 131104 | tf_op jit(solution)/shard_map/ppermute | solution.py:28
  54.6 2.5 %collective-permute-start.17 = (bf16[4,128,128]{2,1,0:T(8,128)(2,1)S(1)}, bf16[4,128,128]{2,1,0:T(8,128)(2,1)S(1)}, u32[]{:S(2)}, u32[]{:S(2)}) collective-permute-start(bf16[4,128,128]{2,1,0:T(8,128)(2,1)S(1)} %add_convert_fusion.refs_0_), channel_id=1, source_target_pairs={{0,12},{4,8},{8,4},{12,0},{1,13},{5,9},{9,5},{13,1},{2,14},{6,10},... | collective-permute-start | bytes 393224 | tf_op jit(solution)/shard_map/ppermute | solution.py:28
  57.1 1.9 %collective-permute-start.15 = (bf16[4,128,128]{2,1,0:T(8,128)(2,1)S(1)}, bf16[4,128,128]{2,1,0:T(8,128)(2,1)S(1)}, u32[]{:S(2)}, u32[]{:S(2)}) collective-permute-start(bf16[4,128,128]{2,1,0:T(8,128)(2,1)S(1)} %add_convert_fusion.refs_0_), channel_id=1, source_target_pairs={{0,4},{4,0},{8,12},{12,8},{1,5},{5,1},{9,13},{13,9},{2,6},{6,2},{1... | collective-permute-start | bytes 393224 | tf_op jit(solution)/shard_map/ppermute | solution.py:28
  59.3 1.6 %collective-permute-start.19 = (bf16[2,448,128]{2,1,0:T(8,128)(2,1)S(1)}, bf16[2,448,128]{2,1,0:T(8,128)(2,1)S(1)}, u32[]{:S(2)}, u32[]{:S(2)}) collective-permute-start(bf16[2,448,128]{2,1,0:T(8,128)(2,1)S(1)} %shard_map.168), channel_id=1, source_target_pairs={{0,2},{2,0},{1,3},{3,1},{4,6},{6,4},{5,7},{7,5},{8,10},{10,8},{9,1... | collective-permute-start | bytes 688136 | tf_op jit(solution)/shard_map/ppermute | solution.py:597
  60.9 2.0 %collective-permute-done.17.refs_3_ = bf16[4,128,128]{2,1,0:T(8,128)(2,1)S(1)} collective-permute-done((bf16[4,128,128]{2,1,0:T(8,128)(2,1)S(1)}, bf16[4,128,128]{2,1,0:T(8,128)(2,1)S(1)}, u32[]{:S(2)}, u32[]{:S(2)}) %collective-permute-start.17) | collective-permute-done | bytes 131104 | tf_op jit(solution)/shard_map/ppermute | solution.py:28
  62.9 5.9 %collective-permute-done.16.refs_2_ = bf16[4,128,128]{2,1,0:T(8,128)(2,1)S(1)} collective-permute-done((bf16[4,128,128]{2,1,0:T(8,128)(2,1)S(1)}, bf16[4,128,128]{2,1,0:T(8,128)(2,1)S(1)}, u32[]{:S(2)}, u32[]{:S(2)}) %collective-permute-start.16) | collective-permute-done | bytes 131104 | tf_op jit(solution)/shard_map/ppermute | solution.py:28
  69.0 1.3 %collective-permute-done.18.also = bf16[4,128,128]{2,1,0:T(8,128)(2,1)S(1)} collective-permute-done((bf16[4,128,128]{2,1,0:T(8,128)(2,1)S(1)}, bf16[4,128,128]{2,1,0:T(8,128)(2,1)S(1)}, u32[]{:S(2)}, u32[]{:S(2)}) %collective-permute-start.18) | collective-permute-done | bytes 131104 | tf_op jit(solution)/shard_map/ppermute | solution.py:28
  70.3 1.7 %shard_map.169 = (f32[448,128]{1,0:T(8,128)S(1)}, f32[2,128,128]{2,1,0:T(8,128)S(1)}, bf16[2,128,128]{2,1,0:T(8,128)(2,1)S(1)}) custom-call(bf16[4,128,128]{2,1,0:T(8,128)(2,1)S(1)} %shard_map.167.mine, bf16[4,128,128]{2,1,0:T(8,128)(2,1)S(1)} %collective-permute-done.18.also, bf16[448,128]{1,0:T(8,128)(2,1)S(1)} %collective-permute-done.13.low, ...), custom_call_target="tpu_custom_call" | custom-call | flops 293601280 | bytes 4276736 | tf_op jit(solution)/shard_map/pallas_call | solution.py:256
  72.3 1.1 %collective-permute-done.20 = bf16[2,128,128]{2,1,0:T(8,128)(2,1)S(1)} collective-permute-done((bf16[2,128,128]{2,1,0:T(8,128)(2,1)S(1)}, bf16[2,128,128]{2,1,0:T(8,128)(2,1)S(1)}, u32[]{:S(2)}, u32[]{:S(2)}) %collective-permute-start.20) | collective-permute-done | bytes 65568 | tf_op jit(solution)/shard_map/ppermute | solution.py:28
  73.4 1.7 %collective-permute-start.23 = (bf16[256,128]{1,0:T(8,128)(2,1)S(1)}, bf16[256,128]{1,0:T(8,128)(2,1)S(1)}, u32[]{:S(2)}, u32[]{:S(2)}) collective-permute-start(bf16[256,128]{1,0:T(8,128)(2,1)S(1)} %bitcast.43), channel_id=1, source_target_pairs={{0,12},{4,8},{8,4},{12,0},{1,13},{5,9},{9,5},{13,1},{2,14},{6,10},... | collective-permute-start | bytes 196616 | tf_op jit(solution)/shard_map/ppermute | solution.py:28
  75.1 2.8 %collective-permute-start.21 = (bf16[256,128]{1,0:T(8,128)(2,1)S(1)}, bf16[256,128]{1,0:T(8,128)(2,1)S(1)}, u32[]{:S(2)}, u32[]{:S(2)}) collective-permute-start(bf16[256,128]{1,0:T(8,128)(2,1)S(1)} %bitcast.45), channel_id=1, source_target_pairs={{0,4},{4,0},{8,12},{12,8},{1,5},{5,1},{9,13},{13,9},{2,6},{6,2},{1... | collective-permute-start | bytes 196616 | tf_op jit(solution)/shard_map/ppermute | solution.py:28
  77.8 2.4 %collective-permute-done.23.refs_3_ = bf16[256,128]{1,0:T(8,128)(2,1)S(1)} collective-permute-done((bf16[256,128]{1,0:T(8,128)(2,1)S(1)}, bf16[256,128]{1,0:T(8,128)(2,1)S(1)}, u32[]{:S(2)}, u32[]{:S(2)}) %collective-permute-start.23) | collective-permute-done | bytes 65568 | tf_op jit(solution)/shard_map/ppermute | solution.py:28
  80.2 2.0 %collective-permute-done.22.refs_2_ = bf16[256,128]{1,0:T(8,128)(2,1)S(1)} collective-permute-done((bf16[256,128]{1,0:T(8,128)(2,1)S(1)}, bf16[256,128]{1,0:T(8,128)(2,1)S(1)}, u32[]{:S(2)}, u32[]{:S(2)}) %collective-permute-start.22) | collective-permute-done | bytes 65568 | tf_op jit(solution)/shard_map/ppermute | solution.py:28
  82.4 1.2 %collective-permute-done.24.refs_1_ = bf16[2,128,128]{2,1,0:T(8,128)(2,1)S(1)} collective-permute-done((bf16[2,128,128]{2,1,0:T(8,128)(2,1)S(1)}, bf16[2,128,128]{2,1,0:T(8,128)(2,1)S(1)}, u32[]{:S(2)}, u32[]{:S(2)}) %collective-permute-start.24) | collective-permute-done | bytes 65568 | tf_op jit(solution)/shard_map/ppermute | solution.py:28
  83.6 1.0 %shard_map.171 = (f32[448,128]{1,0:T(8,128)}, bf16[128,128]{1,0:T(8,128)(2,1)}) custom-call(bf16[2,128,128]{2,1,0:T(8,128)(2,1)S(1)} %shard_map.170.refs_0_, bf16[2,128,128]{2,1,0:T(8,128)(2,1)S(1)} %collective-permute-done.24.refs_1_, bf16[2,448,512]{2,1,0:T(8,128)(2,1)S(1)} %bitcast.31, f32[448,128]{1,0:T(8,128)S(1)} %get-tuple-element.71.refs_3_, ...), custom_call_target="tpu_custom_call" | custom-call | flops 58720256 | bytes 2260992 | tf_op jit(solution)/shard_map/pallas_call | solution.py:256
  (62 shorter events, 9.5 us)
Async XLA Ops:
  0.6 22.0 %copy-start = (bf16[1,1,1792,256]{3,2,1,0:T(8,128)(2,1)S(1)}, bf16[1,1,1792,256]{3,2,1,0:T(8,128)(2,1)}, u32[]{:S(2)}) copy-start(bf16[1,1,1792,256]{3,2,1,0:T(8,128)(2,1)} %param.20) | copy-start | bytes 2752516
  0.6 22.0 %copy-start.4 = (f32[128,1,448]{0,2,1:T(8,128)S(1)}, f32[128,1,448]{0,2,1:T(8,128)}, u32[]{:S(2)}) copy-start(f32[128,1,448]{0,2,1:T(8,128)} %param.15) | copy-start | bytes 688132
  0.6 32.9 %copy-start.9 = (f32[1,128]{1,0:T(1,128)S(1)}, f32[1,128]{1,0:T(1,128)}, u32[]{:S(2)}) copy-start(f32[1,128]{1,0:T(1,128)} %refs_6_.1) | copy-start | bytes 1540
  2.7 30.9 %copy-start.2 = (bf16[1,4,256,2,1,448]{2,5,4,3,1,0:T(8,128)(2,1)S(1)}, bf16[1,4,256,2,1,448]{2,5,4,3,1,0:T(8,128)(2,1)}, u32[]{:S(2)}) copy-start(bf16[1,4,256,2,1,448]{2,5,4,3,1,0:T(8,128)(2,1)} %param.21) | copy-start | bytes 5505028
  2.7 30.9 %copy-start.3 = (bf16[1,1,1792,128]{3,2,1,0:T(8,128)(2,1)S(1)}, bf16[1,1,1792,128]{3,2,1,0:T(8,128)(2,1)}, u32[]{:S(2)}) copy-start(bf16[1,1,1792,128]{3,2,1,0:T(8,128)(2,1)} %param.22) | copy-start | bytes 1376260
  2.7 12.1 %collective-permute-start = (bf16[672,128]{1,0:T(8,128)(2,1)}, bf16[672,128]{1,0:T(8,128)(2,1)S(1)}, u32[]{:S(2)}, u32[]{:S(2)}) collective-permute-start(bf16[672,128]{1,0:T(8,128)(2,1)} %get-tuple-element.39), channel_id=1, source_target_pairs={{0,12},{4,8},{8,4},{12,0},{1,13},{5,9},{9,5},{13,1},{2,14},{6,10},... | collective-permute-start | bytes 516104 | tf_op jit(solution)/shard_map/ppermute | solution.py:28
  7.8 14.8 %collective-permute-start.1 = (bf16[672,128]{1,0:T(8,128)(2,1)}, bf16[672,128]{1,0:T(8,128)(2,1)S(1)}, u32[]{:S(2)}, u32[]{:S(2)}) collective-permute-start(bf16[672,128]{1,0:T(8,128)(2,1)} %get-tuple-element.46), channel_id=1, source_target_pairs={{0,8},{4,12},{8,0},{12,4},{1,9},{5,13},{9,1},{13,5},{2,10},{6,14},... | collective-permute-start | bytes 516104 | tf_op jit(solution)/shard_map/ppermute | solution.py:28
  7.8 14.8 %collective-permute-start.2 = (bf16[672,128]{1,0:T(8,128)(2,1)}, bf16[672,128]{1,0:T(8,128)(2,1)S(1)}, u32[]{:S(2)}, u32[]{:S(2)}) collective-permute-start(bf16[672,128]{1,0:T(8,128)(2,1)} %get-tuple-element.47), channel_id=1, source_target_pairs={{0,4},{4,0},{8,12},{12,8},{1,5},{5,1},{9,13},{13,9},{2,6},{6,2},{1... | collective-permute-start | bytes 516104 | tf_op jit(solution)/shard_map/ppermute | solution.py:28
  22.9 1.7 %collective-permute-start.3 = (f32[128,256]{1,0:T(8,128)S(1)}, f32[128,256]{1,0:T(8,128)S(1)}, u32[]{:S(2)}, u32[]{:S(2)}) collective-permute-start(f32[128,256]{1,0:T(8,128)S(1)} %get-tuple-element.48.own), channel_id=1, source_target_pairs={{0,1},{1,0},{2,3},{3,2},{4,5},{5,4},{6,7},{7,6},{8,9},{9,8},{10,11... | collective-permute-start | bytes 393224 | tf_op jit(solution)/shard_map/ppermute | solution.py:28
  23.0 6.8 %collective-permute-start.7 = (bf16[672,128]{1,0:T(8,128)(2,1)S(1)}, bf16[672,128]{1,0:T(8,128)(2,1)S(1)}, u32[]{:S(2)}, u32[]{:S(2)}) collective-permute-start(bf16[672,128]{1,0:T(8,128)(2,1)S(1)} %get-tuple-element.53), channel_id=1, source_target_pairs={{0,16},{16,0},{1,17},{17,1},{2,18},{18,2},{3,19},{19,3},{4,20},{20... | collective-permute-start | bytes 516104 | tf_op jit(solution)/shard_map/ppermute | solution.py:28
  24.7 6.8 %collective-permute-start.4 = (bf16[256,128]{1,0:T(8,128)(2,1)S(1)}, bf16[256,128]{1,0:T(8,128)(2,1)S(1)}, u32[]{:S(2)}, u32[]{:S(2)}) collective-permute-start(bf16[256,128]{1,0:T(8,128)(2,1)S(1)} %get-tuple-element.50), channel_id=1, source_target_pairs={{0,12},{4,8},{8,4},{12,0},{1,13},{5,9},{9,5},{13,1},{2,14},{6,10},... | collective-permute-start | bytes 196616 | tf_op jit(solution)/shard_map/ppermute | solution.py:28
  27.2 6.3 %collective-permute-start.5 = (bf16[256,128]{1,0:T(8,128)(2,1)S(1)}, bf16[256,128]{1,0:T(8,128)(2,1)S(1)}, u32[]{:S(2)}, u32[]{:S(2)}) collective-permute-start(bf16[256,128]{1,0:T(8,128)(2,1)S(1)} %get-tuple-element.51), channel_id=1, source_target_pairs={{0,8},{4,12},{8,0},{12,4},{1,9},{5,13},{9,1},{13,5},{2,10},{6,14},... | collective-permute-start | bytes 196616 | tf_op jit(solution)/shard_map/ppermute | solution.py:28
  27.2 6.3 %collective-permute-start.6 = (bf16[256,128]{1,0:T(8,128)(2,1)S(1)}, bf16[256,128]{1,0:T(8,128)(2,1)S(1)}, u32[]{:S(2)}, u32[]{:S(2)}) collective-permute-start(bf16[256,128]{1,0:T(8,128)(2,1)S(1)} %get-tuple-element.52), channel_id=1, source_target_pairs={{0,4},{4,0},{8,12},{12,8},{1,5},{5,1},{9,13},{13,9},{2,6},{6,2},{1... | collective-permute-start | bytes 196616 | tf_op jit(solution)/shard_map/ppermute | solution.py:28
  35.2 11.9 %copy-start.1 = (bf16[1,2,512,1,448]{2,4,3,1,0:T(8,128)(2,1)S(1)}, bf16[1,2,512,1,448]{2,4,3,1,0:T(8,128)(2,1)}, u32[]{:S(2)}) copy-start(bf16[1,2,512,1,448]{2,4,3,1,0:T(8,128)(2,1)} %param.24) | copy-start | bytes 2752516
  35.3 11.9 %copy-start.5 = (f32[1,128,1,448]{1,3,2,0:T(8,128)S(1)}, f32[1,128,1,448]{1,3,2,0:T(8,128)}, u32[]{:S(2)}) copy-start(f32[1,128,1,448]{1,3,2,0:T(8,128)} %param.25) | copy-start | bytes 688132
  35.3 1.3 %collective-permute-start.8 = (bf16[2,128,128]{2,1,0:T(8,128)(2,1)S(1)}, bf16[2,128,128]{2,1,0:T(8,128)(2,1)S(1)}, u32[]{:S(2)}, u32[]{:S(2)}) collective-permute-start(bf16[2,128,128]{2,1,0:T(8,128)(2,1)S(1)} %get-tuple-element.56), channel_id=1, source_target_pairs={{0,1},{1,0},{2,3},{3,2},{4,5},{5,4},{6,7},{7,6},{8,9},{9,8},{10,11... | collective-permute-start | bytes 196616 | tf_op jit(solution)/shard_map/ppermute | solution.py:28
  36.6 7.0 %collective-permute-start.9 = (bf16[272,128]{1,0:T(8,128)(2,1)S(1)}, bf16[272,128]{1,0:T(8,128)(2,1)S(1)}, u32[]{:S(2)}, u32[]{:S(2)}) collective-permute-start(bf16[272,128]{1,0:T(8,128)(2,1)S(1)} %get-tuple-element.59), channel_id=1, source_target_pairs={{0,12},{4,8},{8,4},{12,0},{1,13},{5,9},{9,5},{13,1},{2,14},{6,10},... | collective-permute-start | bytes 208904 | tf_op jit(solution)/shard_map/ppermute | solution.py:28
  39.2 6.5 %collective-permute-start.10 = (bf16[272,128]{1,0:T(8,128)(2,1)S(1)}, bf16[272,128]{1,0:T(8,128)(2,1)S(1)}, u32[]{:S(2)}, u32[]{:S(2)}) collective-permute-start(bf16[272,128]{1,0:T(8,128)(2,1)S(1)} %get-tuple-element.60), channel_id=1, source_target_pairs={{0,8},{4,12},{8,0},{12,4},{1,9},{5,13},{9,1},{13,5},{2,10},{6,14},... | collective-permute-start | bytes 208904 | tf_op jit(solution)/shard_map/ppermute | solution.py:28
  39.2 6.5 %collective-permute-start.11 = (bf16[272,128]{1,0:T(8,128)(2,1)S(1)}, bf16[272,128]{1,0:T(8,128)(2,1)S(1)}, u32[]{:S(2)}, u32[]{:S(2)}) collective-permute-start(bf16[272,128]{1,0:T(8,128)(2,1)S(1)} %get-tuple-element.61), channel_id=1, source_target_pairs={{0,4},{4,0},{8,12},{12,8},{1,5},{5,1},{9,13},{13,9},{2,6},{6,2},{1... | collective-permute-start | bytes 208904 | tf_op jit(solution)/shard_map/ppermute | solution.py:28
  45.8 1.3 %collective-permute-start.12 = (bf16[2,128,128]{2,1,0:T(8,128)(2,1)S(1)}, bf16[2,128,128]{2,1,0:T(8,128)(2,1)S(1)}, u32[]{:S(2)}, u32[]{:S(2)}) collective-permute-start(bf16[2,128,128]{2,1,0:T(8,128)(2,1)S(1)} %shard_map.164.refs_0_.mine), channel_id=1, source_target_pairs={{0,1},{1,0},{2,3},{3,2},{4,5},{5,4},{6,7},{7,6},{8,9},{9,8},{10,11... | collective-permute-start | bytes 196616 | tf_op jit(solution)/shard_map/ppermute | solution.py:28
  47.4 5.3 %collective-permute-start.13 = (bf16[448,128]{1,0:T(8,128)(2,1)S(1)}, bf16[448,128]{1,0:T(8,128)(2,1)S(1)}, u32[]{:S(2)}, u32[]{:S(2)}) collective-permute-start(bf16[448,128]{1,0:T(8,128)(2,1)S(1)} %get-tuple-element.64), channel_id=1, source_target_pairs={{0,2},{2,0},{1,3},{3,1},{4,6},{6,4},{5,7},{7,5},{8,10},{10,8},{9,1... | collective-permute-start | bytes 344072 | tf_op jit(solution)/shard_map/ppermute | solution.py:597
  53.2 1.4 %collective-permute-start.14 = (bf16[4,128,128]{2,1,0:T(8,128)(2,1)S(1)}, bf16[4,128,128]{2,1,0:T(8,128)(2,1)S(1)}, u32[]{:S(2)}, u32[]{:S(2)}) collective-permute-start(bf16[4,128,128]{2,1,0:T(8,128)(2,1)S(1)} %get-tuple-element.66), channel_id=1, source_target_pairs={{0,1},{1,0},{2,3},{3,2},{4,5},{5,4},{6,7},{7,6},{8,9},{9,8},{10,11... | collective-permute-start | bytes 393224 | tf_op jit(solution)/shard_map/ppermute | solution.py:28
  54.6 8.3 %collective-permute-start.17 = (bf16[4,128,128]{2,1,0:T(8,128)(2,1)S(1)}, bf16[4,128,128]{2,1,0:T(8,128)(2,1)S(1)}, u32[]{:S(2)}, u32[]{:S(2)}) collective-permute-start(bf16[4,128,128]{2,1,0:T(8,128)(2,1)S(1)} %add_convert_fusion.refs_0_), channel_id=1, source_target_pairs={{0,12},{4,8},{8,4},{12,0},{1,13},{5,9},{9,5},{13,1},{2,14},{6,10},... | collective-permute-start | bytes 393224 | tf_op jit(solution)/shard_map/ppermute | solution.py:28
  57.1 11.7 %collective-permute-start.16 = (bf16[4,128,128]{2,1,0:T(8,128)(2,1)S(1)}, bf16[4,128,128]{2,1,0:T(8,128)(2,1)S(1)}, u32[]{:S(2)}, u32[]{:S(2)}) collective-permute-start(bf16[4,128,128]{2,1,0:T(8,128)(2,1)S(1)} %add_convert_fusion.refs_0_), channel_id=1, source_target_pairs={{0,8},{4,12},{8,0},{12,4},{1,9},{5,13},{9,1},{13,5},{2,10},{6,14},... | collective-permute-start | bytes 393224 | tf_op jit(solution)/shard_map/ppermute | solution.py:28
  57.1 11.7 %collective-permute-start.15 = (bf16[4,128,128]{2,1,0:T(8,128)(2,1)S(1)}, bf16[4,128,128]{2,1,0:T(8,128)(2,1)S(1)}, u32[]{:S(2)}, u32[]{:S(2)}) collective-permute-start(bf16[4,128,128]{2,1,0:T(8,128)(2,1)S(1)} %add_convert_fusion.refs_0_), channel_id=1, source_target_pairs={{0,4},{4,0},{8,12},{12,8},{1,5},{5,1},{9,13},{13,9},{2,6},{6,2},{1... | collective-permute-start | bytes 393224 | tf_op jit(solution)/shard_map/ppermute | solution.py:28
  59.3 9.6 %collective-permute-start.19 = (bf16[2,448,128]{2,1,0:T(8,128)(2,1)S(1)}, bf16[2,448,128]{2,1,0:T(8,128)(2,1)S(1)}, u32[]{:S(2)}, u32[]{:S(2)}) collective-permute-start(bf16[2,448,128]{2,1,0:T(8,128)(2,1)S(1)} %shard_map.168), channel_id=1, source_target_pairs={{0,2},{2,0},{1,3},{3,1},{4,6},{6,4},{5,7},{7,5},{8,10},{10,8},{9,1... | collective-permute-start | bytes 688136 | tf_op jit(solution)/shard_map/ppermute | solution.py:597
  68.9 1.4 %collective-permute-start.18 = (bf16[4,128,128]{2,1,0:T(8,128)(2,1)S(1)}, bf16[4,128,128]{2,1,0:T(8,128)(2,1)S(1)}, u32[]{:S(2)}, u32[]{:S(2)}) collective-permute-start(bf16[4,128,128]{2,1,0:T(8,128)(2,1)S(1)} %shard_map.167.mine), channel_id=1, source_target_pairs={{0,1},{1,0},{2,3},{3,2},{4,5},{5,4},{6,7},{7,6},{8,9},{9,8},{10,11... | collective-permute-start | bytes 393224 | tf_op jit(solution)/shard_map/ppermute | solution.py:28
  72.0 1.3 %collective-permute-start.20 = (bf16[2,128,128]{2,1,0:T(8,128)(2,1)S(1)}, bf16[2,128,128]{2,1,0:T(8,128)(2,1)S(1)}, u32[]{:S(2)}, u32[]{:S(2)}) collective-permute-start(bf16[2,128,128]{2,1,0:T(8,128)(2,1)S(1)} %get-tuple-element.70), channel_id=1, source_target_pairs={{0,1},{1,0},{2,3},{3,2},{4,5},{5,4},{6,7},{7,6},{8,9},{9,8},{10,11... | collective-permute-start | bytes 196616 | tf_op jit(solution)/shard_map/ppermute | solution.py:28
  73.4 6.8 %collective-permute-start.23 = (bf16[256,128]{1,0:T(8,128)(2,1)S(1)}, bf16[256,128]{1,0:T(8,128)(2,1)S(1)}, u32[]{:S(2)}, u32[]{:S(2)}) collective-permute-start(bf16[256,128]{1,0:T(8,128)(2,1)S(1)} %bitcast.43), channel_id=1, source_target_pairs={{0,12},{4,8},{8,4},{12,0},{1,13},{5,9},{9,5},{13,1},{2,14},{6,10},... | collective-permute-start | bytes 196616 | tf_op jit(solution)/shard_map/ppermute | solution.py:28
  75.0 7.2 %collective-permute-start.22 = (bf16[256,128]{1,0:T(8,128)(2,1)S(1)}, bf16[256,128]{1,0:T(8,128)(2,1)S(1)}, u32[]{:S(2)}, u32[]{:S(2)}) collective-permute-start(bf16[256,128]{1,0:T(8,128)(2,1)S(1)} %bitcast.44), channel_id=1, source_target_pairs={{0,8},{4,12},{8,0},{12,4},{1,9},{5,13},{9,1},{13,5},{2,10},{6,14},... | collective-permute-start | bytes 196616 | tf_op jit(solution)/shard_map/ppermute | solution.py:28
  75.1 7.2 %collective-permute-start.21 = (bf16[256,128]{1,0:T(8,128)(2,1)S(1)}, bf16[256,128]{1,0:T(8,128)(2,1)S(1)}, u32[]{:S(2)}, u32[]{:S(2)}) collective-permute-start(bf16[256,128]{1,0:T(8,128)(2,1)S(1)} %bitcast.45), channel_id=1, source_target_pairs={{0,4},{4,0},{8,12},{12,8},{1,5},{5,1},{9,13},{13,9},{2,6},{6,2},{1... | collective-permute-start | bytes 196616 | tf_op jit(solution)/shard_map/ppermute | solution.py:28
  82.3 1.3 %collective-permute-start.24 = (bf16[2,128,128]{2,1,0:T(8,128)(2,1)S(1)}, bf16[2,128,128]{2,1,0:T(8,128)(2,1)S(1)}, u32[]{:S(2)}, u32[]{:S(2)}) collective-permute-start(bf16[2,128,128]{2,1,0:T(8,128)(2,1)S(1)} %shard_map.170.refs_0_), channel_id=1, source_target_pairs={{0,1},{1,0},{2,3},{3,2},{4,5},{5,4},{6,7},{7,6},{8,9},{9,8},{10,11... | collective-permute-start | bytes 196616 | tf_op jit(solution)/shard_map/ppermute | solution.py:28
  (7 other events, 5.0 us)

commit v7 on v6

--- a/solution.py
+++ b/solution.py
@@ -41,6 +41,16 @@
 
 def spread_any(value):
     return [value] + [swap(value, "feat", step) for step in reversed(peers("feat"))]
+
+
+def halving(pairs):
+    count = lax.axis_size("feat")
+    bits = [1 << n for n in range(count.bit_length() - 1)]
+    for near, far in zip(bits, reversed(bits)):
+        sums = [(a.astype(F32) + b.astype(F32)).astype(BF16) for a, b in pairs]
+        got = [swap(value, "feat", count - bit) for value, bit in zip(sums, (near, far))]
+        pairs = list(zip(sums, got))
+    return pairs
 
 
 def exchange(sends):
@@ -434,10 +444,11 @@
         other[n] = jnp.where(first, odd, even).astype(BF16)
 
 
-def scaled_body(scales, *refs):
-    *blocks, out = refs
-    for n in range(out.shape[0]):
-        out[n] = (total([b[n] for b in blocks]) * scales[...]).astype(BF16)
+def scaled_body(scales, even, even_got, odd, odd_got, out):
+    count = even.shape[0]
+    for at, pair in ((0, (even, even_got)), (count, (odd, odd_got))):
+        for n in range(count):
+            out[at + n] = (total([b[n] for b in pair]) * scales[...]).astype(BF16)
 
 
 def finish(ranges, place, acc, blocks, passed, enc, weight_scale, middle, own, other, parts):
@@ -658,10 +669,11 @@
                 [low, value_rows, *carried],
                 flops=2 * rows * value_rows.size,
             )
-            part = (own + swap(other, "tok", 1).astype(F32)).astype(BF16)
-            blocks = spread_any(part)
-            rest = handed_on(after(rest, low))
-            mine = kernel_call(scaled_body, shape(ranges, rows, half, dtype=BF16), [], [scales, *blocks])
+            got = swap(other, "tok", 1).astype(F32)
+            parts = halving([(own[: ranges // 2], got[: ranges // 2]), (own[ranges // 2 :], got[ranges // 2 :])])
+            mine = kernel_call(
+                scaled_body, shape(ranges, rows, half, dtype=BF16), [], [scales, *parts[0], *parts[1]]
+            )
             code = functools.partial(later_code_body, ranges, per_group)
             scalars, given = [], [mine, swap(mine, "tok", 1), low, rest, mixing, *packed]
         middle, own, other = kernel_call(
@@ -718,6 +730,7 @@
                 [mine, also, dec_cols, made[3], *links],
                 flops=2 * rows * dec_cols.size,
             )
+            rest = handed_on(rest)
     return kept[0].T[None, :, None, :], kept[1][None]
 
 
@@ -728,7 +741,7 @@
         and value_proj.shape[3] == out_proj.shape[2]
         and value_proj.shape[3] == 2 * enc_bias.shape[1] == 2 * residual_in.shape[0]
         and residual_in.shape[2] <= residual_in.shape[0] * (2 + lax.axis_size("feat") // 2)
-        and lax.axis_size("feat") % 2 == 0
+        and lax.axis_size("feat") in (1 << n for n in range(1, 16))
         and lax.axis_size("tok") == lax.axis_size("groups") == 2
     )
     run = tiled if whole else plain

time: 84.9 us -> 84.4 us (level)
    ppermute x23 -> x24, waiting for transfers between devices: 36.5 us -> 36 us  [swap(): lax.ppermute(value, axis, [(s, partner(s, step, count)) for s in range(co...]
    ppermute x23 -> x24, starting transfers between devices: 25.8 us -> 25.8 us  [swap(): lax.ppermute(value, axis, [(s, partner(s, step, count)) for s in range(co...]
  transfers between devices with their start and end apart: 25 -> 26, of which waited for: 17 -> 19; matrix products, arithmetic and copies ran while one was open for 0% -> 0% of each run, Pallas kernels for 1% -> 1%
where the time goes in v7:
time: 84.4 us; the launch traced here: 84.1 us
  waiting for transfers between devices  39.7 us (47%)
  starting transfers between devices  28.9 us (34%)
  Pallas kernels  8.75 us (10%)
  local copies, waits for them, and re-layouts  5.04 us (6%)
  between operations  1.53 us (2%)
    ppermute x24, waiting for transfers between devices, swap(): lax.ppermute(value, axis, [(s, partner(s, step, count)) for s in range(co...  36 us
    ppermute x24, starting transfers between devices, swap(): lax.ppermute(value, axis, [(s, partner(s, step, count)) for s in range(co...  25.8 us
    pallas_call x13, Pallas kernels, kernel_call(): pl.pallas_call(body, out_shape=tuple(kept) if many else outs, in_specs=[p...  6.76 us
    unnamed x28, local copies, waits for them, and re-layouts  5.04 us
    ppermute x2, waiting for transfers between devices, handed_on(): lax.ppermute(value, 'layer', [(n, (n + 1) % layers) for n in range(layers)])  3.71 us
    ppermute x2, starting transfers between devices, handed_on(): lax.ppermute(value, 'layer', [(n, (n + 1) % layers) for n in range(layers)])  3.13 us
    pallas_call x1, Pallas kernels, tiled(): pl.pallas_call(functools.partial(start_body, ranges), out_shape=(shape(wi...  1.99 us
  transfers between devices with their start and end apart: 26, of which 19 were waited for; matrix products, arithmetic and copies ran while one was open for 0% of the time, Pallas kernels for 1%

profile of v7, /device:TPU:0, one launch (start us, length us, event | category | flops | bytes accessed | tf_op | source)
XLA Modules:
  0.0 84.1 jit_solution(12341885482501131488)
XLA Ops:
  0.7 2.0 %shard_map.158 = (bf16[672,128]{1,0:T(8,128)(2,1)}, bf16[672,128]{1,0:T(8,128)(2,1)}, bf16[672,128]{1,0:T(8,128)(2,1)}) custom-call(f32[448,128]{1,0:T(8,128)} %bitcast.37, bf16[1792,256]{1,0:T(8,128)(2,1)} %bitcast.24, bf16[1792,128]{1,0:T(8,128)(2,1)} %bitcast.34), custom_call_target="tpu_custom_call" | custom-call | tf_op jit(solution)/shard_map/pallas_call | solution.py:613
  2.7 5.1 %collective-permute-start = (bf16[672,128]{1,0:T(8,128)(2,1)}, bf16[672,128]{1,0:T(8,128)(2,1)S(1)}, u32[]{:S(2)}, u32[]{:S(2)}) collective-permute-start(bf16[672,128]{1,0:T(8,128)(2,1)} %get-tuple-element.38), channel_id=1, source_target_pairs={{0,12},{4,8},{8,4},{12,0},{1,13},{5,9},{9,5},{13,1},{2,14},{6,10},... | collective-permute-start | bytes 516104 | tf_op jit(solution)/shard_map/ppermute | solution.py:28
  14.8 7.8 %collective-permute-done.1.refs_2_.refs_5_.refs_1_ = bf16[672,128]{1,0:T(8,128)(2,1)S(1)} collective-permute-done((bf16[672,128]{1,0:T(8,128)(2,1)}, bf16[672,128]{1,0:T(8,128)(2,1)S(1)}, u32[]{:S(2)}, u32[]{:S(2)}) %collective-permute-start.1) | collective-permute-done | bytes 172064 | tf_op jit(solution)/shard_map/ppermute | solution.py:28
  23.0 1.6 %collective-permute-start.7 = (bf16[672,128]{1,0:T(8,128)(2,1)S(1)}, bf16[672,128]{1,0:T(8,128)(2,1)S(1)}, u32[]{:S(2)}, u32[]{:S(2)}) collective-permute-start(bf16[672,128]{1,0:T(8,128)(2,1)S(1)} %get-tuple-element.52), channel_id=1, source_target_pairs={{0,16},{16,0},{1,17},{17,1},{2,18},{18,2},{3,19},{19,3},{4,20},{20... | collective-permute-start | bytes 516104 | tf_op jit(solution)/shard_map/ppermute | solution.py:28
  24.7 2.5 %collective-permute-start.4 = (bf16[256,128]{1,0:T(8,128)(2,1)S(1)}, bf16[256,128]{1,0:T(8,128)(2,1)S(1)}, u32[]{:S(2)}, u32[]{:S(2)}) collective-permute-start(bf16[256,128]{1,0:T(8,128)(2,1)S(1)} %get-tuple-element.49), channel_id=1, source_target_pairs={{0,12},{4,8},{8,4},{12,0},{1,13},{5,9},{9,5},{13,1},{2,14},{6,10},... | collective-permute-start | bytes 196616 | tf_op jit(solution)/shard_map/ppermute | solution.py:28
  27.2 1.9 %collective-permute-start.6 = (bf16[256,128]{1,0:T(8,128)(2,1)S(1)}, bf16[256,128]{1,0:T(8,128)(2,1)S(1)}, u32[]{:S(2)}, u32[]{:S(2)}) collective-permute-start(bf16[256,128]{1,0:T(8,128)(2,1)S(1)} %get-tuple-element.51), channel_id=1, source_target_pairs={{0,4},{4,0},{8,12},{12,8},{1,5},{5,1},{9,13},{13,9},{2,6},{6,2},{1... | collective-permute-start | bytes 196616 | tf_op jit(solution)/shard_map/ppermute | solution.py:28
  29.8 1.7 %collective-permute-done.4.refs_1_.refs_3_ = bf16[256,128]{1,0:T(8,128)(2,1)S(1)} collective-permute-done((bf16[256,128]{1,0:T(8,128)(2,1)S(1)}, bf16[256,128]{1,0:T(8,128)(2,1)S(1)}, u32[]{:S(2)}, u32[]{:S(2)}) %collective-permute-start.4) | collective-permute-done | bytes 65568 | tf_op jit(solution)/shard_map/ppermute | solution.py:28
  31.5 2.0 %collective-permute-done.5.refs_2_.refs_4_ = bf16[256,128]{1,0:T(8,128)(2,1)S(1)} collective-permute-done((bf16[256,128]{1,0:T(8,128)(2,1)S(1)}, bf16[256,128]{1,0:T(8,128)(2,1)S(1)}, u32[]{:S(2)}, u32[]{:S(2)}) %collective-permute-start.5) | collective-permute-done | bytes 65568 | tf_op jit(solution)/shard_map/ppermute | solution.py:28
  33.5 1.7 %shard_map.162 = (f32[448,128]{1,0:T(8,128)S(1)}, f32[2,128,128]{2,1,0:T(8,128)S(1)}, bf16[2,128,128]{2,1,0:T(8,128)(2,1)S(1)}) custom-call(bf16[256,128]{1,0:T(8,128)(2,1)S(1)} %get-tuple-element.48.refs_0_, bf16[256,128]{1,0:T(8,128)(2,1)S(1)} %collective-permute-done.4.refs_1_.refs_3_, bf16[256,128]{1,0:T(8,128)(2,1)S(1)} %collective-permute-done.5.refs_2_.refs_4_, ...), custom_call_target="tpu_custom_call" | custom-call | flops 293601280 | bytes 4162048 | tf_op jit(solution)/shard_map/pallas_call | solution.py:266
  35.4 1.2 %collective-permute-done.8.got = bf16[2,128,128]{2,1,0:T(8,128)(2,1)S(1)} collective-permute-done((bf16[2,128,128]{2,1,0:T(8,128)(2,1)S(1)}, bf16[2,128,128]{2,1,0:T(8,128)(2,1)S(1)}, u32[]{:S(2)}, u32[]{:S(2)}) %collective-permute-start.8) | collective-permute-done | bytes 65568 | tf_op jit(solution)/shard_map/ppermute | solution.py:28
  36.6 2.5 %collective-permute-start.9 = (bf16[272,128]{1,0:T(8,128)(2,1)S(1)}, bf16[272,128]{1,0:T(8,128)(2,1)S(1)}, u32[]{:S(2)}, u32[]{:S(2)}) collective-permute-start(bf16[272,128]{1,0:T(8,128)(2,1)S(1)} %get-tuple-element.58), channel_id=1, source_target_pairs={{0,12},{4,8},{8,4},{12,0},{1,13},{5,9},{9,5},{13,1},{2,14},{6,10},... | collective-permute-start | bytes 208904 | tf_op jit(solution)/shard_map/ppermute | solution.py:28
  39.2 1.9 %collective-permute-start.11 = (bf16[272,128]{1,0:T(8,128)(2,1)S(1)}, bf16[272,128]{1,0:T(8,128)(2,1)S(1)}, u32[]{:S(2)}, u32[]{:S(2)}) collective-permute-start(bf16[272,128]{1,0:T(8,128)(2,1)S(1)} %get-tuple-element.60), channel_id=1, source_target_pairs={{0,4},{4,0},{8,12},{12,8},{1,5},{5,1},{9,13},{13,9},{2,6},{6,2},{1... | collective-permute-start | bytes 208904 | tf_op jit(solution)/shard_map/ppermute | solution.py:28
  41.1 2.5 %collective-permute-done.9.refs_1_.refs_5_.refs_6_ = bf16[272,128]{1,0:T(8,128)(2,1)S(1)} collective-permute-done((bf16[272,128]{1,0:T(8,128)(2,1)S(1)}, bf16[272,128]{1,0:T(8,128)(2,1)S(1)}, u32[]{:S(2)}, u32[]{:S(2)}) %collective-permute-start.9) | collective-permute-done | bytes 69664 | tf_op jit(solution)/shard_map/ppermute | solution.py:28
  43.6 2.1 %collective-permute-done.10.refs_2_.refs_6_.refs_7_ = bf16[272,128]{1,0:T(8,128)(2,1)S(1)} collective-permute-done((bf16[272,128]{1,0:T(8,128)(2,1)S(1)}, bf16[272,128]{1,0:T(8,128)(2,1)S(1)}, u32[]{:S(2)}, u32[]{:S(2)}) %collective-permute-start.10) | collective-permute-done | bytes 69664 | tf_op jit(solution)/shard_map/ppermute | solution.py:28
  45.9 1.2 %collective-permute-done.12.refs_1_.also = bf16[2,128,128]{2,1,0:T(8,128)(2,1)S(1)} collective-permute-done((bf16[2,128,128]{2,1,0:T(8,128)(2,1)S(1)}, bf16[2,128,128]{2,1,0:T(8,128)(2,1)S(1)}, u32[]{:S(2)}, u32[]{:S(2)}) %collective-permute-start.12) | collective-permute-done | bytes 65568 | tf_op jit(solution)/shard_map/ppermute | solution.py:28
  47.4 1.6 %collective-permute-start.13 = (bf16[448,128]{1,0:T(8,128)(2,1)S(1)}, bf16[448,128]{1,0:T(8,128)(2,1)S(1)}, u32[]{:S(2)}, u32[]{:S(2)}) collective-permute-start(bf16[448,128]{1,0:T(8,128)(2,1)S(1)} %get-tuple-element.63), channel_id=1, source_target_pairs={{0,2},{2,0},{1,3},{3,1},{4,6},{6,4},{5,7},{7,5},{8,10},{10,8},{9,1... | collective-permute-start | bytes 344072 | tf_op jit(solution)/shard_map/ppermute | solution.py:608
  49.0 3.7 %collective-permute-done.13.low = bf16[448,128]{1,0:T(8,128)(2,1)S(1)} collective-permute-done((bf16[448,128]{1,0:T(8,128)(2,1)S(1)}, bf16[448,128]{1,0:T(8,128)(2,1)S(1)}, u32[]{:S(2)}, u32[]{:S(2)}) %collective-permute-start.13) | collective-permute-done | bytes 114720 | tf_op jit(solution)/shard_map/ppermute | solution.py:608
  53.2 1.3 %collective-permute-done.14 = bf16[4,128,128]{2,1,0:T(8,128)(2,1)S(1)} collective-permute-done((bf16[4,128,128]{2,1,0:T(8,128)(2,1)S(1)}, bf16[4,128,128]{2,1,0:T(8,128)(2,1)S(1)}, u32[]{:S(2)}, u32[]{:S(2)}) %collective-permute-start.14) | collective-permute-done | bytes 131104 | tf_op jit(solution)/shard_map/ppermute | solution.py:28
  55.8 1.6 %collective-permute-start.20 = (bf16[2,448,128]{2,1,0:T(8,128)(2,1)S(1)}, bf16[2,448,128]{2,1,0:T(8,128)(2,1)S(1)}, u32[]{:S(2)}, u32[]{:S(2)}) collective-permute-start(bf16[2,448,128]{2,1,0:T(8,128)(2,1)S(1)} %shard_map.168), channel_id=1, source_target_pairs={{0,2},{2,0},{1,3},{3,1},{4,6},{6,4},{5,7},{7,5},{8,10},{10,8},{9,1... | collective-permute-start | bytes 688136 | tf_op jit(solution)/shard_map/ppermute | solution.py:608
  57.4 2.2 %collective-permute-start.15 = (bf16[2,128,128]{2,1,0:T(8,128)(2,1)S(1)}, bf16[2,128,128]{2,1,0:T(8,128)(2,1)S(1)}, u32[]{:S(2)}, u32[]{:S(2)}) collective-permute-start(bf16[2,128,128]{2,1,0:T(8,128)(2,1)S(1)} %get-tuple-element.75), channel_id=1, source_target_pairs={{0,4},{4,0},{8,12},{12,8},{1,5},{5,1},{9,13},{13,9},{2,6},{6,2},{1... | collective-permute-start | bytes 196616 | tf_op jit(solution)/shard_map/ppermute | solution.py:28
  59.6 1.7 %collective-permute-done.17 = bf16[2,128,128]{2,1,0:T(8,128)(2,1)S(1)} collective-permute-done((bf16[2,128,128]{2,1,0:T(8,128)(2,1)S(1)}, bf16[2,128,128]{2,1,0:T(8,128)(2,1)S(1)}, u32[]{:S(2)}, u32[]{:S(2)}) %collective-permute-start.17) | collective-permute-done | bytes 65568 | tf_op jit(solution)/shard_map/ppermute | solution.py:28
  61.3 1.2 %collective-permute-done.15 = bf16[2,128,128]{2,1,0:T(8,128)(2,1)S(1)} collective-permute-done((bf16[2,128,128]{2,1,0:T(8,128)(2,1)S(1)}, bf16[2,128,128]{2,1,0:T(8,128)(2,1)S(1)}, u32[]{:S(2)}, u32[]{:S(2)}) %collective-permute-start.15) | collective-permute-done | bytes 65568 | tf_op jit(solution)/shard_map/ppermute | solution.py:28
  62.5 1.3 %collective-permute-start.16 = (bf16[2,128,128]{2,1,0:T(8,128)(2,1)S(1)}, bf16[2,128,128]{2,1,0:T(8,128)(2,1)S(1)}, u32[]{:S(2)}, u32[]{:S(2)}) collective-permute-start(bf16[2,128,128]{2,1,0:T(8,128)(2,1)S(1)} %add_convert_fusion.2.even), channel_id=1, source_target_pairs={{0,8},{4,12},{8,0},{12,4},{1,9},{5,13},{9,1},{13,5},{2,10},{6,14},... | collective-permute-start | bytes 196616 | tf_op jit(solution)/shard_map/ppermute | solution.py:28
  63.8 1.8 %collective-permute-done.18.odd_got = bf16[2,128,128]{2,1,0:T(8,128)(2,1)S(1)} collective-permute-done((bf16[2,128,128]{2,1,0:T(8,128)(2,1)S(1)}, bf16[2,128,128]{2,1,0:T(8,128)(2,1)S(1)}, u32[]{:S(2)}, u32[]{:S(2)}) %collective-permute-start.18) | collective-permute-done | bytes 65568 | tf_op jit(solution)/shard_map/ppermute | solution.py:28
  65.6 2.3 %collective-permute-done.16.even_got = bf16[2,128,128]{2,1,0:T(8,128)(2,1)S(1)} collective-permute-done((bf16[2,128,128]{2,1,0:T(8,128)(2,1)S(1)}, bf16[2,128,128]{2,1,0:T(8,128)(2,1)S(1)}, u32[]{:S(2)}, u32[]{:S(2)}) %collective-permute-start.16) | collective-permute-done | bytes 65568 | tf_op jit(solution)/shard_map/ppermute | solution.py:28
  68.1 1.3 %collective-permute-done.19.also = bf16[4,128,128]{2,1,0:T(8,128)(2,1)S(1)} collective-permute-done((bf16[4,128,128]{2,1,0:T(8,128)(2,1)S(1)}, bf16[4,128,128]{2,1,0:T(8,128)(2,1)S(1)}, u32[]{:S(2)}, u32[]{:S(2)}) %collective-permute-start.19) | collective-permute-done | bytes 131104 | tf_op jit(solution)/shard_map/ppermute | solution.py:28
  69.4 1.7 %shard_map.169 = (f32[448,128]{1,0:T(8,128)S(1)}, f32[2,128,128]{2,1,0:T(8,128)S(1)}, bf16[2,128,128]{2,1,0:T(8,128)(2,1)S(1)}) custom-call(bf16[4,128,128]{2,1,0:T(8,128)(2,1)S(1)} %shard_map.167.mine, bf16[4,128,128]{2,1,0:T(8,128)(2,1)S(1)} %collective-permute-done.19.also, bf16[448,128]{1,0:T(8,128)(2,1)S(1)} %collective-permute-done.13.low, ...), custom_call_target="tpu_custom_call" | custom-call | flops 293601280 | bytes 4276736 | tf_op jit(solution)/shard_map/pallas_call | solution.py:266
  72.5 2.6 %collective-permute-start.24 = (bf16[256,128]{1,0:T(8,128)(2,1)S(1)}, bf16[256,128]{1,0:T(8,128)(2,1)S(1)}, u32[]{:S(2)}, u32[]{:S(2)}) collective-permute-start(bf16[256,128]{1,0:T(8,128)(2,1)S(1)} %bitcast.43), channel_id=1, source_target_pairs={{0,12},{4,8},{8,4},{12,0},{1,13},{5,9},{9,5},{13,1},{2,14},{6,10},... | collective-permute-start | bytes 196616 | tf_op jit(solution)/shard_map/ppermute | solution.py:28
  75.3 1.7 %collective-permute-start.22 = (bf16[256,128]{1,0:T(8,128)(2,1)S(1)}, bf16[256,128]{1,0:T(8,128)(2,1)S(1)}, u32[]{:S(2)}, u32[]{:S(2)}) collective-permute-start(bf16[256,128]{1,0:T(8,128)(2,1)S(1)} %bitcast.45), channel_id=1, source_target_pairs={{0,4},{4,0},{8,12},{12,8},{1,5},{5,1},{9,13},{13,9},{2,6},{6,2},{1... | collective-permute-start | bytes 196616 | tf_op jit(solution)/shard_map/ppermute | solution.py:28
  76.9 2.4 %collective-permute-done.24.refs_3_ = bf16[256,128]{1,0:T(8,128)(2,1)S(1)} collective-permute-done((bf16[256,128]{1,0:T(8,128)(2,1)S(1)}, bf16[256,128]{1,0:T(8,128)(2,1)S(1)}, u32[]{:S(2)}, u32[]{:S(2)}) %collective-permute-start.24) | collective-permute-done | bytes 65568 | tf_op jit(solution)/shard_map/ppermute | solution.py:28
  79.3 2.4 %collective-permute-done.23.refs_2_ = bf16[256,128]{1,0:T(8,128)(2,1)S(1)} collective-permute-done((bf16[256,128]{1,0:T(8,128)(2,1)S(1)}, bf16[256,128]{1,0:T(8,128)(2,1)S(1)}, u32[]{:S(2)}, u32[]{:S(2)}) %collective-permute-start.23) | collective-permute-done | bytes 65568 | tf_op jit(solution)/shard_map/ppermute | solution.py:28
  81.9 1.2 %collective-permute-done.25.refs_1_ = bf16[2,128,128]{2,1,0:T(8,128)(2,1)S(1)} collective-permute-done((bf16[2,128,128]{2,1,0:T(8,128)(2,1)S(1)}, bf16[2,128,128]{2,1,0:T(8,128)(2,1)S(1)}, u32[]{:S(2)}, u32[]{:S(2)}) %collective-permute-start.25) | collective-permute-done | bytes 65568 | tf_op jit(solution)/shard_map/ppermute | solution.py:28
  (67 shorter events, 12.8 us)
Async XLA Ops:
  0.6 22.0 %copy-start = (bf16[1,1,1792,256]{3,2,1,0:T(8,128)(2,1)S(1)}, bf16[1,1,1792,256]{3,2,1,0:T(8,128)(2,1)}, u32[]{:S(2)}) copy-start(bf16[1,1,1792,256]{3,2,1,0:T(8,128)(2,1)} %param.20) | copy-start | bytes 2752516
  0.6 22.0 %copy-start.4 = (f32[128,1,448]{0,2,1:T(8,128)S(1)}, f32[128,1,448]{0,2,1:T(8,128)}, u32[]{:S(2)}) copy-start(f32[128,1,448]{0,2,1:T(8,128)} %param.15) | copy-start | bytes 688132
  0.6 32.9 %copy-start.9 = (f32[1,128]{1,0:T(1,128)S(1)}, f32[1,128]{1,0:T(1,128)}, u32[]{:S(2)}) copy-start(f32[1,128]{1,0:T(1,128)} %refs_6_.1) | copy-start | bytes 1540
  2.7 30.9 %copy-start.2 = (bf16[1,4,256,2,1,448]{2,5,4,3,1,0:T(8,128)(2,1)S(1)}, bf16[1,4,256,2,1,448]{2,5,4,3,1,0:T(8,128)(2,1)}, u32[]{:S(2)}) copy-start(bf16[1,4,256,2,1,448]{2,5,4,3,1,0:T(8,128)(2,1)} %param.21) | copy-start | bytes 5505028
  2.7 30.8 %copy-start.3 = (bf16[1,1,1792,128]{3,2,1,0:T(8,128)(2,1)S(1)}, bf16[1,1,1792,128]{3,2,1,0:T(8,128)(2,1)}, u32[]{:S(2)}) copy-start(bf16[1,1,1792,128]{3,2,1,0:T(8,128)(2,1)} %param.22) | copy-start | bytes 1376260
  2.7 12.1 %collective-permute-start = (bf16[672,128]{1,0:T(8,128)(2,1)}, bf16[672,128]{1,0:T(8,128)(2,1)S(1)}, u32[]{:S(2)}, u32[]{:S(2)}) collective-permute-start(bf16[672,128]{1,0:T(8,128)(2,1)} %get-tuple-element.38), channel_id=1, source_target_pairs={{0,12},{4,8},{8,4},{12,0},{1,13},{5,9},{9,5},{13,1},{2,14},{6,10},... | collective-permute-start | bytes 516104 | tf_op jit(solution)/shard_map/ppermute | solution.py:28
  7.8 14.8 %collective-permute-start.1 = (bf16[672,128]{1,0:T(8,128)(2,1)}, bf16[672,128]{1,0:T(8,128)(2,1)S(1)}, u32[]{:S(2)}, u32[]{:S(2)}) collective-permute-start(bf16[672,128]{1,0:T(8,128)(2,1)} %get-tuple-element.45), channel_id=1, source_target_pairs={{0,8},{4,12},{8,0},{12,4},{1,9},{5,13},{9,1},{13,5},{2,10},{6,14},... | collective-permute-start | bytes 516104 | tf_op jit(solution)/shard_map/ppermute | solution.py:28
  7.8 14.8 %collective-permute-start.2 = (bf16[672,128]{1,0:T(8,128)(2,1)}, bf16[672,128]{1,0:T(8,128)(2,1)S(1)}, u32[]{:S(2)}, u32[]{:S(2)}) collective-permute-start(bf16[672,128]{1,0:T(8,128)(2,1)} %get-tuple-element.46), channel_id=1, source_target_pairs={{0,4},{4,0},{8,12},{12,8},{1,5},{5,1},{9,13},{13,9},{2,6},{6,2},{1... | collective-permute-start | bytes 516104 | tf_op jit(solution)/shard_map/ppermute | solution.py:28
  22.9 1.7 %collective-permute-start.3 = (f32[128,256]{1,0:T(8,128)S(1)}, f32[128,256]{1,0:T(8,128)S(1)}, u32[]{:S(2)}, u32[]{:S(2)}) collective-permute-start(f32[128,256]{1,0:T(8,128)S(1)} %get-tuple-element.47.own), channel_id=1, source_target_pairs={{0,1},{1,0},{2,3},{3,2},{4,5},{5,4},{6,7},{7,6},{8,9},{9,8},{10,11... | collective-permute-start | bytes 393224 | tf_op jit(solution)/shard_map/ppermute | solution.py:28
  23.0 6.8 %collective-permute-start.7 = (bf16[672,128]{1,0:T(8,128)(2,1)S(1)}, bf16[672,128]{1,0:T(8,128)(2,1)S(1)}, u32[]{:S(2)}, u32[]{:S(2)}) collective-permute-start(bf16[672,128]{1,0:T(8,128)(2,1)S(1)} %get-tuple-element.52), channel_id=1, source_target_pairs={{0,16},{16,0},{1,17},{17,1},{2,18},{18,2},{3,19},{19,3},{4,20},{20... | collective-permute-start | bytes 516104 | tf_op jit(solution)/shard_map/ppermute | solution.py:28
  24.7 6.8 %collective-permute-start.4 = (bf16[256,128]{1,0:T(8,128)(2,1)S(1)}, bf16[256,128]{1,0:T(8,128)(2,1)S(1)}, u32[]{:S(2)}, u32[]{:S(2)}) collective-permute-start(bf16[256,128]{1,0:T(8,128)(2,1)S(1)} %get-tuple-element.49), channel_id=1, source_target_pairs={{0,12},{4,8},{8,4},{12,0},{1,13},{5,9},{9,5},{13,1},{2,14},{6,10},... | collective-permute-start | bytes 196616 | tf_op jit(solution)/shard_map/ppermute | solution.py:28
  27.2 6.3 %collective-permute-start.5 = (bf16[256,128]{1,0:T(8,128)(2,1)S(1)}, bf16[256,128]{1,0:T(8,128)(2,1)S(1)}, u32[]{:S(2)}, u32[]{:S(2)}) collective-permute-start(bf16[256,128]{1,0:T(8,128)(2,1)S(1)} %get-tuple-element.50), channel_id=1, source_target_pairs={{0,8},{4,12},{8,0},{12,4},{1,9},{5,13},{9,1},{13,5},{2,10},{6,14},... | collective-permute-start | bytes 196616 | tf_op jit(solution)/shard_map/ppermute | solution.py:28
  27.2 6.3 %collective-permute-start.6 = (bf16[256,128]{1,0:T(8,128)(2,1)S(1)}, bf16[256,128]{1,0:T(8,128)(2,1)S(1)}, u32[]{:S(2)}, u32[]{:S(2)}) collective-permute-start(bf16[256,128]{1,0:T(8,128)(2,1)S(1)} %get-tuple-element.51), channel_id=1, source_target_pairs={{0,4},{4,0},{8,12},{12,8},{1,5},{5,1},{9,13},{13,9},{2,6},{6,2},{1... | collective-permute-start | bytes 196616 | tf_op jit(solution)/shard_map/ppermute | solution.py:28
  35.2 11.9 %copy-start.1 = (bf16[1,2,512,1,448]{2,4,3,1,0:T(8,128)(2,1)S(1)}, bf16[1,2,512,1,448]{2,4,3,1,0:T(8,128)(2,1)}, u32[]{:S(2)}) copy-start(bf16[1,2,512,1,448]{2,4,3,1,0:T(8,128)(2,1)} %param.24) | copy-start | bytes 2752516
  35.3 1.3 %collective-permute-start.8 = (bf16[2,128,128]{2,1,0:T(8,128)(2,1)S(1)}, bf16[2,128,128]{2,1,0:T(8,128)(2,1)S(1)}, u32[]{:S(2)}, u32[]{:S(2)}) collective-permute-start(bf16[2,128,128]{2,1,0:T(8,128)(2,1)S(1)} %get-tuple-element.55), channel_id=1, source_target_pairs={{0,1},{1,0},{2,3},{3,2},{4,5},{5,4},{6,7},{7,6},{8,9},{9,8},{10,11... | collective-permute-start | bytes 196616 | tf_op jit(solution)/shard_map/ppermute | solution.py:28
  36.6 7.0 %collective-permute-start.9 = (bf16[272,128]{1,0:T(8,128)(2,1)S(1)}, bf16[272,128]{1,0:T(8,128)(2,1)S(1)}, u32[]{:S(2)}, u32[]{:S(2)}) collective-permute-start(bf16[272,128]{1,0:T(8,128)(2,1)S(1)} %get-tuple-element.58), channel_id=1, source_target_pairs={{0,12},{4,8},{8,4},{12,0},{1,13},{5,9},{9,5},{13,1},{2,14},{6,10},... | collective-permute-start | bytes 208904 | tf_op jit(solution)/shard_map/ppermute | solution.py:28
  39.2 6.5 %collective-permute-start.10 = (bf16[272,128]{1,0:T(8,128)(2,1)S(1)}, bf16[272,128]{1,0:T(8,128)(2,1)S(1)}, u32[]{:S(2)}, u32[]{:S(2)}) collective-permute-start(bf16[272,128]{1,0:T(8,128)(2,1)S(1)} %get-tuple-element.59), channel_id=1, source_target_pairs={{0,8},{4,12},{8,0},{12,4},{1,9},{5,13},{9,1},{13,5},{2,10},{6,14},... | collective-permute-start | bytes 208904 | tf_op jit(solution)/shard_map/ppermute | solution.py:28
  39.2 6.5 %collective-permute-start.11 = (bf16[272,128]{1,0:T(8,128)(2,1)S(1)}, bf16[272,128]{1,0:T(8,128)(2,1)S(1)}, u32[]{:S(2)}, u32[]{:S(2)}) collective-permute-start(bf16[272,128]{1,0:T(8,128)(2,1)S(1)} %get-tuple-element.60), channel_id=1, source_target_pairs={{0,4},{4,0},{8,12},{12,8},{1,5},{5,1},{9,13},{13,9},{2,6},{6,2},{1... | collective-permute-start | bytes 208904 | tf_op jit(solution)/shard_map/ppermute | solution.py:28
  45.8 1.3 %collective-permute-start.12 = (bf16[2,128,128]{2,1,0:T(8,128)(2,1)S(1)}, bf16[2,128,128]{2,1,0:T(8,128)(2,1)S(1)}, u32[]{:S(2)}, u32[]{:S(2)}) collective-permute-start(bf16[2,128,128]{2,1,0:T(8,128)(2,1)S(1)} %shard_map.164.refs_0_.mine), channel_id=1, source_target_pairs={{0,1},{1,0},{2,3},{3,2},{4,5},{5,4},{6,7},{7,6},{8,9},{9,8},{10,11... | collective-permute-start | bytes 196616 | tf_op jit(solution)/shard_map/ppermute | solution.py:28
  47.4 5.3 %collective-permute-start.13 = (bf16[448,128]{1,0:T(8,128)(2,1)S(1)}, bf16[448,128]{1,0:T(8,128)(2,1)S(1)}, u32[]{:S(2)}, u32[]{:S(2)}) collective-permute-start(bf16[448,128]{1,0:T(8,128)(2,1)S(1)} %get-tuple-element.63), channel_id=1, source_target_pairs={{0,2},{2,0},{1,3},{3,1},{4,6},{6,4},{5,7},{7,5},{8,10},{10,8},{9,1... | collective-permute-start | bytes 344072 | tf_op jit(solution)/shard_map/ppermute | solution.py:608
  53.1 1.4 %collective-permute-start.14 = (bf16[4,128,128]{2,1,0:T(8,128)(2,1)S(1)}, bf16[4,128,128]{2,1,0:T(8,128)(2,1)S(1)}, u32[]{:S(2)}, u32[]{:S(2)}) collective-permute-start(bf16[4,128,128]{2,1,0:T(8,128)(2,1)S(1)} %get-tuple-element.65), channel_id=1, source_target_pairs={{0,1},{1,0},{2,3},{3,2},{4,5},{5,4},{6,7},{7,6},{8,9},{9,8},{10,11... | collective-permute-start | bytes 393224 | tf_op jit(solution)/shard_map/ppermute | solution.py:28
  54.6 6.6 %collective-permute-start.17 = (bf16[2,128,128]{2,1,0:T(8,128)(2,1)S(1)}, bf16[2,128,128]{2,1,0:T(8,128)(2,1)S(1)}, u32[]{:S(2)}, u32[]{:S(2)}) collective-permute-start(bf16[2,128,128]{2,1,0:T(8,128)(2,1)S(1)} %get-tuple-element.74), channel_id=1, source_target_pairs={{0,8},{4,12},{8,0},{12,4},{1,9},{5,13},{9,1},{13,5},{2,10},{6,14},... | collective-permute-start | bytes 196616 | tf_op jit(solution)/shard_map/ppermute | solution.py:28
  55.8 12.2 %collective-permute-start.20 = (bf16[2,448,128]{2,1,0:T(8,128)(2,1)S(1)}, bf16[2,448,128]{2,1,0:T(8,128)(2,1)S(1)}, u32[]{:S(2)}, u32[]{:S(2)}) collective-permute-start(bf16[2,448,128]{2,1,0:T(8,128)(2,1)S(1)} %shard_map.168), channel_id=1, source_target_pairs={{0,2},{2,0},{1,3},{3,1},{4,6},{6,4},{5,7},{7,5},{8,10},{10,8},{9,1... | collective-permute-start | bytes 688136 | tf_op jit(solution)/shard_map/ppermute | solution.py:608
  57.4 5.1 %collective-permute-start.15 = (bf16[2,128,128]{2,1,0:T(8,128)(2,1)S(1)}, bf16[2,128,128]{2,1,0:T(8,128)(2,1)S(1)}, u32[]{:S(2)}, u32[]{:S(2)}) collective-permute-start(bf16[2,128,128]{2,1,0:T(8,128)(2,1)S(1)} %get-tuple-element.75), channel_id=1, source_target_pairs={{0,4},{4,0},{8,12},{12,8},{1,5},{5,1},{9,13},{13,9},{2,6},{6,2},{1... | collective-permute-start | bytes 196616 | tf_op jit(solution)/shard_map/ppermute | solution.py:28
  61.2 4.3 %collective-permute-start.18 = (bf16[2,128,128]{2,1,0:T(8,128)(2,1)S(1)}, bf16[2,128,128]{2,1,0:T(8,128)(2,1)S(1)}, u32[]{:S(2)}, u32[]{:S(2)}) collective-permute-start(bf16[2,128,128]{2,1,0:T(8,128)(2,1)S(1)} %add_convert_fusion.1.odd), channel_id=1, source_target_pairs={{0,4},{4,0},{8,12},{12,8},{1,5},{5,1},{9,13},{13,9},{2,6},{6,2},{1... | collective-permute-start | bytes 196616 | tf_op jit(solution)/shard_map/ppermute | solution.py:28
  62.5 5.4 %collective-permute-start.16 = (bf16[2,128,128]{2,1,0:T(8,128)(2,1)S(1)}, bf16[2,128,128]{2,1,0:T(8,128)(2,1)S(1)}, u32[]{:S(2)}, u32[]{:S(2)}) collective-permute-start(bf16[2,128,128]{2,1,0:T(8,128)(2,1)S(1)} %add_convert_fusion.2.even), channel_id=1, source_target_pairs={{0,8},{4,12},{8,0},{12,4},{1,9},{5,13},{9,1},{13,5},{2,10},{6,14},... | collective-permute-start | bytes 196616 | tf_op jit(solution)/shard_map/ppermute | solution.py:28
  68.0 1.4 %collective-permute-start.19 = (bf16[4,128,128]{2,1,0:T(8,128)(2,1)S(1)}, bf16[4,128,128]{2,1,0:T(8,128)(2,1)S(1)}, u32[]{:S(2)}, u32[]{:S(2)}) collective-permute-start(bf16[4,128,128]{2,1,0:T(8,128)(2,1)S(1)} %shard_map.167.mine), channel_id=1, source_target_pairs={{0,1},{1,0},{2,3},{3,2},{4,5},{5,4},{6,7},{7,6},{8,9},{9,8},{10,11... | collective-permute-start | bytes 393224 | tf_op jit(solution)/shard_map/ppermute | solution.py:28
  71.1 1.3 %collective-permute-start.21 = (bf16[2,128,128]{2,1,0:T(8,128)(2,1)S(1)}, bf16[2,128,128]{2,1,0:T(8,128)(2,1)S(1)}, u32[]{:S(2)}, u32[]{:S(2)}) collective-permute-start(bf16[2,128,128]{2,1,0:T(8,128)(2,1)S(1)} %get-tuple-element.68), channel_id=1, source_target_pairs={{0,1},{1,0},{2,3},{3,2},{4,5},{5,4},{6,7},{7,6},{8,9},{9,8},{10,11... | collective-permute-start | bytes 196616 | tf_op jit(solution)/shard_map/ppermute | solution.py:28
  72.5 6.8 %collective-permute-start.24 = (bf16[256,128]{1,0:T(8,128)(2,1)S(1)}, bf16[256,128]{1,0:T(8,128)(2,1)S(1)}, u32[]{:S(2)}, u32[]{:S(2)}) collective-permute-start(bf16[256,128]{1,0:T(8,128)(2,1)S(1)} %bitcast.43), channel_id=1, source_target_pairs={{0,12},{4,8},{8,4},{12,0},{1,13},{5,9},{9,5},{13,1},{2,14},{6,10},... | collective-permute-start | bytes 196616 | tf_op jit(solution)/shard_map/ppermute | solution.py:28
  75.1 6.6 %collective-permute-start.23 = (bf16[256,128]{1,0:T(8,128)(2,1)S(1)}, bf16[256,128]{1,0:T(8,128)(2,1)S(1)}, u32[]{:S(2)}, u32[]{:S(2)}) collective-permute-start(bf16[256,128]{1,0:T(8,128)(2,1)S(1)} %bitcast.44), channel_id=1, source_target_pairs={{0,8},{4,12},{8,0},{12,4},{1,9},{5,13},{9,1},{13,5},{2,10},{6,14},... | collective-permute-start | bytes 196616 | tf_op jit(solution)/shard_map/ppermute | solution.py:28
  75.3 6.5 %collective-permute-start.22 = (bf16[256,128]{1,0:T(8,128)(2,1)S(1)}, bf16[256,128]{1,0:T(8,128)(2,1)S(1)}, u32[]{:S(2)}, u32[]{:S(2)}) collective-permute-start(bf16[256,128]{1,0:T(8,128)(2,1)S(1)} %bitcast.45), channel_id=1, source_target_pairs={{0,4},{4,0},{8,12},{12,8},{1,5},{5,1},{9,13},{13,9},{2,6},{6,2},{1... | collective-permute-start | bytes 196616 | tf_op jit(solution)/shard_map/ppermute | solution.py:28
  81.8 1.3 %collective-permute-start.25 = (bf16[2,128,128]{2,1,0:T(8,128)(2,1)S(1)}, bf16[2,128,128]{2,1,0:T(8,128)(2,1)S(1)}, u32[]{:S(2)}, u32[]{:S(2)}) collective-permute-start(bf16[2,128,128]{2,1,0:T(8,128)(2,1)S(1)} %shard_map.170.refs_0_), channel_id=1, source_target_pairs={{0,1},{1,0},{2,3},{3,2},{4,5},{5,4},{6,7},{7,6},{8,9},{9,8},{10,11... | collective-permute-start | bytes 196616 | tf_op jit(solution)/shard_map/ppermute | solution.py:28
  (8 other events, 16.9 us)

commit v8 on v7

--- a/solution.py
+++ b/solution.py
@@ -730,6 +730,7 @@
                 [mine, also, dec_cols, made[3], *links],
                 flops=2 * rows * dec_cols.size,
             )
+            low, rest = lax.optimization_barrier((low, rest))
             rest = handed_on(rest)
     return kept[0].T[None, :, None, :], kept[1][None]
 

time: 84.4 us -> 84.1 us (level)
  no operation moved by 1% of the time
where the time goes in v8:
time: 84.1 us; the launch traced here: 83.7 us
  waiting for transfers between devices  39.1 us (46%)
  starting transfers between devices  29.1 us (35%)
  Pallas kernels  8.77 us (10%)
  local copies, waits for them, and re-layouts  5.04 us (6%)
  between operations  1.52 us (2%)
    ppermute x24, waiting for transfers between devices, swap(): lax.ppermute(value, axis, [(s, partner(s, step, count)) for s in range(co...  35.7 us
    ppermute x24, starting transfers between devices, swap(): lax.ppermute(value, axis, [(s, partner(s, step, count)) for s in range(co...  26.1 us
    pallas_call x13, Pallas kernels, kernel_call(): pl.pallas_call(body, out_shape=tuple(kept) if many else outs, in_specs=[p...  6.78 us
    unnamed x28, local copies, waits for them, and re-layouts  5.04 us
    ppermute x2, waiting for transfers between devices, handed_on(): lax.ppermute(value, 'layer', [(n, (n + 1) % layers) for n in range(layers)])  3.42 us
    ppermute x2, starting transfers between devices, handed_on(): lax.ppermute(value, 'layer', [(n, (n + 1) % layers) for n in range(layers)])  3.04 us
    pallas_call x1, Pallas kernels, tiled(): pl.pallas_call(functools.partial(start_body, ranges), out_shape=(shape(wi...  1.99 us
  transfers between devices with their start and end apart: 26, of which 19 were waited for; matrix products, arithmetic and copies ran while one was open for 0% of the time, Pallas kernels for 1%

profile of v8, /device:TPU:0, one launch (start us, length us, event | category | flops | bytes accessed | tf_op | source)
XLA Modules:
  0.0 83.7 jit_solution(12108373215457222852)
XLA Ops:
  0.7 2.0 %shard_map.158 = (bf16[672,128]{1,0:T(8,128)(2,1)}, bf16[672,128]{1,0:T(8,128)(2,1)}, bf16[672,128]{1,0:T(8,128)(2,1)}) custom-call(f32[448,128]{1,0:T(8,128)} %bitcast.37, bf16[1792,256]{1,0:T(8,128)(2,1)} %bitcast.24, bf16[1792,128]{1,0:T(8,128)(2,1)} %bitcast.34), custom_call_target="tpu_custom_call" | custom-call | tf_op jit(solution)/shard_map/pallas_call | solution.py:613
  2.7 5.1 %collective-permute-start = (bf16[672,128]{1,0:T(8,128)(2,1)}, bf16[672,128]{1,0:T(8,128)(2,1)S(1)}, u32[]{:S(2)}, u32[]{:S(2)}) collective-permute-start(bf16[672,128]{1,0:T(8,128)(2,1)} %get-tuple-element.40), channel_id=1, source_target_pairs={{0,12},{4,8},{8,4},{12,0},{1,13},{5,9},{9,5},{13,1},{2,14},{6,10},... | collective-permute-start | bytes 516104 | tf_op jit(solution)/shard_map/ppermute | solution.py:28
  14.8 7.8 %collective-permute-done.1.refs_2_.refs_5_.refs_1_ = bf16[672,128]{1,0:T(8,128)(2,1)S(1)} collective-permute-done((bf16[672,128]{1,0:T(8,128)(2,1)}, bf16[672,128]{1,0:T(8,128)(2,1)S(1)}, u32[]{:S(2)}, u32[]{:S(2)}) %collective-permute-start.1) | collective-permute-done | bytes 172064 | tf_op jit(solution)/shard_map/ppermute | solution.py:28
  23.0 1.6 %collective-permute-start.7 = (bf16[672,128]{1,0:T(8,128)(2,1)S(1)}, bf16[672,128]{1,0:T(8,128)(2,1)S(1)}, u32[]{:S(2)}, u32[]{:S(2)}) collective-permute-start(bf16[672,128]{1,0:T(8,128)(2,1)S(1)} %get-tuple-element.54), channel_id=1, source_target_pairs={{0,16},{16,0},{1,17},{17,1},{2,18},{18,2},{3,19},{19,3},{4,20},{20... | collective-permute-start | bytes 516104 | tf_op jit(solution)/shard_map/ppermute | solution.py:28
  24.7 2.5 %collective-permute-start.4 = (bf16[256,128]{1,0:T(8,128)(2,1)S(1)}, bf16[256,128]{1,0:T(8,128)(2,1)S(1)}, u32[]{:S(2)}, u32[]{:S(2)}) collective-permute-start(bf16[256,128]{1,0:T(8,128)(2,1)S(1)} %get-tuple-element.51), channel_id=1, source_target_pairs={{0,12},{4,8},{8,4},{12,0},{1,13},{5,9},{9,5},{13,1},{2,14},{6,10},... | collective-permute-start | bytes 196616 | tf_op jit(solution)/shard_map/ppermute | solution.py:28
  27.2 1.9 %collective-permute-start.6 = (bf16[256,128]{1,0:T(8,128)(2,1)S(1)}, bf16[256,128]{1,0:T(8,128)(2,1)S(1)}, u32[]{:S(2)}, u32[]{:S(2)}) collective-permute-start(bf16[256,128]{1,0:T(8,128)(2,1)S(1)} %get-tuple-element.53), channel_id=1, source_target_pairs={{0,4},{4,0},{8,12},{12,8},{1,5},{5,1},{9,13},{13,9},{2,6},{6,2},{1... | collective-permute-start | bytes 196616 | tf_op jit(solution)/shard_map/ppermute | solution.py:28
  29.8 1.7 %collective-permute-done.4.refs_1_.refs_3_ = bf16[256,128]{1,0:T(8,128)(2,1)S(1)} collective-permute-done((bf16[256,128]{1,0:T(8,128)(2,1)S(1)}, bf16[256,128]{1,0:T(8,128)(2,1)S(1)}, u32[]{:S(2)}, u32[]{:S(2)}) %collective-permute-start.4) | collective-permute-done | bytes 65568 | tf_op jit(solution)/shard_map/ppermute | solution.py:28
  31.5 2.0 %collective-permute-done.5.refs_2_.refs_4_ = bf16[256,128]{1,0:T(8,128)(2,1)S(1)} collective-permute-done((bf16[256,128]{1,0:T(8,128)(2,1)S(1)}, bf16[256,128]{1,0:T(8,128)(2,1)S(1)}, u32[]{:S(2)}, u32[]{:S(2)}) %collective-permute-start.5) | collective-permute-done | bytes 65568 | tf_op jit(solution)/shard_map/ppermute | solution.py:28
  33.5 1.7 %shard_map.162 = (f32[448,128]{1,0:T(8,128)S(1)}, f32[2,128,128]{2,1,0:T(8,128)S(1)}, bf16[2,128,128]{2,1,0:T(8,128)(2,1)S(1)}) custom-call(bf16[256,128]{1,0:T(8,128)(2,1)S(1)} %get-tuple-element.50.refs_0_, bf16[256,128]{1,0:T(8,128)(2,1)S(1)} %collective-permute-done.4.refs_1_.refs_3_, bf16[256,128]{1,0:T(8,128)(2,1)S(1)} %collective-permute-done.5.refs_2_.refs_4_, ...), custom_call_target="tpu_custom_call" | custom-call | flops 293601280 | bytes 4162048 | tf_op jit(solution)/shard_map/pallas_call | solution.py:266
  35.4 1.2 %collective-permute-done.8.got = bf16[2,128,128]{2,1,0:T(8,128)(2,1)S(1)} collective-permute-done((bf16[2,128,128]{2,1,0:T(8,128)(2,1)S(1)}, bf16[2,128,128]{2,1,0:T(8,128)(2,1)S(1)}, u32[]{:S(2)}, u32[]{:S(2)}) %collective-permute-start.8) | collective-permute-done | bytes 65568 | tf_op jit(solution)/shard_map/ppermute | solution.py:28
  36.6 2.5 %collective-permute-start.9 = (bf16[272,128]{1,0:T(8,128)(2,1)S(1)}, bf16[272,128]{1,0:T(8,128)(2,1)S(1)}, u32[]{:S(2)}, u32[]{:S(2)}) collective-permute-start(bf16[272,128]{1,0:T(8,128)(2,1)S(1)} %get-tuple-element.60), channel_id=1, source_target_pairs={{0,12},{4,8},{8,4},{12,0},{1,13},{5,9},{9,5},{13,1},{2,14},{6,10},... | collective-permute-start | bytes 208904 | tf_op jit(solution)/shard_map/ppermute | solution.py:28
  39.2 1.9 %collective-permute-start.11 = (bf16[272,128]{1,0:T(8,128)(2,1)S(1)}, bf16[272,128]{1,0:T(8,128)(2,1)S(1)}, u32[]{:S(2)}, u32[]{:S(2)}) collective-permute-start(bf16[272,128]{1,0:T(8,128)(2,1)S(1)} %get-tuple-element.62), channel_id=1, source_target_pairs={{0,4},{4,0},{8,12},{12,8},{1,5},{5,1},{9,13},{13,9},{2,6},{6,2},{1... | collective-permute-start | bytes 208904 | tf_op jit(solution)/shard_map/ppermute | solution.py:28
  41.1 2.5 %collective-permute-done.9.refs_1_.refs_5_.refs_6_ = bf16[272,128]{1,0:T(8,128)(2,1)S(1)} collective-permute-done((bf16[272,128]{1,0:T(8,128)(2,1)S(1)}, bf16[272,128]{1,0:T(8,128)(2,1)S(1)}, u32[]{:S(2)}, u32[]{:S(2)}) %collective-permute-start.9) | collective-permute-done | bytes 69664 | tf_op jit(solution)/shard_map/ppermute | solution.py:28
  43.6 2.1 %collective-permute-done.10.refs_2_.refs_6_.refs_7_ = bf16[272,128]{1,0:T(8,128)(2,1)S(1)} collective-permute-done((bf16[272,128]{1,0:T(8,128)(2,1)S(1)}, bf16[272,128]{1,0:T(8,128)(2,1)S(1)}, u32[]{:S(2)}, u32[]{:S(2)}) %collective-permute-start.10) | collective-permute-done | bytes 69664 | tf_op jit(solution)/shard_map/ppermute | solution.py:28
  45.9 1.2 %collective-permute-done.12.refs_1_.also = bf16[2,128,128]{2,1,0:T(8,128)(2,1)S(1)} collective-permute-done((bf16[2,128,128]{2,1,0:T(8,128)(2,1)S(1)}, bf16[2,128,128]{2,1,0:T(8,128)(2,1)S(1)}, u32[]{:S(2)}, u32[]{:S(2)}) %collective-permute-start.12) | collective-permute-done | bytes 65568 | tf_op jit(solution)/shard_map/ppermute | solution.py:28
  47.4 1.6 %collective-permute-start.13 = (bf16[448,128]{1,0:T(8,128)(2,1)S(1)}, bf16[448,128]{1,0:T(8,128)(2,1)S(1)}, u32[]{:S(2)}, u32[]{:S(2)}) collective-permute-start(bf16[448,128]{1,0:T(8,128)(2,1)S(1)} %get-tuple-element.65), channel_id=1, source_target_pairs={{0,2},{2,0},{1,3},{3,1},{4,6},{6,4},{5,7},{7,5},{8,10},{10,8},{9,1... | collective-permute-start | bytes 344072 | tf_op jit(solution)/shard_map/ppermute | solution.py:608
  49.3 3.4 %collective-permute-done.13.low = bf16[448,128]{1,0:T(8,128)(2,1)S(1)} collective-permute-done((bf16[448,128]{1,0:T(8,128)(2,1)S(1)}, bf16[448,128]{1,0:T(8,128)(2,1)S(1)}, u32[]{:S(2)}, u32[]{:S(2)}) %collective-permute-start.13) | collective-permute-done | bytes 114720 | tf_op jit(solution)/shard_map/ppermute | solution.py:608
  53.2 1.3 %collective-permute-done.14 = bf16[4,128,128]{2,1,0:T(8,128)(2,1)S(1)} collective-permute-done((bf16[4,128,128]{2,1,0:T(8,128)(2,1)S(1)}, bf16[4,128,128]{2,1,0:T(8,128)(2,1)S(1)}, u32[]{:S(2)}, u32[]{:S(2)}) %collective-permute-start.14) | collective-permute-done | bytes 131104 | tf_op jit(solution)/shard_map/ppermute | solution.py:28
  55.6 1.5 %collective-permute-start.20 = (bf16[2,448,128]{2,1,0:T(8,128)(2,1)S(1)}, bf16[2,448,128]{2,1,0:T(8,128)(2,1)S(1)}, u32[]{:S(2)}, u32[]{:S(2)}) collective-permute-start(bf16[2,448,128]{2,1,0:T(8,128)(2,1)S(1)} %shard_map.166), channel_id=1, source_target_pairs={{0,2},{2,0},{1,3},{3,1},{4,6},{6,4},{5,7},{7,5},{8,10},{10,8},{9,1... | collective-permute-start | bytes 688136 | tf_op jit(solution)/shard_map/ppermute | solution.py:608
  57.0 2.2 %collective-permute-start.15 = (bf16[2,128,128]{2,1,0:T(8,128)(2,1)S(1)}, bf16[2,128,128]{2,1,0:T(8,128)(2,1)S(1)}, u32[]{:S(2)}, u32[]{:S(2)}) collective-permute-start(bf16[2,128,128]{2,1,0:T(8,128)(2,1)S(1)} %get-tuple-element.79), channel_id=1, source_target_pairs={{0,4},{4,0},{8,12},{12,8},{1,5},{5,1},{9,13},{13,9},{2,6},{6,2},{1... | collective-permute-start | bytes 196616 | tf_op jit(solution)/shard_map/ppermute | solution.py:28
  59.2 2.0 %collective-permute-done.17 = bf16[2,128,128]{2,1,0:T(8,128)(2,1)S(1)} collective-permute-done((bf16[2,128,128]{2,1,0:T(8,128)(2,1)S(1)}, bf16[2,128,128]{2,1,0:T(8,128)(2,1)S(1)}, u32[]{:S(2)}, u32[]{:S(2)}) %collective-permute-start.17) | collective-permute-done | bytes 65568 | tf_op jit(solution)/shard_map/ppermute | solution.py:28
  62.2 1.5 %collective-permute-start.16 = (bf16[2,128,128]{2,1,0:T(8,128)(2,1)S(1)}, bf16[2,128,128]{2,1,0:T(8,128)(2,1)S(1)}, u32[]{:S(2)}, u32[]{:S(2)}) collective-permute-start(bf16[2,128,128]{2,1,0:T(8,128)(2,1)S(1)} %add_convert_fusion.2.even), channel_id=1, source_target_pairs={{0,8},{4,12},{8,0},{12,4},{1,9},{5,13},{9,1},{13,5},{2,10},{6,14},... | collective-permute-start | bytes 196616 | tf_op jit(solution)/shard_map/ppermute | solution.py:28
  63.8 2.4 %collective-permute-done.18.odd_got = bf16[2,128,128]{2,1,0:T(8,128)(2,1)S(1)} collective-permute-done((bf16[2,128,128]{2,1,0:T(8,128)(2,1)S(1)}, bf16[2,128,128]{2,1,0:T(8,128)(2,1)S(1)}, u32[]{:S(2)}, u32[]{:S(2)}) %collective-permute-start.18) | collective-permute-done | bytes 65568 | tf_op jit(solution)/shard_map/ppermute | solution.py:28
  66.1 1.4 %collective-permute-done.16.even_got = bf16[2,128,128]{2,1,0:T(8,128)(2,1)S(1)} collective-permute-done((bf16[2,128,128]{2,1,0:T(8,128)(2,1)S(1)}, bf16[2,128,128]{2,1,0:T(8,128)(2,1)S(1)}, u32[]{:S(2)}, u32[]{:S(2)}) %collective-permute-start.16) | collective-permute-done | bytes 65568 | tf_op jit(solution)/shard_map/ppermute | solution.py:28
  67.7 1.3 %collective-permute-done.19.also = bf16[4,128,128]{2,1,0:T(8,128)(2,1)S(1)} collective-permute-done((bf16[4,128,128]{2,1,0:T(8,128)(2,1)S(1)}, bf16[4,128,128]{2,1,0:T(8,128)(2,1)S(1)}, u32[]{:S(2)}, u32[]{:S(2)}) %collective-permute-start.19) | collective-permute-done | bytes 131104 | tf_op jit(solution)/shard_map/ppermute | solution.py:28
  69.0 1.7 %shard_map.169 = (f32[448,128]{1,0:T(8,128)S(1)}, f32[2,128,128]{2,1,0:T(8,128)S(1)}, bf16[2,128,128]{2,1,0:T(8,128)(2,1)S(1)}) custom-call(bf16[4,128,128]{2,1,0:T(8,128)(2,1)S(1)} %shard_map.168.mine, bf16[4,128,128]{2,1,0:T(8,128)(2,1)S(1)} %collective-permute-done.19.also, bf16[448,128]{1,0:T(8,128)(2,1)S(1)} %collective-permute-done.13.low, ...), custom_call_target="tpu_custom_call" | custom-call | flops 293601280 | bytes 4276736 | tf_op jit(solution)/shard_map/pallas_call | solution.py:266
  71.0 1.1 %collective-permute-done.21 = bf16[2,128,128]{2,1,0:T(8,128)(2,1)S(1)} collective-permute-done((bf16[2,128,128]{2,1,0:T(8,128)(2,1)S(1)}, bf16[2,128,128]{2,1,0:T(8,128)(2,1)S(1)}, u32[]{:S(2)}, u32[]{:S(2)}) %collective-permute-start.21) | collective-permute-done | bytes 65568 | tf_op jit(solution)/shard_map/ppermute | solution.py:28
  72.1 2.6 %collective-permute-start.24 = (bf16[256,128]{1,0:T(8,128)(2,1)S(1)}, bf16[256,128]{1,0:T(8,128)(2,1)S(1)}, u32[]{:S(2)}, u32[]{:S(2)}) collective-permute-start(bf16[256,128]{1,0:T(8,128)(2,1)S(1)} %bitcast.43), channel_id=1, source_target_pairs={{0,12},{4,8},{8,4},{12,0},{1,13},{5,9},{9,5},{13,1},{2,14},{6,10},... | collective-permute-start | bytes 196616 | tf_op jit(solution)/shard_map/ppermute | solution.py:28
  74.9 1.7 %collective-permute-start.22 = (bf16[256,128]{1,0:T(8,128)(2,1)S(1)}, bf16[256,128]{1,0:T(8,128)(2,1)S(1)}, u32[]{:S(2)}, u32[]{:S(2)}) collective-permute-start(bf16[256,128]{1,0:T(8,128)(2,1)S(1)} %bitcast.45), channel_id=1, source_target_pairs={{0,4},{4,0},{8,12},{12,8},{1,5},{5,1},{9,13},{13,9},{2,6},{6,2},{1... | collective-permute-start | bytes 196616 | tf_op jit(solution)/shard_map/ppermute | solution.py:28
  76.6 2.4 %collective-permute-done.24.refs_3_ = bf16[256,128]{1,0:T(8,128)(2,1)S(1)} collective-permute-done((bf16[256,128]{1,0:T(8,128)(2,1)S(1)}, bf16[256,128]{1,0:T(8,128)(2,1)S(1)}, u32[]{:S(2)}, u32[]{:S(2)}) %collective-permute-start.24) | collective-permute-done | bytes 65568 | tf_op jit(solution)/shard_map/ppermute | solution.py:28
  78.9 2.4 %collective-permute-done.23.refs_2_ = bf16[256,128]{1,0:T(8,128)(2,1)S(1)} collective-permute-done((bf16[256,128]{1,0:T(8,128)(2,1)S(1)}, bf16[256,128]{1,0:T(8,128)(2,1)S(1)}, u32[]{:S(2)}, u32[]{:S(2)}) %collective-permute-start.23) | collective-permute-done | bytes 65568 | tf_op jit(solution)/shard_map/ppermute | solution.py:28
  81.5 1.2 %collective-permute-done.25.refs_1_ = bf16[2,128,128]{2,1,0:T(8,128)(2,1)S(1)} collective-permute-done((bf16[2,128,128]{2,1,0:T(8,128)(2,1)S(1)}, bf16[2,128,128]{2,1,0:T(8,128)(2,1)S(1)}, u32[]{:S(2)}, u32[]{:S(2)}) %collective-permute-start.25) | collective-permute-done | bytes 65568 | tf_op jit(solution)/shard_map/ppermute | solution.py:28
  (67 shorter events, 12.5 us)
Async XLA Ops:
  0.6 22.0 %copy-start = (bf16[1,1,1792,256]{3,2,1,0:T(8,128)(2,1)S(1)}, bf16[1,1,1792,256]{3,2,1,0:T(8,128)(2,1)}, u32[]{:S(2)}) copy-start(bf16[1,1,1792,256]{3,2,1,0:T(8,128)(2,1)} %param.20) | copy-start | bytes 2752516
  0.6 22.0 %copy-start.4 = (f32[128,1,448]{0,2,1:T(8,128)S(1)}, f32[128,1,448]{0,2,1:T(8,128)}, u32[]{:S(2)}) copy-start(f32[128,1,448]{0,2,1:T(8,128)} %param.15) | copy-start | bytes 688132
  0.6 32.9 %copy-start.9 = (f32[1,128]{1,0:T(1,128)S(1)}, f32[1,128]{1,0:T(1,128)}, u32[]{:S(2)}) copy-start(f32[1,128]{1,0:T(1,128)} %refs_6_.1) | copy-start | bytes 1540
  2.7 30.9 %copy-start.2 = (bf16[1,4,256,2,1,448]{2,5,4,3,1,0:T(8,128)(2,1)S(1)}, bf16[1,4,256,2,1,448]{2,5,4,3,1,0:T(8,128)(2,1)}, u32[]{:S(2)}) copy-start(bf16[1,4,256,2,1,448]{2,5,4,3,1,0:T(8,128)(2,1)} %param.21) | copy-start | bytes 5505028
  2.7 30.9 %copy-start.3 = (bf16[1,1,1792,128]{3,2,1,0:T(8,128)(2,1)S(1)}, bf16[1,1,1792,128]{3,2,1,0:T(8,128)(2,1)}, u32[]{:S(2)}) copy-start(bf16[1,1,1792,128]{3,2,1,0:T(8,128)(2,1)} %param.22) | copy-start | bytes 1376260
  2.7 12.1 %collective-permute-start = (bf16[672,128]{1,0:T(8,128)(2,1)}, bf16[672,128]{1,0:T(8,128)(2,1)S(1)}, u32[]{:S(2)}, u32[]{:S(2)}) collective-permute-start(bf16[672,128]{1,0:T(8,128)(2,1)} %get-tuple-element.40), channel_id=1, source_target_pairs={{0,12},{4,8},{8,4},{12,0},{1,13},{5,9},{9,5},{13,1},{2,14},{6,10},... | collective-permute-start | bytes 516104 | tf_op jit(solution)/shard_map/ppermute | solution.py:28
  7.8 14.8 %collective-permute-start.1 = (bf16[672,128]{1,0:T(8,128)(2,1)}, bf16[672,128]{1,0:T(8,128)(2,1)S(1)}, u32[]{:S(2)}, u32[]{:S(2)}) collective-permute-start(bf16[672,128]{1,0:T(8,128)(2,1)} %get-tuple-element.47), channel_id=1, source_target_pairs={{0,8},{4,12},{8,0},{12,4},{1,9},{5,13},{9,1},{13,5},{2,10},{6,14},... | collective-permute-start | bytes 516104 | tf_op jit(solution)/shard_map/ppermute | solution.py:28
  7.8 14.8 %collective-permute-start.2 = (bf16[672,128]{1,0:T(8,128)(2,1)}, bf16[672,128]{1,0:T(8,128)(2,1)S(1)}, u32[]{:S(2)}, u32[]{:S(2)}) collective-permute-start(bf16[672,128]{1,0:T(8,128)(2,1)} %get-tuple-element.48), channel_id=1, source_target_pairs={{0,4},{4,0},{8,12},{12,8},{1,5},{5,1},{9,13},{13,9},{2,6},{6,2},{1... | collective-permute-start | bytes 516104 | tf_op jit(solution)/shard_map/ppermute | solution.py:28
  22.9 1.7 %collective-permute-start.3 = (f32[128,256]{1,0:T(8,128)S(1)}, f32[128,256]{1,0:T(8,128)S(1)}, u32[]{:S(2)}, u32[]{:S(2)}) collective-permute-start(f32[128,256]{1,0:T(8,128)S(1)} %get-tuple-element.49.own), channel_id=1, source_target_pairs={{0,1},{1,0},{2,3},{3,2},{4,5},{5,4},{6,7},{7,6},{8,9},{9,8},{10,11... | collective-permute-start | bytes 393224 | tf_op jit(solution)/shard_map/ppermute | solution.py:28
  23.0 6.8 %collective-permute-start.7 = (bf16[672,128]{1,0:T(8,128)(2,1)S(1)}, bf16[672,128]{1,0:T(8,128)(2,1)S(1)}, u32[]{:S(2)}, u32[]{:S(2)}) collective-permute-start(bf16[672,128]{1,0:T(8,128)(2,1)S(1)} %get-tuple-element.54), channel_id=1, source_target_pairs={{0,16},{16,0},{1,17},{17,1},{2,18},{18,2},{3,19},{19,3},{4,20},{20... | collective-permute-start | bytes 516104 | tf_op jit(solution)/shard_map/ppermute | solution.py:28
  24.7 6.8 %collective-permute-start.4 = (bf16[256,128]{1,0:T(8,128)(2,1)S(1)}, bf16[256,128]{1,0:T(8,128)(2,1)S(1)}, u32[]{:S(2)}, u32[]{:S(2)}) collective-permute-start(bf16[256,128]{1,0:T(8,128)(2,1)S(1)} %get-tuple-element.51), channel_id=1, source_target_pairs={{0,12},{4,8},{8,4},{12,0},{1,13},{5,9},{9,5},{13,1},{2,14},{6,10},... | collective-permute-start | bytes 196616 | tf_op jit(solution)/shard_map/ppermute | solution.py:28
  27.2 6.3 %collective-permute-start.5 = (bf16[256,128]{1,0:T(8,128)(2,1)S(1)}, bf16[256,128]{1,0:T(8,128)(2,1)S(1)}, u32[]{:S(2)}, u32[]{:S(2)}) collective-permute-start(bf16[256,128]{1,0:T(8,128)(2,1)S(1)} %get-tuple-element.52), channel_id=1, source_target_pairs={{0,8},{4,12},{8,0},{12,4},{1,9},{5,13},{9,1},{13,5},{2,10},{6,14},... | collective-permute-start | bytes 196616 | tf_op jit(solution)/shard_map/ppermute | solution.py:28
  27.2 6.3 %collective-permute-start.6 = (bf16[256,128]{1,0:T(8,128)(2,1)S(1)}, bf16[256,128]{1,0:T(8,128)(2,1)S(1)}, u32[]{:S(2)}, u32[]{:S(2)}) collective-permute-start(bf16[256,128]{1,0:T(8,128)(2,1)S(1)} %get-tuple-element.53), channel_id=1, source_target_pairs={{0,4},{4,0},{8,12},{12,8},{1,5},{5,1},{9,13},{13,9},{2,6},{6,2},{1... | collective-permute-start | bytes 196616 | tf_op jit(solution)/shard_map/ppermute | solution.py:28
  35.3 11.9 %copy-start.1 = (bf16[1,2,512,1,448]{2,4,3,1,0:T(8,128)(2,1)S(1)}, bf16[1,2,512,1,448]{2,4,3,1,0:T(8,128)(2,1)}, u32[]{:S(2)}) copy-start(bf16[1,2,512,1,448]{2,4,3,1,0:T(8,128)(2,1)} %param.24) | copy-start | bytes 2752516
  35.3 1.3 %collective-permute-start.8 = (bf16[2,128,128]{2,1,0:T(8,128)(2,1)S(1)}, bf16[2,128,128]{2,1,0:T(8,128)(2,1)S(1)}, u32[]{:S(2)}, u32[]{:S(2)}) collective-permute-start(bf16[2,128,128]{2,1,0:T(8,128)(2,1)S(1)} %get-tuple-element.57), channel_id=1, source_target_pairs={{0,1},{1,0},{2,3},{3,2},{4,5},{5,4},{6,7},{7,6},{8,9},{9,8},{10,11... | collective-permute-start | bytes 196616 | tf_op jit(solution)/shard_map/ppermute | solution.py:28
  36.6 7.0 %collective-permute-start.9 = (bf16[272,128]{1,0:T(8,128)(2,1)S(1)}, bf16[272,128]{1,0:T(8,128)(2,1)S(1)}, u32[]{:S(2)}, u32[]{:S(2)}) collective-permute-start(bf16[272,128]{1,0:T(8,128)(2,1)S(1)} %get-tuple-element.60), channel_id=1, source_target_pairs={{0,12},{4,8},{8,4},{12,0},{1,13},{5,9},{9,5},{13,1},{2,14},{6,10},... | collective-permute-start | bytes 208904 | tf_op jit(solution)/shard_map/ppermute | solution.py:28
  39.2 6.6 %collective-permute-start.10 = (bf16[272,128]{1,0:T(8,128)(2,1)S(1)}, bf16[272,128]{1,0:T(8,128)(2,1)S(1)}, u32[]{:S(2)}, u32[]{:S(2)}) collective-permute-start(bf16[272,128]{1,0:T(8,128)(2,1)S(1)} %get-tuple-element.61), channel_id=1, source_target_pairs={{0,8},{4,12},{8,0},{12,4},{1,9},{5,13},{9,1},{13,5},{2,10},{6,14},... | collective-permute-start | bytes 208904 | tf_op jit(solution)/shard_map/ppermute | solution.py:28
  39.2 6.6 %collective-permute-start.11 = (bf16[272,128]{1,0:T(8,128)(2,1)S(1)}, bf16[272,128]{1,0:T(8,128)(2,1)S(1)}, u32[]{:S(2)}, u32[]{:S(2)}) collective-permute-start(bf16[272,128]{1,0:T(8,128)(2,1)S(1)} %get-tuple-element.62), channel_id=1, source_target_pairs={{0,4},{4,0},{8,12},{12,8},{1,5},{5,1},{9,13},{13,9},{2,6},{6,2},{1... | collective-permute-start | bytes 208904 | tf_op jit(solution)/shard_map/ppermute | solution.py:28
  45.8 1.3 %collective-permute-start.12 = (bf16[2,128,128]{2,1,0:T(8,128)(2,1)S(1)}, bf16[2,128,128]{2,1,0:T(8,128)(2,1)S(1)}, u32[]{:S(2)}, u32[]{:S(2)}) collective-permute-start(bf16[2,128,128]{2,1,0:T(8,128)(2,1)S(1)} %shard_map.164.refs_0_.mine), channel_id=1, source_target_pairs={{0,1},{1,0},{2,3},{3,2},{4,5},{5,4},{6,7},{7,6},{8,9},{9,8},{10,11... | collective-permute-start | bytes 196616 | tf_op jit(solution)/shard_map/ppermute | solution.py:28
  47.4 5.3 %collective-permute-start.13 = (bf16[448,128]{1,0:T(8,128)(2,1)S(1)}, bf16[448,128]{1,0:T(8,128)(2,1)S(1)}, u32[]{:S(2)}, u32[]{:S(2)}) collective-permute-start(bf16[448,128]{1,0:T(8,128)(2,1)S(1)} %get-tuple-element.65), channel_id=1, source_target_pairs={{0,2},{2,0},{1,3},{3,1},{4,6},{6,4},{5,7},{7,5},{8,10},{10,8},{9,1... | collective-permute-start | bytes 344072 | tf_op jit(solution)/shard_map/ppermute | solution.py:608
  53.2 1.4 %collective-permute-start.14 = (bf16[4,128,128]{2,1,0:T(8,128)(2,1)S(1)}, bf16[4,128,128]{2,1,0:T(8,128)(2,1)S(1)}, u32[]{:S(2)}, u32[]{:S(2)}) collective-permute-start(bf16[4,128,128]{2,1,0:T(8,128)(2,1)S(1)} %get-tuple-element.69), channel_id=1, source_target_pairs={{0,1},{1,0},{2,3},{3,2},{4,5},{5,4},{6,7},{7,6},{8,9},{9,8},{10,11... | collective-permute-start | bytes 393224 | tf_op jit(solution)/shard_map/ppermute | solution.py:28
  54.6 6.6 %collective-permute-start.17 = (bf16[2,128,128]{2,1,0:T(8,128)(2,1)S(1)}, bf16[2,128,128]{2,1,0:T(8,128)(2,1)S(1)}, u32[]{:S(2)}, u32[]{:S(2)}) collective-permute-start(bf16[2,128,128]{2,1,0:T(8,128)(2,1)S(1)} %get-tuple-element.78), channel_id=1, source_target_pairs={{0,8},{4,12},{8,0},{12,4},{1,9},{5,13},{9,1},{13,5},{2,10},{6,14},... | collective-permute-start | bytes 196616 | tf_op jit(solution)/shard_map/ppermute | solution.py:28
  55.6 12.1 %collective-permute-start.20 = (bf16[2,448,128]{2,1,0:T(8,128)(2,1)S(1)}, bf16[2,448,128]{2,1,0:T(8,128)(2,1)S(1)}, u32[]{:S(2)}, u32[]{:S(2)}) collective-permute-start(bf16[2,448,128]{2,1,0:T(8,128)(2,1)S(1)} %shard_map.166), channel_id=1, source_target_pairs={{0,2},{2,0},{1,3},{3,1},{4,6},{6,4},{5,7},{7,5},{8,10},{10,8},{9,1... | collective-permute-start | bytes 688136 | tf_op jit(solution)/shard_map/ppermute | solution.py:608
  57.0 5.2 %collective-permute-start.15 = (bf16[2,128,128]{2,1,0:T(8,128)(2,1)S(1)}, bf16[2,128,128]{2,1,0:T(8,128)(2,1)S(1)}, u32[]{:S(2)}, u32[]{:S(2)}) collective-permute-start(bf16[2,128,128]{2,1,0:T(8,128)(2,1)S(1)} %get-tuple-element.79), channel_id=1, source_target_pairs={{0,4},{4,0},{8,12},{12,8},{1,5},{5,1},{9,13},{13,9},{2,6},{6,2},{1... | collective-permute-start | bytes 196616 | tf_op jit(solution)/shard_map/ppermute | solution.py:28
  61.3 4.8 %collective-permute-start.18 = (bf16[2,128,128]{2,1,0:T(8,128)(2,1)S(1)}, bf16[2,128,128]{2,1,0:T(8,128)(2,1)S(1)}, u32[]{:S(2)}, u32[]{:S(2)}) collective-permute-start(bf16[2,128,128]{2,1,0:T(8,128)(2,1)S(1)} %add_convert_fusion.1.odd), channel_id=1, source_target_pairs={{0,4},{4,0},{8,12},{12,8},{1,5},{5,1},{9,13},{13,9},{2,6},{6,2},{1... | collective-permute-start | bytes 196616 | tf_op jit(solution)/shard_map/ppermute | solution.py:28
  62.2 5.3 %collective-permute-start.16 = (bf16[2,128,128]{2,1,0:T(8,128)(2,1)S(1)}, bf16[2,128,128]{2,1,0:T(8,128)(2,1)S(1)}, u32[]{:S(2)}, u32[]{:S(2)}) collective-permute-start(bf16[2,128,128]{2,1,0:T(8,128)(2,1)S(1)} %add_convert_fusion.2.even), channel_id=1, source_target_pairs={{0,8},{4,12},{8,0},{12,4},{1,9},{5,13},{9,1},{13,5},{2,10},{6,14},... | collective-permute-start | bytes 196616 | tf_op jit(solution)/shard_map/ppermute | solution.py:28
  67.6 1.4 %collective-permute-start.19 = (bf16[4,128,128]{2,1,0:T(8,128)(2,1)S(1)}, bf16[4,128,128]{2,1,0:T(8,128)(2,1)S(1)}, u32[]{:S(2)}, u32[]{:S(2)}) collective-permute-start(bf16[4,128,128]{2,1,0:T(8,128)(2,1)S(1)} %shard_map.168.mine), channel_id=1, source_target_pairs={{0,1},{1,0},{2,3},{3,2},{4,5},{5,4},{6,7},{7,6},{8,9},{9,8},{10,11... | collective-permute-start | bytes 393224 | tf_op jit(solution)/shard_map/ppermute | solution.py:28
  70.8 1.3 %collective-permute-start.21 = (bf16[2,128,128]{2,1,0:T(8,128)(2,1)S(1)}, bf16[2,128,128]{2,1,0:T(8,128)(2,1)S(1)}, u32[]{:S(2)}, u32[]{:S(2)}) collective-permute-start(bf16[2,128,128]{2,1,0:T(8,128)(2,1)S(1)} %get-tuple-element.72), channel_id=1, source_target_pairs={{0,1},{1,0},{2,3},{3,2},{4,5},{5,4},{6,7},{7,6},{8,9},{9,8},{10,11... | collective-permute-start | bytes 196616 | tf_op jit(solution)/shard_map/ppermute | solution.py:28
  72.1 6.8 %collective-permute-start.24 = (bf16[256,128]{1,0:T(8,128)(2,1)S(1)}, bf16[256,128]{1,0:T(8,128)(2,1)S(1)}, u32[]{:S(2)}, u32[]{:S(2)}) collective-permute-start(bf16[256,128]{1,0:T(8,128)(2,1)S(1)} %bitcast.43), channel_id=1, source_target_pairs={{0,12},{4,8},{8,4},{12,0},{1,13},{5,9},{9,5},{13,1},{2,14},{6,10},... | collective-permute-start | bytes 196616 | tf_op jit(solution)/shard_map/ppermute | solution.py:28
  74.7 6.6 %collective-permute-start.23 = (bf16[256,128]{1,0:T(8,128)(2,1)S(1)}, bf16[256,128]{1,0:T(8,128)(2,1)S(1)}, u32[]{:S(2)}, u32[]{:S(2)}) collective-permute-start(bf16[256,128]{1,0:T(8,128)(2,1)S(1)} %bitcast.44), channel_id=1, source_target_pairs={{0,8},{4,12},{8,0},{12,4},{1,9},{5,13},{9,1},{13,5},{2,10},{6,14},... | collective-permute-start | bytes 196616 | tf_op jit(solution)/shard_map/ppermute | solution.py:28
  74.9 6.5 %collective-permute-start.22 = (bf16[256,128]{1,0:T(8,128)(2,1)S(1)}, bf16[256,128]{1,0:T(8,128)(2,1)S(1)}, u32[]{:S(2)}, u32[]{:S(2)}) collective-permute-start(bf16[256,128]{1,0:T(8,128)(2,1)S(1)} %bitcast.45), channel_id=1, source_target_pairs={{0,4},{4,0},{8,12},{12,8},{1,5},{5,1},{9,13},{13,9},{2,6},{6,2},{1... | collective-permute-start | bytes 196616 | tf_op jit(solution)/shard_map/ppermute | solution.py:28
  81.4 1.3 %collective-permute-start.25 = (bf16[2,128,128]{2,1,0:T(8,128)(2,1)S(1)}, bf16[2,128,128]{2,1,0:T(8,128)(2,1)S(1)}, u32[]{:S(2)}, u32[]{:S(2)}) collective-permute-start(bf16[2,128,128]{2,1,0:T(8,128)(2,1)S(1)} %shard_map.170.refs_0_), channel_id=1, source_target_pairs={{0,1},{1,0},{2,3},{3,2},{4,5},{5,4},{6,7},{7,6},{8,9},{9,8},{10,11... | collective-permute-start | bytes 196616 | tf_op jit(solution)/shard_map/ppermute | solution.py:28
  (8 other events, 16.9 us)
